TPU v7x, 512 devices: a whole 4x4x16 slice. The times are simulated.
512 devices in a mesh: shot: 32 (over y, z_lo), dom: 16 (over z_hi, x, core).
Axes of the slice: x: 4, y: 4, z: 16 (z_hi: 2, z_lo: 8; z = z_hi * 8 + z_lo), core: 2. Of those that a mesh axis runs over, the one named last changes fastest.
Arguments:
- pressure_now: float32 [32, 128, 32, 128], P('shot', 'dom'), may hold values from -6 to 6
- pressure_prev: float32 [32, 128, 32, 128], P('shot', 'dom'), may hold values from -6 to 6
- adjoint_last: float32 [32, 128, 32, 128], P('shot', 'dom'), may hold values from -6 to 6
- adjoint_after: float32 [32, 128, 32, 128], P('shot', 'dom'), may hold values from -6 to 6
- kappa_model: float32 [4, 128, 4096], P(None, 'dom', 'shot'), may hold values from 1 to 4
- buoy_model: float32 [4, 128, 4096], P(None, 'dom', 'shot'), may hold values from 0.5 to 2
- aperture: int32 [32, 16], replicated, may hold values from 0 to 3
- source_cell: int32 [32], P('shot'), may hold values from 0 to 524287
- source_wave: float32 [32, 3], P('shot'), may hold values from -8 to 8
- receiver_cell: int32 [32, 512], P('shot'), may hold values from 0 to 524287
- observed: float32 [32, 3, 512], P('shot'), may hold values from -6 to 6
Outputs:
- grad_kappa: float32 [4, 128, 4096], P(None, 'dom', 'shot')
- grad_buoy: float32 [4, 128, 4096], P(None, 'dom', 'shot')
- adjoint_first: float32 [32, 128, 32, 128], P('shot', 'dom')
- adjoint_second: float32 [32, 128, 32, 128], P('shot', 'dom')
Inputs may be any that keep to these rules, and one draw needn't show every extreme that they name: `aperture`: the tile of the survey model that lies under slab x // 8 of each shot. `source_cell`: a flat cell index x * 32 * 128 + y * 128 + z of the shot's grid. `receiver_cell`: flat cell indices x * 32 * 128 + y * 128 + z of the shot's grid; cells may repeat.
All inputs are finite; a program needn't handle non-finite values.
Results may differ from a plain program's by a relative error of at most 0.0003.
Values sent between devices are 32-bit elements; how exact they have to be, the bound alone decides.
No kernel may reach another device: no remote copies, remote signals or barrier semaphores. Data moves between devices by JAX's collectives and lax.ppermute only.
A program may use at most 64 MiB of HBM per device.

v0:
```python
import jax
import jax.numpy as jnp
from jax import lax
from jax.sharding import PartitionSpec as P

CY = 32
CZ = 128
TILES = 4
STEPS = 3


COEFFS = (1225.0 / 1024.0, -245.0 / 3072.0, 49.0 / 5120.0, -5.0 / 7168.0)
step_squared = 0.02


def extended(cells, sides, width):
    for axis, dim in sides:
        count = lax.axis_size(axis)
        ends = count - 1
        head = lax.slice_in_dim(cells, 0, width, axis=dim)
        tail = lax.slice_in_dim(cells, cells.shape[dim] - width, cells.shape[dim], axis=dim)
        cells = jnp.concatenate(
            [
                lax.ppermute(tail, axis, [(i, (i + 1) % count) for i in range(ends)]),
                cells,
                lax.ppermute(head, axis, [((i + 1) % count, i) for i in range(ends)]),
            ],
            axis=dim,
        )
    return cells


def minus_diff(wavefield, dim_axis):
    length = wavefield.shape[dim_axis]
    widths = [(0, 0), (0, 0), (0, 0)]
    widths[dim_axis] = (4, 4)
    padded = jnp.pad(wavefield, widths)
    summed = jnp.zeros_like(wavefield)
    for k, weight in enumerate(COEFFS):
        leading = lax.slice_in_dim(padded, 4 + k, 4 + k + length, axis=dim_axis)
        trailing = lax.slice_in_dim(padded, 3 - k, 3 - k + length, axis=dim_axis)
        summed = summed + weight * (leading - trailing)
    return summed


def plus_diff(wavefield, dim_axis):
    length = wavefield.shape[dim_axis]
    widths = [(0, 0), (0, 0), (0, 0)]
    widths[dim_axis] = (4, 4)
    padded = jnp.pad(wavefield, widths)
    summed = jnp.zeros_like(wavefield)
    for k, weight in enumerate(COEFFS):
        leading = lax.slice_in_dim(padded, 5 + k, 5 + k + length, axis=dim_axis)
        trailing = lax.slice_in_dim(padded, 4 - k, 4 - k + length, axis=dim_axis)
        summed = summed + weight * (leading - trailing)
    return summed


def slab_minus(widened, length):
    span = length + 7
    summed = jnp.zeros((span,) + widened.shape[1:], jnp.float32)
    for k, weight in enumerate(COEFFS):
        summed = summed + weight * (widened[4 + k : 4 + k + span] - widened[3 - k : 3 - k + span])
    return summed


def slab_plus(fluxes, length):
    summed = jnp.zeros((length,) + fluxes.shape[1:], jnp.float32)
    for k, weight in enumerate(COEFFS):
        summed = summed + weight * (fluxes[4 + k : 4 + k + length] - fluxes[3 - k : 3 - k + length])
    return summed


def widen(wavefield):
    return extended(wavefield, (("dom", 0),), 7)


def slab_operator(widened, buoy_wide, length):
    centre = widened[7 : 7 + length]
    slopes_x = slab_minus(widened, length)
    divergence = slab_plus(buoy_wide[1 : length + 8] * slopes_x, length)
    buoyancy = buoy_wide[4 : 4 + length]
    slope_y = minus_diff(centre, 1)
    slope_z = minus_diff(centre, 2)
    divergence = divergence + plus_diff(buoyancy * slope_y, 1)
    divergence = divergence + plus_diff(buoyancy * slope_z, 2)
    return (divergence, (slopes_x[3 : 3 + length], slope_y, slope_z))


def shards(
    pressure_now,
    pressure_prev,
    adjoint_last,
    adjoint_after,
    kappa_model,
    buoy_model,
    aperture,
    source_cell,
    source_wave,
    receiver_cell,
    observed,
):
    shot_index = lax.axis_index("shot")
    dom_index = lax.axis_index("dom")
    length = pressure_now.shape[1]
    grid_shape = (length, CY, CZ)
    cell_count = length * CY * CZ
    column = lax.dynamic_index_in_dim(aperture, dom_index, 1, keepdims=False)
    my_tile = lax.dynamic_index_in_dim(column, shot_index, 0, keepdims=False)
    tile_ids = jnp.arange(TILES, dtype=jnp.int32)
    stacked = jnp.stack((kappa_model, buoy_model))
    gathered = lax.all_gather(stacked, "shot", axis=3, tiled=True)
    my_block = lax.dynamic_index_in_dim(gathered, my_tile, 1, keepdims=False)
    stiffness = my_block[0].reshape(grid_shape)
    buoyancy = my_block[1].reshape(grid_shape)
    buoy_wide = extended(buoyancy, (("dom", 0),), 4)
    offset = dom_index * cell_count
    source_local = source_cell[0] - offset
    source_owned = (source_local >= 0) & (source_local < cell_count)
    source_slot = jnp.clip(source_local, 0, cell_count - 1)
    receiver_local = receiver_cell[0] - offset
    receiver_owned = (receiver_local >= 0) & (receiver_local < cell_count)
    receiver_slot = jnp.clip(receiver_local, 0, cell_count - 1)
    present = pressure_now[0]
    previous = pressure_prev[0]
    history = []
    residuals = []
    for n in range(STEPS):
        divergence, slopes = slab_operator(widen(present), buoy_wide, length)
        history.append((divergence, slopes))
        following = 2.0 * present - previous + step_squared * stiffness * divergence
        amount = jnp.where(source_owned, source_wave[0, n], 0.0)
        following = following.reshape(-1).at[source_slot].add(amount).reshape(grid_shape)
        recorded = following.reshape(-1)[receiver_slot]
        residuals.append(jnp.where(receiver_owned, recorded - observed[0, n], 0.0))
        previous, present = (present, following)
    current = adjoint_last[0]
    later = adjoint_after[0]
    image_kappa = jnp.zeros(grid_shape, jnp.float32)
    image_buoy = jnp.zeros(grid_shape, jnp.float32)
    for m in range(STEPS + 1, 0, -1):
        divergence, slopes = slab_operator(widen(stiffness * current), buoy_wide, length)
        if m <= STEPS:
            stored_div, stored_slopes = history[m - 1]
            image_kappa = image_kappa + current * stored_div
            image_buoy = image_buoy + (
                stored_slopes[0] * slopes[0]
                + stored_slopes[1] * slopes[1]
                + stored_slopes[2] * slopes[2]
            )
        if m >= 2:
            earlier = 2.0 * current - later + step_squared * divergence
            earlier = (
                earlier.reshape(-1).at[receiver_slot].add(residuals[m - 2]).reshape(grid_shape)
            )
            later, current = (current, earlier)
    image_stack = jnp.stack((step_squared * image_kappa, -step_squared * image_buoy)).reshape(
        2, length, CY * CZ
    )
    picked = (tile_ids == my_tile).astype(jnp.float32)
    spread = picked[None, :, None, None] * image_stack[:, None]
    owned = lax.psum_scatter(spread, "shot", scatter_dimension=3, tiled=True)
    return (owned[0], owned[1], current[None], later[None])


def solution(mesh):
    in_specs = (
        P("shot", "dom", None, None),
        P("shot", "dom", None, None),
        P("shot", "dom", None, None),
        P("shot", "dom", None, None),
        P(None, "dom", "shot"),
        P(None, "dom", "shot"),
        P(),
        P("shot"),
        P("shot", None),
        P("shot", None),
        P("shot", None, None),
    )
    out_specs = (
        P(None, "dom", "shot"),
        P(None, "dom", "shot"),
        P("shot", "dom", None, None),
        P("shot", "dom", None, None),
    )
    return jax.shard_map(shards, mesh=mesh, in_specs=in_specs, out_specs=out_specs, check_vma=False)
```

profile of v0, /device:TPU:4, one launch (start us, length us, event | category | flops | bytes accessed | tf_op | source)
XLA Modules:
  0.0 616.9 jit_solution(722540684135713405)
XLA Ops:
  9.7 1.9 collective-permute-start.5
  11.6 2.4 collective-permute-start.4
  21.8 174.4 %all-gather.2.cloned.1.call-done = f32[2,4,8,4096]{3,2,1,0:T(8,128)} async-done(((f32[2,4,8,128]{3,2,1,0:T(8,128)}), f32[2,4,8,4096]{3,2,1,0:T(8,128)}) %all-gather.2.cloned.1.call-update) | async-done | bytes 1048592 | tf_op jit(solution)/shard_map/all_gather | solution.py:112
  197.2 1.9 collective-permute-start.1
  199.2 2.4 collective-permute-start
  206.8 1.9 collective-permute-start.6
  208.7 3.6 collective-permute-start.7
  212.7 3.1 gather_fusion.2
  217.2 2.4 collective-permute-start.8
  219.5 3.2 collective-permute-start.9
  223.1 3.1 gather_fusion.1
  226.2 7.5 %collective-permute-done.9 = f32[7,32,128]{2,1,0:T(8,128)S(1)} collective-permute-done((f32[7,32,128]{2,1,0:T(8,128)S(1)}, f32[7,32,128]{2,1,0:T(8,128)S(1)}, u32[]{:S(2)}, u32[]{:S(2)}) %collective-permute-start.9) | collective-permute-done | bytes 114720 | tf_op jit(solution)/shard_map/ppermute | solution.py:26
  235.5 3.1 gather_fusion
  238.7 17.8 %collective-permute-start.2 = (f32[7,32,128]{2,1,0:T(8,128)S(1)}, f32[7,32,128]{2,1,0:T(8,128)S(1)}, u32[]{:S(2)}, u32[]{:S(2)}) collective-permute-start(f32[7,32,128]{2,1,0:T(8,128)S(1)} %get-tuple-element.114), channel_id=1, source_target_pairs={{0,1},{1,2},{2,3},{3,4},{4,5},{5,6},{6,7},{7,8},{8,9},{9,10},{10,1... | collective-permute-start | bytes 344072 | tf_op jit(solution)/shard_map/ppermute | solution.py:24
  258.4 2.3 collective-permute-done.3
  262.0 3.5 scatter_fusion
  265.6 3.9 collective-permute-start.11
  269.4 13.9 %collective-permute-start.10 = (f32[7,32,128]{2,1,0:T(8,128)S(1)}, f32[7,32,128]{2,1,0:T(8,128)S(1)}, u32[]{:S(2)}, u32[]{:S(2)}) collective-permute-start(f32[7,32,128]{2,1,0:T(8,128)S(1)} %get-tuple-element.105), channel_id=1, source_target_pairs={{0,1},{1,2},{2,3},{3,4},{4,5},{5,6},{6,7},{7,8},{8,9},{9,10},{10,1... | collective-permute-start | bytes 344072 | tf_op jit(solution)/shard_map/ppermute | solution.py:24
  284.8 3.5 scatter_fusion.1
  290.3 4.4 collective-permute-start.12
  296.9 3.5 scatter_fusion.2
  301.0 12.7 %collective-permute-start.14 = (f32[7,32,128]{2,1,0:T(8,128)S(1)}, f32[7,32,128]{2,1,0:T(8,128)S(1)}, u32[]{:S(2)}, u32[]{:S(2)}) collective-permute-start(f32[7,32,128]{2,1,0:T(8,128)S(1)} %get-tuple-element.100), channel_id=1, source_target_pairs={{0,1},{1,2},{2,3},{3,4},{4,5},{5,6},{6,7},{7,8},{8,9},{9,10},{10,1... | collective-permute-start | bytes 344072 | tf_op jit(solution)/shard_map/ppermute | solution.py:24
  316.3 12.7 %collective-permute-done.15 = f32[7,32,128]{2,1,0:T(8,128)S(1)} collective-permute-done((f32[7,32,128]{2,1,0:T(8,128)S(1)}, f32[7,32,128]{2,1,0:T(8,128)S(1)}, u32[]{:S(2)}, u32[]{:S(2)}) %collective-permute-start.15) | collective-permute-done | bytes 114720 | tf_op jit(solution)/shard_map/ppermute | solution.py:26
  331.7 277.0 %reduce-scatter.2.cloned.1.call-done = f32[2,4,8,128]{3,2,1,0:T(8,128)} async-done(((f32[2,4,8,4096]{3,2,1,0:T(8,128)}), f32[2,4,8,128]{3,2,1,0:T(8,128)}) %reduce-scatter.2.cloned.1.call-update) | async-done | bytes 32784 | tf_op jit(solution)/shard_map/reduce_scatter | solution.py:162
  (106 shorter events, 31.6 us)
Async XLA Ops:
  7.2 189.0 %all-gather.2.cloned.1.call-start = ((), (), s32[]{:S(2)}) async-start(), calls=%async_computation.1 | async-start | bytes 1081344 | tf_op jit(solution)/shard_map/all_gather | solution.py:112
  8.6 600.1 %reduce-scatter.2.cloned.1.call-start = ((), (), s32[]{:S(2)}) async-start(), calls=%async_computation.2 | async-start | bytes 1081344 | tf_op jit(solution)/shard_map/reduce_scatter | solution.py:162
  8.6 13.2 %copy-start.2 = (f32[1,8,32,128]{3,2,1,0:T(8,128)S(1)}, f32[1,8,32,128]{3,2,1,0:T(8,128)}, u32[]{:S(2)}) copy-start(f32[1,8,32,128]{3,2,1,0:T(8,128)} %param.17) | copy-start | bytes 393220
  9.7 12.1 %collective-permute-start.5 = (f32[7,32,128]{2,1,0:T(8,128)S(1)}, f32[7,32,128]{2,1,0:T(8,128)S(1)}, u32[]{:S(2)}, u32[]{:S(2)}) collective-permute-start(f32[7,32,128]{2,1,0:T(8,128)S(1)} %get-tuple-element.111), channel_id=1, source_target_pairs={{1,0},{2,1},{3,2},{4,3},{5,4},{6,5},{7,6},{8,7},{9,8},{10,9},{11,1... | collective-permute-start | bytes 344072 | tf_op jit(solution)/shard_map/ppermute | solution.py:26
  11.6 10.1 %collective-permute-start.4 = (f32[7,32,128]{2,1,0:T(8,128)S(1)}, f32[7,32,128]{2,1,0:T(8,128)S(1)}, u32[]{:S(2)}, u32[]{:S(2)}) collective-permute-start(f32[7,32,128]{2,1,0:T(8,128)S(1)} %get-tuple-element.112), channel_id=1, source_target_pairs={{0,1},{1,2},{2,3},{3,4},{4,5},{5,6},{6,7},{7,8},{8,9},{9,10},{10,1... | collective-permute-start | bytes 344072 | tf_op jit(solution)/shard_map/ppermute | solution.py:24
  15.4 1.3 copy-start.12
  197.2 5.7 collective-permute-start.1
  199.2 5.6 collective-permute-start
  206.8 9.0 %collective-permute-start.6 = (f32[7,32,128]{2,1,0:T(8,128)S(1)}, f32[7,32,128]{2,1,0:T(8,128)S(1)}, u32[]{:S(2)}, u32[]{:S(2)}) collective-permute-start(f32[7,32,128]{2,1,0:T(8,128)S(1)} %bitcast.114), channel_id=1, source_target_pairs={{0,1},{1,2},{2,3},{3,4},{4,5},{5,6},{6,7},{7,8},{8,9},{9,10},{10,1... | collective-permute-start | bytes 344072 | tf_op jit(solution)/shard_map/ppermute | solution.py:24
  208.7 7.1 %collective-permute-start.7 = (f32[7,32,128]{2,1,0:T(8,128)S(1)}, f32[7,32,128]{2,1,0:T(8,128)S(1)}, u32[]{:S(2)}, u32[]{:S(2)}) collective-permute-start(f32[7,32,128]{2,1,0:T(8,128)S(1)} %bitcast.112), channel_id=1, source_target_pairs={{1,0},{2,1},{3,2},{4,3},{5,4},{6,5},{7,6},{8,7},{9,8},{10,9},{11,1... | collective-permute-start | bytes 344072 | tf_op jit(solution)/shard_map/ppermute | solution.py:26
  217.2 9.0 %collective-permute-start.8 = (f32[7,32,128]{2,1,0:T(8,128)S(1)}, f32[7,32,128]{2,1,0:T(8,128)S(1)}, u32[]{:S(2)}, u32[]{:S(2)}) collective-permute-start(f32[7,32,128]{2,1,0:T(8,128)S(1)} %bitcast.115), channel_id=1, source_target_pairs={{0,1},{1,2},{2,3},{3,4},{4,5},{5,6},{6,7},{7,8},{8,9},{9,10},{10,1... | collective-permute-start | bytes 344072 | tf_op jit(solution)/shard_map/ppermute | solution.py:24
  219.5 14.2 %collective-permute-start.9 = (f32[7,32,128]{2,1,0:T(8,128)S(1)}, f32[7,32,128]{2,1,0:T(8,128)S(1)}, u32[]{:S(2)}, u32[]{:S(2)}) collective-permute-start(f32[7,32,128]{2,1,0:T(8,128)S(1)} %bitcast.113), channel_id=1, source_target_pairs={{1,0},{2,1},{3,2},{4,3},{5,4},{6,5},{7,6},{8,7},{9,8},{10,9},{11,1... | collective-permute-start | bytes 344072 | tf_op jit(solution)/shard_map/ppermute | solution.py:26
  238.7 19.7 %collective-permute-start.2 = (f32[7,32,128]{2,1,0:T(8,128)S(1)}, f32[7,32,128]{2,1,0:T(8,128)S(1)}, u32[]{:S(2)}, u32[]{:S(2)}) collective-permute-start(f32[7,32,128]{2,1,0:T(8,128)S(1)} %get-tuple-element.114), channel_id=1, source_target_pairs={{0,1},{1,2},{2,3},{3,4},{4,5},{5,6},{6,7},{7,8},{8,9},{9,10},{10,1... | collective-permute-start | bytes 344072 | tf_op jit(solution)/shard_map/ppermute | solution.py:24
  256.5 4.3 collective-permute-start.3
  265.6 18.7 %collective-permute-start.11 = (f32[7,32,128]{2,1,0:T(8,128)S(1)}, f32[7,32,128]{2,1,0:T(8,128)S(1)}, u32[]{:S(2)}, u32[]{:S(2)}) collective-permute-start(f32[7,32,128]{2,1,0:T(8,128)S(1)} %get-tuple-element.104), channel_id=1, source_target_pairs={{1,0},{2,1},{3,2},{4,3},{5,4},{6,5},{7,6},{8,7},{9,8},{10,9},{11,1... | collective-permute-start | bytes 344072 | tf_op jit(solution)/shard_map/ppermute | solution.py:26
  269.4 14.9 %collective-permute-start.10 = (f32[7,32,128]{2,1,0:T(8,128)S(1)}, f32[7,32,128]{2,1,0:T(8,128)S(1)}, u32[]{:S(2)}, u32[]{:S(2)}) collective-permute-start(f32[7,32,128]{2,1,0:T(8,128)S(1)} %get-tuple-element.105), channel_id=1, source_target_pairs={{0,1},{1,2},{2,3},{3,4},{4,5},{5,6},{6,7},{7,8},{8,9},{9,10},{10,1... | collective-permute-start | bytes 344072 | tf_op jit(solution)/shard_map/ppermute | solution.py:24
  288.3 12.1 %copy-start = (f32[32768]{0:T(1024)}, f32[32768]{0:T(1024)S(1)}, u32[]{:S(2)}) copy-start(f32[32768]{0:T(1024)S(1)} %scatter_fusion.1) | copy-start | bytes 393220
  288.3 7.3 %collective-permute-start.13 = (f32[7,32,128]{2,1,0:T(8,128)S(1)}, f32[7,32,128]{2,1,0:T(8,128)S(1)}, u32[]{:S(2)}, u32[]{:S(2)}) collective-permute-start(f32[7,32,128]{2,1,0:T(8,128)S(1)} %get-tuple-element.102), channel_id=1, source_target_pairs={{1,0},{2,1},{3,2},{4,3},{5,4},{6,5},{7,6},{8,7},{9,8},{10,9},{11,1... | collective-permute-start | bytes 344072 | tf_op jit(solution)/shard_map/ppermute | solution.py:26
  290.3 6.1 collective-permute-start.12
  296.8 3.5 copy-start.7
  296.9 3.5 copy-start.8
  301.0 15.3 %collective-permute-start.14 = (f32[7,32,128]{2,1,0:T(8,128)S(1)}, f32[7,32,128]{2,1,0:T(8,128)S(1)}, u32[]{:S(2)}, u32[]{:S(2)}) collective-permute-start(f32[7,32,128]{2,1,0:T(8,128)S(1)} %get-tuple-element.100), channel_id=1, source_target_pairs={{0,1},{1,2},{2,3},{3,4},{4,5},{5,6},{6,7},{7,8},{8,9},{9,10},{10,1... | collective-permute-start | bytes 344072 | tf_op jit(solution)/shard_map/ppermute | solution.py:24
  313.7 15.3 %collective-permute-start.15 = (f32[7,32,128]{2,1,0:T(8,128)S(1)}, f32[7,32,128]{2,1,0:T(8,128)S(1)}, u32[]{:S(2)}, u32[]{:S(2)}) collective-permute-start(f32[7,32,128]{2,1,0:T(8,128)S(1)} %get-tuple-element.101), channel_id=1, source_target_pairs={{1,0},{2,1},{3,2},{4,3},{5,4},{6,5},{7,6},{8,7},{9,8},{10,9},{11,1... | collective-permute-start | bytes 344072 | tf_op jit(solution)/shard_map/ppermute | solution.py:26
  329.0 1.0 copy-start.6
  (8 other events, 6.6 us)
Sparse Core Ops, SparseCore 0:
  10.6 185.5 all-gather.1
  331.9 276.8 reduce-scatter.1
where the time goes:
time: 618 us; the launch traced here: 617 us
  waiting for transfers between devices  477 us (77%)
  starting transfers between devices  78.2 us (13%)
  other arithmetic  21.9 us (4%)
  local copies, waits for them, and re-layouts  21.1 us (3%)
  between operations  19.1 us (3%)
    reduce_scatter x1, waiting for transfers between devices, shards(): owned = lax.psum_scatter(spread, 'shot', scatter_dimension=3, tiled=True)  277 us
    all_gather x1, waiting for transfers between devices, shards(): gathered = lax.all_gather(stacked, 'shot', axis=3, tiled=True)  174 us
    ppermute x8, starting transfers between devices, extended(): lax.ppermute(tail, axis, [(i, (i + 1) % count) for i in range(ends)])  57.8 us
    ppermute x8, waiting for transfers between devices, extended(): lax.ppermute(head, axis, [((i + 1) % count, i) for i in range(ends)])  22.5 us
    ppermute x8, starting transfers between devices, extended(): lax.ppermute(head, axis, [((i + 1) % count, i) for i in range(ends)])  20.3 us
  transfers between devices with their start and end apart: 18, of which 8 were waited for; matrix products, arithmetic and copies ran while one was open for 2% of the time, Pallas kernels for 0%

commit v1 on v0

--- a/solution.py
+++ b/solution.py
@@ -100,19 +100,19 @@
     receiver_cell,
     observed,
 ):
-    shot_index = lax.axis_index("shot")
     dom_index = lax.axis_index("dom")
     length = pressure_now.shape[1]
     grid_shape = (length, CY, CZ)
     cell_count = length * CY * CZ
     column = lax.dynamic_index_in_dim(aperture, dom_index, 1, keepdims=False)
-    my_tile = lax.dynamic_index_in_dim(column, shot_index, 0, keepdims=False)
-    tile_ids = jnp.arange(TILES, dtype=jnp.int32)
-    stacked = jnp.stack((kappa_model, buoy_model))
-    gathered = lax.all_gather(stacked, "shot", axis=3, tiled=True)
-    my_block = lax.dynamic_index_in_dim(gathered, my_tile, 1, keepdims=False)
-    stiffness = my_block[0].reshape(grid_shape)
-    buoyancy = my_block[1].reshape(grid_shape)
+    stacked = jnp.stack((kappa_model, buoy_model), axis=1)
+    picks = column[:, None, None, None]
+    chosen = stacked[0][None]
+    for t in range(1, TILES):
+        chosen = jnp.where(picks == t, stacked[t][None], chosen)
+    my_block = lax.all_to_all(chosen, "shot", 0, 0, tiled=True)
+    stiffness = my_block[:, 0].transpose(1, 0, 2)
+    buoyancy = my_block[:, 1].transpose(1, 0, 2)
     buoy_wide = extended(buoyancy, (("dom", 0),), 4)
     offset = dom_index * cell_count
     source_local = source_cell[0] - offset
@@ -154,13 +154,17 @@
                 earlier.reshape(-1).at[receiver_slot].add(residuals[m - 2]).reshape(grid_shape)
             )
             later, current = (current, earlier)
-    image_stack = jnp.stack((step_squared * image_kappa, -step_squared * image_buoy)).reshape(
-        2, length, CY * CZ
+    image_stack = jnp.stack((step_squared * image_kappa, -step_squared * image_buoy))
+    arrived = lax.all_to_all(image_stack.transpose(2, 0, 1, 3), "shot", 0, 0, tiled=True)
+    owned = [
+        jnp.sum(jnp.where(picks == t, arrived, 0.0), axis=0) for t in range(TILES)
+    ]
+    return (
+        jnp.stack([o[0] for o in owned]),
+        jnp.stack([o[1] for o in owned]),
+        current[None],
+        later[None],
     )
-    picked = (tile_ids == my_tile).astype(jnp.float32)
-    spread = picked[None, :, None, None] * image_stack[:, None]
-    owned = lax.psum_scatter(spread, "shot", scatter_dimension=3, tiled=True)
-    return (owned[0], owned[1], current[None], later[None])
 
 
 def solution(mesh):

time: 618 us -> 252 us (0.41)
  the two profiles are of different devices: /device:TPU:4 before, /device:TPU:7 now
where the time goes in v1:
time: 252 us; the launch traced here: 251 us
  starting transfers between devices  112 us (44%)
  waiting for transfers between devices  68.5 us (27%)
  blocking collectives  30.2 us (12%)
  other arithmetic  22.4 us (9%)
  local copies, waits for them, and re-layouts  13.4 us (5%)
  between operations  3.89 us (2%)
    ppermute x8, starting transfers between devices, extended(): lax.ppermute(tail, axis, [(i, (i + 1) % count) for i in range(ends)])  80.1 us
    ppermute x8, waiting for transfers between devices, extended(): lax.ppermute(head, axis, [((i + 1) % count, i) for i in range(ends)])  66.7 us
    all_to_all x1, blocking collectives, shards(): lax.all_to_all(image_stack.transpose(2, 0, 1, 3), 'shot', 0, 0, tiled=True)  30.2 us
    ppermute x8, starting transfers between devices, extended(): lax.ppermute(head, axis, [((i + 1) % count, i) for i in range(ends)])  16.8 us
    all_to_all x1, starting transfers between devices, shards(): my_block = lax.all_to_all(chosen, 'shot', 0, 0, tiled=True)  15.4 us
    scatter-add x3, other arithmetic, shards(): earlier.reshape(-1).at[receiver_slot].add(residuals[m - 2])  10.4 us
    gather x3, local copies, waits for them, and re-layouts, shards(): recorded = following.reshape(-1)[receiver_slot]  9.42 us
  transfers between devices with their start and end apart: 17, of which 7 were waited for; matrix products, arithmetic and copies ran while one was open for 4% of the time, Pallas kernels for 0%

profile of v1, /device:TPU:7, one launch (start us, length us, event | category | flops | bytes accessed | tf_op | source)
XLA Modules:
  0.0 250.7 jit_solution(6222674423780568836)
XLA Ops:
  3.0 15.4 %all-to-all-start = ((f32[32,2,8,128]{3,2,1,0:T(8,128)}), f32[32,2,8,128]{3,2,1,0:T(8,128)S(1)}, u32[]{:S(2)}, u32[]{:S(2)}) async-start(f32[32,2,8,128]{3,2,1,0:T(8,128)} %select_select_fusion), calls=%async_computation | async-start | bytes 524288 | tf_op jit(solution)/shard_map/all_to_all | solution.py:113
  18.4 2.9 %collective-permute-start.5 = (f32[7,32,128]{2,1,0:T(8,128)S(1)}, f32[7,32,128]{2,1,0:T(8,128)S(1)}, u32[]{:S(2)}, u32[]{:S(2)}) collective-permute-start(f32[7,32,128]{2,1,0:T(8,128)S(1)} %get-tuple-element.115), channel_id=1, source_target_pairs={{1,0},{2,1},{3,2},{4,3},{5,4},{6,5},{7,6},{8,7},{9,8},{10,9},{11,1... | collective-permute-start | bytes 344072 | tf_op jit(solution)/shard_map/ppermute | solution.py:26
  21.3 13.5 %collective-permute-start.4 = (f32[7,32,128]{2,1,0:T(8,128)S(1)}, f32[7,32,128]{2,1,0:T(8,128)S(1)}, u32[]{:S(2)}, u32[]{:S(2)}) collective-permute-start(f32[7,32,128]{2,1,0:T(8,128)S(1)} %get-tuple-element.116), channel_id=1, source_target_pairs={{0,1},{1,2},{2,3},{3,4},{4,5},{5,6},{6,7},{7,8},{8,9},{9,10},{10,1... | collective-permute-start | bytes 344072 | tf_op jit(solution)/shard_map/ppermute | solution.py:24
  38.3 13.9 %collective-permute-start = (f32[4,32,128]{2,1,0:T(8,128)S(1)}, f32[4,32,128]{2,1,0:T(8,128)S(1)}, u32[]{:S(2)}, u32[]{:S(2)}) collective-permute-start(f32[4,32,128]{2,1,0:T(8,128)S(1)} %get-tuple-element.117), channel_id=1, source_target_pairs={{0,1},{1,2},{2,3},{3,4},{4,5},{5,6},{6,7},{7,8},{8,9},{9,10},{10,1... | collective-permute-start | bytes 196616 | tf_op jit(solution)/shard_map/ppermute | solution.py:24
  52.2 1.9 collective-permute-start.1
  54.5 14.1 %collective-permute-done.1 = f32[4,32,128]{2,1,0:T(8,128)S(1)} collective-permute-done((f32[4,32,128]{2,1,0:T(8,128)S(1)}, f32[4,32,128]{2,1,0:T(8,128)S(1)}, u32[]{:S(2)}, u32[]{:S(2)}) %collective-permute-start.1) | collective-permute-done | bytes 65568 | tf_op jit(solution)/shard_map/ppermute | solution.py:26
  71.8 2.4 collective-permute-start.7
  74.5 3.1 %gather_fusion.2 = f32[512]{0:T(512)S(1)} fusion(f32[32768]{0:T(1024)S(1)} %fusion.423, s32[1024]{0:T(1024)S(1)} %pad_clamp_fusion), kind=kCustom, calls=%fused_computation.2 | custom fusion | bytes 6144 | tf_op jit(solution)/shard_map/gather | solution.py:134
  77.7 11.1 %collective-permute-done.7 = f32[7,32,128]{2,1,0:T(8,128)S(1)} collective-permute-done((f32[7,32,128]{2,1,0:T(8,128)S(1)}, f32[7,32,128]{2,1,0:T(8,128)S(1)}, u32[]{:S(2)}, u32[]{:S(2)}) %collective-permute-start.7) | collective-permute-done | bytes 114720 | tf_op jit(solution)/shard_map/ppermute | solution.py:26
  90.0 2.9 %collective-permute-start.8 = (f32[7,32,128]{2,1,0:T(8,128)S(1)}, f32[7,32,128]{2,1,0:T(8,128)S(1)}, u32[]{:S(2)}, u32[]{:S(2)}) collective-permute-start(f32[7,32,128]{2,1,0:T(8,128)S(1)} %bitcast.164), channel_id=1, source_target_pairs={{0,1},{1,2},{2,3},{3,4},{4,5},{5,6},{6,7},{7,8},{8,9},{9,10},{10,1... | collective-permute-start | bytes 344072 | tf_op jit(solution)/shard_map/ppermute | solution.py:24
  95.2 3.1 %gather_fusion.1 = f32[512]{0:T(512)S(1)} fusion(f32[32768]{0:T(1024)S(1)} %fusion.424, s32[1024]{0:T(1024)S(1)} %pad_clamp_fusion), kind=kCustom, calls=%fused_computation.1 | custom fusion | bytes 6144 | tf_op jit(solution)/shard_map/gather | solution.py:134
  98.4 11.5 %collective-permute-done.9 = f32[7,32,128]{2,1,0:T(8,128)S(1)} collective-permute-done((f32[7,32,128]{2,1,0:T(8,128)S(1)}, f32[7,32,128]{2,1,0:T(8,128)S(1)}, u32[]{:S(2)}, u32[]{:S(2)}) %collective-permute-start.9) | collective-permute-done | bytes 114720 | tf_op jit(solution)/shard_map/ppermute | solution.py:26
  111.7 3.1 %gather_fusion = f32[512]{0:T(512)S(1)} fusion(f32[32768]{0:T(1024)S(1)} %fusion.425, s32[1024]{0:T(1024)S(1)} %pad_clamp_fusion), kind=kCustom, calls=%fused_computation | custom fusion | bytes 6144 | tf_op jit(solution)/shard_map/gather | solution.py:134
  114.8 2.9 %collective-permute-start.2 = (f32[7,32,128]{2,1,0:T(8,128)S(1)}, f32[7,32,128]{2,1,0:T(8,128)S(1)}, u32[]{:S(2)}, u32[]{:S(2)}) collective-permute-start(f32[7,32,128]{2,1,0:T(8,128)S(1)} %get-tuple-element.119), channel_id=1, source_target_pairs={{0,1},{1,2},{2,3},{3,4},{4,5},{5,6},{6,7},{7,8},{8,9},{9,10},{10,1... | collective-permute-start | bytes 344072 | tf_op jit(solution)/shard_map/ppermute | solution.py:24
  119.7 15.0 %collective-permute-done.3 = f32[7,32,128]{2,1,0:T(8,128)S(1)} collective-permute-done((f32[7,32,128]{2,1,0:T(8,128)S(1)}, f32[7,32,128]{2,1,0:T(8,128)S(1)}, u32[]{:S(2)}, u32[]{:S(2)}) %collective-permute-start.3) | collective-permute-done | bytes 114720 | tf_op jit(solution)/shard_map/ppermute | solution.py:26
  136.0 3.4 %scatter_fusion = f32[32768]{0:T(1024)S(1)} fusion(f32[32768]{0:T(1024)S(1)} %bitcast.137, s32[512]{0:T(512)S(1)} %bitcast.166, f32[512]{0:T(512)S(1)} %get-tuple-element.138), kind=kCustom, calls=%fused_computation.3 | custom fusion | flops 512 | bytes 8192 | tf_op jit(solution)/shard_map/scatter-add | solution.py:154
  141.4 14.5 %collective-permute-start.10 = (f32[7,32,128]{2,1,0:T(8,128)S(1)}, f32[7,32,128]{2,1,0:T(8,128)S(1)}, u32[]{:S(2)}, u32[]{:S(2)}) collective-permute-start(f32[7,32,128]{2,1,0:T(8,128)S(1)} %get-tuple-element.109), channel_id=1, source_target_pairs={{0,1},{1,2},{2,3},{3,4},{4,5},{5,6},{6,7},{7,8},{8,9},{9,10},{10,1... | collective-permute-start | bytes 344072 | tf_op jit(solution)/shard_map/ppermute | solution.py:24
  158.1 3.4 %scatter_fusion.1 = f32[32768]{0:T(1024)S(1)} fusion(f32[32768]{0:T(1024)S(1)} %bitcast.142, s32[512]{0:T(512)S(1)} %bitcast.167, f32[512]{0:T(512)S(1)} %get-tuple-element.137), kind=kCustom, calls=%fused_computation.4 | custom fusion | flops 512 | bytes 8192 | tf_op jit(solution)/shard_map/scatter-add | solution.py:154
  161.6 1.9 collective-permute-start.13
  163.5 15.2 %collective-permute-start.12 = (f32[7,32,128]{2,1,0:T(8,128)S(1)}, f32[7,32,128]{2,1,0:T(8,128)S(1)}, u32[]{:S(2)}, u32[]{:S(2)}) collective-permute-start(f32[7,32,128]{2,1,0:T(8,128)S(1)} %get-tuple-element.107), channel_id=1, source_target_pairs={{0,1},{1,2},{2,3},{3,4},{4,5},{5,6},{6,7},{7,8},{8,9},{9,10},{10,1... | collective-permute-start | bytes 344072 | tf_op jit(solution)/shard_map/ppermute | solution.py:24
  181.0 3.6 %scatter_fusion.2 = f32[32768]{0:T(1024)S(1)} fusion(f32[32768]{0:T(1024)S(1)} %bitcast.147, s32[512]{0:T(512)S(1)} %bitcast.168, f32[512]{0:T(512)S(1)} %get-tuple-element.136), kind=kCustom, calls=%fused_computation.5 | custom fusion | flops 512 | bytes 8192 | tf_op jit(solution)/shard_map/scatter-add | solution.py:154
  185.3 15.2 %collective-permute-start.14 = (f32[7,32,128]{2,1,0:T(8,128)S(1)}, f32[7,32,128]{2,1,0:T(8,128)S(1)}, u32[]{:S(2)}, u32[]{:S(2)}) collective-permute-start(f32[7,32,128]{2,1,0:T(8,128)S(1)} %get-tuple-element.104), channel_id=1, source_target_pairs={{0,1},{1,2},{2,3},{3,4},{4,5},{5,6},{6,7},{7,8},{8,9},{9,10},{10,1... | collective-permute-start | bytes 344072 | tf_op jit(solution)/shard_map/ppermute | solution.py:24
  202.4 15.0 %collective-permute-done.15 = f32[7,32,128]{2,1,0:T(8,128)S(1)} collective-permute-done((f32[7,32,128]{2,1,0:T(8,128)S(1)}, f32[7,32,128]{2,1,0:T(8,128)S(1)}, u32[]{:S(2)}, u32[]{:S(2)}) %collective-permute-start.15) | collective-permute-done | bytes 114720 | tf_op jit(solution)/shard_map/ppermute | solution.py:26
  219.0 30.2 %all_to_all.10 = f32[32,2,8,128]{3,2,1,0:T(8,128)S(1)} all-to-all(f32[32,2,8,128]{3,2,1,0:T(8,128)S(1)} %copy.25), channel_id=1, replica_groups=mesh['shot'=32,'dom'=16] {'shot'}, dimensions={0} | all-to-all | bytes 524288 | tf_op jit(solution)/shard_map/all_to_all | solution.py:158
  (105 shorter events, 27.4 us)
Async XLA Ops:
  3.0 15.4 %copy-start.2 = (f32[1,8,32,128]{3,2,1,0:T(8,128)S(1)}, f32[1,8,32,128]{3,2,1,0:T(8,128)}, u32[]{:S(2)}) copy-start(f32[1,8,32,128]{3,2,1,0:T(8,128)} %param.17) | copy-start | bytes 393220
  3.0 35.2 %all-to-all-start = ((f32[32,2,8,128]{3,2,1,0:T(8,128)}), f32[32,2,8,128]{3,2,1,0:T(8,128)S(1)}, u32[]{:S(2)}, u32[]{:S(2)}) async-start(f32[32,2,8,128]{3,2,1,0:T(8,128)} %select_select_fusion), calls=%async_computation | async-start | bytes 524288 | tf_op jit(solution)/shard_map/all_to_all | solution.py:113
  18.4 16.5 %copy-start.13 = (f32[1,3]{1,0:T(1,128)S(1)}, f32[1,3]{1,0:T(1,128)}, u32[]{:S(2)}) copy-start(f32[1,3]{1,0:T(1,128)} %param.25) | copy-start | bytes 40
  18.4 17.0 %copy-start.12 = (f32[1,3,512]{2,0,1:T(1,128)S(1)}, f32[1,3,512]{2,0,1:T(1,128)}, u32[]{:S(2)}) copy-start(f32[1,3,512]{2,0,1:T(1,128)} %param.27) | copy-start | bytes 18436
  18.4 19.7 %collective-permute-start.5 = (f32[7,32,128]{2,1,0:T(8,128)S(1)}, f32[7,32,128]{2,1,0:T(8,128)S(1)}, u32[]{:S(2)}, u32[]{:S(2)}) collective-permute-start(f32[7,32,128]{2,1,0:T(8,128)S(1)} %get-tuple-element.115), channel_id=1, source_target_pairs={{1,0},{2,1},{3,2},{4,3},{5,4},{6,5},{7,6},{8,7},{9,8},{10,9},{11,1... | collective-permute-start | bytes 344072 | tf_op jit(solution)/shard_map/ppermute | solution.py:26
  21.3 14.1 %copy-start.11 = (s32[1,512]{1,0:T(1,128)S(1)}, s32[1,512]{1,0:T(1,128)}, u32[]{:S(2)}) copy-start(s32[1,512]{1,0:T(1,128)} %param.26) | copy-start | bytes 6148
  21.3 16.8 %collective-permute-start.4 = (f32[7,32,128]{2,1,0:T(8,128)S(1)}, f32[7,32,128]{2,1,0:T(8,128)S(1)}, u32[]{:S(2)}, u32[]{:S(2)}) collective-permute-start(f32[7,32,128]{2,1,0:T(8,128)S(1)} %get-tuple-element.116), channel_id=1, source_target_pairs={{0,1},{1,2},{2,3},{3,4},{4,5},{5,6},{6,7},{7,8},{8,9},{9,10},{10,1... | collective-permute-start | bytes 344072 | tf_op jit(solution)/shard_map/ppermute | solution.py:24
  38.3 16.2 %collective-permute-start = (f32[4,32,128]{2,1,0:T(8,128)S(1)}, f32[4,32,128]{2,1,0:T(8,128)S(1)}, u32[]{:S(2)}, u32[]{:S(2)}) collective-permute-start(f32[4,32,128]{2,1,0:T(8,128)S(1)} %get-tuple-element.117), channel_id=1, source_target_pairs={{0,1},{1,2},{2,3},{3,4},{4,5},{5,6},{6,7},{7,8},{8,9},{9,10},{10,1... | collective-permute-start | bytes 196616 | tf_op jit(solution)/shard_map/ppermute | solution.py:24
  52.2 16.4 %collective-permute-start.1 = (f32[4,32,128]{2,1,0:T(8,128)S(1)}, f32[4,32,128]{2,1,0:T(8,128)S(1)}, u32[]{:S(2)}, u32[]{:S(2)}) collective-permute-start(f32[4,32,128]{2,1,0:T(8,128)S(1)} %get-tuple-element.118), channel_id=1, source_target_pairs={{1,0},{2,1},{3,2},{4,3},{5,4},{6,5},{7,6},{8,7},{9,8},{10,9},{11,1... | collective-permute-start | bytes 196616 | tf_op jit(solution)/shard_map/ppermute | solution.py:26
  54.4 14.3 %copy-start.9 = (f32[1,8,32,128]{3,2,1,0:T(8,128)S(1)}, f32[1,8,32,128]{3,2,1,0:T(8,128)}, u32[]{:S(2)}) copy-start(f32[1,8,32,128]{3,2,1,0:T(8,128)} %param.18) | copy-start | bytes 393220
  69.9 7.8 %collective-permute-start.6 = (f32[7,32,128]{2,1,0:T(8,128)S(1)}, f32[7,32,128]{2,1,0:T(8,128)S(1)}, u32[]{:S(2)}, u32[]{:S(2)}) collective-permute-start(f32[7,32,128]{2,1,0:T(8,128)S(1)} %bitcast.163), channel_id=1, source_target_pairs={{0,1},{1,2},{2,3},{3,4},{4,5},{5,6},{6,7},{7,8},{8,9},{9,10},{10,1... | collective-permute-start | bytes 344072 | tf_op jit(solution)/shard_map/ppermute | solution.py:24
  71.8 16.9 %collective-permute-start.7 = (f32[7,32,128]{2,1,0:T(8,128)S(1)}, f32[7,32,128]{2,1,0:T(8,128)S(1)}, u32[]{:S(2)}, u32[]{:S(2)}) collective-permute-start(f32[7,32,128]{2,1,0:T(8,128)S(1)} %bitcast.161), channel_id=1, source_target_pairs={{1,0},{2,1},{3,2},{4,3},{5,4},{6,5},{7,6},{8,7},{9,8},{10,9},{11,1... | collective-permute-start | bytes 344072 | tf_op jit(solution)/shard_map/ppermute | solution.py:26
  90.0 8.3 %collective-permute-start.8 = (f32[7,32,128]{2,1,0:T(8,128)S(1)}, f32[7,32,128]{2,1,0:T(8,128)S(1)}, u32[]{:S(2)}, u32[]{:S(2)}) collective-permute-start(f32[7,32,128]{2,1,0:T(8,128)S(1)} %bitcast.164), channel_id=1, source_target_pairs={{0,1},{1,2},{2,3},{3,4},{4,5},{5,6},{6,7},{7,8},{8,9},{9,10},{10,1... | collective-permute-start | bytes 344072 | tf_op jit(solution)/shard_map/ppermute | solution.py:24
  93.0 16.9 %collective-permute-start.9 = (f32[7,32,128]{2,1,0:T(8,128)S(1)}, f32[7,32,128]{2,1,0:T(8,128)S(1)}, u32[]{:S(2)}, u32[]{:S(2)}) collective-permute-start(f32[7,32,128]{2,1,0:T(8,128)S(1)} %bitcast.162), channel_id=1, source_target_pairs={{1,0},{2,1},{3,2},{4,3},{5,4},{6,5},{7,6},{8,7},{9,8},{10,9},{11,1... | collective-permute-start | bytes 344072 | tf_op jit(solution)/shard_map/ppermute | solution.py:26
  114.8 4.9 %collective-permute-start.2 = (f32[7,32,128]{2,1,0:T(8,128)S(1)}, f32[7,32,128]{2,1,0:T(8,128)S(1)}, u32[]{:S(2)}, u32[]{:S(2)}) collective-permute-start(f32[7,32,128]{2,1,0:T(8,128)S(1)} %get-tuple-element.119), channel_id=1, source_target_pairs={{0,1},{1,2},{2,3},{3,4},{4,5},{5,6},{6,7},{7,8},{8,9},{9,10},{10,1... | collective-permute-start | bytes 344072 | tf_op jit(solution)/shard_map/ppermute | solution.py:24
  117.8 16.9 %collective-permute-start.3 = (f32[7,32,128]{2,1,0:T(8,128)S(1)}, f32[7,32,128]{2,1,0:T(8,128)S(1)}, u32[]{:S(2)}, u32[]{:S(2)}) collective-permute-start(f32[7,32,128]{2,1,0:T(8,128)S(1)} %get-tuple-element.120), channel_id=1, source_target_pairs={{1,0},{2,1},{3,2},{4,3},{5,4},{6,5},{7,6},{8,7},{9,8},{10,9},{11,1... | collective-permute-start | bytes 344072 | tf_op jit(solution)/shard_map/ppermute | solution.py:26
  139.5 17.3 %collective-permute-start.11 = (f32[7,32,128]{2,1,0:T(8,128)S(1)}, f32[7,32,128]{2,1,0:T(8,128)S(1)}, u32[]{:S(2)}, u32[]{:S(2)}) collective-permute-start(f32[7,32,128]{2,1,0:T(8,128)S(1)} %get-tuple-element.108), channel_id=1, source_target_pairs={{1,0},{2,1},{3,2},{4,3},{5,4},{6,5},{7,6},{8,7},{9,8},{10,9},{11,1... | collective-permute-start | bytes 344072 | tf_op jit(solution)/shard_map/ppermute | solution.py:26
  141.4 16.2 %collective-permute-start.10 = (f32[7,32,128]{2,1,0:T(8,128)S(1)}, f32[7,32,128]{2,1,0:T(8,128)S(1)}, u32[]{:S(2)}, u32[]{:S(2)}) collective-permute-start(f32[7,32,128]{2,1,0:T(8,128)S(1)} %get-tuple-element.109), channel_id=1, source_target_pairs={{0,1},{1,2},{2,3},{3,4},{4,5},{5,6},{6,7},{7,8},{8,9},{9,10},{10,1... | collective-permute-start | bytes 344072 | tf_op jit(solution)/shard_map/ppermute | solution.py:24
  161.5 23.1 %copy-start = (f32[32768]{0:T(1024)}, f32[32768]{0:T(1024)S(1)}, u32[]{:S(2)}) copy-start(f32[32768]{0:T(1024)S(1)} %scatter_fusion.1) | copy-start | bytes 393220
  161.6 18.0 %collective-permute-start.13 = (f32[7,32,128]{2,1,0:T(8,128)S(1)}, f32[7,32,128]{2,1,0:T(8,128)S(1)}, u32[]{:S(2)}, u32[]{:S(2)}) collective-permute-start(f32[7,32,128]{2,1,0:T(8,128)S(1)} %get-tuple-element.106), channel_id=1, source_target_pairs={{1,0},{2,1},{3,2},{4,3},{5,4},{6,5},{7,6},{8,7},{9,8},{10,9},{11,1... | collective-permute-start | bytes 344072 | tf_op jit(solution)/shard_map/ppermute | solution.py:26
  163.5 16.9 %collective-permute-start.12 = (f32[7,32,128]{2,1,0:T(8,128)S(1)}, f32[7,32,128]{2,1,0:T(8,128)S(1)}, u32[]{:S(2)}, u32[]{:S(2)}) collective-permute-start(f32[7,32,128]{2,1,0:T(8,128)S(1)} %get-tuple-element.107), channel_id=1, source_target_pairs={{0,1},{1,2},{2,3},{3,4},{4,5},{5,6},{6,7},{7,8},{8,9},{9,10},{10,1... | collective-permute-start | bytes 344072 | tf_op jit(solution)/shard_map/ppermute | solution.py:24
  181.0 3.6 %copy-start.6 = (f32[8,32,128]{2,1,0:T(8,128)S(1)}, f32[8,32,128]{2,1,0:T(8,128)}, u32[]{:S(2)}) copy-start(f32[8,32,128]{2,1,0:T(8,128)} %get-tuple-element.75) | copy-start | bytes 393220
  185.3 17.1 %collective-permute-start.14 = (f32[7,32,128]{2,1,0:T(8,128)S(1)}, f32[7,32,128]{2,1,0:T(8,128)S(1)}, u32[]{:S(2)}, u32[]{:S(2)}) collective-permute-start(f32[7,32,128]{2,1,0:T(8,128)S(1)} %get-tuple-element.104), channel_id=1, source_target_pairs={{0,1},{1,2},{2,3},{3,4},{4,5},{5,6},{6,7},{7,8},{8,9},{9,10},{10,1... | collective-permute-start | bytes 344072 | tf_op jit(solution)/shard_map/ppermute | solution.py:24
  200.4 16.9 %collective-permute-start.15 = (f32[7,32,128]{2,1,0:T(8,128)S(1)}, f32[7,32,128]{2,1,0:T(8,128)S(1)}, u32[]{:S(2)}, u32[]{:S(2)}) collective-permute-start(f32[7,32,128]{2,1,0:T(8,128)S(1)} %get-tuple-element.105), channel_id=1, source_target_pairs={{1,0},{2,1},{3,2},{4,3},{5,4},{6,5},{7,6},{8,7},{9,8},{10,9},{11,1... | collective-permute-start | bytes 344072 | tf_op jit(solution)/shard_map/ppermute | solution.py:26
  (7 other events, 8.7 us)

commit v2 on v1

v2 whole, which is shorter than its diff:
```python
import jax
import jax.numpy as jnp
from jax import lax
from jax.experimental import pallas as pl
from jax.experimental.pallas import tpu as pltpu
from jax.sharding import PartitionSpec as P

CX = 8
CY = 32
CZ = 128
TILES = 4
STEPS = 3
REC = 512
PAD = 8
ROWS = CY + 2 * PAD
WIDE = CX + 14

COEFFS = (1225.0 / 1024.0, -245.0 / 3072.0, 49.0 / 5120.0, -5.0 / 7168.0)
step_squared = 0.02

VMEM = pl.BlockSpec(memory_space=pltpu.VMEM)
SMEM = pl.BlockSpec(memory_space=pltpu.SMEM)
F32 = jnp.float32


def plane_field(count):
    return jax.ShapeDtypeStruct((count, CY, CZ), F32)


def lane_shift(plane, by, lane):
    if by == 0:
        return plane
    moved = pltpu.roll(plane, (-by) % CZ, 1)
    keep = lane < CZ - by if by > 0 else lane >= -by
    return jnp.where(keep, moved, 0.0)


def stencil(at):
    total = COEFFS[0] * (at(0) - at(-1))
    for k in range(2, 5):
        total = total + COEFFS[k - 1] * (at(k - 1) - at(-k))
    return total


def place(info, target, own, first, second, width):
    target[:, 0:PAD, :] = jnp.zeros((target.shape[0], PAD, CZ), F32)
    target[:, PAD + CY : ROWS, :] = jnp.zeros((target.shape[0], PAD, CZ), F32)
    inner = slice(PAD, PAD + CY)
    target[width : width + CX, inner, :] = own
    odd = info[0] == 1

    @pl.when(odd)
    def _():
        target[0:width, inner, :] = first
        target[width + CX : 2 * width + CX, inner, :] = second

    @pl.when(jnp.logical_not(odd))
    def _():
        target[0:width, inner, :] = second
        target[width + CX : 2 * width + CX, inner, :] = first


def hand_over(info, first, second, head, tail):
    odd = info[0] == 1

    @pl.when(odd)
    def _():
        first[...] = head()
        second[...] = tail()

    @pl.when(jnp.logical_not(odd))
    def _():
        first[...] = tail()
        second[...] = head()


def slope_x(field, at):
    return stencil(lambda s: field[at + s, PAD : PAD + CY, :])


def slope_y(field, at):
    return stencil(lambda s: field[at, PAD + s : PAD + CY + s, :])


def slope_z(plane, lane):
    return stencil(lambda s: lane_shift(plane, s, lane))


def operate(field, width, buoy, gx, gy, acc, slopes):
    lane = lax.broadcasted_iota(jnp.int32, (CY, CZ), 1)
    gy[:, 0:PAD, :] = jnp.zeros((CX, PAD, CZ), F32)
    gy[:, PAD + CY : ROWS, :] = jnp.zeros((CX, PAD, CZ), F32)
    for cell in range(-3, CX + 4):
        sx = slope_x(field, cell + width)
        gx[cell + 3] = buoy[cell + 4] * sx
        if 0 <= cell < CX:
            weight = buoy[cell + 4]
            plane = field[cell + width, PAD : PAD + CY, :]
            sy = slope_y(field, cell + width)
            sz = slope_z(plane, lane)
            gy[cell, PAD : PAD + CY, :] = weight * sy
            gz = weight * sz
            acc[cell] = stencil(lambda s: lane_shift(gz, s + 1, lane))
            slopes(cell, sx, sy, sz)
    for cell in range(CX):
        div = stencil(lambda s: gx[cell + 4 + s])
        div = div + stencil(lambda s: gy[cell, PAD + 1 + s : PAD + 1 + s + CY, :])
        yield cell, div + acc[cell]


def receivers_kernel(info, cells, seen, out):
    index = cells[...] - info[4]
    row = lax.shift_right_arithmetic(index, 7)
    z = lax.bitwise_and(index, 127)
    rows = lax.broadcasted_iota(jnp.int32, (CX * CY, REC), 0)
    pick = jnp.where(rows == row, 1.0, 0.0).astype(jnp.bfloat16)
    lanes = lax.broadcasted_iota(jnp.int32, (CZ, REC), 0)
    here = lanes == z

    def spread(values):
        right = jnp.where(here, values, 0.0).astype(jnp.bfloat16)
        return lax.dot_general(
            pick, right, (((1,), (1,)), ((), ())), preferred_element_type=F32
        )

    out[0] = spread(jnp.ones((1, REC), F32)).reshape(CX, CY, CZ)
    for n in range(STEPS):
        rest = seen[n : n + 1, :]
        total = None
        for _ in range(3):
            part = rest.astype(jnp.bfloat16).astype(F32)
            rest = rest - part
            total = spread(part) if total is None else total + spread(part)
        out[n + 1] = total.reshape(CX, CY, CZ)


def model_kernel(info, stiff, buoy, last, send_a, send_b, scaled):
    scaled[...] = stiff[...] * last[...]
    hand_over(
        info,
        send_a,
        send_b,
        lambda: jnp.concatenate([buoy[0:4], scaled[0:7]], axis=0),
        lambda: jnp.concatenate([buoy[4:8], scaled[1:8]], axis=0),
    )


def source_plane(info, amount):
    y = lax.broadcasted_iota(jnp.int32, (CY, CZ), 0)
    z = lax.broadcasted_iota(jnp.int32, (CY, CZ), 1)
    hit = (y == info[2]) & (z == info[3])
    spot = jnp.where(hit, amount, 0.0)
    return lambda cell: jnp.where(info[1] == cell, spot, 0.0)


def forward(info, wave, n, now, before, stiff, field, buoy, gx, gy, acc, div_out, slope_out, after):
    source = source_plane(info, wave[n])

    def keep(cell, sx, sy, sz):
        slope_out[0, cell] = sx
        slope_out[1, cell] = sy
        slope_out[2, cell] = sz

    for cell, div in operate(field, 7, buoy, gx, gy, acc, keep):
        div_out[cell] = div
        value = 2.0 * now[cell] - before[cell] + step_squared * stiff[cell] * div
        after(cell, value + source(cell))


def widen_buoy(info, buoy, first, second, target):
    target[4 : 4 + CX] = buoy[...]
    odd = info[0] == 1

    @pl.when(odd)
    def _():
        target[0:4] = first[0:4]
        target[4 + CX : 8 + CX] = second[0:4]

    @pl.when(jnp.logical_not(odd))
    def _():
        target[0:4] = second[0:4]
        target[4 + CX : 8 + CX] = first[0:4]


def first_kernel(
    info, wave, now, now_a, now_b, before, last, after, stiff, buoy, edge_a, edge_b, scaled,
    p_out, send_a, send_b, div_out, slope_out, buoy_out, q_out,
    field, gx, gy, acc,
):
    widen_buoy(info, buoy, edge_a, edge_b, buoy_out)
    place(info, field, now[...], now_a[...], now_b[...], 7)

    def store(cell, value):
        p_out[cell] = value

    forward(info, wave, 0, now, before, stiff, field, buoy_out, gx, gy, acc, div_out, slope_out, store)
    hand_over(info, send_a, send_b, lambda: p_out[0:7], lambda: p_out[1:8])
    place(info, field, scaled[...], edge_a[4:11], edge_b[4:11], 7)
    for cell, div in operate(field, 7, buoy_out, gx, gy, acc, lambda *_: None):
        q_out[cell] = 2.0 * last[cell] - after[cell] + step_squared * div


def second_kernel(
    info, wave, now, now_a, now_b, before, stiff, buoy,
    p_out, send_a, send_b, div_out, slope_out,
    field, gx, gy, acc,
):
    place(info, field, now[...], now_a[...], now_b[...], 7)

    def store(cell, value):
        p_out[cell] = value

    forward(info, wave, 1, now, before, stiff, field, buoy, gx, gy, acc, div_out, slope_out, store)
    hand_over(info, send_a, send_b, lambda: p_out[0:7], lambda: p_out[1:8])


def third_kernel(
    info, wave, now, now_a, now_b, before, stiff, buoy, q_part, spots,
    q_out, scaled, send_a, send_b, div_out, slope_out,
    field, gx, gy, acc,
):
    place(info, field, now[...], now_a[...], now_b[...], 7)

    def store(cell, value):
        q = q_part[cell] + (spots[0, cell] * value - spots[3, cell])
        q_out[cell] = q
        scaled[cell] = stiff[cell] * q

    forward(info, wave, 2, now, before, stiff, field, buoy, gx, gy, acc, div_out, slope_out, store)
    hand_over(info, send_a, send_b, lambda: scaled[0:7], lambda: scaled[1:8])


def adjoint_kernel(
    n, width, info, q_now, q_after, scaled, scaled_a, scaled_b, stiff, buoy, spots, p_then, div, slope, images,
    q_out, scaled_out, send_a, send_b, images_out,
    field, gx, gy, acc,
):
    place(info, field, scaled[...], scaled_a[...], scaled_b[...], 7)

    def image(cell, sx, sy, sz):
        kappa = q_now[cell] * div[cell]
        rho = slope[0, cell] * sx + slope[1, cell] * sy + slope[2, cell] * sz
        if images is not None:
            kappa = images[0, cell] + kappa
            rho = images[1, cell] + rho
        images_out[0, cell] = kappa
        images_out[1, cell] = rho

    for cell, total in operate(field, 7, buoy, gx, gy, acc, image):
        q = 2.0 * q_now[cell] - q_after[cell] + step_squared * total
        q = q + (spots[0, cell] * p_then[cell] - spots[n + 1, cell])
        q_out[cell] = q
        scaled_out[cell] = stiff[cell] * q
    hand_over(info, send_a, send_b, lambda: scaled_out[0:width], lambda: scaled_out[CX - width : CX])


def adjoint_first_kernel(info, q_now, q_after, scaled, scaled_a, scaled_b, stiff, buoy, spots, p_then, div, slope, *rest):
    adjoint_kernel(1, 7, info, q_now, q_after, scaled, scaled_a, scaled_b, stiff, buoy, spots, p_then, div, slope, None, *rest)


def adjoint_second_kernel(info, q_now, q_after, scaled, scaled_a, scaled_b, stiff, buoy, spots, p_then, div, slope, images, *rest):
    adjoint_kernel(0, 4, info, q_now, q_after, scaled, scaled_a, scaled_b, stiff, buoy, spots, p_then, div, slope, images, *rest)


def image_kernel(info, q_now, scaled, scaled_a, scaled_b, div, slope, images, out, field):
    lane = lax.broadcasted_iota(jnp.int32, (CY, CZ), 1)
    place(info, field, scaled[...], scaled_a[...], scaled_b[...], 4)
    for cell in range(CX):
        plane = field[cell + 4, PAD : PAD + CY, :]
        rho = images[1, cell] + slope[0, cell] * slope_x(field, cell + 4)
        rho = rho + slope[1, cell] * slope_y(field, cell + 4)
        rho = rho + slope[2, cell] * slope_z(plane, lane)
        out[0, cell] = step_squared * (images[0, cell] + q_now[cell] * div[cell])
        out[1, cell] = -step_squared * rho


def gather_kernel(column, arrived, out_kappa, out_buoy):
    out_kappa[...] = jnp.zeros_like(out_kappa)
    out_buoy[...] = jnp.zeros_like(out_buoy)
    for s in range(arrived.shape[0]):
        t = column[s]
        out_kappa[t] = out_kappa[t] + arrived[s, 0]
        out_buoy[t] = out_buoy[t] + arrived[s, 1]


def work():
    return [
        pltpu.VMEM((WIDE, ROWS, CZ), F32),
        pltpu.VMEM((CX + 7, CY, CZ), F32),
        pltpu.VMEM((CX, ROWS, CZ), F32),
        pltpu.VMEM((CX, CY, CZ), F32),
    ]


def call(kernel, scalars, arrays, outs, scratch=(), flops=2_000_000):
    moved = sum(4 * a.size for a in arrays) + sum(4 * o.size for o in outs)
    return pl.pallas_call(
        kernel,
        out_shape=outs,
        in_specs=[SMEM] * len(scalars) + [VMEM] * len(arrays),
        out_specs=[VMEM] * len(outs),
        scratch_shapes=list(scratch),
        compiler_params=pltpu.CompilerParams(vmem_limit_bytes=32 * 1024 * 1024),
        cost_estimate=pl.CostEstimate(flops=flops, bytes_accessed=moved, transcendentals=0),
    )(*scalars, *arrays)


def swap(first, second):
    count = lax.axis_size("dom")
    pairs_a = [(i ^ 1, i) for i in range(count)]
    pairs_b = []
    for i in range(1, count - 1, 2):
        pairs_b += [(i, i + 1), (i + 1, i)]
    second = lax.ppermute(second, "dom", pairs_b)
    return lax.ppermute(first, "dom", pairs_a), second


def shards(
    pressure_now,
    pressure_prev,
    adjoint_last,
    adjoint_after,
    kappa_model,
    buoy_model,
    aperture,
    source_cell,
    source_wave,
    receiver_cell,
    observed,
):
    dom = lax.axis_index("dom")
    odd = lax.rem(dom, 2)
    offset = dom * (CX * CY * CZ)
    source = source_cell[0]
    info = jnp.stack(
        [odd, source // (CY * CZ) - dom * CX, (source // CZ) % CY, source % CZ, offset]
    ).astype(jnp.int32)
    wave = source_wave[0]
    column = lax.dynamic_index_in_dim(aperture, dom, 1, keepdims=False)

    stacked = jnp.stack((kappa_model, buoy_model), axis=1)
    picks = column[:, None, None, None]
    chosen = stacked[0][None]
    for t in range(1, TILES):
        chosen = jnp.where(picks == t, stacked[t][None], chosen)
    block = lax.all_to_all(chosen, "shot", 0, 0, tiled=True)

    p0, p_prev = pressure_now[0], pressure_prev[0]
    q4, q5 = adjoint_last[0], adjoint_after[0]
    head, tail = p0[0:7], p0[1:8]
    p0_a, p0_b = swap(jnp.where(odd == 1, head, tail), jnp.where(odd == 1, tail, head))
    (spots,) = call(
        receivers_kernel,
        [info],
        [receiver_cell, observed[0]],
        [jax.ShapeDtypeStruct((STEPS + 1, CX, CY, CZ), F32)],
        flops=400_000_000,
    )

    stiff = block[:, 0].transpose(1, 0, 2)
    buoy = block[:, 1].transpose(1, 0, 2)
    own, seven, four = plane_field(CX), plane_field(7), plane_field(4)
    slopes = jax.ShapeDtypeStruct((3, CX, CY, CZ), F32)
    images = jax.ShapeDtypeStruct((2, CX, CY, CZ), F32)

    send_a, send_b, f4 = call(
        model_kernel, [info], [stiff, buoy, q4], [plane_field(11), plane_field(11), own]
    )
    edge_a, edge_b = swap(send_a, send_b)
    p1, send_a, send_b, div0, slope0, wide, q_part = call(
        first_kernel,
        [info, wave],
        [p0, p0_a, p0_b, p_prev, q4, q5, stiff, buoy, edge_a, edge_b, f4],
        [own, seven, seven, own, slopes, plane_field(CX + 8), own],
        work(),
    )
    from_a, from_b = swap(send_a, send_b)
    p2, send_a, send_b, div1, slope1 = call(
        second_kernel,
        [info, wave],
        [p1, from_a, from_b, p0, stiff, wide],
        [own, seven, seven, own, slopes],
        work(),
    )
    from_a, from_b = swap(send_a, send_b)
    q3, f3, send_a, send_b, div2, slope2 = call(
        third_kernel,
        [info, wave],
        [p2, from_a, from_b, p1, stiff, wide, q_part, spots],
        [own, own, seven, seven, own, slopes],
        work(),
    )
    from_a, from_b = swap(send_a, send_b)
    q2, f2, send_a, send_b, image = call(
        adjoint_first_kernel,
        [info],
        [q3, q4, f3, from_a, from_b, stiff, wide, spots, p2, div2, slope2],
        [own, own, seven, seven, images],
        work(),
    )
    from_a, from_b = swap(send_a, send_b)
    q1, f1, send_a, send_b, image = call(
        adjoint_second_kernel,
        [info],
        [q2, q3, f2, from_a, from_b, stiff, wide, spots, p1, div1, slope1, image],
        [own, own, four, four, images],
        work(),
    )
    from_a, from_b = swap(send_a, send_b)
    (image,) = call(
        image_kernel,
        [info],
        [q1, f1, from_a, from_b, div0, slope0, image],
        [images],
        [pltpu.VMEM((CX + 8, ROWS, CZ), F32)],
    )
    arrived = lax.all_to_all(image.transpose(2, 0, 1, 3), "shot", 0, 0, tiled=True)
    tiles = jax.ShapeDtypeStruct((TILES, CX, CZ), F32)
    grad_kappa, grad_buoy = call(gather_kernel, [column], [arrived], [tiles, tiles])
    return (grad_kappa, grad_buoy, q1[None], q2[None])


def solution(mesh):
    in_specs = (
        P("shot", "dom", None, None),
        P("shot", "dom", None, None),
        P("shot", "dom", None, None),
        P("shot", "dom", None, None),
        P(None, "dom", "shot"),
        P(None, "dom", "shot"),
        P(),
        P("shot"),
        P("shot", None),
        P("shot", None),
        P("shot", None, None),
    )
    out_specs = (
        P(None, "dom", "shot"),
        P(None, "dom", "shot"),
        P("shot", "dom", None, None),
        P("shot", "dom", None, None),
    )
    return jax.shard_map(shards, mesh=mesh, in_specs=in_specs, out_specs=out_specs, check_vma=False)
```

time: 252 us -> 198 us (0.79)
  starting transfers between devices: 112 us -> 90.1 us
  other arithmetic: 22.4 us -> 2.34 us
  Pallas kernels: 0 us -> 14.8 us
  local copies, waits for them, and re-layouts: 13.4 us -> 3.63 us
  blocking collectives: 30.2 us -> 20.6 us
  waiting for transfers between devices: 68.5 us -> 63.8 us
    ppermute x16 -> x14, waiting for transfers between devices: 68.5 us -> 45.8 us  [the longest x7 45.8 us: swap(): second = lax.ppermute(second, 'dom', pairs_b)]
    ppermute x16 -> x14, starting transfers between devices: 96.8 us -> 74.9 us  [the longest x7 59.7 us: swap(): second = lax.ppermute(second, 'dom', pairs_b)]
    all_to_all x1, waiting for transfers between devices: 0.01 us -> 18 us  [shards(): block = lax.all_to_all(chosen, 'shot', 0, 0, tiled=True)]
    pallas_call x0 -> x9, Pallas kernels: none -> 14.8 us  [call(): pl.pallas_call(kernel, out_shape=outs, in_specs=[SMEM] * len(scalars) + [...]
    scatter-add x6 -> x0, other arithmetic: 10.9 us -> none  [the longest x3 10.4 us: shards(): earlier.reshape(-1).at[receiver_slot].add(residuals[m - 2])]
    all_to_all x1, blocking collectives: 30.2 us -> 20.6 us  [shards(): lax.all_to_all(image.transpose(2, 0, 1, 3), 'shot', 0, 0, tiled=True)]
    gather x3 -> x0, local copies, waits for them, and re-layouts: 9.42 us -> none  [shards(): recorded = following.reshape(-1)[receiver_slot]]
    mul x14 -> x0, other arithmetic: 3.77 us -> none  [the longest x4 2.39 us: slab_operator(): divergence = divergence + plus_diff(buoyancy * slope_z, 2)]
  transfers between devices with their start and end apart: 17 -> 15, of which waited for: 7 -> 7; matrix products, arithmetic and copies ran while one was open for 4% -> 0% of each run, Pallas kernels for 0% -> 1%
where the time goes in v2:
time: 198 us; the launch traced here: 197 us
  starting transfers between devices  90.1 us (46%)
  waiting for transfers between devices  63.8 us (32%)
  blocking collectives  20.6 us (10%)
  Pallas kernels  14.8 us (7%)
  local copies, waits for them, and re-layouts  3.63 us (2%)
  other arithmetic  2.34 us (1%)
    ppermute x7, starting transfers between devices, swap(): second = lax.ppermute(second, 'dom', pairs_b)  59.7 us
    ppermute x7, waiting for transfers between devices, swap(): second = lax.ppermute(second, 'dom', pairs_b)  45.8 us
    all_to_all x1, blocking collectives, shards(): lax.all_to_all(image.transpose(2, 0, 1, 3), 'shot', 0, 0, tiled=True)  20.6 us
    all_to_all x1, waiting for transfers between devices, shards(): block = lax.all_to_all(chosen, 'shot', 0, 0, tiled=True)  18 us
    all_to_all x1, starting transfers between devices, shards(): block = lax.all_to_all(chosen, 'shot', 0, 0, tiled=True)  15.3 us
    ppermute x7, starting transfers between devices, swap(): return (lax.ppermute(first, 'dom', pairs_a), second)  15.2 us
    pallas_call x9, Pallas kernels, call(): pl.pallas_call(kernel, out_shape=outs, in_specs=[SMEM] * len(scalars) + [...  14.8 us
  transfers between devices with their start and end apart: 15, of which 7 were waited for; matrix products, arithmetic and copies ran while one was open for 0% of the time, Pallas kernels for 1%

profile of v2, /device:TPU:7, one launch (start us, length us, event | category | flops | bytes accessed | tf_op | source)
XLA Modules:
  0.0 197.0 jit_solution(9069672539791203373)
XLA Ops:
  3.0 15.3 %all-to-all-start = ((f32[32,2,8,128]{3,2,1,0:T(8,128)}), f32[32,2,8,128]{3,2,1,0:T(8,128)S(1)}, u32[]{:S(2)}, u32[]{:S(2)}) async-start(f32[32,2,8,128]{3,2,1,0:T(8,128)} %select_select_fusion), calls=%async_computation | async-start | bytes 524288 | tf_op jit(solution)/shard_map/all_to_all | solution.py:346
  19.0 18.0 %all-to-all-done = f32[32,2,8,128]{3,2,1,0:T(8,128)S(1)} async-done(((f32[32,2,8,128]{3,2,1,0:T(8,128)}), f32[32,2,8,128]{3,2,1,0:T(8,128)S(1)}, u32[]{:S(2)}, u32[]{:S(2)}) %all-to-all-start) | async-done | bytes 262176 | tf_op jit(solution)/shard_map/all_to_all | solution.py:346
  38.5 3.7 %collective-permute-start.2 = (f32[11,32,128]{2,1,0:T(8,128)S(1)}, f32[11,32,128]{2,1,0:T(8,128)S(1)}, u32[]{:S(2)}, u32[]{:S(2)}) collective-permute-start(f32[11,32,128]{2,1,0:T(8,128)S(1)} %get-tuple-element.37), channel_id=1, source_target_pairs={{1,0},{0,1},{3,2},{2,3},{5,4},{4,5},{7,6},{6,7},{9,8},{8,9},{11,10... | collective-permute-start | bytes 540680 | tf_op jit(solution)/shard_map/ppermute | solution.py:315
  42.2 7.9 %collective-permute-start.3 = (f32[11,32,128]{2,1,0:T(8,128)S(1)}, f32[11,32,128]{2,1,0:T(8,128)S(1)}, u32[]{:S(2)}, u32[]{:S(2)}) collective-permute-start(f32[11,32,128]{2,1,0:T(8,128)S(1)} %get-tuple-element.38), channel_id=1, source_target_pairs={{1,2},{2,1},{3,4},{4,3},{5,6},{6,5},{7,8},{8,7},{9,10},{10,9},{11,... | collective-permute-start | bytes 540680 | tf_op jit(solution)/shard_map/ppermute | solution.py:314
  50.1 8.6 %collective-permute-start.1 = (f32[7,32,128]{2,1,0:T(8,128)S(1)}, f32[7,32,128]{2,1,0:T(8,128)S(1)}, u32[]{:S(2)}, u32[]{:S(2)}) collective-permute-start(f32[7,32,128]{2,1,0:T(8,128)S(1)} %get-tuple-element.74), channel_id=1, source_target_pairs={{1,2},{2,1},{3,4},{4,3},{5,6},{6,5},{7,8},{8,7},{9,10},{10,9},{11,... | collective-permute-start | bytes 344072 | tf_op jit(solution)/shard_map/ppermute | solution.py:314
  58.8 1.9 collective-permute-start
  60.7 6.4 %collective-permute-done.1.now_b = f32[7,32,128]{2,1,0:T(8,128)S(1)} collective-permute-done((f32[7,32,128]{2,1,0:T(8,128)S(1)}, f32[7,32,128]{2,1,0:T(8,128)S(1)}, u32[]{:S(2)}, u32[]{:S(2)}) %collective-permute-start.1) | collective-permute-done | bytes 114720 | tf_op jit(solution)/shard_map/ppermute | solution.py:314
  67.7 2.7 %shard_map.139 = (f32[8,32,128]{2,1,0:T(8,128)S(1)}, f32[7,32,128]{2,1,0:T(8,128)S(1)}, f32[7,32,128]{2,1,0:T(8,128)S(1)}, f32[8,32,128]{2,1,0:T(8,128)S(1)}, f3...) custom-call(s32[5]{0:T(128)S(1)} %stack.32.info, f32[3]{0:T(128)S(1)} %bitcast.58, ...), custom_call_target="tpu_custom_call" | custom-call | flops 2000000 | bytes 2785280 | tf_op jit(solution)/shard_map/pallas_call | solution.py:297
  70.4 1.9 collective-permute-start.4
  72.3 8.6 %collective-permute-start.5 = (f32[7,32,128]{2,1,0:T(8,128)S(1)}, f32[7,32,128]{2,1,0:T(8,128)S(1)}, u32[]{:S(2)}, u32[]{:S(2)}) collective-permute-start(f32[7,32,128]{2,1,0:T(8,128)S(1)} %get-tuple-element.42), channel_id=1, source_target_pairs={{1,2},{2,1},{3,4},{4,3},{5,6},{6,5},{7,8},{8,7},{9,10},{10,9},{11,... | collective-permute-start | bytes 344072 | tf_op jit(solution)/shard_map/ppermute | solution.py:314
  81.0 8.3 %collective-permute-done.5.now_b = f32[7,32,128]{2,1,0:T(8,128)S(1)} collective-permute-done((f32[7,32,128]{2,1,0:T(8,128)S(1)}, f32[7,32,128]{2,1,0:T(8,128)S(1)}, u32[]{:S(2)}, u32[]{:S(2)}) %collective-permute-start.5) | collective-permute-done | bytes 114720 | tf_op jit(solution)/shard_map/ppermute | solution.py:314
  91.0 1.9 collective-permute-start.6
  92.9 8.6 %collective-permute-start.7 = (f32[7,32,128]{2,1,0:T(8,128)S(1)}, f32[7,32,128]{2,1,0:T(8,128)S(1)}, u32[]{:S(2)}, u32[]{:S(2)}) collective-permute-start(f32[7,32,128]{2,1,0:T(8,128)S(1)} %get-tuple-element.46), channel_id=1, source_target_pairs={{1,2},{2,1},{3,4},{4,3},{5,6},{6,5},{7,8},{8,7},{9,10},{10,9},{11,... | collective-permute-start | bytes 344072 | tf_op jit(solution)/shard_map/ppermute | solution.py:314
  103.0 6.9 %collective-permute-done.7.now_b = f32[7,32,128]{2,1,0:T(8,128)S(1)} collective-permute-done((f32[7,32,128]{2,1,0:T(8,128)S(1)}, f32[7,32,128]{2,1,0:T(8,128)S(1)}, u32[]{:S(2)}, u32[]{:S(2)}) %collective-permute-start.7) | collective-permute-done | bytes 114720 | tf_op jit(solution)/shard_map/ppermute | solution.py:314
  111.5 1.9 collective-permute-start.8
  113.4 8.6 %collective-permute-start.9 = (f32[7,32,128]{2,1,0:T(8,128)S(1)}, f32[7,32,128]{2,1,0:T(8,128)S(1)}, u32[]{:S(2)}, u32[]{:S(2)}) collective-permute-start(f32[7,32,128]{2,1,0:T(8,128)S(1)} %get-tuple-element.51), channel_id=1, source_target_pairs={{1,2},{2,1},{3,4},{4,3},{5,6},{6,5},{7,8},{8,7},{9,10},{10,9},{11,... | collective-permute-start | bytes 344072 | tf_op jit(solution)/shard_map/ppermute | solution.py:314
  122.1 8.3 %collective-permute-done.9.scaled_b = f32[7,32,128]{2,1,0:T(8,128)S(1)} collective-permute-done((f32[7,32,128]{2,1,0:T(8,128)S(1)}, f32[7,32,128]{2,1,0:T(8,128)S(1)}, u32[]{:S(2)}, u32[]{:S(2)}) %collective-permute-start.9) | collective-permute-done | bytes 114720 | tf_op jit(solution)/shard_map/ppermute | solution.py:314
  130.3 2.4 %shard_map.143 = (f32[8,32,128]{2,1,0:T(8,128)}, f32[8,32,128]{2,1,0:T(8,128)S(1)}, f32[7,32,128]{2,1,0:T(8,128)S(1)}, f32[7,32,128]{2,1,0:T(8,128)S(1)}, f32[2,8,32,128]{3,2,1,0:T(8,128)S(1)}) custom-call(s32[5]{0:T(128)S(1)} %stack.32.info, f32[8,32,128]{2,1,0:T(8,128)S(1)} %get-tuple-element.48.q_now.q_after, f32[8,32,128]{2,1,0:T(8,128)S(1)} %bitcast.52, ...), custom_call_target="tpu_custom_call" | custom-call | flops 2000000 | bytes 2949120 | tf_op jit(solution)/shard_map/pallas_call | solution.py:297
  134.6 8.6 %collective-permute-start.11 = (f32[7,32,128]{2,1,0:T(8,128)S(1)}, f32[7,32,128]{2,1,0:T(8,128)S(1)}, u32[]{:S(2)}, u32[]{:S(2)}) collective-permute-start(f32[7,32,128]{2,1,0:T(8,128)S(1)} %get-tuple-element.57), channel_id=1, source_target_pairs={{1,2},{2,1},{3,4},{4,3},{5,6},{6,5},{7,8},{8,7},{9,10},{10,9},{11,... | collective-permute-start | bytes 344072 | tf_op jit(solution)/shard_map/ppermute | solution.py:314
  143.3 8.3 %collective-permute-done.11.scaled_b = f32[7,32,128]{2,1,0:T(8,128)S(1)} collective-permute-done((f32[7,32,128]{2,1,0:T(8,128)S(1)}, f32[7,32,128]{2,1,0:T(8,128)S(1)}, u32[]{:S(2)}, u32[]{:S(2)}) %collective-permute-start.11) | collective-permute-done | bytes 114720 | tf_op jit(solution)/shard_map/ppermute | solution.py:314
  152.5 2.4 %shard_map.144 = (f32[8,32,128]{2,1,0:T(8,128)}, f32[8,32,128]{2,1,0:T(8,128)S(1)}, f32[4,32,128]{2,1,0:T(8,128)S(1)}, f32[4,32,128]{2,1,0:T(8,128)S(1)}, f32[2,8,32,128]{3,2,1,0:T(8,128)S(1)}) custom-call(s32[5]{0:T(128)S(1)} %stack.32.info, f32[8,32,128]{2,1,0:T(8,128)S(1)} %copy-done.5, f32[8,32,128]{2,1,0:T(8,128)S(1)} %get-tuple-element.48.q_now.q_after, ...), custom_call_target="tpu_custom_call" | custom-call | flops 2000000 | bytes 3112960 | tf_op jit(solution)/shard_map/pallas_call | solution.py:297
  156.7 8.6 %collective-permute-start.13 = (f32[4,32,128]{2,1,0:T(8,128)S(1)}, f32[4,32,128]{2,1,0:T(8,128)S(1)}, u32[]{:S(2)}, u32[]{:S(2)}) collective-permute-start(f32[4,32,128]{2,1,0:T(8,128)S(1)} %get-tuple-element.64), channel_id=1, source_target_pairs={{1,2},{2,1},{3,4},{4,3},{5,6},{6,5},{7,8},{8,7},{9,10},{10,9},{11,... | collective-permute-start | bytes 196616 | tf_op jit(solution)/shard_map/ppermute | solution.py:314
  165.4 7.7 %collective-permute-done.13.scaled_b = f32[4,32,128]{2,1,0:T(8,128)S(1)} collective-permute-done((f32[4,32,128]{2,1,0:T(8,128)S(1)}, f32[4,32,128]{2,1,0:T(8,128)S(1)}, u32[]{:S(2)}, u32[]{:S(2)}) %collective-permute-start.13) | collective-permute-done | bytes 65568 | tf_op jit(solution)/shard_map/ppermute | solution.py:314
  175.1 20.6 %all_to_all.10.arrived = f32[32,2,8,128]{3,2,1,0:T(8,128)S(1)} all-to-all(f32[32,2,8,128]{3,2,1,0:T(8,128)S(1)} %bitcast.61), channel_id=1, replica_groups=mesh['shot'=32,'dom'=16] {'shot'}, dimensions={0} | all-to-all | bytes 524288 | tf_op jit(solution)/shard_map/all_to_all | solution.py:417
  (46 shorter events, 17.2 us)
Async XLA Ops:
  0.6 0.7 copy-start.8
  3.0 34.0 %all-to-all-start = ((f32[32,2,8,128]{3,2,1,0:T(8,128)}), f32[32,2,8,128]{3,2,1,0:T(8,128)S(1)}, u32[]{:S(2)}, u32[]{:S(2)}) async-start(f32[32,2,8,128]{3,2,1,0:T(8,128)} %select_select_fusion), calls=%async_computation | async-start | bytes 524288 | tf_op jit(solution)/shard_map/all_to_all | solution.py:346
  37.0 0.9 copy-start.1
  37.9 12.2 %copy-start = (f32[1,8,32,128]{3,2,1,0:T(8,128)S(1)}, f32[1,8,32,128]{3,2,1,0:T(8,128)}, u32[]{:S(2)}) copy-start(f32[1,8,32,128]{3,2,1,0:T(8,128)} %param.11) | copy-start | bytes 393220
  38.5 28.6 %collective-permute-start.2 = (f32[11,32,128]{2,1,0:T(8,128)S(1)}, f32[11,32,128]{2,1,0:T(8,128)S(1)}, u32[]{:S(2)}, u32[]{:S(2)}) collective-permute-start(f32[11,32,128]{2,1,0:T(8,128)S(1)} %get-tuple-element.37), channel_id=1, source_target_pairs={{1,0},{0,1},{3,2},{2,3},{5,4},{4,5},{7,6},{6,7},{9,8},{8,9},{11,10... | collective-permute-start | bytes 540680 | tf_op jit(solution)/shard_map/ppermute | solution.py:315
  42.2 24.9 %copy-start.2 = (f32[1,8,32,128]{3,2,1,0:T(8,128)S(1)}, f32[1,8,32,128]{3,2,1,0:T(8,128)}, u32[]{:S(2)}) copy-start(f32[1,8,32,128]{3,2,1,0:T(8,128)} %param.12) | copy-start | bytes 393220
  42.2 24.9 %copy-start.3 = (f32[1,8,32,128]{3,2,1,0:T(8,128)S(1)}, f32[1,8,32,128]{3,2,1,0:T(8,128)}, u32[]{:S(2)}) copy-start(f32[1,8,32,128]{3,2,1,0:T(8,128)} %param.14) | copy-start | bytes 393220
  42.2 24.9 %collective-permute-start.3 = (f32[11,32,128]{2,1,0:T(8,128)S(1)}, f32[11,32,128]{2,1,0:T(8,128)S(1)}, u32[]{:S(2)}, u32[]{:S(2)}) collective-permute-start(f32[11,32,128]{2,1,0:T(8,128)S(1)} %get-tuple-element.38), channel_id=1, source_target_pairs={{1,2},{2,1},{3,4},{4,3},{5,6},{6,5},{7,8},{8,7},{9,10},{10,9},{11,... | collective-permute-start | bytes 540680 | tf_op jit(solution)/shard_map/ppermute | solution.py:314
  50.1 16.9 %collective-permute-start.1 = (f32[7,32,128]{2,1,0:T(8,128)S(1)}, f32[7,32,128]{2,1,0:T(8,128)S(1)}, u32[]{:S(2)}, u32[]{:S(2)}) collective-permute-start(f32[7,32,128]{2,1,0:T(8,128)S(1)} %get-tuple-element.74), channel_id=1, source_target_pairs={{1,2},{2,1},{3,4},{4,3},{5,6},{6,5},{7,8},{8,7},{9,10},{10,9},{11,... | collective-permute-start | bytes 344072 | tf_op jit(solution)/shard_map/ppermute | solution.py:314
  58.8 8.3 %collective-permute-start = (f32[7,32,128]{2,1,0:T(8,128)S(1)}, f32[7,32,128]{2,1,0:T(8,128)S(1)}, u32[]{:S(2)}, u32[]{:S(2)}) collective-permute-start(f32[7,32,128]{2,1,0:T(8,128)S(1)} %get-tuple-element.75), channel_id=1, source_target_pairs={{1,0},{0,1},{3,2},{2,3},{5,4},{4,5},{7,6},{6,7},{9,8},{8,9},{11,10... | collective-permute-start | bytes 344072 | tf_op jit(solution)/shard_map/ppermute | solution.py:315
  70.4 10.6 %collective-permute-start.4 = (f32[7,32,128]{2,1,0:T(8,128)S(1)}, f32[7,32,128]{2,1,0:T(8,128)S(1)}, u32[]{:S(2)}, u32[]{:S(2)}) collective-permute-start(f32[7,32,128]{2,1,0:T(8,128)S(1)} %get-tuple-element.41), channel_id=1, source_target_pairs={{1,0},{0,1},{3,2},{2,3},{5,4},{4,5},{7,6},{6,7},{9,8},{8,9},{11,10... | collective-permute-start | bytes 344072 | tf_op jit(solution)/shard_map/ppermute | solution.py:315
  72.3 16.9 %collective-permute-start.5 = (f32[7,32,128]{2,1,0:T(8,128)S(1)}, f32[7,32,128]{2,1,0:T(8,128)S(1)}, u32[]{:S(2)}, u32[]{:S(2)}) collective-permute-start(f32[7,32,128]{2,1,0:T(8,128)S(1)} %get-tuple-element.42), channel_id=1, source_target_pairs={{1,2},{2,1},{3,4},{4,3},{5,6},{6,5},{7,8},{8,7},{9,10},{10,9},{11,... | collective-permute-start | bytes 344072 | tf_op jit(solution)/shard_map/ppermute | solution.py:314
  89.3 12.3 %copy-start.9 = (f32[1,3,512]{2,0,1:T(1,128)S(1)}, f32[1,3,512]{2,0,1:T(1,128)}, u32[]{:S(2)}) copy-start(f32[1,3,512]{2,0,1:T(1,128)} %param.21) | copy-start | bytes 18436
  91.0 12.0 %collective-permute-start.6 = (f32[7,32,128]{2,1,0:T(8,128)S(1)}, f32[7,32,128]{2,1,0:T(8,128)S(1)}, u32[]{:S(2)}, u32[]{:S(2)}) collective-permute-start(f32[7,32,128]{2,1,0:T(8,128)S(1)} %get-tuple-element.45), channel_id=1, source_target_pairs={{1,0},{0,1},{3,2},{2,3},{5,4},{4,5},{7,6},{6,7},{9,8},{8,9},{11,10... | collective-permute-start | bytes 344072 | tf_op jit(solution)/shard_map/ppermute | solution.py:315
  92.9 8.7 %copy-start.7 = (s32[1,512]{1,0:T(1,128)S(1)}, s32[1,512]{1,0:T(1,128)}, u32[]{:S(2)}) copy-start(s32[1,512]{1,0:T(1,128)} %cells.1) | copy-start | bytes 6148
  92.9 16.9 %collective-permute-start.7 = (f32[7,32,128]{2,1,0:T(8,128)S(1)}, f32[7,32,128]{2,1,0:T(8,128)S(1)}, u32[]{:S(2)}, u32[]{:S(2)}) collective-permute-start(f32[7,32,128]{2,1,0:T(8,128)S(1)} %get-tuple-element.46), channel_id=1, source_target_pairs={{1,2},{2,1},{3,4},{4,3},{5,6},{6,5},{7,8},{8,7},{9,10},{10,9},{11,... | collective-permute-start | bytes 344072 | tf_op jit(solution)/shard_map/ppermute | solution.py:314
  111.5 10.6 %collective-permute-start.8 = (f32[7,32,128]{2,1,0:T(8,128)S(1)}, f32[7,32,128]{2,1,0:T(8,128)S(1)}, u32[]{:S(2)}, u32[]{:S(2)}) collective-permute-start(f32[7,32,128]{2,1,0:T(8,128)S(1)} %get-tuple-element.50), channel_id=1, source_target_pairs={{1,0},{0,1},{3,2},{2,3},{5,4},{4,5},{7,6},{6,7},{9,8},{8,9},{11,10... | collective-permute-start | bytes 344072 | tf_op jit(solution)/shard_map/ppermute | solution.py:315
  113.4 16.9 %collective-permute-start.9 = (f32[7,32,128]{2,1,0:T(8,128)S(1)}, f32[7,32,128]{2,1,0:T(8,128)S(1)}, u32[]{:S(2)}, u32[]{:S(2)}) collective-permute-start(f32[7,32,128]{2,1,0:T(8,128)S(1)} %get-tuple-element.51), channel_id=1, source_target_pairs={{1,2},{2,1},{3,4},{4,3},{5,6},{6,5},{7,8},{8,7},{9,10},{10,9},{11,... | collective-permute-start | bytes 344072 | tf_op jit(solution)/shard_map/ppermute | solution.py:314
  132.7 10.6 %collective-permute-start.10 = (f32[7,32,128]{2,1,0:T(8,128)S(1)}, f32[7,32,128]{2,1,0:T(8,128)S(1)}, u32[]{:S(2)}, u32[]{:S(2)}) collective-permute-start(f32[7,32,128]{2,1,0:T(8,128)S(1)} %get-tuple-element.56), channel_id=1, source_target_pairs={{1,0},{0,1},{3,2},{2,3},{5,4},{4,5},{7,6},{6,7},{9,8},{8,9},{11,10... | collective-permute-start | bytes 344072 | tf_op jit(solution)/shard_map/ppermute | solution.py:315
  134.6 16.9 %collective-permute-start.11 = (f32[7,32,128]{2,1,0:T(8,128)S(1)}, f32[7,32,128]{2,1,0:T(8,128)S(1)}, u32[]{:S(2)}, u32[]{:S(2)}) collective-permute-start(f32[7,32,128]{2,1,0:T(8,128)S(1)} %get-tuple-element.57), channel_id=1, source_target_pairs={{1,2},{2,1},{3,4},{4,3},{5,6},{6,5},{7,8},{8,7},{9,10},{10,9},{11,... | collective-permute-start | bytes 344072 | tf_op jit(solution)/shard_map/ppermute | solution.py:314
  151.6 0.9 copy-start.5
  154.8 10.6 %collective-permute-start.12 = (f32[4,32,128]{2,1,0:T(8,128)S(1)}, f32[4,32,128]{2,1,0:T(8,128)S(1)}, u32[]{:S(2)}, u32[]{:S(2)}) collective-permute-start(f32[4,32,128]{2,1,0:T(8,128)S(1)} %get-tuple-element.63), channel_id=1, source_target_pairs={{1,0},{0,1},{3,2},{2,3},{5,4},{4,5},{7,6},{6,7},{9,8},{8,9},{11,10... | collective-permute-start | bytes 196616 | tf_op jit(solution)/shard_map/ppermute | solution.py:315
  156.7 16.4 %collective-permute-start.13 = (f32[4,32,128]{2,1,0:T(8,128)S(1)}, f32[4,32,128]{2,1,0:T(8,128)S(1)}, u32[]{:S(2)}, u32[]{:S(2)}) collective-permute-start(f32[4,32,128]{2,1,0:T(8,128)S(1)} %get-tuple-element.64), channel_id=1, source_target_pairs={{1,2},{2,1},{3,4},{4,3},{5,6},{6,5},{7,8},{8,7},{9,10},{10,9},{11,... | collective-permute-start | bytes 196616 | tf_op jit(solution)/shard_map/ppermute | solution.py:314
  173.1 0.9 copy-start.4
  (1 other events, 0.7 us)

commit v3 on v2

--- a/solution.py
+++ b/solution.py
@@ -14,6 +14,7 @@
 PAD = 8
 ROWS = CY + 2 * PAD
 WIDE = CX + 14
+BESIDE = 400_000_000
 
 COEFFS = (1225.0 / 1024.0, -245.0 / 3072.0, 49.0 / 5120.0, -5.0 / 7168.0)
 step_squared = 0.02
@@ -60,18 +61,28 @@
         target[width + CX : 2 * width + CX, inner, :] = first
 
 
-def hand_over(info, first, second, head, tail):
+def for_partner(info, target, head, tail):
     odd = info[0] == 1
 
     @pl.when(odd)
     def _():
-        first[...] = head()
-        second[...] = tail()
+        target[...] = head()
 
     @pl.when(jnp.logical_not(odd))
     def _():
-        first[...] = tail()
-        second[...] = head()
+        target[...] = tail()
+
+
+def choose_kernel(where, aperture, kappa, buoy, out):
+    for s in range(out.shape[0]):
+        t = aperture[s, where[0]]
+        out[s, 0] = kappa[t]
+        out[s, 1] = buoy[t]
+
+
+def first_swap_kernel(info, field, out):
+    width = out.shape[0]
+    for_partner(info, out, lambda: field[0:width], lambda: field[CX - width : CX])
 
 
 def slope_x(field, at):
@@ -134,12 +145,20 @@
         out[n + 1] = total.reshape(CX, CY, CZ)
 
 
-def model_kernel(info, stiff, buoy, last, send_a, send_b, scaled):
+def model_kernel(info, stiff, buoy, last, send_b, scaled):
     scaled[...] = stiff[...] * last[...]
-    hand_over(
+    for_partner(
         info,
-        send_a,
         send_b,
+        lambda: jnp.concatenate([buoy[4:8], scaled[1:8]], axis=0),
+        lambda: jnp.concatenate([buoy[0:4], scaled[0:7]], axis=0),
+    )
+
+
+def model_swap_kernel(info, buoy, scaled, out):
+    for_partner(
+        info,
+        out,
         lambda: jnp.concatenate([buoy[0:4], scaled[0:7]], axis=0),
         lambda: jnp.concatenate([buoy[4:8], scaled[1:8]], axis=0),
     )
@@ -183,8 +202,8 @@
 
 
 def first_kernel(
-    info, wave, now, now_a, now_b, before, last, after, stiff, buoy, edge_a, edge_b, scaled,
-    p_out, send_a, send_b, div_out, slope_out, buoy_out, q_out,
+    info, wave, now, now_a, now_b, before, stiff, buoy, edge_a, edge_b,
+    p_out, send_b, div_out, slope_out, buoy_out,
     field, gx, gy, acc,
 ):
     widen_buoy(info, buoy, edge_a, edge_b, buoy_out)
@@ -194,15 +213,23 @@
         p_out[cell] = value
 
     forward(info, wave, 0, now, before, stiff, field, buoy_out, gx, gy, acc, div_out, slope_out, store)
-    hand_over(info, send_a, send_b, lambda: p_out[0:7], lambda: p_out[1:8])
+    for_partner(info, send_b, lambda: p_out[1:8], lambda: p_out[0:7])
+
+
+def adjoint_part_kernel(
+    info, p, last, after, scaled, edge_a, edge_b, buoy,
+    send_a, q_out,
+    field, gx, gy, acc,
+):
+    for_partner(info, send_a, lambda: p[0:7], lambda: p[1:8])
     place(info, field, scaled[...], edge_a[4:11], edge_b[4:11], 7)
-    for cell, div in operate(field, 7, buoy_out, gx, gy, acc, lambda *_: None):
+    for cell, div in operate(field, 7, buoy, gx, gy, acc, lambda *_: None):
         q_out[cell] = 2.0 * last[cell] - after[cell] + step_squared * div
 
 
 def second_kernel(
     info, wave, now, now_a, now_b, before, stiff, buoy,
-    p_out, send_a, send_b, div_out, slope_out,
+    p_out, send_b, div_out, slope_out,
     field, gx, gy, acc,
 ):
     place(info, field, now[...], now_a[...], now_b[...], 7)
@@ -211,12 +238,12 @@
         p_out[cell] = value
 
     forward(info, wave, 1, now, before, stiff, field, buoy, gx, gy, acc, div_out, slope_out, store)
-    hand_over(info, send_a, send_b, lambda: p_out[0:7], lambda: p_out[1:8])
+    for_partner(info, send_b, lambda: p_out[1:8], lambda: p_out[0:7])
 
 
 def third_kernel(
     info, wave, now, now_a, now_b, before, stiff, buoy, q_part, spots,
-    q_out, scaled, send_a, send_b, div_out, slope_out,
+    q_out, scaled, send_b, div_out, slope_out,
     field, gx, gy, acc,
 ):
     place(info, field, now[...], now_a[...], now_b[...], 7)
@@ -227,39 +254,57 @@
         scaled[cell] = stiff[cell] * q
 
     forward(info, wave, 2, now, before, stiff, field, buoy, gx, gy, acc, div_out, slope_out, store)
-    hand_over(info, send_a, send_b, lambda: scaled[0:7], lambda: scaled[1:8])
+    for_partner(info, send_b, lambda: scaled[1:8], lambda: scaled[0:7])
 
 
 def adjoint_kernel(
-    n, width, info, q_now, q_after, scaled, scaled_a, scaled_b, stiff, buoy, spots, p_then, div, slope, images,
-    q_out, scaled_out, send_a, send_b, images_out,
+    n, width, info, q_now, q_after, scaled, scaled_a, scaled_b, stiff, buoy, spots, p_then,
+    q_out, scaled_out, send_b, slope_out,
     field, gx, gy, acc,
 ):
     place(info, field, scaled[...], scaled_a[...], scaled_b[...], 7)
 
-    def image(cell, sx, sy, sz):
-        kappa = q_now[cell] * div[cell]
-        rho = slope[0, cell] * sx + slope[1, cell] * sy + slope[2, cell] * sz
-        if images is not None:
-            kappa = images[0, cell] + kappa
-            rho = images[1, cell] + rho
-        images_out[0, cell] = kappa
-        images_out[1, cell] = rho
-
-    for cell, total in operate(field, 7, buoy, gx, gy, acc, image):
+    def keep(cell, sx, sy, sz):
+        slope_out[0, cell] = sx
+        slope_out[1, cell] = sy
+        slope_out[2, cell] = sz
+
+    for cell, total in operate(field, 7, buoy, gx, gy, acc, keep):
         q = 2.0 * q_now[cell] - q_after[cell] + step_squared * total
         q = q + (spots[0, cell] * p_then[cell] - spots[n + 1, cell])
         q_out[cell] = q
         scaled_out[cell] = stiff[cell] * q
-    hand_over(info, send_a, send_b, lambda: scaled_out[0:width], lambda: scaled_out[CX - width : CX])
-
-
-def adjoint_first_kernel(info, q_now, q_after, scaled, scaled_a, scaled_b, stiff, buoy, spots, p_then, div, slope, *rest):
-    adjoint_kernel(1, 7, info, q_now, q_after, scaled, scaled_a, scaled_b, stiff, buoy, spots, p_then, div, slope, None, *rest)
-
-
-def adjoint_second_kernel(info, q_now, q_after, scaled, scaled_a, scaled_b, stiff, buoy, spots, p_then, div, slope, images, *rest):
-    adjoint_kernel(0, 4, info, q_now, q_after, scaled, scaled_a, scaled_b, stiff, buoy, spots, p_then, div, slope, images, *rest)
+    for_partner(info, send_b, lambda: scaled_out[CX - width : CX], lambda: scaled_out[0:width])
+
+
+def adjoint_first_kernel(*refs):
+    adjoint_kernel(1, 7, *refs)
+
+
+def adjoint_second_kernel(*refs):
+    adjoint_kernel(0, 4, *refs)
+
+
+def image_first_kernel(info, scaled, q_now, slope_q, div, slope_p, q_new, send_a, out, q_out):
+    q_out[...] = q_new[...]
+    width = send_a.shape[0]
+    for_partner(info, send_a, lambda: scaled[0:width], lambda: scaled[CX - width : CX])
+    for cell in range(CX):
+        out[0, cell] = q_now[cell] * div[cell]
+        rho = slope_p[0, cell] * slope_q[0, cell] + slope_p[1, cell] * slope_q[1, cell]
+        out[1, cell] = rho + slope_p[2, cell] * slope_q[2, cell]
+
+
+def image_second_kernel(
+    info, scaled, q_now, slope_q, div, slope_p, images, q_new, send_a, out, q_out
+):
+    q_out[...] = q_new[...]
+    width = send_a.shape[0]
+    for_partner(info, send_a, lambda: scaled[0:width], lambda: scaled[CX - width : CX])
+    for cell in range(CX):
+        out[0, cell] = images[0, cell] + q_now[cell] * div[cell]
+        rho = slope_p[0, cell] * slope_q[0, cell] + slope_p[1, cell] * slope_q[1, cell]
+        out[1, cell] = images[1, cell] + (rho + slope_p[2, cell] * slope_q[2, cell])
 
 
 def image_kernel(info, q_now, scaled, scaled_a, scaled_b, div, slope, images, out, field):
@@ -305,14 +350,16 @@
     )(*scalars, *arrays)
 
 
-def swap(first, second):
+def swap_first(planes):
     count = lax.axis_size("dom")
-    pairs_a = [(i ^ 1, i) for i in range(count)]
-    pairs_b = []
-    for i in range(1, count - 1, 2):
-        pairs_b += [(i, i + 1), (i + 1, i)]
-    second = lax.ppermute(second, "dom", pairs_b)
-    return lax.ppermute(first, "dom", pairs_a), second
+    return lax.ppermute(planes, "dom", [(i ^ 1, i) for i in range(count)])
+
+
+def swap_second(planes):
+    pairs = []
+    for i in range(1, lax.axis_size("dom") - 1, 2):
+        pairs += [(i, i + 1), (i + 1, i)]
+    return lax.ppermute(planes, "dom", pairs)
 
 
 def shards(
@@ -338,17 +385,20 @@
     wave = source_wave[0]
     column = lax.dynamic_index_in_dim(aperture, dom, 1, keepdims=False)
 
-    stacked = jnp.stack((kappa_model, buoy_model), axis=1)
-    picks = column[:, None, None, None]
-    chosen = stacked[0][None]
-    for t in range(1, TILES):
-        chosen = jnp.where(picks == t, stacked[t][None], chosen)
+    shots = aperture.shape[0]
+    (chosen,) = call(
+        choose_kernel,
+        [dom.reshape(1).astype(jnp.int32), aperture],
+        [kappa_model, buoy_model],
+        [jax.ShapeDtypeStruct((shots, 2, CX, CZ), F32)],
+    )
     block = lax.all_to_all(chosen, "shot", 0, 0, tiled=True)
 
     p0, p_prev = pressure_now[0], pressure_prev[0]
     q4, q5 = adjoint_last[0], adjoint_after[0]
     head, tail = p0[0:7], p0[1:8]
-    p0_a, p0_b = swap(jnp.where(odd == 1, head, tail), jnp.where(odd == 1, tail, head))
+    p0_b = swap_second(jnp.where(odd == 1, tail, head))
+    p0_a = swap_first(jnp.where(odd == 1, head, tail))
     (spots,) = call(
         receivers_kernel,
         [info],
@@ -356,6 +406,7 @@
         [jax.ShapeDtypeStruct((STEPS + 1, CX, CY, CZ), F32)],
         flops=400_000_000,
     )
+    block, p0_a, p0_b, spots = lax.optimization_barrier((block, p0_a, p0_b, spots))
 
     stiff = block[:, 0].transpose(1, 0, 2)
     buoy = block[:, 1].transpose(1, 0, 2)
@@ -363,50 +414,80 @@
     slopes = jax.ShapeDtypeStruct((3, CX, CY, CZ), F32)
     images = jax.ShapeDtypeStruct((2, CX, CY, CZ), F32)
 
-    send_a, send_b, f4 = call(
-        model_kernel, [info], [stiff, buoy, q4], [plane_field(11), plane_field(11), own]
-    )
-    edge_a, edge_b = swap(send_a, send_b)
-    p1, send_a, send_b, div0, slope0, wide, q_part = call(
+    send_b, f4 = call(model_kernel, [info], [stiff, buoy, q4], [plane_field(11), own])
+    edge_b = swap_second(send_b)
+    (send_a,) = call(model_swap_kernel, [info], [buoy, f4], [plane_field(11)], flops=BESIDE)
+    edge_a = swap_first(send_a)
+
+    p1, send_b, div0, slope0, wide = call(
         first_kernel,
         [info, wave],
-        [p0, p0_a, p0_b, p_prev, q4, q5, stiff, buoy, edge_a, edge_b, f4],
-        [own, seven, seven, own, slopes, plane_field(CX + 8), own],
+        [p0, p0_a, p0_b, p_prev, stiff, buoy, edge_a, edge_b],
+        [own, seven, own, slopes, plane_field(CX + 8)],
         work(),
     )
-    from_a, from_b = swap(send_a, send_b)
-    p2, send_a, send_b, div1, slope1 = call(
+    from_b = swap_second(send_b)
+    send_a, q_part = call(
+        adjoint_part_kernel, [info], [p1, q4, q5, f4, edge_a, edge_b, wide], [seven, own], work(), BESIDE
+    )
+    from_a = swap_first(send_a)
+
+    p2, send_b, div1, slope1 = call(
         second_kernel,
         [info, wave],
         [p1, from_a, from_b, p0, stiff, wide],
-        [own, seven, seven, own, slopes],
+        [own, seven, own, slopes],
         work(),
     )
-    from_a, from_b = swap(send_a, send_b)
-    q3, f3, send_a, send_b, div2, slope2 = call(
+    from_b = swap_second(send_b)
+    (send_a,) = call(first_swap_kernel, [info], [p2], [seven], flops=BESIDE)
+    from_a = swap_first(send_a)
+
+    q3, f3, send_b, div2, slope2 = call(
         third_kernel,
         [info, wave],
         [p2, from_a, from_b, p1, stiff, wide, q_part, spots],
-        [own, own, seven, seven, own, slopes],
+        [own, own, seven, own, slopes],
         work(),
     )
-    from_a, from_b = swap(send_a, send_b)
-    q2, f2, send_a, send_b, image = call(
+    from_b = swap_second(send_b)
+    (send_a,) = call(first_swap_kernel, [info], [f3], [seven], flops=BESIDE)
+    from_a = swap_first(send_a)
+
+    q2, f2, send_b, slope_q = call(
         adjoint_first_kernel,
         [info],
-        [q3, q4, f3, from_a, from_b, stiff, wide, spots, p2, div2, slope2],
-        [own, own, seven, seven, images],
+        [q3, q4, f3, from_a, from_b, stiff, wide, spots, p2],
+        [own, own, seven, slopes],
         work(),
     )
-    from_a, from_b = swap(send_a, send_b)
-    q1, f1, send_a, send_b, image = call(
+    from_b = swap_second(send_b)
+    send_a, image, q2_out = call(
+        image_first_kernel,
+        [info],
+        [f2, q3, slope_q, div2, slope2, q2],
+        [seven, images, own],
+        flops=BESIDE,
+    )
+    from_a = swap_first(send_a)
+
+    q1, f1, send_b, slope_q = call(
         adjoint_second_kernel,
         [info],
-        [q2, q3, f2, from_a, from_b, stiff, wide, spots, p1, div1, slope1, image],
-        [own, own, four, four, images],
+        [q2, q3, f2, from_a, from_b, stiff, wide, spots, p1],
+        [own, own, four, slopes],
         work(),
     )
-    from_a, from_b = swap(send_a, send_b)
+    from_b = swap_second(send_b)
+    send_a, image, q1_out = call(
+        image_second_kernel,
+        [info],
+        [f1, q2, slope_q, div1, slope1, image, q1],
+        [four, images, own],
+        flops=BESIDE,
+    )
+    from_a = swap_first(send_a)
+
     (image,) = call(
         image_kernel,
         [info],
@@ -417,7 +498,7 @@
     arrived = lax.all_to_all(image.transpose(2, 0, 1, 3), "shot", 0, 0, tiled=True)
     tiles = jax.ShapeDtypeStruct((TILES, CX, CZ), F32)
     grad_kappa, grad_buoy = call(gather_kernel, [column], [arrived], [tiles, tiles])
-    return (grad_kappa, grad_buoy, q1[None], q2[None])
+    return (grad_kappa, grad_buoy, q1_out[None], q2_out[None])
 
 
 def solution(mesh):

time: 198 us -> 201 us (1.015)
  blocking collectives: 20.6 us -> 0 us
  waiting for transfers between devices: 63.8 us -> 84.1 us
  Pallas kernels: 14.8 us -> 20 us
  local copies, waits for them, and re-layouts: 3.63 us -> 6.06 us
  other arithmetic: 2.34 us -> 0.02 us
  starting transfers between devices: 90.1 us -> 88 us
    ppermute x14, waiting for transfers between devices: 45.8 us -> 68.6 us  [the longest x7 68.6 us: swap_second(): return lax.ppermute(planes, 'dom', pairs)]
    all_to_all x1 -> x0, blocking collectives: 20.6 us -> none  [shards(): lax.all_to_all(image.transpose(2, 0, 1, 3), 'shot', 0, 0, tiled=True)]
    all_to_all x1, waiting for transfers between devices: 18 us -> 1.66 us  [shards(): block = lax.all_to_all(chosen, 'shot', 0, 0, tiled=True)]
    ppermute x14, starting transfers between devices: 74.9 us -> 58.8 us  [the longest x7 41.4 us: swap_second(): return lax.ppermute(planes, 'dom', pairs)]
    all_to_all x0 -> x1, waiting for transfers between devices: none -> 13.8 us  [shards(): lax.all_to_all(image.transpose(2, 0, 1, 3), 'shot', 0, 0, tiled=True)]
    all_to_all x0 -> x1, starting transfers between devices: none -> 13.8 us  [shards(): lax.all_to_all(image.transpose(2, 0, 1, 3), 'shot', 0, 0, tiled=True)]
    pallas_call x9 -> x16, Pallas kernels: 14.8 us -> 20 us  [call(): pl.pallas_call(kernel, out_shape=outs, in_specs=[SMEM] * len(scalars) + [...]
    unnamed x21 -> x20, local copies, waits for them, and re-layouts: 3.31 us -> 4.31 us
  transfers between devices with their start and end apart: 15 -> 16, of which waited for: 7 -> 9; matrix products, arithmetic and copies ran while one was open for 0% -> 0% of each run, Pallas kernels for 1% -> 2%
where the time goes in v3:
time: 201 us; the launch traced here: 200 us
  starting transfers between devices  88 us (44%)
  waiting for transfers between devices  84.1 us (42%)
  Pallas kernels  20 us (10%)
  local copies, waits for them, and re-layouts  6.06 us (3%)
    ppermute x7, waiting for transfers between devices, swap_second(): return lax.ppermute(planes, 'dom', pairs)  68.6 us
    ppermute x7, starting transfers between devices, swap_second(): return lax.ppermute(planes, 'dom', pairs)  41.4 us
    pallas_call x16, Pallas kernels, call(): pl.pallas_call(kernel, out_shape=outs, in_specs=[SMEM] * len(scalars) + [...  20 us
    ppermute x7, starting transfers between devices, swap_first(): return lax.ppermute(planes, 'dom', [(i ^ 1, i) for i in range(count)])  17.4 us
    all_to_all x1, starting transfers between devices, shards(): block = lax.all_to_all(chosen, 'shot', 0, 0, tiled=True)  15.4 us
    all_to_all x1, waiting for transfers between devices, shards(): lax.all_to_all(image.transpose(2, 0, 1, 3), 'shot', 0, 0, tiled=True)  13.8 us
    all_to_all x1, starting transfers between devices, shards(): lax.all_to_all(image.transpose(2, 0, 1, 3), 'shot', 0, 0, tiled=True)  13.8 us
    unnamed x20, local copies, waits for them, and re-layouts  4.31 us
  transfers between devices with their start and end apart: 16, of which 9 were waited for; matrix products, arithmetic and copies ran while one was open for 0% of the time, Pallas kernels for 2%

profile of v3, /device:TPU:7, one launch (start us, length us, event | category | flops | bytes accessed | tf_op | source)
XLA Modules:
  0.0 199.8 jit_solution(13546042474535148692)
XLA Ops:
  3.7 15.4 %all-to-all-start = ((f32[32,2,8,128]{3,2,1,0:T(8,128)}), f32[32,2,8,128]{3,2,1,0:T(8,128)S(1)}, u32[]{:S(2)}, u32[]{:S(2)}) async-start(f32[32,2,8,128]{3,2,1,0:T(8,128)} %shard_map.138), calls=%async_computation | async-start | bytes 524288 | tf_op jit(solution)/shard_map/all_to_all | solution.py:395
  19.1 8.7 %collective-permute-start.1 = (f32[7,32,128]{2,1,0:T(8,128)S(1)}, f32[7,32,128]{2,1,0:T(8,128)S(1)}, u32[]{:S(2)}, u32[]{:S(2)}) collective-permute-start(f32[7,32,128]{2,1,0:T(8,128)S(1)} %get-tuple-element.82), channel_id=1, source_target_pairs={{1,2},{2,1},{3,4},{4,3},{5,6},{6,5},{7,8},{8,7},{9,10},{10,9},{11,... | collective-permute-start | bytes 344072 | tf_op jit(solution)/shard_map/ppermute | solution.py:362
  27.8 1.9 collective-permute-start
  33.2 3.0 %collective-permute-done.1.now_b = f32[7,32,128]{2,1,0:T(8,128)S(1)} collective-permute-done((f32[7,32,128]{2,1,0:T(8,128)S(1)}, f32[7,32,128]{2,1,0:T(8,128)S(1)}, u32[]{:S(2)}, u32[]{:S(2)}) %collective-permute-start.1) | collective-permute-done | bytes 114720 | tf_op jit(solution)/shard_map/ppermute | solution.py:362
  40.0 5.9 %collective-permute-start.2 = (f32[11,32,128]{2,1,0:T(8,128)S(1)}, f32[11,32,128]{2,1,0:T(8,128)S(1)}, u32[]{:S(2)}, u32[]{:S(2)}) collective-permute-start(f32[11,32,128]{2,1,0:T(8,128)S(1)} %shard_map.141), channel_id=1, source_target_pairs={{1,0},{0,1},{3,2},{2,3},{5,4},{4,5},{7,6},{6,7},{9,8},{8,9},{11,10... | collective-permute-start | bytes 540680 | tf_op jit(solution)/shard_map/ppermute | solution.py:355
  46.0 5.5 %collective-permute-start.3 = (f32[11,32,128]{2,1,0:T(8,128)S(1)}, f32[11,32,128]{2,1,0:T(8,128)S(1)}, u32[]{:S(2)}, u32[]{:S(2)}) collective-permute-start(f32[11,32,128]{2,1,0:T(8,128)S(1)} %get-tuple-element.46), channel_id=1, source_target_pairs={{1,2},{2,1},{3,4},{4,3},{5,6},{6,5},{7,8},{8,7},{9,10},{10,9},{11,... | collective-permute-start | bytes 540680 | tf_op jit(solution)/shard_map/ppermute | solution.py:362
  51.4 12.4 %collective-permute-done.3.edge_b = f32[11,32,128]{2,1,0:T(8,128)S(1)} collective-permute-done((f32[11,32,128]{2,1,0:T(8,128)S(1)}, f32[11,32,128]{2,1,0:T(8,128)S(1)}, u32[]{:S(2)}, u32[]{:S(2)}) %collective-permute-start.3) | collective-permute-done | bytes 180256 | tf_op jit(solution)/shard_map/ppermute | solution.py:362
  66.2 5.4 %collective-permute-start.5 = (f32[7,32,128]{2,1,0:T(8,128)S(1)}, f32[7,32,128]{2,1,0:T(8,128)S(1)}, u32[]{:S(2)}, u32[]{:S(2)}) collective-permute-start(f32[7,32,128]{2,1,0:T(8,128)S(1)} %get-tuple-element.50), channel_id=1, source_target_pairs={{1,2},{2,1},{3,4},{4,3},{5,6},{6,5},{7,8},{8,7},{9,10},{10,9},{11,... | collective-permute-start | bytes 344072 | tf_op jit(solution)/shard_map/ppermute | solution.py:362
  73.3 1.9 collective-permute-start.4
  75.3 7.8 %collective-permute-done.5.now_b = f32[7,32,128]{2,1,0:T(8,128)S(1)} collective-permute-done((f32[7,32,128]{2,1,0:T(8,128)S(1)}, f32[7,32,128]{2,1,0:T(8,128)S(1)}, u32[]{:S(2)}, u32[]{:S(2)}) %collective-permute-start.5) | collective-permute-done | bytes 114720 | tf_op jit(solution)/shard_map/ppermute | solution.py:362
  85.4 1.9 collective-permute-start.6
  87.3 5.4 %collective-permute-start.7 = (f32[7,32,128]{2,1,0:T(8,128)S(1)}, f32[7,32,128]{2,1,0:T(8,128)S(1)}, u32[]{:S(2)}, u32[]{:S(2)}) collective-permute-start(f32[7,32,128]{2,1,0:T(8,128)S(1)} %get-tuple-element.52), channel_id=1, source_target_pairs={{1,2},{2,1},{3,4},{4,3},{5,6},{6,5},{7,8},{8,7},{9,10},{10,9},{11,... | collective-permute-start | bytes 344072 | tf_op jit(solution)/shard_map/ppermute | solution.py:362
  92.7 11.5 %collective-permute-done.7.now_b = f32[7,32,128]{2,1,0:T(8,128)S(1)} collective-permute-done((f32[7,32,128]{2,1,0:T(8,128)S(1)}, f32[7,32,128]{2,1,0:T(8,128)S(1)}, u32[]{:S(2)}, u32[]{:S(2)}) %collective-permute-start.7) | collective-permute-done | bytes 114720 | tf_op jit(solution)/shard_map/ppermute | solution.py:362
  106.4 1.9 collective-permute-start.8
  108.4 5.4 %collective-permute-start.9 = (f32[7,32,128]{2,1,0:T(8,128)S(1)}, f32[7,32,128]{2,1,0:T(8,128)S(1)}, u32[]{:S(2)}, u32[]{:S(2)}) collective-permute-start(f32[7,32,128]{2,1,0:T(8,128)S(1)} %get-tuple-element.57), channel_id=1, source_target_pairs={{1,2},{2,1},{3,4},{4,3},{5,6},{6,5},{7,8},{8,7},{9,10},{10,9},{11,... | collective-permute-start | bytes 344072 | tf_op jit(solution)/shard_map/ppermute | solution.py:362
  113.8 11.5 %collective-permute-done.9.refs_5_ = f32[7,32,128]{2,1,0:T(8,128)S(1)} collective-permute-done((f32[7,32,128]{2,1,0:T(8,128)S(1)}, f32[7,32,128]{2,1,0:T(8,128)S(1)}, u32[]{:S(2)}, u32[]{:S(2)}) %collective-permute-start.9) | collective-permute-done | bytes 114720 | tf_op jit(solution)/shard_map/ppermute | solution.py:362
  128.3 1.9 collective-permute-start.10
  130.2 5.4 %collective-permute-start.11 = (f32[7,32,128]{2,1,0:T(8,128)S(1)}, f32[7,32,128]{2,1,0:T(8,128)S(1)}, u32[]{:S(2)}, u32[]{:S(2)}) collective-permute-start(f32[7,32,128]{2,1,0:T(8,128)S(1)} %get-tuple-element.64), channel_id=1, source_target_pairs={{1,2},{2,1},{3,4},{4,3},{5,6},{6,5},{7,8},{8,7},{9,10},{10,9},{11,... | collective-permute-start | bytes 344072 | tf_op jit(solution)/shard_map/ppermute | solution.py:362
  135.6 11.5 %collective-permute-done.11.refs_5_ = f32[7,32,128]{2,1,0:T(8,128)S(1)} collective-permute-done((f32[7,32,128]{2,1,0:T(8,128)S(1)}, f32[7,32,128]{2,1,0:T(8,128)S(1)}, u32[]{:S(2)}, u32[]{:S(2)}) %collective-permute-start.11) | collective-permute-done | bytes 114720 | tf_op jit(solution)/shard_map/ppermute | solution.py:362
  150.1 1.9 collective-permute-start.12
  152.0 5.4 %collective-permute-start.13 = (f32[4,32,128]{2,1,0:T(8,128)S(1)}, f32[4,32,128]{2,1,0:T(8,128)S(1)}, u32[]{:S(2)}, u32[]{:S(2)}) collective-permute-start(f32[4,32,128]{2,1,0:T(8,128)S(1)} %get-tuple-element.72), channel_id=1, source_target_pairs={{1,2},{2,1},{3,4},{4,3},{5,6},{6,5},{7,8},{8,7},{9,10},{10,9},{11,... | collective-permute-start | bytes 196616 | tf_op jit(solution)/shard_map/ppermute | solution.py:362
  157.5 11.0 %collective-permute-done.13.scaled_b = f32[4,32,128]{2,1,0:T(8,128)S(1)} collective-permute-done((f32[4,32,128]{2,1,0:T(8,128)S(1)}, f32[4,32,128]{2,1,0:T(8,128)S(1)}, u32[]{:S(2)}, u32[]{:S(2)}) %collective-permute-start.13) | collective-permute-done | bytes 65568 | tf_op jit(solution)/shard_map/ppermute | solution.py:362
  170.2 13.8 %all-to-all-start.1 = ((f32[32,2,8,128]{3,2,1,0:T(8,128)}), f32[32,2,8,128]{3,2,1,0:T(8,128)S(1)}, u32[]{:S(2)}, u32[]{:S(2)}) async-start(f32[32,2,8,128]{3,2,1,0:T(8,128)} %bitcast.32), calls=%async_computation.1 | async-start | bytes 524288 | tf_op jit(solution)/shard_map/all_to_all | solution.py:498
  184.7 13.8 %all-to-all-done.1.arrived = f32[32,2,8,128]{3,2,1,0:T(8,128)S(1)} async-done(((f32[32,2,8,128]{3,2,1,0:T(8,128)}), f32[32,2,8,128]{3,2,1,0:T(8,128)S(1)}, u32[]{:S(2)}, u32[]{:S(2)}) %all-to-all-start.1) | async-done | bytes 262176 | tf_op jit(solution)/shard_map/all_to_all | solution.py:498
  (50 shorter events, 27.8 us)
Async XLA Ops:
  0.6 0.8 copy-start.3
  1.4 0.7 copy-start.4
  3.7 15.4 %copy-start = (f32[1,8,32,128]{3,2,1,0:T(8,128)S(1)}, f32[1,8,32,128]{3,2,1,0:T(8,128)}, u32[]{:S(2)}) copy-start(f32[1,8,32,128]{3,2,1,0:T(8,128)} %param.11) | copy-start | bytes 393220
  3.7 34.1 %all-to-all-start = ((f32[32,2,8,128]{3,2,1,0:T(8,128)}), f32[32,2,8,128]{3,2,1,0:T(8,128)S(1)}, u32[]{:S(2)}, u32[]{:S(2)}) async-start(f32[32,2,8,128]{3,2,1,0:T(8,128)} %shard_map.138), calls=%async_computation | async-start | bytes 524288 | tf_op jit(solution)/shard_map/all_to_all | solution.py:395
  19.1 17.0 %collective-permute-start.1 = (f32[7,32,128]{2,1,0:T(8,128)S(1)}, f32[7,32,128]{2,1,0:T(8,128)S(1)}, u32[]{:S(2)}, u32[]{:S(2)}) collective-permute-start(f32[7,32,128]{2,1,0:T(8,128)S(1)} %get-tuple-element.82), channel_id=1, source_target_pairs={{1,2},{2,1},{3,4},{4,3},{5,6},{6,5},{7,8},{8,7},{9,10},{10,9},{11,... | collective-permute-start | bytes 344072 | tf_op jit(solution)/shard_map/ppermute | solution.py:362
  27.8 8.3 %collective-permute-start = (f32[7,32,128]{2,1,0:T(8,128)S(1)}, f32[7,32,128]{2,1,0:T(8,128)S(1)}, u32[]{:S(2)}, u32[]{:S(2)}) collective-permute-start(f32[7,32,128]{2,1,0:T(8,128)S(1)} %get-tuple-element.83), channel_id=1, source_target_pairs={{1,0},{0,1},{3,2},{2,3},{5,4},{4,5},{7,6},{6,7},{9,8},{8,9},{11,10... | collective-permute-start | bytes 344072 | tf_op jit(solution)/shard_map/ppermute | solution.py:355
  30.5 0.7 copy-start.8
  31.2 0.7 copy-start.7
  37.9 0.9 copy-start.1
  39.4 24.4 %copy-start.2 = (f32[1,8,32,128]{3,2,1,0:T(8,128)S(1)}, f32[1,8,32,128]{3,2,1,0:T(8,128)}, u32[]{:S(2)}) copy-start(f32[1,8,32,128]{3,2,1,0:T(8,128)} %param.12) | copy-start | bytes 393220
  40.0 11.4 %collective-permute-start.2 = (f32[11,32,128]{2,1,0:T(8,128)S(1)}, f32[11,32,128]{2,1,0:T(8,128)S(1)}, u32[]{:S(2)}, u32[]{:S(2)}) collective-permute-start(f32[11,32,128]{2,1,0:T(8,128)S(1)} %shard_map.141), channel_id=1, source_target_pairs={{1,0},{0,1},{3,2},{2,3},{5,4},{4,5},{7,6},{6,7},{9,8},{8,9},{11,10... | collective-permute-start | bytes 540680 | tf_op jit(solution)/shard_map/ppermute | solution.py:355
  46.0 17.9 %collective-permute-start.3 = (f32[11,32,128]{2,1,0:T(8,128)S(1)}, f32[11,32,128]{2,1,0:T(8,128)S(1)}, u32[]{:S(2)}, u32[]{:S(2)}) collective-permute-start(f32[11,32,128]{2,1,0:T(8,128)S(1)} %get-tuple-element.46), channel_id=1, source_target_pairs={{1,2},{2,1},{3,4},{4,3},{5,6},{6,5},{7,8},{8,7},{9,10},{10,9},{11,... | collective-permute-start | bytes 540680 | tf_op jit(solution)/shard_map/ppermute | solution.py:362
  64.5 7.2 %copy-start.6 = (f32[1,8,32,128]{3,2,1,0:T(8,128)S(1)}, f32[1,8,32,128]{3,2,1,0:T(8,128)}, u32[]{:S(2)}) copy-start(f32[1,8,32,128]{3,2,1,0:T(8,128)} %param.14) | copy-start | bytes 393220
  66.2 16.9 %collective-permute-start.5 = (f32[7,32,128]{2,1,0:T(8,128)S(1)}, f32[7,32,128]{2,1,0:T(8,128)S(1)}, u32[]{:S(2)}, u32[]{:S(2)}) collective-permute-start(f32[7,32,128]{2,1,0:T(8,128)S(1)} %get-tuple-element.50), channel_id=1, source_target_pairs={{1,2},{2,1},{3,4},{4,3},{5,6},{6,5},{7,8},{8,7},{9,10},{10,9},{11,... | collective-permute-start | bytes 344072 | tf_op jit(solution)/shard_map/ppermute | solution.py:362
  73.3 9.8 %collective-permute-start.4 = (f32[7,32,128]{2,1,0:T(8,128)S(1)}, f32[7,32,128]{2,1,0:T(8,128)S(1)}, u32[]{:S(2)}, u32[]{:S(2)}) collective-permute-start(f32[7,32,128]{2,1,0:T(8,128)S(1)} %get-tuple-element.49), channel_id=1, source_target_pairs={{1,0},{0,1},{3,2},{2,3},{5,4},{4,5},{7,6},{6,7},{9,8},{8,9},{11,10... | collective-permute-start | bytes 344072 | tf_op jit(solution)/shard_map/ppermute | solution.py:355
  85.4 7.4 %collective-permute-start.6 = (f32[7,32,128]{2,1,0:T(8,128)S(1)}, f32[7,32,128]{2,1,0:T(8,128)S(1)}, u32[]{:S(2)}, u32[]{:S(2)}) collective-permute-start(f32[7,32,128]{2,1,0:T(8,128)S(1)} %shard_map.145), channel_id=1, source_target_pairs={{1,0},{0,1},{3,2},{2,3},{5,4},{4,5},{7,6},{6,7},{9,8},{8,9},{11,10... | collective-permute-start | bytes 344072 | tf_op jit(solution)/shard_map/ppermute | solution.py:355
  87.3 16.9 %collective-permute-start.7 = (f32[7,32,128]{2,1,0:T(8,128)S(1)}, f32[7,32,128]{2,1,0:T(8,128)S(1)}, u32[]{:S(2)}, u32[]{:S(2)}) collective-permute-start(f32[7,32,128]{2,1,0:T(8,128)S(1)} %get-tuple-element.52), channel_id=1, source_target_pairs={{1,2},{2,1},{3,4},{4,3},{5,6},{6,5},{7,8},{8,7},{9,10},{10,9},{11,... | collective-permute-start | bytes 344072 | tf_op jit(solution)/shard_map/ppermute | solution.py:362
  106.4 7.4 %collective-permute-start.8 = (f32[7,32,128]{2,1,0:T(8,128)S(1)}, f32[7,32,128]{2,1,0:T(8,128)S(1)}, u32[]{:S(2)}, u32[]{:S(2)}) collective-permute-start(f32[7,32,128]{2,1,0:T(8,128)S(1)} %shard_map.147), channel_id=1, source_target_pairs={{1,0},{0,1},{3,2},{2,3},{5,4},{4,5},{7,6},{6,7},{9,8},{8,9},{11,10... | collective-permute-start | bytes 344072 | tf_op jit(solution)/shard_map/ppermute | solution.py:355
  108.4 16.9 %collective-permute-start.9 = (f32[7,32,128]{2,1,0:T(8,128)S(1)}, f32[7,32,128]{2,1,0:T(8,128)S(1)}, u32[]{:S(2)}, u32[]{:S(2)}) collective-permute-start(f32[7,32,128]{2,1,0:T(8,128)S(1)} %get-tuple-element.57), channel_id=1, source_target_pairs={{1,2},{2,1},{3,4},{4,3},{5,6},{6,5},{7,8},{8,7},{9,10},{10,9},{11,... | collective-permute-start | bytes 344072 | tf_op jit(solution)/shard_map/ppermute | solution.py:362
  128.3 7.4 %collective-permute-start.10 = (f32[7,32,128]{2,1,0:T(8,128)S(1)}, f32[7,32,128]{2,1,0:T(8,128)S(1)}, u32[]{:S(2)}, u32[]{:S(2)}) collective-permute-start(f32[7,32,128]{2,1,0:T(8,128)S(1)} %get-tuple-element.63), channel_id=1, source_target_pairs={{1,0},{0,1},{3,2},{2,3},{5,4},{4,5},{7,6},{6,7},{9,8},{8,9},{11,10... | collective-permute-start | bytes 344072 | tf_op jit(solution)/shard_map/ppermute | solution.py:355
  130.2 16.9 %collective-permute-start.11 = (f32[7,32,128]{2,1,0:T(8,128)S(1)}, f32[7,32,128]{2,1,0:T(8,128)S(1)}, u32[]{:S(2)}, u32[]{:S(2)}) collective-permute-start(f32[7,32,128]{2,1,0:T(8,128)S(1)} %get-tuple-element.64), channel_id=1, source_target_pairs={{1,2},{2,1},{3,4},{4,3},{5,6},{6,5},{7,8},{8,7},{9,10},{10,9},{11,... | collective-permute-start | bytes 344072 | tf_op jit(solution)/shard_map/ppermute | solution.py:362
  150.1 7.4 %collective-permute-start.12 = (f32[4,32,128]{2,1,0:T(8,128)S(1)}, f32[4,32,128]{2,1,0:T(8,128)S(1)}, u32[]{:S(2)}, u32[]{:S(2)}) collective-permute-start(f32[4,32,128]{2,1,0:T(8,128)S(1)} %get-tuple-element.71), channel_id=1, source_target_pairs={{1,0},{0,1},{3,2},{2,3},{5,4},{4,5},{7,6},{6,7},{9,8},{8,9},{11,10... | collective-permute-start | bytes 196616 | tf_op jit(solution)/shard_map/ppermute | solution.py:355
  152.0 16.4 %collective-permute-start.13 = (f32[4,32,128]{2,1,0:T(8,128)S(1)}, f32[4,32,128]{2,1,0:T(8,128)S(1)}, u32[]{:S(2)}, u32[]{:S(2)}) collective-permute-start(f32[4,32,128]{2,1,0:T(8,128)S(1)} %get-tuple-element.72), channel_id=1, source_target_pairs={{1,2},{2,1},{3,4},{4,3},{5,6},{6,5},{7,8},{8,7},{9,10},{10,9},{11,... | collective-permute-start | bytes 196616 | tf_op jit(solution)/shard_map/ppermute | solution.py:362
  170.2 28.4 %all-to-all-start.1 = ((f32[32,2,8,128]{3,2,1,0:T(8,128)}), f32[32,2,8,128]{3,2,1,0:T(8,128)S(1)}, u32[]{:S(2)}, u32[]{:S(2)}) async-start(f32[32,2,8,128]{3,2,1,0:T(8,128)} %bitcast.32), calls=%async_computation.1 | async-start | bytes 524288 | tf_op jit(solution)/shard_map/all_to_all | solution.py:498
  (1 other events, 0.7 us)

commit v4 on v3

--- a/solution.py
+++ b/solution.py
@@ -14,7 +14,6 @@
 PAD = 8
 ROWS = CY + 2 * PAD
 WIDE = CX + 14
-BESIDE = 400_000_000
 
 COEFFS = (1225.0 / 1024.0, -245.0 / 3072.0, 49.0 / 5120.0, -5.0 / 7168.0)
 step_squared = 0.02
@@ -53,11 +52,11 @@
     @pl.when(odd)
     def _():
         target[0:width, inner, :] = first
-        target[width + CX : 2 * width + CX, inner, :] = second
+        target[width + CX : 2 * width + CX, inner, :] = second[0:width]
 
     @pl.when(jnp.logical_not(odd))
     def _():
-        target[0:width, inner, :] = second
+        target[0:width, inner, :] = second[CX - width : CX]
         target[width + CX : 2 * width + CX, inner, :] = first
 
 
@@ -73,16 +72,9 @@
         target[...] = tail()
 
 
-def choose_kernel(where, aperture, kappa, buoy, out):
-    for s in range(out.shape[0]):
-        t = aperture[s, where[0]]
-        out[s, 0] = kappa[t]
-        out[s, 1] = buoy[t]
-
-
-def first_swap_kernel(info, field, out):
-    width = out.shape[0]
-    for_partner(info, out, lambda: field[0:width], lambda: field[CX - width : CX])
+def hand_over(info, send_a, field):
+    width = send_a.shape[0]
+    for_partner(info, send_a, lambda: field[0:width], lambda: field[CX - width : CX])
 
 
 def slope_x(field, at):
@@ -119,7 +111,18 @@
         yield cell, div + acc[cell]
 
 
-def receivers_kernel(info, cells, seen, out):
+def prepare_kernel(
+    info, wave, cells, seen, now, before, last, after, out, base_p, base_q, last_out, source_out
+):
+    base_p[...] = 2.0 * now[...] - before[...]
+    base_q[...] = 2.0 * last[...] - after[...]
+    last_out[...] = last[...]
+    y = lax.broadcasted_iota(jnp.int32, (CY, CZ), 0)
+    z = lax.broadcasted_iota(jnp.int32, (CY, CZ), 1)
+    hit = (y == info[2]) & (z == info[3])
+    for n in range(STEPS):
+        source_out[n] = jnp.where(hit, wave[n], 0.0)
+
     index = cells[...] - info[4]
     row = lax.shift_right_arithmetic(index, 7)
     z = lax.bitwise_and(index, 127)
@@ -145,36 +148,19 @@
         out[n + 1] = total.reshape(CX, CY, CZ)
 
 
-def model_kernel(info, stiff, buoy, last, send_b, scaled):
+def model_kernel(info, stiff, buoy, last, send_a, send_b, scaled):
     scaled[...] = stiff[...] * last[...]
+    send_b[0:8] = buoy[...]
+    send_b[8:16] = scaled[...]
     for_partner(
         info,
-        send_b,
-        lambda: jnp.concatenate([buoy[4:8], scaled[1:8]], axis=0),
-        lambda: jnp.concatenate([buoy[0:4], scaled[0:7]], axis=0),
-    )
-
-
-def model_swap_kernel(info, buoy, scaled, out):
-    for_partner(
-        info,
-        out,
+        send_a,
         lambda: jnp.concatenate([buoy[0:4], scaled[0:7]], axis=0),
         lambda: jnp.concatenate([buoy[4:8], scaled[1:8]], axis=0),
     )
 
 
-def source_plane(info, amount):
-    y = lax.broadcasted_iota(jnp.int32, (CY, CZ), 0)
-    z = lax.broadcasted_iota(jnp.int32, (CY, CZ), 1)
-    hit = (y == info[2]) & (z == info[3])
-    spot = jnp.where(hit, amount, 0.0)
-    return lambda cell: jnp.where(info[1] == cell, spot, 0.0)
-
-
-def forward(info, wave, n, now, before, stiff, field, buoy, gx, gy, acc, div_out, slope_out, after):
-    source = source_plane(info, wave[n])
-
+def forward(info, source, base, stiff, field, buoy, gx, gy, acc, div_out, slope_out, store):
     def keep(cell, sx, sy, sz):
         slope_out[0, cell] = sx
         slope_out[1, cell] = sy
@@ -182,8 +168,8 @@
 
     for cell, div in operate(field, 7, buoy, gx, gy, acc, keep):
         div_out[cell] = div
-        value = 2.0 * now[cell] - before[cell] + step_squared * stiff[cell] * div
-        after(cell, value + source(cell))
+        value = base(cell) + step_squared * stiff[cell] * div
+        store(cell, value + jnp.where(info[1] == cell, source, 0.0))
 
 
 def widen_buoy(info, buoy, first, second, target):
@@ -197,13 +183,13 @@
 
     @pl.when(jnp.logical_not(odd))
     def _():
-        target[0:4] = second[0:4]
+        target[0:4] = second[4:8]
         target[4 + CX : 8 + CX] = first[0:4]
 
 
 def first_kernel(
-    info, wave, now, now_a, now_b, before, stiff, buoy, edge_a, edge_b,
-    p_out, send_b, div_out, slope_out, buoy_out,
+    info, now, now_a, now_b, base, source, stiff, buoy, edge_a, edge_b,
+    p_out, send_a, div_out, slope_out, buoy_out,
     field, gx, gy, acc,
 ):
     widen_buoy(info, buoy, edge_a, edge_b, buoy_out)
@@ -212,24 +198,26 @@
     def store(cell, value):
         p_out[cell] = value
 
-    forward(info, wave, 0, now, before, stiff, field, buoy_out, gx, gy, acc, div_out, slope_out, store)
-    for_partner(info, send_b, lambda: p_out[1:8], lambda: p_out[0:7])
+    forward(
+        info, source[0], lambda cell: base[cell],
+        stiff, field, buoy_out, gx, gy, acc, div_out, slope_out, store,
+    )
+    hand_over(info, send_a, p_out)
 
 
 def adjoint_part_kernel(
-    info, p, last, after, scaled, edge_a, edge_b, buoy,
-    send_a, q_out,
+    info, base, scaled, edge_a, edge_b, buoy,
+    q_out,
     field, gx, gy, acc,
 ):
-    for_partner(info, send_a, lambda: p[0:7], lambda: p[1:8])
-    place(info, field, scaled[...], edge_a[4:11], edge_b[4:11], 7)
+    place(info, field, scaled[...], edge_a[4:11], edge_b[8:16], 7)
     for cell, div in operate(field, 7, buoy, gx, gy, acc, lambda *_: None):
-        q_out[cell] = 2.0 * last[cell] - after[cell] + step_squared * div
+        q_out[cell] = base[cell] + step_squared * div
 
 
 def second_kernel(
-    info, wave, now, now_a, now_b, before, stiff, buoy,
-    p_out, send_b, div_out, slope_out,
+    info, now, now_a, now_b, before, source, stiff, buoy,
+    p_out, send_a, div_out, slope_out,
     field, gx, gy, acc,
 ):
     place(info, field, now[...], now_a[...], now_b[...], 7)
@@ -237,13 +225,16 @@
     def store(cell, value):
         p_out[cell] = value
 
-    forward(info, wave, 1, now, before, stiff, field, buoy, gx, gy, acc, div_out, slope_out, store)
-    for_partner(info, send_b, lambda: p_out[1:8], lambda: p_out[0:7])
+    forward(
+        info, source[1], lambda cell: 2.0 * now[cell] - before[cell],
+        stiff, field, buoy, gx, gy, acc, div_out, slope_out, store,
+    )
+    hand_over(info, send_a, p_out)
 
 
 def third_kernel(
-    info, wave, now, now_a, now_b, before, stiff, buoy, q_part, spots,
-    q_out, scaled, send_b, div_out, slope_out,
+    info, now, now_a, now_b, before, source, stiff, buoy, q_part, spots,
+    q_out, scaled, send_a, div_out, slope_out,
     field, gx, gy, acc,
 ):
     place(info, field, now[...], now_a[...], now_b[...], 7)
@@ -253,13 +244,16 @@
         q_out[cell] = q
         scaled[cell] = stiff[cell] * q
 
-    forward(info, wave, 2, now, before, stiff, field, buoy, gx, gy, acc, div_out, slope_out, store)
-    for_partner(info, send_b, lambda: scaled[1:8], lambda: scaled[0:7])
+    forward(
+        info, source[2], lambda cell: 2.0 * now[cell] - before[cell],
+        stiff, field, buoy, gx, gy, acc, div_out, slope_out, store,
+    )
+    hand_over(info, send_a, scaled)
 
 
 def adjoint_kernel(
-    n, width, info, q_now, q_after, scaled, scaled_a, scaled_b, stiff, buoy, spots, p_then,
-    q_out, scaled_out, send_b, slope_out,
+    n, info, q_now, q_after, scaled, scaled_a, scaled_b, stiff, buoy, spots, p_then,
+    q_out, scaled_out, send_a, slope_out,
     field, gx, gy, acc,
 ):
     place(info, field, scaled[...], scaled_a[...], scaled_b[...], 7)
@@ -274,21 +268,19 @@
         q = q + (spots[0, cell] * p_then[cell] - spots[n + 1, cell])
         q_out[cell] = q
         scaled_out[cell] = stiff[cell] * q
-    for_partner(info, send_b, lambda: scaled_out[CX - width : CX], lambda: scaled_out[0:width])
+    hand_over(info, send_a, scaled_out)
 
 
 def adjoint_first_kernel(*refs):
-    adjoint_kernel(1, 7, *refs)
+    adjoint_kernel(1, *refs)
 
 
 def adjoint_second_kernel(*refs):
-    adjoint_kernel(0, 4, *refs)
-
-
-def image_first_kernel(info, scaled, q_now, slope_q, div, slope_p, q_new, send_a, out, q_out):
+    adjoint_kernel(0, *refs)
+
+
+def image_first_kernel(q_now, slope_q, div, slope_p, q_new, out, q_out):
     q_out[...] = q_new[...]
-    width = send_a.shape[0]
-    for_partner(info, send_a, lambda: scaled[0:width], lambda: scaled[CX - width : CX])
     for cell in range(CX):
         out[0, cell] = q_now[cell] * div[cell]
         rho = slope_p[0, cell] * slope_q[0, cell] + slope_p[1, cell] * slope_q[1, cell]
@@ -296,11 +288,9 @@
 
 
 def image_second_kernel(
-    info, scaled, q_now, slope_q, div, slope_p, images, q_new, send_a, out, q_out
+    q_now, slope_q, div, slope_p, images, q_new, out, q_out
 ):
     q_out[...] = q_new[...]
-    width = send_a.shape[0]
-    for_partner(info, send_a, lambda: scaled[0:width], lambda: scaled[CX - width : CX])
     for cell in range(CX):
         out[0, cell] = images[0, cell] + q_now[cell] * div[cell]
         rho = slope_p[0, cell] * slope_q[0, cell] + slope_p[1, cell] * slope_q[1, cell]
@@ -319,13 +309,16 @@
         out[1, cell] = -step_squared * rho
 
 
-def gather_kernel(column, arrived, out_kappa, out_buoy):
-    out_kappa[...] = jnp.zeros_like(out_kappa)
-    out_buoy[...] = jnp.zeros_like(out_buoy)
-    for s in range(arrived.shape[0]):
-        t = column[s]
-        out_kappa[t] = out_kappa[t] + arrived[s, 0]
-        out_buoy[t] = out_buoy[t] + arrived[s, 1]
+def gather_kernel(picked, arrived, out_kappa, out_buoy):
+    for t in range(TILES):
+        kappa = jnp.zeros((CX, CZ), F32)
+        rho = jnp.zeros((CX, CZ), F32)
+        for s in range(arrived.shape[0]):
+            here = picked[t, s : s + 1, :] > 0.0
+            kappa = kappa + jnp.where(here, arrived[s, 0], 0.0)
+            rho = rho + jnp.where(here, arrived[s, 1], 0.0)
+        out_kappa[t] = kappa
+        out_buoy[t] = rho
 
 
 def work():
@@ -382,111 +375,100 @@
     info = jnp.stack(
         [odd, source // (CY * CZ) - dom * CX, (source // CZ) % CY, source % CZ, offset]
     ).astype(jnp.int32)
-    wave = source_wave[0]
+
     column = lax.dynamic_index_in_dim(aperture, dom, 1, keepdims=False)
-
-    shots = aperture.shape[0]
-    (chosen,) = call(
-        choose_kernel,
-        [dom.reshape(1).astype(jnp.int32), aperture],
-        [kappa_model, buoy_model],
-        [jax.ShapeDtypeStruct((shots, 2, CX, CZ), F32)],
-    )
+    stacked = jnp.stack((kappa_model, buoy_model), axis=1)
+    picks = column[:, None, None, None]
+    chosen = stacked[0][None]
+    for t in range(1, TILES):
+        chosen = jnp.where(picks == t, stacked[t][None], chosen)
     block = lax.all_to_all(chosen, "shot", 0, 0, tiled=True)
 
     p0, p_prev = pressure_now[0], pressure_prev[0]
     q4, q5 = adjoint_last[0], adjoint_after[0]
-    head, tail = p0[0:7], p0[1:8]
-    p0_b = swap_second(jnp.where(odd == 1, tail, head))
-    p0_a = swap_first(jnp.where(odd == 1, head, tail))
-    (spots,) = call(
-        receivers_kernel,
-        [info],
-        [receiver_cell, observed[0]],
-        [jax.ShapeDtypeStruct((STEPS + 1, CX, CY, CZ), F32)],
+    p0_b = swap_second(p0)
+    p0_a = swap_first(jnp.where(odd == 1, p0[0:7], p0[1:8]))
+    own, seven, four = plane_field(CX), plane_field(7), plane_field(4)
+    spots, base_p, base_q, q4, source_planes = call(
+        prepare_kernel,
+        [info, source_wave[0]],
+        [receiver_cell, observed[0], p0, p_prev, q4, q5],
+        [jax.ShapeDtypeStruct((STEPS + 1, CX, CY, CZ), F32), own, own, own, plane_field(STEPS)],
         flops=400_000_000,
     )
-    block, p0_a, p0_b, spots = lax.optimization_barrier((block, p0_a, p0_b, spots))
+    ids = jnp.arange(TILES, dtype=jnp.int32)[:, None, None]
+    picked = jnp.broadcast_to(
+        (column[None, :, None] == ids).astype(F32), (TILES, column.shape[0], CZ)
+    )
+    block, p0_a, p0_b, spots, base_p, base_q, q4, source_planes, picked = lax.optimization_barrier(
+        (block, p0_a, p0_b, spots, base_p, base_q, q4, source_planes, picked)
+    )
 
     stiff = block[:, 0].transpose(1, 0, 2)
     buoy = block[:, 1].transpose(1, 0, 2)
-    own, seven, four = plane_field(CX), plane_field(7), plane_field(4)
     slopes = jax.ShapeDtypeStruct((3, CX, CY, CZ), F32)
     images = jax.ShapeDtypeStruct((2, CX, CY, CZ), F32)
 
-    send_b, f4 = call(model_kernel, [info], [stiff, buoy, q4], [plane_field(11), own])
+    send_a, send_b, f4 = call(
+        model_kernel, [info], [stiff, buoy, q4], [plane_field(11), plane_field(16), own]
+    )
     edge_b = swap_second(send_b)
-    (send_a,) = call(model_swap_kernel, [info], [buoy, f4], [plane_field(11)], flops=BESIDE)
     edge_a = swap_first(send_a)
 
-    p1, send_b, div0, slope0, wide = call(
+    p1, send_a, div0, slope0, wide = call(
         first_kernel,
-        [info, wave],
-        [p0, p0_a, p0_b, p_prev, stiff, buoy, edge_a, edge_b],
+        [info],
+        [p0, p0_a, p0_b, base_p, source_planes, stiff, buoy, edge_a, edge_b],
         [own, seven, own, slopes, plane_field(CX + 8)],
         work(),
     )
-    from_b = swap_second(send_b)
-    send_a, q_part = call(
-        adjoint_part_kernel, [info], [p1, q4, q5, f4, edge_a, edge_b, wide], [seven, own], work(), BESIDE
-    )
+    from_b = swap_second(p1)
+    (q_part,) = call(adjoint_part_kernel, [info], [base_q, f4, edge_a, edge_b, wide], [own], work())
     from_a = swap_first(send_a)
 
-    p2, send_b, div1, slope1 = call(
+    p2, send_a, div1, slope1 = call(
         second_kernel,
-        [info, wave],
-        [p1, from_a, from_b, p0, stiff, wide],
+        [info],
+        [p1, from_a, from_b, p0, source_planes, stiff, wide],
         [own, seven, own, slopes],
         work(),
     )
-    from_b = swap_second(send_b)
-    (send_a,) = call(first_swap_kernel, [info], [p2], [seven], flops=BESIDE)
+    from_b = swap_second(p2)
     from_a = swap_first(send_a)
 
-    q3, f3, send_b, div2, slope2 = call(
+    q3, f3, send_a, div2, slope2 = call(
         third_kernel,
-        [info, wave],
-        [p2, from_a, from_b, p1, stiff, wide, q_part, spots],
+        [info],
+        [p2, from_a, from_b, p1, source_planes, stiff, wide, q_part, spots],
         [own, own, seven, own, slopes],
         work(),
     )
-    from_b = swap_second(send_b)
-    (send_a,) = call(first_swap_kernel, [info], [f3], [seven], flops=BESIDE)
+    from_b = swap_second(f3)
     from_a = swap_first(send_a)
 
-    q2, f2, send_b, slope_q = call(
+    q2, f2, send_a, slope_q = call(
         adjoint_first_kernel,
         [info],
         [q3, q4, f3, from_a, from_b, stiff, wide, spots, p2],
         [own, own, seven, slopes],
         work(),
     )
-    from_b = swap_second(send_b)
-    send_a, image, q2_out = call(
-        image_first_kernel,
-        [info],
-        [f2, q3, slope_q, div2, slope2, q2],
-        [seven, images, own],
-        flops=BESIDE,
-    )
+    from_b = swap_second(f2)
     from_a = swap_first(send_a)
-
-    q1, f1, send_b, slope_q = call(
+    image, q2_out = call(image_first_kernel, [], [q3, slope_q, div2, slope2, q2], [images, own])
+
+    q1, f1, send_a, slope_q = call(
         adjoint_second_kernel,
         [info],
         [q2, q3, f2, from_a, from_b, stiff, wide, spots, p1],
         [own, own, four, slopes],
         work(),
     )
-    from_b = swap_second(send_b)
-    send_a, image, q1_out = call(
-        image_second_kernel,
-        [info],
-        [f1, q2, slope_q, div1, slope1, image, q1],
-        [four, images, own],
-        flops=BESIDE,
-    )
+    from_b = swap_second(f1)
     from_a = swap_first(send_a)
+    image, q1_out = call(
+        image_second_kernel, [], [q2, slope_q, div1, slope1, image, q1], [images, own]
+    )
 
     (image,) = call(
         image_kernel,
@@ -497,7 +479,7 @@
     )
     arrived = lax.all_to_all(image.transpose(2, 0, 1, 3), "shot", 0, 0, tiled=True)
     tiles = jax.ShapeDtypeStruct((TILES, CX, CZ), F32)
-    grad_kappa, grad_buoy = call(gather_kernel, [column], [arrived], [tiles, tiles])
+    grad_kappa, grad_buoy = call(gather_kernel, [], [picked, arrived], [tiles, tiles])
     return (grad_kappa, grad_buoy, q1_out[None], q2_out[None])
 
 

time: 201 us -> 189 us (0.940)
  blocking collectives: 0 us -> 34.5 us
  waiting for transfers between devices: 84.1 us -> 49.9 us
  local copies, waits for them, and re-layouts: 6.06 us -> 1.13 us
  Pallas kernels: 20 us -> 15.1 us
  starting transfers between devices: 88 us -> 84 us
  other arithmetic: 0.02 us -> 2.32 us
    all_to_all x0 -> x1, blocking collectives: none -> 34.5 us  [shards(): lax.all_to_all(image.transpose(2, 0, 1, 3), 'shot', 0, 0, tiled=True)]
    ppermute x7, waiting for transfers between devices: 68.6 us -> 44.6 us  [swap_second(): return lax.ppermute(planes, 'dom', pairs)]
    all_to_all x1 -> x0, waiting for transfers between devices: 13.8 us -> none  [shards(): lax.all_to_all(image.transpose(2, 0, 1, 3), 'shot', 0, 0, tiled=True)]
    all_to_all x1 -> x0, starting transfers between devices: 13.8 us -> none  [shards(): lax.all_to_all(image.transpose(2, 0, 1, 3), 'shot', 0, 0, tiled=True)]
    ppermute x7, starting transfers between devices: 41.4 us -> 54 us  [swap_second(): return lax.ppermute(planes, 'dom', pairs)]
    ppermute x7, waiting for transfers between devices: 0.02 us -> 5.26 us  [swap_first(): return lax.ppermute(planes, 'dom', [(i ^ 1, i) for i in range(count)])]
    pallas_call x16 -> x12, Pallas kernels: 20 us -> 15.1 us  [call(): pl.pallas_call(kernel, out_shape=outs, in_specs=[SMEM] * len(scalars) + [...]
    unnamed x20 -> x17, local copies, waits for them, and re-layouts: 4.31 us -> 0.7 us
  transfers between devices with their start and end apart: 16 -> 15, of which waited for: 9 -> 11; matrix products, arithmetic and copies ran while one was open for 0% -> 0% of each run, Pallas kernels for 2% -> 2%
where the time goes in v4:
time: 189 us
  starting transfers between devices  84 us (44%)
  waiting for transfers between devices  49.9 us (26%)
  blocking collectives  34.5 us (18%)
  Pallas kernels  15.1 us (8%)
  other arithmetic  2.32 us (1%)
    ppermute x7, starting transfers between devices, swap_second(): return lax.ppermute(planes, 'dom', pairs)  54 us
    ppermute x7, waiting for transfers between devices, swap_second(): return lax.ppermute(planes, 'dom', pairs)  44.6 us
    all_to_all x1, blocking collectives, shards(): lax.all_to_all(image.transpose(2, 0, 1, 3), 'shot', 0, 0, tiled=True)  34.5 us
    all_to_all x1, starting transfers between devices, shards(): block = lax.all_to_all(chosen, 'shot', 0, 0, tiled=True)  15.4 us
    pallas_call x12, Pallas kernels, call(): pl.pallas_call(kernel, out_shape=outs, in_specs=[SMEM] * len(scalars) + [...  15.1 us
    ppermute x7, starting transfers between devices, swap_first(): return lax.ppermute(planes, 'dom', [(i ^ 1, i) for i in range(count)])  14.5 us
    ppermute x7, waiting for transfers between devices, swap_first(): return lax.ppermute(planes, 'dom', [(i ^ 1, i) for i in range(count)])  5.26 us
  transfers between devices with their start and end apart: 15, of which 11 were waited for; matrix products, arithmetic and copies ran while one was open for 0% of the time, Pallas kernels for 2%

profile of v4, /device:TPU:7, one launch (start us, length us, event | category | flops | bytes accessed | tf_op | source)
XLA Modules:
  0.0 188.6 jit_solution(7500926162572520135)
XLA Ops:
  3.0 15.4 %all-to-all-start = ((f32[32,2,8,128]{3,2,1,0:T(8,128)}), f32[32,2,8,128]{3,2,1,0:T(8,128)S(1)}, u32[]{:S(2)}, u32[]{:S(2)}) async-start(f32[32,2,8,128]{3,2,1,0:T(8,128)} %select_select_fusion), calls=%async_computation | async-start | bytes 524288 | tf_op jit(solution)/shard_map/all_to_all | solution.py:385
  18.4 3.0 %collective-permute-start = (f32[7,32,128]{2,1,0:T(8,128)S(1)}, f32[7,32,128]{2,1,0:T(8,128)S(1)}, u32[]{:S(2)}, u32[]{:S(2)}) collective-permute-start(f32[7,32,128]{2,1,0:T(8,128)S(1)} %select_bitcast_fusion), channel_id=1, source_target_pairs={{1,0},{0,1},{3,2},{2,3},{5,4},{4,5},{7,6},{6,7},{9,8},{8,9},{11,10... | collective-permute-start | bytes 344072 | tf_op jit(solution)/shard_map/ppermute | solution.py:348
  21.5 7.8 %collective-permute-start.1 = (f32[8,32,128]{2,1,0:T(8,128)S(1)}, f32[8,32,128]{2,1,0:T(8,128)S(1)}, u32[]{:S(2)}, u32[]{:S(2)}) collective-permute-start(f32[8,32,128]{2,1,0:T(8,128)S(1)} %bitcast.46), channel_id=1, source_target_pairs={{1,2},{2,1},{3,4},{4,3},{5,6},{6,5},{7,8},{8,7},{9,10},{10,9},{11,... | collective-permute-start | bytes 393224 | tf_op jit(solution)/shard_map/ppermute | solution.py:355
  32.2 6.7 %collective-permute-done.1.now_b = f32[8,32,128]{2,1,0:T(8,128)S(1)} collective-permute-done((f32[8,32,128]{2,1,0:T(8,128)S(1)}, f32[8,32,128]{2,1,0:T(8,128)S(1)}, u32[]{:S(2)}, u32[]{:S(2)}) %collective-permute-start.1) | collective-permute-done | bytes 131104 | tf_op jit(solution)/shard_map/ppermute | solution.py:355
  39.7 7.7 %collective-permute-start.3 = (f32[16,32,128]{2,1,0:T(8,128)S(1)}, f32[16,32,128]{2,1,0:T(8,128)S(1)}, u32[]{:S(2)}, u32[]{:S(2)}) collective-permute-start(f32[16,32,128]{2,1,0:T(8,128)S(1)} %get-tuple-element.62), channel_id=1, source_target_pairs={{1,2},{2,1},{3,4},{4,3},{5,6},{6,5},{7,8},{8,7},{9,10},{10,9},{11,... | collective-permute-start | bytes 786440 | tf_op jit(solution)/shard_map/ppermute | solution.py:355
  47.4 1.9 %collective-permute-start.2 = (f32[11,32,128]{2,1,0:T(8,128)S(1)}, f32[11,32,128]{2,1,0:T(8,128)S(1)}, u32[]{:S(2)}, u32[]{:S(2)}) collective-permute-start(f32[11,32,128]{2,1,0:T(8,128)S(1)} %get-tuple-element.61), channel_id=1, source_target_pairs={{1,0},{0,1},{3,2},{2,3},{5,4},{4,5},{7,6},{6,7},{9,8},{8,9},{11,10... | collective-permute-start | bytes 540680 | tf_op jit(solution)/shard_map/ppermute | solution.py:348
  50.7 7.6 %collective-permute-done.3.edge_b = f32[16,32,128]{2,1,0:T(8,128)S(1)} collective-permute-done((f32[16,32,128]{2,1,0:T(8,128)S(1)}, f32[16,32,128]{2,1,0:T(8,128)S(1)}, u32[]{:S(2)}, u32[]{:S(2)}) %collective-permute-start.3) | collective-permute-done | bytes 262176 | tf_op jit(solution)/shard_map/ppermute | solution.py:355
  58.3 1.7 shard_map.140
  60.0 7.7 %collective-permute-start.5 = (f32[8,32,128]{2,1,0:T(8,128)S(1)}, f32[8,32,128]{2,1,0:T(8,128)S(1)}, u32[]{:S(2)}, u32[]{:S(2)}) collective-permute-start(f32[8,32,128]{2,1,0:T(8,128)S(1)} %get-tuple-element.63.now.before.refs_9_), channel_id=1, source_target_pairs={{1,2},{2,1},{3,4},{4,3},{5,6},{6,5},{7,8},{8,7},{9,10},{10,9},{11,... | collective-permute-start | bytes 393224 | tf_op jit(solution)/shard_map/ppermute | solution.py:355
  67.7 1.9 %collective-permute-start.4 = (f32[7,32,128]{2,1,0:T(8,128)S(1)}, f32[7,32,128]{2,1,0:T(8,128)S(1)}, u32[]{:S(2)}, u32[]{:S(2)}) collective-permute-start(f32[7,32,128]{2,1,0:T(8,128)S(1)} %get-tuple-element.64), channel_id=1, source_target_pairs={{1,0},{0,1},{3,2},{2,3},{5,4},{4,5},{7,6},{6,7},{9,8},{8,9},{11,10... | collective-permute-start | bytes 344072 | tf_op jit(solution)/shard_map/ppermute | solution.py:348
  70.9 6.2 %collective-permute-done.5.now_b = f32[8,32,128]{2,1,0:T(8,128)S(1)} collective-permute-done((f32[8,32,128]{2,1,0:T(8,128)S(1)}, f32[8,32,128]{2,1,0:T(8,128)S(1)}, u32[]{:S(2)}, u32[]{:S(2)}) %collective-permute-start.5) | collective-permute-done | bytes 131104 | tf_op jit(solution)/shard_map/ppermute | solution.py:355
  78.8 7.7 %collective-permute-start.7 = (f32[8,32,128]{2,1,0:T(8,128)S(1)}, f32[8,32,128]{2,1,0:T(8,128)S(1)}, u32[]{:S(2)}, u32[]{:S(2)}) collective-permute-start(f32[8,32,128]{2,1,0:T(8,128)S(1)} %get-tuple-element.66.now.refs_9_), channel_id=1, source_target_pairs={{1,2},{2,1},{3,4},{4,3},{5,6},{6,5},{7,8},{8,7},{9,10},{10,9},{11,... | collective-permute-start | bytes 393224 | tf_op jit(solution)/shard_map/ppermute | solution.py:355
  86.5 1.9 %collective-permute-start.6 = (f32[7,32,128]{2,1,0:T(8,128)S(1)}, f32[7,32,128]{2,1,0:T(8,128)S(1)}, u32[]{:S(2)}, u32[]{:S(2)}) collective-permute-start(f32[7,32,128]{2,1,0:T(8,128)S(1)} %get-tuple-element.67), channel_id=1, source_target_pairs={{1,0},{0,1},{3,2},{2,3},{5,4},{4,5},{7,6},{6,7},{9,8},{8,9},{11,10... | collective-permute-start | bytes 344072 | tf_op jit(solution)/shard_map/ppermute | solution.py:348
  90.1 5.8 %collective-permute-done.7.now_b = f32[8,32,128]{2,1,0:T(8,128)S(1)} collective-permute-done((f32[8,32,128]{2,1,0:T(8,128)S(1)}, f32[8,32,128]{2,1,0:T(8,128)S(1)}, u32[]{:S(2)}, u32[]{:S(2)}) %collective-permute-start.7) | collective-permute-done | bytes 131104 | tf_op jit(solution)/shard_map/ppermute | solution.py:355
  97.5 7.7 %collective-permute-start.9 = (f32[8,32,128]{2,1,0:T(8,128)S(1)}, f32[8,32,128]{2,1,0:T(8,128)S(1)}, u32[]{:S(2)}, u32[]{:S(2)}) collective-permute-start(f32[8,32,128]{2,1,0:T(8,128)S(1)} %get-tuple-element.72.refs_3_), channel_id=1, source_target_pairs={{1,2},{2,1},{3,4},{4,3},{5,6},{6,5},{7,8},{8,7},{9,10},{10,9},{11,... | collective-permute-start | bytes 393224 | tf_op jit(solution)/shard_map/ppermute | solution.py:355
  105.2 1.9 %collective-permute-start.8 = (f32[7,32,128]{2,1,0:T(8,128)S(1)}, f32[7,32,128]{2,1,0:T(8,128)S(1)}, u32[]{:S(2)}, u32[]{:S(2)}) collective-permute-start(f32[7,32,128]{2,1,0:T(8,128)S(1)} %get-tuple-element.73), channel_id=1, source_target_pairs={{1,0},{0,1},{3,2},{2,3},{5,4},{4,5},{7,6},{6,7},{9,8},{8,9},{11,10... | collective-permute-start | bytes 344072 | tf_op jit(solution)/shard_map/ppermute | solution.py:348
  108.5 6.2 %collective-permute-done.9.refs_5_ = f32[8,32,128]{2,1,0:T(8,128)S(1)} collective-permute-done((f32[8,32,128]{2,1,0:T(8,128)S(1)}, f32[8,32,128]{2,1,0:T(8,128)S(1)}, u32[]{:S(2)}, u32[]{:S(2)}) %collective-permute-start.9) | collective-permute-done | bytes 131104 | tf_op jit(solution)/shard_map/ppermute | solution.py:355
  116.3 7.7 %collective-permute-start.11 = (f32[8,32,128]{2,1,0:T(8,128)S(1)}, f32[8,32,128]{2,1,0:T(8,128)S(1)}, u32[]{:S(2)}, u32[]{:S(2)}) collective-permute-start(f32[8,32,128]{2,1,0:T(8,128)S(1)} %get-tuple-element.75.refs_3_), channel_id=1, source_target_pairs={{1,2},{2,1},{3,4},{4,3},{5,6},{6,5},{7,8},{8,7},{9,10},{10,9},{11,... | collective-permute-start | bytes 393224 | tf_op jit(solution)/shard_map/ppermute | solution.py:355
  124.0 1.9 %collective-permute-start.10 = (f32[7,32,128]{2,1,0:T(8,128)S(1)}, f32[7,32,128]{2,1,0:T(8,128)S(1)}, u32[]{:S(2)}, u32[]{:S(2)}) collective-permute-start(f32[7,32,128]{2,1,0:T(8,128)S(1)} %get-tuple-element.76), channel_id=1, source_target_pairs={{1,0},{0,1},{3,2},{2,3},{5,4},{4,5},{7,6},{6,7},{9,8},{8,9},{11,10... | collective-permute-start | bytes 344072 | tf_op jit(solution)/shard_map/ppermute | solution.py:348
  127.2 6.2 %collective-permute-done.11.refs_5_ = f32[8,32,128]{2,1,0:T(8,128)S(1)} collective-permute-done((f32[8,32,128]{2,1,0:T(8,128)S(1)}, f32[8,32,128]{2,1,0:T(8,128)S(1)}, u32[]{:S(2)}, u32[]{:S(2)}) %collective-permute-start.11) | collective-permute-done | bytes 131104 | tf_op jit(solution)/shard_map/ppermute | solution.py:355
  135.1 7.7 %collective-permute-start.13 = (f32[8,32,128]{2,1,0:T(8,128)S(1)}, f32[8,32,128]{2,1,0:T(8,128)S(1)}, u32[]{:S(2)}, u32[]{:S(2)}) collective-permute-start(f32[8,32,128]{2,1,0:T(8,128)S(1)} %get-tuple-element.78.scaled), channel_id=1, source_target_pairs={{1,2},{2,1},{3,4},{4,3},{5,6},{6,5},{7,8},{8,7},{9,10},{10,9},{11,... | collective-permute-start | bytes 393224 | tf_op jit(solution)/shard_map/ppermute | solution.py:355
  142.8 1.9 %collective-permute-start.12 = (f32[4,32,128]{2,1,0:T(8,128)S(1)}, f32[4,32,128]{2,1,0:T(8,128)S(1)}, u32[]{:S(2)}, u32[]{:S(2)}) collective-permute-start(f32[4,32,128]{2,1,0:T(8,128)S(1)} %get-tuple-element.79), channel_id=1, source_target_pairs={{1,0},{0,1},{3,2},{2,3},{5,4},{4,5},{7,6},{6,7},{9,8},{8,9},{11,10... | collective-permute-start | bytes 196616 | tf_op jit(solution)/shard_map/ppermute | solution.py:348
  146.2 6.0 %collective-permute-done.13.scaled_b = f32[8,32,128]{2,1,0:T(8,128)S(1)} collective-permute-done((f32[8,32,128]{2,1,0:T(8,128)S(1)}, f32[8,32,128]{2,1,0:T(8,128)S(1)}, u32[]{:S(2)}, u32[]{:S(2)}) %collective-permute-start.13) | collective-permute-done | bytes 131104 | tf_op jit(solution)/shard_map/ppermute | solution.py:355
  153.3 34.5 %all_to_all.10.arrived = f32[32,2,8,128]{3,2,1,0:T(8,128)S(1)} all-to-all(f32[32,2,8,128]{3,2,1,0:T(8,128)S(1)} %bitcast.55), channel_id=1, replica_groups=mesh['shot'=32,'dom'=16] {'shot'}, dimensions={0} | all-to-all | bytes 524288 | tf_op jit(solution)/shard_map/all_to_all | solution.py:480
  (47 shorter events, 22.1 us)
Async XLA Ops:
  0.6 0.7 copy-start.6
  3.0 15.4 %copy-start = (f32[1,8,32,128]{3,2,1,0:T(8,128)S(1)}, f32[1,8,32,128]{3,2,1,0:T(8,128)}, u32[]{:S(2)}) copy-start(f32[1,8,32,128]{3,2,1,0:T(8,128)} %param.11) | copy-start | bytes 393220
  3.0 35.9 %all-to-all-start = ((f32[32,2,8,128]{3,2,1,0:T(8,128)}), f32[32,2,8,128]{3,2,1,0:T(8,128)S(1)}, u32[]{:S(2)}, u32[]{:S(2)}) async-start(f32[32,2,8,128]{3,2,1,0:T(8,128)} %select_select_fusion), calls=%async_computation | async-start | bytes 524288 | tf_op jit(solution)/shard_map/all_to_all | solution.py:385
  18.4 11.5 %copy-start.7 = (f32[1,3,512]{2,0,1:T(1,128)S(1)}, f32[1,3,512]{2,0,1:T(1,128)}, u32[]{:S(2)}) copy-start(f32[1,3,512]{2,0,1:T(1,128)} %param.21) | copy-start | bytes 18436
  18.4 11.7 %copy-start.2 = (f32[1,8,32,128]{3,2,1,0:T(8,128)S(1)}, f32[1,8,32,128]{3,2,1,0:T(8,128)}, u32[]{:S(2)}) copy-start(f32[1,8,32,128]{3,2,1,0:T(8,128)} %param.13) | copy-start | bytes 393220
  18.4 11.7 %copy-start.3 = (f32[1,8,32,128]{3,2,1,0:T(8,128)S(1)}, f32[1,8,32,128]{3,2,1,0:T(8,128)}, u32[]{:S(2)}) copy-start(f32[1,8,32,128]{3,2,1,0:T(8,128)} %param.14) | copy-start | bytes 393220
  18.4 11.6 %copy-start.1 = (f32[1,8,32,128]{3,2,1,0:T(8,128)S(1)}, f32[1,8,32,128]{3,2,1,0:T(8,128)}, u32[]{:S(2)}) copy-start(f32[1,8,32,128]{3,2,1,0:T(8,128)} %param.12) | copy-start | bytes 393220
  18.4 13.7 %collective-permute-start = (f32[7,32,128]{2,1,0:T(8,128)S(1)}, f32[7,32,128]{2,1,0:T(8,128)S(1)}, u32[]{:S(2)}, u32[]{:S(2)}) collective-permute-start(f32[7,32,128]{2,1,0:T(8,128)S(1)} %select_bitcast_fusion), channel_id=1, source_target_pairs={{1,0},{0,1},{3,2},{2,3},{5,4},{4,5},{7,6},{6,7},{9,8},{8,9},{11,10... | collective-permute-start | bytes 344072 | tf_op jit(solution)/shard_map/ppermute | solution.py:348
  21.5 17.4 %collective-permute-start.1 = (f32[8,32,128]{2,1,0:T(8,128)S(1)}, f32[8,32,128]{2,1,0:T(8,128)S(1)}, u32[]{:S(2)}, u32[]{:S(2)}) collective-permute-start(f32[8,32,128]{2,1,0:T(8,128)S(1)} %bitcast.46), channel_id=1, source_target_pairs={{1,2},{2,1},{3,4},{4,3},{5,6},{6,5},{7,8},{8,7},{9,10},{10,9},{11,... | collective-permute-start | bytes 393224 | tf_op jit(solution)/shard_map/ppermute | solution.py:355
  30.1 0.7 copy-start.4
  30.1 0.7 copy-start.5
  39.7 18.6 %collective-permute-start.3 = (f32[16,32,128]{2,1,0:T(8,128)S(1)}, f32[16,32,128]{2,1,0:T(8,128)S(1)}, u32[]{:S(2)}, u32[]{:S(2)}) collective-permute-start(f32[16,32,128]{2,1,0:T(8,128)S(1)} %get-tuple-element.62), channel_id=1, source_target_pairs={{1,2},{2,1},{3,4},{4,3},{5,6},{6,5},{7,8},{8,7},{9,10},{10,9},{11,... | collective-permute-start | bytes 786440 | tf_op jit(solution)/shard_map/ppermute | solution.py:355
  47.4 3.3 %collective-permute-start.2 = (f32[11,32,128]{2,1,0:T(8,128)S(1)}, f32[11,32,128]{2,1,0:T(8,128)S(1)}, u32[]{:S(2)}, u32[]{:S(2)}) collective-permute-start(f32[11,32,128]{2,1,0:T(8,128)S(1)} %get-tuple-element.61), channel_id=1, source_target_pairs={{1,0},{0,1},{3,2},{2,3},{5,4},{4,5},{7,6},{6,7},{9,8},{8,9},{11,10... | collective-permute-start | bytes 540680 | tf_op jit(solution)/shard_map/ppermute | solution.py:348
  60.0 17.1 %collective-permute-start.5 = (f32[8,32,128]{2,1,0:T(8,128)S(1)}, f32[8,32,128]{2,1,0:T(8,128)S(1)}, u32[]{:S(2)}, u32[]{:S(2)}) collective-permute-start(f32[8,32,128]{2,1,0:T(8,128)S(1)} %get-tuple-element.63.now.before.refs_9_), channel_id=1, source_target_pairs={{1,2},{2,1},{3,4},{4,3},{5,6},{6,5},{7,8},{8,7},{9,10},{10,9},{11,... | collective-permute-start | bytes 393224 | tf_op jit(solution)/shard_map/ppermute | solution.py:355
  67.7 3.2 %collective-permute-start.4 = (f32[7,32,128]{2,1,0:T(8,128)S(1)}, f32[7,32,128]{2,1,0:T(8,128)S(1)}, u32[]{:S(2)}, u32[]{:S(2)}) collective-permute-start(f32[7,32,128]{2,1,0:T(8,128)S(1)} %get-tuple-element.64), channel_id=1, source_target_pairs={{1,0},{0,1},{3,2},{2,3},{5,4},{4,5},{7,6},{6,7},{9,8},{8,9},{11,10... | collective-permute-start | bytes 344072 | tf_op jit(solution)/shard_map/ppermute | solution.py:348
  78.8 17.1 %collective-permute-start.7 = (f32[8,32,128]{2,1,0:T(8,128)S(1)}, f32[8,32,128]{2,1,0:T(8,128)S(1)}, u32[]{:S(2)}, u32[]{:S(2)}) collective-permute-start(f32[8,32,128]{2,1,0:T(8,128)S(1)} %get-tuple-element.66.now.refs_9_), channel_id=1, source_target_pairs={{1,2},{2,1},{3,4},{4,3},{5,6},{6,5},{7,8},{8,7},{9,10},{10,9},{11,... | collective-permute-start | bytes 393224 | tf_op jit(solution)/shard_map/ppermute | solution.py:355
  86.5 3.6 %collective-permute-start.6 = (f32[7,32,128]{2,1,0:T(8,128)S(1)}, f32[7,32,128]{2,1,0:T(8,128)S(1)}, u32[]{:S(2)}, u32[]{:S(2)}) collective-permute-start(f32[7,32,128]{2,1,0:T(8,128)S(1)} %get-tuple-element.67), channel_id=1, source_target_pairs={{1,0},{0,1},{3,2},{2,3},{5,4},{4,5},{7,6},{6,7},{9,8},{8,9},{11,10... | collective-permute-start | bytes 344072 | tf_op jit(solution)/shard_map/ppermute | solution.py:348
  97.5 17.1 %collective-permute-start.9 = (f32[8,32,128]{2,1,0:T(8,128)S(1)}, f32[8,32,128]{2,1,0:T(8,128)S(1)}, u32[]{:S(2)}, u32[]{:S(2)}) collective-permute-start(f32[8,32,128]{2,1,0:T(8,128)S(1)} %get-tuple-element.72.refs_3_), channel_id=1, source_target_pairs={{1,2},{2,1},{3,4},{4,3},{5,6},{6,5},{7,8},{8,7},{9,10},{10,9},{11,... | collective-permute-start | bytes 393224 | tf_op jit(solution)/shard_map/ppermute | solution.py:355
  105.2 3.2 %collective-permute-start.8 = (f32[7,32,128]{2,1,0:T(8,128)S(1)}, f32[7,32,128]{2,1,0:T(8,128)S(1)}, u32[]{:S(2)}, u32[]{:S(2)}) collective-permute-start(f32[7,32,128]{2,1,0:T(8,128)S(1)} %get-tuple-element.73), channel_id=1, source_target_pairs={{1,0},{0,1},{3,2},{2,3},{5,4},{4,5},{7,6},{6,7},{9,8},{8,9},{11,10... | collective-permute-start | bytes 344072 | tf_op jit(solution)/shard_map/ppermute | solution.py:348
  116.3 17.1 %collective-permute-start.11 = (f32[8,32,128]{2,1,0:T(8,128)S(1)}, f32[8,32,128]{2,1,0:T(8,128)S(1)}, u32[]{:S(2)}, u32[]{:S(2)}) collective-permute-start(f32[8,32,128]{2,1,0:T(8,128)S(1)} %get-tuple-element.75.refs_3_), channel_id=1, source_target_pairs={{1,2},{2,1},{3,4},{4,3},{5,6},{6,5},{7,8},{8,7},{9,10},{10,9},{11,... | collective-permute-start | bytes 393224 | tf_op jit(solution)/shard_map/ppermute | solution.py:355
  124.0 3.2 %collective-permute-start.10 = (f32[7,32,128]{2,1,0:T(8,128)S(1)}, f32[7,32,128]{2,1,0:T(8,128)S(1)}, u32[]{:S(2)}, u32[]{:S(2)}) collective-permute-start(f32[7,32,128]{2,1,0:T(8,128)S(1)} %get-tuple-element.76), channel_id=1, source_target_pairs={{1,0},{0,1},{3,2},{2,3},{5,4},{4,5},{7,6},{6,7},{9,8},{8,9},{11,10... | collective-permute-start | bytes 344072 | tf_op jit(solution)/shard_map/ppermute | solution.py:348
  135.1 17.1 %collective-permute-start.13 = (f32[8,32,128]{2,1,0:T(8,128)S(1)}, f32[8,32,128]{2,1,0:T(8,128)S(1)}, u32[]{:S(2)}, u32[]{:S(2)}) collective-permute-start(f32[8,32,128]{2,1,0:T(8,128)S(1)} %get-tuple-element.78.scaled), channel_id=1, source_target_pairs={{1,2},{2,1},{3,4},{4,3},{5,6},{6,5},{7,8},{8,7},{9,10},{10,9},{11,... | collective-permute-start | bytes 393224 | tf_op jit(solution)/shard_map/ppermute | solution.py:355
  142.8 3.4 %collective-permute-start.12 = (f32[4,32,128]{2,1,0:T(8,128)S(1)}, f32[4,32,128]{2,1,0:T(8,128)S(1)}, u32[]{:S(2)}, u32[]{:S(2)}) collective-permute-start(f32[4,32,128]{2,1,0:T(8,128)S(1)} %get-tuple-element.79), channel_id=1, source_target_pairs={{1,0},{0,1},{3,2},{2,3},{5,4},{4,5},{7,6},{6,7},{9,8},{8,9},{11,10... | collective-permute-start | bytes 196616 | tf_op jit(solution)/shard_map/ppermute | solution.py:348

commit v5 on v4

--- a/solution.py
+++ b/solution.py
@@ -56,7 +56,7 @@
 
     @pl.when(jnp.logical_not(odd))
     def _():
-        target[0:width, inner, :] = second[CX - width : CX]
+        target[0:width, inner, :] = second[second.shape[0] - width :]
         target[width + CX : 2 * width + CX, inner, :] = first
 
 
@@ -112,10 +112,11 @@
 
 
 def prepare_kernel(
-    info, wave, cells, seen, now, before, last, after, out, base_p, base_q, last_out, source_out
+    info, wave, cells, seen, now, before, last, after, out, base_p, base_q, now_out, last_out, source_out
 ):
     base_p[...] = 2.0 * now[...] - before[...]
     base_q[...] = 2.0 * last[...] - after[...]
+    now_out[...] = now[...]
     last_out[...] = last[...]
     y = lax.broadcasted_iota(jnp.int32, (CY, CZ), 0)
     z = lax.broadcasted_iota(jnp.int32, (CY, CZ), 1)
@@ -148,16 +149,16 @@
         out[n + 1] = total.reshape(CX, CY, CZ)
 
 
-def model_kernel(info, stiff, buoy, last, send_a, send_b, scaled):
+def model_kernel(info, stiff, buoy, last, now, send_a, send_b, scaled):
     scaled[...] = stiff[...] * last[...]
-    send_b[0:8] = buoy[...]
-    send_b[8:16] = scaled[...]
+    send_b[4:12] = now[...]
     for_partner(
         info,
         send_a,
-        lambda: jnp.concatenate([buoy[0:4], scaled[0:7]], axis=0),
-        lambda: jnp.concatenate([buoy[4:8], scaled[1:8]], axis=0),
-    )
+        lambda: jnp.concatenate([buoy[0:4], now[0:7]], axis=0),
+        lambda: jnp.concatenate([buoy[4:8], now[1:8]], axis=0),
+    )
+    for_partner(info, send_b.at[0:4], lambda: buoy[4:8], lambda: buoy[0:4])
 
 
 def forward(info, source, base, stiff, field, buoy, gx, gy, acc, div_out, slope_out, store):
@@ -183,17 +184,17 @@
 
     @pl.when(jnp.logical_not(odd))
     def _():
-        target[0:4] = second[4:8]
+        target[0:4] = second[0:4]
         target[4 + CX : 8 + CX] = first[0:4]
 
 
 def first_kernel(
-    info, now, now_a, now_b, base, source, stiff, buoy, edge_a, edge_b,
-    p_out, send_a, div_out, slope_out, buoy_out,
+    info, now, base, source, stiff, buoy, edge_a, edge_b, scaled,
+    p_out, send_a, send_b, div_out, slope_out, buoy_out,
     field, gx, gy, acc,
 ):
     widen_buoy(info, buoy, edge_a, edge_b, buoy_out)
-    place(info, field, now[...], now_a[...], now_b[...], 7)
+    place(info, field, now[...], edge_a[4:11], edge_b[4:12], 7)
 
     def store(cell, value):
         p_out[cell] = value
@@ -202,15 +203,22 @@
         info, source[0], lambda cell: base[cell],
         stiff, field, buoy_out, gx, gy, acc, div_out, slope_out, store,
     )
-    hand_over(info, send_a, p_out)
+    send_b[0:8] = p_out[...]
+    for_partner(
+        info,
+        send_a,
+        lambda: jnp.concatenate([p_out[0:7], scaled[0:7]], axis=0),
+        lambda: jnp.concatenate([p_out[1:8], scaled[1:8]], axis=0),
+    )
+    for_partner(info, send_b.at[8:15], lambda: scaled[1:8], lambda: scaled[0:7])
 
 
 def adjoint_part_kernel(
-    info, base, scaled, edge_a, edge_b, buoy,
+    info, base, scaled, both_a, both_b, buoy,
     q_out,
     field, gx, gy, acc,
 ):
-    place(info, field, scaled[...], edge_a[4:11], edge_b[8:16], 7)
+    place(info, field, scaled[...], both_a[7:14], both_b[8:15], 7)
     for cell, div in operate(field, 7, buoy, gx, gy, acc, lambda *_: None):
         q_out[cell] = base[cell] + step_squared * div
 
@@ -220,7 +228,7 @@
     p_out, send_a, div_out, slope_out,
     field, gx, gy, acc,
 ):
-    place(info, field, now[...], now_a[...], now_b[...], 7)
+    place(info, field, now[...], now_a[0:7], now_b[0:8], 7)
 
     def store(cell, value):
         p_out[cell] = value
@@ -386,22 +394,20 @@
 
     p0, p_prev = pressure_now[0], pressure_prev[0]
     q4, q5 = adjoint_last[0], adjoint_after[0]
-    p0_b = swap_second(p0)
-    p0_a = swap_first(jnp.where(odd == 1, p0[0:7], p0[1:8]))
     own, seven, four = plane_field(CX), plane_field(7), plane_field(4)
-    spots, base_p, base_q, q4, source_planes = call(
+    spots, base_p, base_q, p0, q4, source_planes = call(
         prepare_kernel,
         [info, source_wave[0]],
         [receiver_cell, observed[0], p0, p_prev, q4, q5],
-        [jax.ShapeDtypeStruct((STEPS + 1, CX, CY, CZ), F32), own, own, own, plane_field(STEPS)],
+        [jax.ShapeDtypeStruct((STEPS + 1, CX, CY, CZ), F32), own, own, own, own, plane_field(STEPS)],
         flops=400_000_000,
     )
     ids = jnp.arange(TILES, dtype=jnp.int32)[:, None, None]
     picked = jnp.broadcast_to(
         (column[None, :, None] == ids).astype(F32), (TILES, column.shape[0], CZ)
     )
-    block, p0_a, p0_b, spots, base_p, base_q, q4, source_planes, picked = lax.optimization_barrier(
-        (block, p0_a, p0_b, spots, base_p, base_q, q4, source_planes, picked)
+    block, spots, base_p, base_q, p0, q4, source_planes, picked = lax.optimization_barrier(
+        (block, spots, base_p, base_q, p0, q4, source_planes, picked)
     )
 
     stiff = block[:, 0].transpose(1, 0, 2)
@@ -410,26 +416,26 @@
     images = jax.ShapeDtypeStruct((2, CX, CY, CZ), F32)
 
     send_a, send_b, f4 = call(
-        model_kernel, [info], [stiff, buoy, q4], [plane_field(11), plane_field(16), own]
+        model_kernel, [info], [stiff, buoy, q4, p0], [plane_field(11), plane_field(12), own]
     )
     edge_b = swap_second(send_b)
     edge_a = swap_first(send_a)
 
-    p1, send_a, div0, slope0, wide = call(
+    p1, send_a, send_b, div0, slope0, wide = call(
         first_kernel,
         [info],
-        [p0, p0_a, p0_b, base_p, source_planes, stiff, buoy, edge_a, edge_b],
-        [own, seven, own, slopes, plane_field(CX + 8)],
+        [p0, base_p, source_planes, stiff, buoy, edge_a, edge_b, f4],
+        [own, plane_field(14), plane_field(15), own, slopes, plane_field(CX + 8)],
         work(),
     )
-    from_b = swap_second(p1)
-    (q_part,) = call(adjoint_part_kernel, [info], [base_q, f4, edge_a, edge_b, wide], [own], work())
-    from_a = swap_first(send_a)
+    both_b = swap_second(send_b)
+    both_a = swap_first(send_a)
+    (q_part,) = call(adjoint_part_kernel, [info], [base_q, f4, both_a, both_b, wide], [own], work())
 
     p2, send_a, div1, slope1 = call(
         second_kernel,
         [info],
-        [p1, from_a, from_b, p0, source_planes, stiff, wide],
+        [p1, both_a, both_b, p0, source_planes, stiff, wide],
         [own, seven, own, slopes],
         work(),
     )

time: 189 us -> 184 us (0.974)
  blocking collectives: 34.5 us -> 30.6 us
    ppermute x7 -> x6, waiting for transfers between devices: 44.6 us -> 28 us  [swap_second(): return lax.ppermute(planes, 'dom', pairs)]
    all_to_all x1, waiting for transfers between devices: 0.01 us -> 15.7 us  [shards(): block = lax.all_to_all(chosen, 'shot', 0, 0, tiled=True)]
    all_to_all x1, blocking collectives: 34.5 us -> 30.6 us  [shards(): lax.all_to_all(image.transpose(2, 0, 1, 3), 'shot', 0, 0, tiled=True)]
    ppermute x7 -> x6, starting transfers between devices: 14.5 us -> 11.5 us  [swap_first(): return lax.ppermute(planes, 'dom', [(i ^ 1, i) for i in range(count)])]
    ppermute x7 -> x6, starting transfers between devices: 54 us -> 56.8 us  [swap_second(): return lax.ppermute(planes, 'dom', pairs)]
    ppermute x7 -> x6, waiting for transfers between devices: 5.26 us -> 5.42 us  [swap_first(): return lax.ppermute(planes, 'dom', [(i ^ 1, i) for i in range(count)])]
  transfers between devices with their start and end apart: 15 -> 13, of which waited for: 11 -> 11; matrix products, arithmetic and copies ran while one was open for 0% -> 0% of each run, Pallas kernels for 2% -> 2%
where the time goes in v5:
time: 184 us
  starting transfers between devices  83.7 us (45%)
  waiting for transfers between devices  49.1 us (27%)
  blocking collectives  30.6 us (17%)
  Pallas kernels  15.1 us (8%)
  other arithmetic  2.31 us (1%)
    ppermute x6, starting transfers between devices, swap_second(): return lax.ppermute(planes, 'dom', pairs)  56.8 us
    all_to_all x1, blocking collectives, shards(): lax.all_to_all(image.transpose(2, 0, 1, 3), 'shot', 0, 0, tiled=True)  30.6 us
    ppermute x6, waiting for transfers between devices, swap_second(): return lax.ppermute(planes, 'dom', pairs)  28 us
    all_to_all x1, waiting for transfers between devices, shards(): block = lax.all_to_all(chosen, 'shot', 0, 0, tiled=True)  15.7 us
    all_to_all x1, starting transfers between devices, shards(): block = lax.all_to_all(chosen, 'shot', 0, 0, tiled=True)  15.4 us
    pallas_call x12, Pallas kernels, call(): pl.pallas_call(kernel, out_shape=outs, in_specs=[SMEM] * len(scalars) + [...  15.1 us
    ppermute x6, starting transfers between devices, swap_first(): return lax.ppermute(planes, 'dom', [(i ^ 1, i) for i in range(count)])  11.5 us
    ppermute x6, waiting for transfers between devices, swap_first(): return lax.ppermute(planes, 'dom', [(i ^ 1, i) for i in range(count)])  5.42 us
  transfers between devices with their start and end apart: 13, of which 11 were waited for; matrix products, arithmetic and copies ran while one was open for 0% of the time, Pallas kernels for 2%

profile of v5, /device:TPU:7, one launch (start us, length us, event | category | flops | bytes accessed | tf_op | source)
XLA Modules:
  0.0 183.7 jit_solution(15555947943920261079)
XLA Ops:
  3.0 15.4 %all-to-all-start = ((f32[32,2,8,128]{3,2,1,0:T(8,128)}), f32[32,2,8,128]{3,2,1,0:T(8,128)S(1)}, u32[]{:S(2)}, u32[]{:S(2)}) async-start(f32[32,2,8,128]{3,2,1,0:T(8,128)} %select_select_fusion), calls=%async_computation | async-start | bytes 524288 | tf_op jit(solution)/shard_map/all_to_all | solution.py:393
  21.4 15.7 %all-to-all-done = f32[32,2,8,128]{3,2,1,0:T(8,128)S(1)} async-done(((f32[32,2,8,128]{3,2,1,0:T(8,128)}), f32[32,2,8,128]{3,2,1,0:T(8,128)S(1)}, u32[]{:S(2)}, u32[]{:S(2)}) %all-to-all-start) | async-done | bytes 262176 | tf_op jit(solution)/shard_map/all_to_all | solution.py:393
  37.9 9.5 %collective-permute-start.1 = (f32[12,32,128]{2,1,0:T(8,128)S(1)}, f32[12,32,128]{2,1,0:T(8,128)S(1)}, u32[]{:S(2)}, u32[]{:S(2)}) collective-permute-start(f32[12,32,128]{2,1,0:T(8,128)S(1)} %get-tuple-element.63), channel_id=1, source_target_pairs={{1,2},{2,1},{3,4},{4,3},{5,6},{6,5},{7,8},{8,7},{9,10},{10,9},{11,... | collective-permute-start | bytes 589832 | tf_op jit(solution)/shard_map/ppermute | solution.py:363
  47.4 1.9 %collective-permute-start = (f32[11,32,128]{2,1,0:T(8,128)S(1)}, f32[11,32,128]{2,1,0:T(8,128)S(1)}, u32[]{:S(2)}, u32[]{:S(2)}) collective-permute-start(f32[11,32,128]{2,1,0:T(8,128)S(1)} %get-tuple-element.62), channel_id=1, source_target_pairs={{1,0},{0,1},{3,2},{2,3},{5,4},{4,5},{7,6},{6,7},{9,8},{8,9},{11,10... | collective-permute-start | bytes 540680 | tf_op jit(solution)/shard_map/ppermute | solution.py:356
  50.7 5.1 %collective-permute-done.1.edge_b = f32[12,32,128]{2,1,0:T(8,128)S(1)} collective-permute-done((f32[12,32,128]{2,1,0:T(8,128)S(1)}, f32[12,32,128]{2,1,0:T(8,128)S(1)}, u32[]{:S(2)}, u32[]{:S(2)}) %collective-permute-start.1) | collective-permute-done | bytes 196640 | tf_op jit(solution)/shard_map/ppermute | solution.py:363
  57.5 9.5 %collective-permute-start.3 = (f32[15,32,128]{2,1,0:T(8,128)S(1)}, f32[15,32,128]{2,1,0:T(8,128)S(1)}, u32[]{:S(2)}, u32[]{:S(2)}) collective-permute-start(f32[15,32,128]{2,1,0:T(8,128)S(1)} %get-tuple-element.67), channel_id=1, source_target_pairs={{1,2},{2,1},{3,4},{4,3},{5,6},{6,5},{7,8},{8,7},{9,10},{10,9},{11,... | collective-permute-start | bytes 737288 | tf_op jit(solution)/shard_map/ppermute | solution.py:363
  67.0 1.9 %collective-permute-start.2 = (f32[14,32,128]{2,1,0:T(8,128)S(1)}, f32[14,32,128]{2,1,0:T(8,128)S(1)}, u32[]{:S(2)}, u32[]{:S(2)}) collective-permute-start(f32[14,32,128]{2,1,0:T(8,128)S(1)} %get-tuple-element.66), channel_id=1, source_target_pairs={{1,0},{0,1},{3,2},{2,3},{5,4},{4,5},{7,6},{6,7},{9,8},{8,9},{11,10... | collective-permute-start | bytes 688136 | tf_op jit(solution)/shard_map/ppermute | solution.py:356
  70.4 5.6 %collective-permute-done.3.now_b.both_b = f32[15,32,128]{2,1,0:T(8,128)S(1)} collective-permute-done((f32[15,32,128]{2,1,0:T(8,128)S(1)}, f32[15,32,128]{2,1,0:T(8,128)S(1)}, u32[]{:S(2)}, u32[]{:S(2)}) %collective-permute-start.3) | collective-permute-done | bytes 245792 | tf_op jit(solution)/shard_map/ppermute | solution.py:363
  76.0 1.7 shard_map.141
  77.6 9.5 %collective-permute-start.5 = (f32[8,32,128]{2,1,0:T(8,128)S(1)}, f32[8,32,128]{2,1,0:T(8,128)S(1)}, u32[]{:S(2)}, u32[]{:S(2)}) collective-permute-start(f32[8,32,128]{2,1,0:T(8,128)S(1)} %get-tuple-element.69.now.refs_9_), channel_id=1, source_target_pairs={{1,2},{2,1},{3,4},{4,3},{5,6},{6,5},{7,8},{8,7},{9,10},{10,9},{11,... | collective-permute-start | bytes 393224 | tf_op jit(solution)/shard_map/ppermute | solution.py:363
  87.2 1.9 %collective-permute-start.4 = (f32[7,32,128]{2,1,0:T(8,128)S(1)}, f32[7,32,128]{2,1,0:T(8,128)S(1)}, u32[]{:S(2)}, u32[]{:S(2)}) collective-permute-start(f32[7,32,128]{2,1,0:T(8,128)S(1)} %get-tuple-element.70), channel_id=1, source_target_pairs={{1,0},{0,1},{3,2},{2,3},{5,4},{4,5},{7,6},{6,7},{9,8},{8,9},{11,10... | collective-permute-start | bytes 344072 | tf_op jit(solution)/shard_map/ppermute | solution.py:356
  90.8 4.1 %collective-permute-done.5.now_b = f32[8,32,128]{2,1,0:T(8,128)S(1)} collective-permute-done((f32[8,32,128]{2,1,0:T(8,128)S(1)}, f32[8,32,128]{2,1,0:T(8,128)S(1)}, u32[]{:S(2)}, u32[]{:S(2)}) %collective-permute-start.5) | collective-permute-done | bytes 131104 | tf_op jit(solution)/shard_map/ppermute | solution.py:363
  96.5 9.4 %collective-permute-start.7 = (f32[8,32,128]{2,1,0:T(8,128)S(1)}, f32[8,32,128]{2,1,0:T(8,128)S(1)}, u32[]{:S(2)}, u32[]{:S(2)}) collective-permute-start(f32[8,32,128]{2,1,0:T(8,128)S(1)} %get-tuple-element.74.refs_3_), channel_id=1, source_target_pairs={{1,2},{2,1},{3,4},{4,3},{5,6},{6,5},{7,8},{8,7},{9,10},{10,9},{11,... | collective-permute-start | bytes 393224 | tf_op jit(solution)/shard_map/ppermute | solution.py:363
  105.9 1.9 %collective-permute-start.6 = (f32[7,32,128]{2,1,0:T(8,128)S(1)}, f32[7,32,128]{2,1,0:T(8,128)S(1)}, u32[]{:S(2)}, u32[]{:S(2)}) collective-permute-start(f32[7,32,128]{2,1,0:T(8,128)S(1)} %get-tuple-element.75), channel_id=1, source_target_pairs={{1,0},{0,1},{3,2},{2,3},{5,4},{4,5},{7,6},{6,7},{9,8},{8,9},{11,10... | collective-permute-start | bytes 344072 | tf_op jit(solution)/shard_map/ppermute | solution.py:356
  109.1 4.4 %collective-permute-done.7.refs_5_ = f32[8,32,128]{2,1,0:T(8,128)S(1)} collective-permute-done((f32[8,32,128]{2,1,0:T(8,128)S(1)}, f32[8,32,128]{2,1,0:T(8,128)S(1)}, u32[]{:S(2)}, u32[]{:S(2)}) %collective-permute-start.7) | collective-permute-done | bytes 131104 | tf_op jit(solution)/shard_map/ppermute | solution.py:363
  113.6 1.7 shard_map.144
  115.3 9.4 %collective-permute-start.9 = (f32[8,32,128]{2,1,0:T(8,128)S(1)}, f32[8,32,128]{2,1,0:T(8,128)S(1)}, u32[]{:S(2)}, u32[]{:S(2)}) collective-permute-start(f32[8,32,128]{2,1,0:T(8,128)S(1)} %get-tuple-element.77.refs_3_), channel_id=1, source_target_pairs={{1,2},{2,1},{3,4},{4,3},{5,6},{6,5},{7,8},{8,7},{9,10},{10,9},{11,... | collective-permute-start | bytes 393224 | tf_op jit(solution)/shard_map/ppermute | solution.py:363
  124.7 1.9 %collective-permute-start.8 = (f32[7,32,128]{2,1,0:T(8,128)S(1)}, f32[7,32,128]{2,1,0:T(8,128)S(1)}, u32[]{:S(2)}, u32[]{:S(2)}) collective-permute-start(f32[7,32,128]{2,1,0:T(8,128)S(1)} %get-tuple-element.78), channel_id=1, source_target_pairs={{1,0},{0,1},{3,2},{2,3},{5,4},{4,5},{7,6},{6,7},{9,8},{8,9},{11,10... | collective-permute-start | bytes 344072 | tf_op jit(solution)/shard_map/ppermute | solution.py:356
  127.9 4.4 %collective-permute-done.9.refs_5_ = f32[8,32,128]{2,1,0:T(8,128)S(1)} collective-permute-done((f32[8,32,128]{2,1,0:T(8,128)S(1)}, f32[8,32,128]{2,1,0:T(8,128)S(1)}, u32[]{:S(2)}, u32[]{:S(2)}) %collective-permute-start.9) | collective-permute-done | bytes 131104 | tf_op jit(solution)/shard_map/ppermute | solution.py:363
  132.4 1.7 shard_map.145
  134.1 9.4 %collective-permute-start.11 = (f32[8,32,128]{2,1,0:T(8,128)S(1)}, f32[8,32,128]{2,1,0:T(8,128)S(1)}, u32[]{:S(2)}, u32[]{:S(2)}) collective-permute-start(f32[8,32,128]{2,1,0:T(8,128)S(1)} %get-tuple-element.80.scaled), channel_id=1, source_target_pairs={{1,2},{2,1},{3,4},{4,3},{5,6},{6,5},{7,8},{8,7},{9,10},{10,9},{11,... | collective-permute-start | bytes 393224 | tf_op jit(solution)/shard_map/ppermute | solution.py:363
  143.5 1.9 %collective-permute-start.10 = (f32[4,32,128]{2,1,0:T(8,128)S(1)}, f32[4,32,128]{2,1,0:T(8,128)S(1)}, u32[]{:S(2)}, u32[]{:S(2)}) collective-permute-start(f32[4,32,128]{2,1,0:T(8,128)S(1)} %get-tuple-element.81), channel_id=1, source_target_pairs={{1,0},{0,1},{3,2},{2,3},{5,4},{4,5},{7,6},{6,7},{9,8},{8,9},{11,10... | collective-permute-start | bytes 196616 | tf_op jit(solution)/shard_map/ppermute | solution.py:356
  146.9 4.3 %collective-permute-done.11.scaled_b = f32[8,32,128]{2,1,0:T(8,128)S(1)} collective-permute-done((f32[8,32,128]{2,1,0:T(8,128)S(1)}, f32[8,32,128]{2,1,0:T(8,128)S(1)}, u32[]{:S(2)}, u32[]{:S(2)}) %collective-permute-start.11) | collective-permute-done | bytes 131104 | tf_op jit(solution)/shard_map/ppermute | solution.py:363
  152.2 30.6 %all_to_all.10.arrived = f32[32,2,8,128]{3,2,1,0:T(8,128)S(1)} all-to-all(f32[32,2,8,128]{3,2,1,0:T(8,128)S(1)} %bitcast.50), channel_id=1, replica_groups=mesh['shot'=32,'dom'=16] {'shot'}, dimensions={0} | all-to-all | bytes 524288 | tf_op jit(solution)/shard_map/all_to_all | solution.py:486
  (42 shorter events, 18.9 us)
Async XLA Ops:
  0.6 0.7 copy-start.6
  3.0 16.2 %copy-start.7 = (f32[1,3,512]{2,0,1:T(1,128)S(1)}, f32[1,3,512]{2,0,1:T(1,128)}, u32[]{:S(2)}) copy-start(f32[1,3,512]{2,0,1:T(1,128)} %param.21) | copy-start | bytes 18436
  3.0 16.3 %copy-start.1 = (f32[1,8,32,128]{3,2,1,0:T(8,128)S(1)}, f32[1,8,32,128]{3,2,1,0:T(8,128)}, u32[]{:S(2)}) copy-start(f32[1,8,32,128]{3,2,1,0:T(8,128)} %param.12) | copy-start | bytes 393220
  3.0 16.3 %copy-start.2 = (f32[1,8,32,128]{3,2,1,0:T(8,128)S(1)}, f32[1,8,32,128]{3,2,1,0:T(8,128)}, u32[]{:S(2)}) copy-start(f32[1,8,32,128]{3,2,1,0:T(8,128)} %param.13) | copy-start | bytes 393220
  3.0 16.3 %copy-start.3 = (f32[1,8,32,128]{3,2,1,0:T(8,128)S(1)}, f32[1,8,32,128]{3,2,1,0:T(8,128)}, u32[]{:S(2)}) copy-start(f32[1,8,32,128]{3,2,1,0:T(8,128)} %param.14) | copy-start | bytes 393220
  3.0 34.2 %all-to-all-start = ((f32[32,2,8,128]{3,2,1,0:T(8,128)}), f32[32,2,8,128]{3,2,1,0:T(8,128)S(1)}, u32[]{:S(2)}, u32[]{:S(2)}) async-start(f32[32,2,8,128]{3,2,1,0:T(8,128)} %select_select_fusion), calls=%async_computation | async-start | bytes 524288 | tf_op jit(solution)/shard_map/all_to_all | solution.py:393
  18.4 0.9 copy-start
  19.3 0.7 copy-start.4
  19.3 0.7 copy-start.5
  37.9 17.9 %collective-permute-start.1 = (f32[12,32,128]{2,1,0:T(8,128)S(1)}, f32[12,32,128]{2,1,0:T(8,128)S(1)}, u32[]{:S(2)}, u32[]{:S(2)}) collective-permute-start(f32[12,32,128]{2,1,0:T(8,128)S(1)} %get-tuple-element.63), channel_id=1, source_target_pairs={{1,2},{2,1},{3,4},{4,3},{5,6},{6,5},{7,8},{8,7},{9,10},{10,9},{11,... | collective-permute-start | bytes 589832 | tf_op jit(solution)/shard_map/ppermute | solution.py:363
  47.4 3.3 %collective-permute-start = (f32[11,32,128]{2,1,0:T(8,128)S(1)}, f32[11,32,128]{2,1,0:T(8,128)S(1)}, u32[]{:S(2)}, u32[]{:S(2)}) collective-permute-start(f32[11,32,128]{2,1,0:T(8,128)S(1)} %get-tuple-element.62), channel_id=1, source_target_pairs={{1,0},{0,1},{3,2},{2,3},{5,4},{4,5},{7,6},{6,7},{9,8},{8,9},{11,10... | collective-permute-start | bytes 540680 | tf_op jit(solution)/shard_map/ppermute | solution.py:356
  57.5 18.5 %collective-permute-start.3 = (f32[15,32,128]{2,1,0:T(8,128)S(1)}, f32[15,32,128]{2,1,0:T(8,128)S(1)}, u32[]{:S(2)}, u32[]{:S(2)}) collective-permute-start(f32[15,32,128]{2,1,0:T(8,128)S(1)} %get-tuple-element.67), channel_id=1, source_target_pairs={{1,2},{2,1},{3,4},{4,3},{5,6},{6,5},{7,8},{8,7},{9,10},{10,9},{11,... | collective-permute-start | bytes 737288 | tf_op jit(solution)/shard_map/ppermute | solution.py:363
  67.0 3.4 %collective-permute-start.2 = (f32[14,32,128]{2,1,0:T(8,128)S(1)}, f32[14,32,128]{2,1,0:T(8,128)S(1)}, u32[]{:S(2)}, u32[]{:S(2)}) collective-permute-start(f32[14,32,128]{2,1,0:T(8,128)S(1)} %get-tuple-element.66), channel_id=1, source_target_pairs={{1,0},{0,1},{3,2},{2,3},{5,4},{4,5},{7,6},{6,7},{9,8},{8,9},{11,10... | collective-permute-start | bytes 688136 | tf_op jit(solution)/shard_map/ppermute | solution.py:356
  77.6 17.2 %collective-permute-start.5 = (f32[8,32,128]{2,1,0:T(8,128)S(1)}, f32[8,32,128]{2,1,0:T(8,128)S(1)}, u32[]{:S(2)}, u32[]{:S(2)}) collective-permute-start(f32[8,32,128]{2,1,0:T(8,128)S(1)} %get-tuple-element.69.now.refs_9_), channel_id=1, source_target_pairs={{1,2},{2,1},{3,4},{4,3},{5,6},{6,5},{7,8},{8,7},{9,10},{10,9},{11,... | collective-permute-start | bytes 393224 | tf_op jit(solution)/shard_map/ppermute | solution.py:363
  87.2 3.6 %collective-permute-start.4 = (f32[7,32,128]{2,1,0:T(8,128)S(1)}, f32[7,32,128]{2,1,0:T(8,128)S(1)}, u32[]{:S(2)}, u32[]{:S(2)}) collective-permute-start(f32[7,32,128]{2,1,0:T(8,128)S(1)} %get-tuple-element.70), channel_id=1, source_target_pairs={{1,0},{0,1},{3,2},{2,3},{5,4},{4,5},{7,6},{6,7},{9,8},{8,9},{11,10... | collective-permute-start | bytes 344072 | tf_op jit(solution)/shard_map/ppermute | solution.py:356
  96.5 17.1 %collective-permute-start.7 = (f32[8,32,128]{2,1,0:T(8,128)S(1)}, f32[8,32,128]{2,1,0:T(8,128)S(1)}, u32[]{:S(2)}, u32[]{:S(2)}) collective-permute-start(f32[8,32,128]{2,1,0:T(8,128)S(1)} %get-tuple-element.74.refs_3_), channel_id=1, source_target_pairs={{1,2},{2,1},{3,4},{4,3},{5,6},{6,5},{7,8},{8,7},{9,10},{10,9},{11,... | collective-permute-start | bytes 393224 | tf_op jit(solution)/shard_map/ppermute | solution.py:363
  105.9 3.2 %collective-permute-start.6 = (f32[7,32,128]{2,1,0:T(8,128)S(1)}, f32[7,32,128]{2,1,0:T(8,128)S(1)}, u32[]{:S(2)}, u32[]{:S(2)}) collective-permute-start(f32[7,32,128]{2,1,0:T(8,128)S(1)} %get-tuple-element.75), channel_id=1, source_target_pairs={{1,0},{0,1},{3,2},{2,3},{5,4},{4,5},{7,6},{6,7},{9,8},{8,9},{11,10... | collective-permute-start | bytes 344072 | tf_op jit(solution)/shard_map/ppermute | solution.py:356
  115.3 17.1 %collective-permute-start.9 = (f32[8,32,128]{2,1,0:T(8,128)S(1)}, f32[8,32,128]{2,1,0:T(8,128)S(1)}, u32[]{:S(2)}, u32[]{:S(2)}) collective-permute-start(f32[8,32,128]{2,1,0:T(8,128)S(1)} %get-tuple-element.77.refs_3_), channel_id=1, source_target_pairs={{1,2},{2,1},{3,4},{4,3},{5,6},{6,5},{7,8},{8,7},{9,10},{10,9},{11,... | collective-permute-start | bytes 393224 | tf_op jit(solution)/shard_map/ppermute | solution.py:363
  124.7 3.2 %collective-permute-start.8 = (f32[7,32,128]{2,1,0:T(8,128)S(1)}, f32[7,32,128]{2,1,0:T(8,128)S(1)}, u32[]{:S(2)}, u32[]{:S(2)}) collective-permute-start(f32[7,32,128]{2,1,0:T(8,128)S(1)} %get-tuple-element.78), channel_id=1, source_target_pairs={{1,0},{0,1},{3,2},{2,3},{5,4},{4,5},{7,6},{6,7},{9,8},{8,9},{11,10... | collective-permute-start | bytes 344072 | tf_op jit(solution)/shard_map/ppermute | solution.py:356
  134.1 17.1 %collective-permute-start.11 = (f32[8,32,128]{2,1,0:T(8,128)S(1)}, f32[8,32,128]{2,1,0:T(8,128)S(1)}, u32[]{:S(2)}, u32[]{:S(2)}) collective-permute-start(f32[8,32,128]{2,1,0:T(8,128)S(1)} %get-tuple-element.80.scaled), channel_id=1, source_target_pairs={{1,2},{2,1},{3,4},{4,3},{5,6},{6,5},{7,8},{8,7},{9,10},{10,9},{11,... | collective-permute-start | bytes 393224 | tf_op jit(solution)/shard_map/ppermute | solution.py:363
  143.5 3.4 %collective-permute-start.10 = (f32[4,32,128]{2,1,0:T(8,128)S(1)}, f32[4,32,128]{2,1,0:T(8,128)S(1)}, u32[]{:S(2)}, u32[]{:S(2)}) collective-permute-start(f32[4,32,128]{2,1,0:T(8,128)S(1)} %get-tuple-element.81), channel_id=1, source_target_pairs={{1,0},{0,1},{3,2},{2,3},{5,4},{4,5},{7,6},{6,7},{9,8},{8,9},{11,10... | collective-permute-start | bytes 196616 | tf_op jit(solution)/shard_map/ppermute | solution.py:356

commit v6 on v4

--- a/solution.py
+++ b/solution.py
@@ -56,7 +56,7 @@
 
     @pl.when(jnp.logical_not(odd))
     def _():
-        target[0:width, inner, :] = second[CX - width : CX]
+        target[0:width, inner, :] = second[second.shape[0] - width :]
         target[width + CX : 2 * width + CX, inner, :] = first
 
 
@@ -112,10 +112,11 @@
 
 
 def prepare_kernel(
-    info, wave, cells, seen, now, before, last, after, out, base_p, base_q, last_out, source_out
+    info, wave, cells, seen, now, before, last, after, out, base_p, base_q, now_out, last_out, source_out
 ):
     base_p[...] = 2.0 * now[...] - before[...]
     base_q[...] = 2.0 * last[...] - after[...]
+    now_out[...] = now[...]
     last_out[...] = last[...]
     y = lax.broadcasted_iota(jnp.int32, (CY, CZ), 0)
     z = lax.broadcasted_iota(jnp.int32, (CY, CZ), 1)
@@ -150,14 +151,9 @@
 
 def model_kernel(info, stiff, buoy, last, send_a, send_b, scaled):
     scaled[...] = stiff[...] * last[...]
-    send_b[0:8] = buoy[...]
-    send_b[8:16] = scaled[...]
-    for_partner(
-        info,
-        send_a,
-        lambda: jnp.concatenate([buoy[0:4], scaled[0:7]], axis=0),
-        lambda: jnp.concatenate([buoy[4:8], scaled[1:8]], axis=0),
-    )
+    send_b[4:5] = buoy[0:1]
+    for_partner(info, send_a, lambda: buoy[0:4], lambda: buoy[4:8])
+    for_partner(info, send_b.at[0:4], lambda: buoy[4:8], lambda: buoy[0:4])
 
 
 def forward(info, source, base, stiff, field, buoy, gx, gy, acc, div_out, slope_out, store):
@@ -183,13 +179,13 @@
 
     @pl.when(jnp.logical_not(odd))
     def _():
-        target[0:4] = second[4:8]
+        target[0:4] = second[0:4]
         target[4 + CX : 8 + CX] = first[0:4]
 
 
 def first_kernel(
-    info, now, now_a, now_b, base, source, stiff, buoy, edge_a, edge_b,
-    p_out, send_a, div_out, slope_out, buoy_out,
+    info, now, now_a, now_b, base, source, stiff, buoy, edge_a, edge_b, scaled,
+    p_out, send_a, near, far, div_out, slope_out, buoy_out,
     field, gx, gy, acc,
 ):
     widen_buoy(info, buoy, edge_a, edge_b, buoy_out)
@@ -203,14 +199,16 @@
         stiff, field, buoy_out, gx, gy, acc, div_out, slope_out, store,
     )
     hand_over(info, send_a, p_out)
+    hand_over(info, near, scaled)
+    far[...] = scaled[...]
 
 
 def adjoint_part_kernel(
-    info, base, scaled, edge_a, edge_b, buoy,
+    info, base, scaled, near, far, buoy,
     q_out,
     field, gx, gy, acc,
 ):
-    place(info, field, scaled[...], edge_a[4:11], edge_b[8:16], 7)
+    place(info, field, scaled[...], near[...], far[...], 7)
     for cell, div in operate(field, 7, buoy, gx, gy, acc, lambda *_: None):
         q_out[cell] = base[cell] + step_squared * div
 
@@ -389,19 +387,19 @@
     p0_b = swap_second(p0)
     p0_a = swap_first(jnp.where(odd == 1, p0[0:7], p0[1:8]))
     own, seven, four = plane_field(CX), plane_field(7), plane_field(4)
-    spots, base_p, base_q, q4, source_planes = call(
+    spots, base_p, base_q, p0, q4, source_planes = call(
         prepare_kernel,
         [info, source_wave[0]],
         [receiver_cell, observed[0], p0, p_prev, q4, q5],
-        [jax.ShapeDtypeStruct((STEPS + 1, CX, CY, CZ), F32), own, own, own, plane_field(STEPS)],
+        [jax.ShapeDtypeStruct((STEPS + 1, CX, CY, CZ), F32), own, own, own, own, plane_field(STEPS)],
         flops=400_000_000,
     )
     ids = jnp.arange(TILES, dtype=jnp.int32)[:, None, None]
     picked = jnp.broadcast_to(
         (column[None, :, None] == ids).astype(F32), (TILES, column.shape[0], CZ)
     )
-    block, p0_a, p0_b, spots, base_p, base_q, q4, source_planes, picked = lax.optimization_barrier(
-        (block, p0_a, p0_b, spots, base_p, base_q, q4, source_planes, picked)
+    block, p0_a, p0_b, spots, base_p, base_q, p0, q4, source_planes, picked = lax.optimization_barrier(
+        (block, p0_a, p0_b, spots, base_p, base_q, p0, q4, source_planes, picked)
     )
 
     stiff = block[:, 0].transpose(1, 0, 2)
@@ -410,21 +408,23 @@
     images = jax.ShapeDtypeStruct((2, CX, CY, CZ), F32)
 
     send_a, send_b, f4 = call(
-        model_kernel, [info], [stiff, buoy, q4], [plane_field(11), plane_field(16), own]
+        model_kernel, [info], [stiff, buoy, q4], [four, plane_field(5), own]
     )
     edge_b = swap_second(send_b)
     edge_a = swap_first(send_a)
 
-    p1, send_a, div0, slope0, wide = call(
+    p1, send_a, near, far, div0, slope0, wide = call(
         first_kernel,
         [info],
-        [p0, p0_a, p0_b, base_p, source_planes, stiff, buoy, edge_a, edge_b],
-        [own, seven, own, slopes, plane_field(CX + 8)],
+        [p0, p0_a, p0_b, base_p, source_planes, stiff, buoy, edge_a, edge_b, f4],
+        [own, seven, seven, own, own, slopes, plane_field(CX + 8)],
         work(),
     )
     from_b = swap_second(p1)
-    (q_part,) = call(adjoint_part_kernel, [info], [base_q, f4, edge_a, edge_b, wide], [own], work())
     from_a = swap_first(send_a)
+    far = swap_second(far)
+    near = swap_first(near)
+    (q_part,) = call(adjoint_part_kernel, [info], [base_q, f4, near, far, wide], [own], work())
 
     p2, send_a, div1, slope1 = call(
         second_kernel,

time: 189 us -> 185 us (0.979)
  waiting for transfers between devices: 49.9 us -> 37.8 us
  starting transfers between devices: 84 us -> 95.2 us
  blocking collectives: 34.5 us -> 30.8 us
    ppermute x7 -> x8, waiting for transfers between devices: 44.6 us -> 34 us  [swap_second(): return lax.ppermute(planes, 'dom', pairs)]
    ppermute x7 -> x8, starting transfers between devices: 54 us -> 62.9 us  [swap_second(): return lax.ppermute(planes, 'dom', pairs)]
    all_to_all x1, blocking collectives: 34.5 us -> 30.8 us  [shards(): lax.all_to_all(image.transpose(2, 0, 1, 3), 'shot', 0, 0, tiled=True)]
    ppermute x7 -> x8, starting transfers between devices: 14.5 us -> 16.9 us  [swap_first(): return lax.ppermute(planes, 'dom', [(i ^ 1, i) for i in range(count)])]
    ppermute x7 -> x8, waiting for transfers between devices: 5.26 us -> 3.81 us  [swap_first(): return lax.ppermute(planes, 'dom', [(i ^ 1, i) for i in range(count)])]
  transfers between devices with their start and end apart: 15 -> 17, of which waited for: 11 -> 9; matrix products, arithmetic and copies ran while one was open for 0% -> 0% of each run, Pallas kernels for 2% -> 3%
where the time goes in v6:
time: 185 us; the launch traced here: 184 us
  starting transfers between devices  95.2 us (51%)
  waiting for transfers between devices  37.8 us (20%)
  blocking collectives  30.8 us (17%)
  Pallas kernels  15.1 us (8%)
  other arithmetic  2.33 us (1%)
    ppermute x8, starting transfers between devices, swap_second(): return lax.ppermute(planes, 'dom', pairs)  62.9 us
    ppermute x8, waiting for transfers between devices, swap_second(): return lax.ppermute(planes, 'dom', pairs)  34 us
    all_to_all x1, blocking collectives, shards(): lax.all_to_all(image.transpose(2, 0, 1, 3), 'shot', 0, 0, tiled=True)  30.8 us
    ppermute x8, starting transfers between devices, swap_first(): return lax.ppermute(planes, 'dom', [(i ^ 1, i) for i in range(count)])  16.9 us
    all_to_all x1, starting transfers between devices, shards(): block = lax.all_to_all(chosen, 'shot', 0, 0, tiled=True)  15.4 us
    pallas_call x12, Pallas kernels, call(): pl.pallas_call(kernel, out_shape=outs, in_specs=[SMEM] * len(scalars) + [...  15.1 us
    ppermute x8, waiting for transfers between devices, swap_first(): return lax.ppermute(planes, 'dom', [(i ^ 1, i) for i in range(count)])  3.81 us
  transfers between devices with their start and end apart: 17, of which 9 were waited for; matrix products, arithmetic and copies ran while one was open for 0% of the time, Pallas kernels for 3%

profile of v6, /device:TPU:7, one launch (start us, length us, event | category | flops | bytes accessed | tf_op | source)
XLA Modules:
  0.0 184.0 jit_solution(6544679051139004293)
XLA Ops:
  3.0 15.4 %all-to-all-start = ((f32[32,2,8,128]{3,2,1,0:T(8,128)}), f32[32,2,8,128]{3,2,1,0:T(8,128)S(1)}, u32[]{:S(2)}, u32[]{:S(2)}) async-start(f32[32,2,8,128]{3,2,1,0:T(8,128)} %select_select_fusion), calls=%async_computation | async-start | bytes 524288 | tf_op jit(solution)/shard_map/all_to_all | solution.py:383
  18.5 3.0 %collective-permute-start = (f32[7,32,128]{2,1,0:T(8,128)S(1)}, f32[7,32,128]{2,1,0:T(8,128)S(1)}, u32[]{:S(2)}, u32[]{:S(2)}) collective-permute-start(f32[7,32,128]{2,1,0:T(8,128)S(1)} %select_bitcast_fusion), channel_id=1, source_target_pairs={{1,0},{0,1},{3,2},{2,3},{5,4},{4,5},{7,6},{6,7},{9,8},{8,9},{11,10... | collective-permute-start | bytes 344072 | tf_op jit(solution)/shard_map/ppermute | solution.py:346
  21.5 7.8 %collective-permute-start.1 = (f32[8,32,128]{2,1,0:T(8,128)S(1)}, f32[8,32,128]{2,1,0:T(8,128)S(1)}, u32[]{:S(2)}, u32[]{:S(2)}) collective-permute-start(f32[8,32,128]{2,1,0:T(8,128)S(1)} %bitcast.46), channel_id=1, source_target_pairs={{1,2},{2,1},{3,4},{4,3},{5,6},{6,5},{7,8},{8,7},{9,10},{10,9},{11,... | collective-permute-start | bytes 393224 | tf_op jit(solution)/shard_map/ppermute | solution.py:353
  32.2 6.7 %collective-permute-done.1.now_b = f32[8,32,128]{2,1,0:T(8,128)S(1)} collective-permute-done((f32[8,32,128]{2,1,0:T(8,128)S(1)}, f32[8,32,128]{2,1,0:T(8,128)S(1)}, u32[]{:S(2)}, u32[]{:S(2)}) %collective-permute-start.1) | collective-permute-done | bytes 131104 | tf_op jit(solution)/shard_map/ppermute | solution.py:353
  39.7 7.7 %collective-permute-start.3 = (f32[5,32,128]{2,1,0:T(8,128)S(1)}, f32[5,32,128]{2,1,0:T(8,128)S(1)}, u32[]{:S(2)}, u32[]{:S(2)}) collective-permute-start(f32[5,32,128]{2,1,0:T(8,128)S(1)} %get-tuple-element.68), channel_id=1, source_target_pairs={{1,2},{2,1},{3,4},{4,3},{5,6},{6,5},{7,8},{8,7},{9,10},{10,9},{11,... | collective-permute-start | bytes 245768 | tf_op jit(solution)/shard_map/ppermute | solution.py:353
  47.4 1.9 %collective-permute-start.2 = (f32[4,32,128]{2,1,0:T(8,128)S(1)}, f32[4,32,128]{2,1,0:T(8,128)S(1)}, u32[]{:S(2)}, u32[]{:S(2)}) collective-permute-start(f32[4,32,128]{2,1,0:T(8,128)S(1)} %get-tuple-element.67), channel_id=1, source_target_pairs={{1,0},{0,1},{3,2},{2,3},{5,4},{4,5},{7,6},{6,7},{9,8},{8,9},{11,10... | collective-permute-start | bytes 196616 | tf_op jit(solution)/shard_map/ppermute | solution.py:346
  50.6 5.7 %collective-permute-done.3.edge_b = f32[5,32,128]{2,1,0:T(8,128)S(1)} collective-permute-done((f32[5,32,128]{2,1,0:T(8,128)S(1)}, f32[5,32,128]{2,1,0:T(8,128)S(1)}, u32[]{:S(2)}, u32[]{:S(2)}) %collective-permute-start.3) | collective-permute-done | bytes 81952 | tf_op jit(solution)/shard_map/ppermute | solution.py:353
  58.0 7.7 %collective-permute-start.5 = (f32[8,32,128]{2,1,0:T(8,128)S(1)}, f32[8,32,128]{2,1,0:T(8,128)S(1)}, u32[]{:S(2)}, u32[]{:S(2)}) collective-permute-start(f32[8,32,128]{2,1,0:T(8,128)S(1)} %get-tuple-element.70.now.before.refs_9_), channel_id=1, source_target_pairs={{1,2},{2,1},{3,4},{4,3},{5,6},{6,5},{7,8},{8,7},{9,10},{10,9},{11,... | collective-permute-start | bytes 393224 | tf_op jit(solution)/shard_map/ppermute | solution.py:353
  65.7 1.9 %collective-permute-start.4 = (f32[7,32,128]{2,1,0:T(8,128)S(1)}, f32[7,32,128]{2,1,0:T(8,128)S(1)}, u32[]{:S(2)}, u32[]{:S(2)}) collective-permute-start(f32[7,32,128]{2,1,0:T(8,128)S(1)} %get-tuple-element.71), channel_id=1, source_target_pairs={{1,0},{0,1},{3,2},{2,3},{5,4},{4,5},{7,6},{6,7},{9,8},{8,9},{11,10... | collective-permute-start | bytes 344072 | tf_op jit(solution)/shard_map/ppermute | solution.py:346
  67.6 8.6 %collective-permute-start.9 = (f32[8,32,128]{2,1,0:T(8,128)S(1)}, f32[8,32,128]{2,1,0:T(8,128)S(1)}, u32[]{:S(2)}, u32[]{:S(2)}) collective-permute-start(f32[8,32,128]{2,1,0:T(8,128)S(1)} %get-tuple-element.77), channel_id=1, source_target_pairs={{1,2},{2,1},{3,4},{4,3},{5,6},{6,5},{7,8},{8,7},{9,10},{10,9},{11,... | collective-permute-start | bytes 393224 | tf_op jit(solution)/shard_map/ppermute | solution.py:353
  78.0 7.7 %collective-permute-start.7 = (f32[8,32,128]{2,1,0:T(8,128)S(1)}, f32[8,32,128]{2,1,0:T(8,128)S(1)}, u32[]{:S(2)}, u32[]{:S(2)}) collective-permute-start(f32[8,32,128]{2,1,0:T(8,128)S(1)} %get-tuple-element.73.now.refs_9_), channel_id=1, source_target_pairs={{1,2},{2,1},{3,4},{4,3},{5,6},{6,5},{7,8},{8,7},{9,10},{10,9},{11,... | collective-permute-start | bytes 393224 | tf_op jit(solution)/shard_map/ppermute | solution.py:353
  85.7 1.9 %collective-permute-start.8 = (f32[7,32,128]{2,1,0:T(8,128)S(1)}, f32[7,32,128]{2,1,0:T(8,128)S(1)}, u32[]{:S(2)}, u32[]{:S(2)}) collective-permute-start(f32[7,32,128]{2,1,0:T(8,128)S(1)} %get-tuple-element.76), channel_id=1, source_target_pairs={{1,0},{0,1},{3,2},{2,3},{5,4},{4,5},{7,6},{6,7},{9,8},{8,9},{11,10... | collective-permute-start | bytes 344072 | tf_op jit(solution)/shard_map/ppermute | solution.py:346
  87.7 2.4 %collective-permute-start.6 = (f32[7,32,128]{2,1,0:T(8,128)S(1)}, f32[7,32,128]{2,1,0:T(8,128)S(1)}, u32[]{:S(2)}, u32[]{:S(2)}) collective-permute-start(f32[7,32,128]{2,1,0:T(8,128)S(1)} %get-tuple-element.74), channel_id=1, source_target_pairs={{1,0},{0,1},{3,2},{2,3},{5,4},{4,5},{7,6},{6,7},{9,8},{8,9},{11,10... | collective-permute-start | bytes 344072 | tf_op jit(solution)/shard_map/ppermute | solution.py:346
  91.8 3.3 %collective-permute-done.7.now_b = f32[8,32,128]{2,1,0:T(8,128)S(1)} collective-permute-done((f32[8,32,128]{2,1,0:T(8,128)S(1)}, f32[8,32,128]{2,1,0:T(8,128)S(1)}, u32[]{:S(2)}, u32[]{:S(2)}) %collective-permute-start.7) | collective-permute-done | bytes 131104 | tf_op jit(solution)/shard_map/ppermute | solution.py:353
  96.7 7.8 %collective-permute-start.11 = (f32[8,32,128]{2,1,0:T(8,128)S(1)}, f32[8,32,128]{2,1,0:T(8,128)S(1)}, u32[]{:S(2)}, u32[]{:S(2)}) collective-permute-start(f32[8,32,128]{2,1,0:T(8,128)S(1)} %get-tuple-element.80.refs_3_), channel_id=1, source_target_pairs={{1,2},{2,1},{3,4},{4,3},{5,6},{6,5},{7,8},{8,7},{9,10},{10,9},{11,... | collective-permute-start | bytes 393224 | tf_op jit(solution)/shard_map/ppermute | solution.py:353
  104.5 1.9 %collective-permute-start.10 = (f32[7,32,128]{2,1,0:T(8,128)S(1)}, f32[7,32,128]{2,1,0:T(8,128)S(1)}, u32[]{:S(2)}, u32[]{:S(2)}) collective-permute-start(f32[7,32,128]{2,1,0:T(8,128)S(1)} %get-tuple-element.81), channel_id=1, source_target_pairs={{1,0},{0,1},{3,2},{2,3},{5,4},{4,5},{7,6},{6,7},{9,8},{8,9},{11,10... | collective-permute-start | bytes 344072 | tf_op jit(solution)/shard_map/ppermute | solution.py:346
  107.7 6.1 %collective-permute-done.11.refs_5_ = f32[8,32,128]{2,1,0:T(8,128)S(1)} collective-permute-done((f32[8,32,128]{2,1,0:T(8,128)S(1)}, f32[8,32,128]{2,1,0:T(8,128)S(1)}, u32[]{:S(2)}, u32[]{:S(2)}) %collective-permute-start.11) | collective-permute-done | bytes 131104 | tf_op jit(solution)/shard_map/ppermute | solution.py:353
  115.5 7.8 %collective-permute-start.13 = (f32[8,32,128]{2,1,0:T(8,128)S(1)}, f32[8,32,128]{2,1,0:T(8,128)S(1)}, u32[]{:S(2)}, u32[]{:S(2)}) collective-permute-start(f32[8,32,128]{2,1,0:T(8,128)S(1)} %get-tuple-element.83.refs_3_), channel_id=1, source_target_pairs={{1,2},{2,1},{3,4},{4,3},{5,6},{6,5},{7,8},{8,7},{9,10},{10,9},{11,... | collective-permute-start | bytes 393224 | tf_op jit(solution)/shard_map/ppermute | solution.py:353
  123.3 1.9 %collective-permute-start.12 = (f32[7,32,128]{2,1,0:T(8,128)S(1)}, f32[7,32,128]{2,1,0:T(8,128)S(1)}, u32[]{:S(2)}, u32[]{:S(2)}) collective-permute-start(f32[7,32,128]{2,1,0:T(8,128)S(1)} %get-tuple-element.84), channel_id=1, source_target_pairs={{1,0},{0,1},{3,2},{2,3},{5,4},{4,5},{7,6},{6,7},{9,8},{8,9},{11,10... | collective-permute-start | bytes 344072 | tf_op jit(solution)/shard_map/ppermute | solution.py:346
  126.5 6.1 %collective-permute-done.13.refs_5_ = f32[8,32,128]{2,1,0:T(8,128)S(1)} collective-permute-done((f32[8,32,128]{2,1,0:T(8,128)S(1)}, f32[8,32,128]{2,1,0:T(8,128)S(1)}, u32[]{:S(2)}, u32[]{:S(2)}) %collective-permute-start.13) | collective-permute-done | bytes 131104 | tf_op jit(solution)/shard_map/ppermute | solution.py:353
  134.3 7.8 %collective-permute-start.15 = (f32[8,32,128]{2,1,0:T(8,128)S(1)}, f32[8,32,128]{2,1,0:T(8,128)S(1)}, u32[]{:S(2)}, u32[]{:S(2)}) collective-permute-start(f32[8,32,128]{2,1,0:T(8,128)S(1)} %get-tuple-element.86.scaled), channel_id=1, source_target_pairs={{1,2},{2,1},{3,4},{4,3},{5,6},{6,5},{7,8},{8,7},{9,10},{10,9},{11,... | collective-permute-start | bytes 393224 | tf_op jit(solution)/shard_map/ppermute | solution.py:353
  142.1 1.9 %collective-permute-start.14 = (f32[4,32,128]{2,1,0:T(8,128)S(1)}, f32[4,32,128]{2,1,0:T(8,128)S(1)}, u32[]{:S(2)}, u32[]{:S(2)}) collective-permute-start(f32[4,32,128]{2,1,0:T(8,128)S(1)} %get-tuple-element.87), channel_id=1, source_target_pairs={{1,0},{0,1},{3,2},{2,3},{5,4},{4,5},{7,6},{6,7},{9,8},{8,9},{11,10... | collective-permute-start | bytes 196616 | tf_op jit(solution)/shard_map/ppermute | solution.py:346
  145.5 6.0 %collective-permute-done.15.scaled_b = f32[8,32,128]{2,1,0:T(8,128)S(1)} collective-permute-done((f32[8,32,128]{2,1,0:T(8,128)S(1)}, f32[8,32,128]{2,1,0:T(8,128)S(1)}, u32[]{:S(2)}, u32[]{:S(2)}) %collective-permute-start.15) | collective-permute-done | bytes 131104 | tf_op jit(solution)/shard_map/ppermute | solution.py:353
  152.5 30.8 %all_to_all.10.arrived = f32[32,2,8,128]{3,2,1,0:T(8,128)S(1)} all-to-all(f32[32,2,8,128]{3,2,1,0:T(8,128)S(1)} %bitcast.53), channel_id=1, replica_groups=mesh['shot'=32,'dom'=16] {'shot'}, dimensions={0} | all-to-all | bytes 524288 | tf_op jit(solution)/shard_map/all_to_all | solution.py:480
  (51 shorter events, 22.4 us)
Async XLA Ops:
  0.6 0.7 copy-start.6
  3.0 15.4 %copy-start = (f32[1,8,32,128]{3,2,1,0:T(8,128)S(1)}, f32[1,8,32,128]{3,2,1,0:T(8,128)}, u32[]{:S(2)}) copy-start(f32[1,8,32,128]{3,2,1,0:T(8,128)} %param.11) | copy-start | bytes 393220
  3.0 35.9 %all-to-all-start = ((f32[32,2,8,128]{3,2,1,0:T(8,128)}), f32[32,2,8,128]{3,2,1,0:T(8,128)S(1)}, u32[]{:S(2)}, u32[]{:S(2)}) async-start(f32[32,2,8,128]{3,2,1,0:T(8,128)} %select_select_fusion), calls=%async_computation | async-start | bytes 524288 | tf_op jit(solution)/shard_map/all_to_all | solution.py:383
  18.4 11.5 %copy-start.7 = (f32[1,3,512]{2,0,1:T(1,128)S(1)}, f32[1,3,512]{2,0,1:T(1,128)}, u32[]{:S(2)}) copy-start(f32[1,3,512]{2,0,1:T(1,128)} %param.21) | copy-start | bytes 18436
  18.4 11.7 %copy-start.2 = (f32[1,8,32,128]{3,2,1,0:T(8,128)S(1)}, f32[1,8,32,128]{3,2,1,0:T(8,128)}, u32[]{:S(2)}) copy-start(f32[1,8,32,128]{3,2,1,0:T(8,128)} %param.13) | copy-start | bytes 393220
  18.4 11.7 %copy-start.3 = (f32[1,8,32,128]{3,2,1,0:T(8,128)S(1)}, f32[1,8,32,128]{3,2,1,0:T(8,128)}, u32[]{:S(2)}) copy-start(f32[1,8,32,128]{3,2,1,0:T(8,128)} %param.14) | copy-start | bytes 393220
  18.4 11.6 %copy-start.1 = (f32[1,8,32,128]{3,2,1,0:T(8,128)S(1)}, f32[1,8,32,128]{3,2,1,0:T(8,128)}, u32[]{:S(2)}) copy-start(f32[1,8,32,128]{3,2,1,0:T(8,128)} %param.12) | copy-start | bytes 393220
  18.5 13.7 %collective-permute-start = (f32[7,32,128]{2,1,0:T(8,128)S(1)}, f32[7,32,128]{2,1,0:T(8,128)S(1)}, u32[]{:S(2)}, u32[]{:S(2)}) collective-permute-start(f32[7,32,128]{2,1,0:T(8,128)S(1)} %select_bitcast_fusion), channel_id=1, source_target_pairs={{1,0},{0,1},{3,2},{2,3},{5,4},{4,5},{7,6},{6,7},{9,8},{8,9},{11,10... | collective-permute-start | bytes 344072 | tf_op jit(solution)/shard_map/ppermute | solution.py:346
  21.5 17.4 %collective-permute-start.1 = (f32[8,32,128]{2,1,0:T(8,128)S(1)}, f32[8,32,128]{2,1,0:T(8,128)S(1)}, u32[]{:S(2)}, u32[]{:S(2)}) collective-permute-start(f32[8,32,128]{2,1,0:T(8,128)S(1)} %bitcast.46), channel_id=1, source_target_pairs={{1,2},{2,1},{3,4},{4,3},{5,6},{6,5},{7,8},{8,7},{9,10},{10,9},{11,... | collective-permute-start | bytes 393224 | tf_op jit(solution)/shard_map/ppermute | solution.py:353
  30.1 0.7 copy-start.5
  39.7 16.6 %collective-permute-start.3 = (f32[5,32,128]{2,1,0:T(8,128)S(1)}, f32[5,32,128]{2,1,0:T(8,128)S(1)}, u32[]{:S(2)}, u32[]{:S(2)}) collective-permute-start(f32[5,32,128]{2,1,0:T(8,128)S(1)} %get-tuple-element.68), channel_id=1, source_target_pairs={{1,2},{2,1},{3,4},{4,3},{5,6},{6,5},{7,8},{8,7},{9,10},{10,9},{11,... | collective-permute-start | bytes 245768 | tf_op jit(solution)/shard_map/ppermute | solution.py:353
  47.4 3.1 %collective-permute-start.2 = (f32[4,32,128]{2,1,0:T(8,128)S(1)}, f32[4,32,128]{2,1,0:T(8,128)S(1)}, u32[]{:S(2)}, u32[]{:S(2)}) collective-permute-start(f32[4,32,128]{2,1,0:T(8,128)S(1)} %get-tuple-element.67), channel_id=1, source_target_pairs={{1,0},{0,1},{3,2},{2,3},{5,4},{4,5},{7,6},{6,7},{9,8},{8,9},{11,10... | collective-permute-start | bytes 196616 | tf_op jit(solution)/shard_map/ppermute | solution.py:346
  58.0 18.3 %collective-permute-start.5 = (f32[8,32,128]{2,1,0:T(8,128)S(1)}, f32[8,32,128]{2,1,0:T(8,128)S(1)}, u32[]{:S(2)}, u32[]{:S(2)}) collective-permute-start(f32[8,32,128]{2,1,0:T(8,128)S(1)} %get-tuple-element.70.now.before.refs_9_), channel_id=1, source_target_pairs={{1,2},{2,1},{3,4},{4,3},{5,6},{6,5},{7,8},{8,7},{9,10},{10,9},{11,... | collective-permute-start | bytes 393224 | tf_op jit(solution)/shard_map/ppermute | solution.py:353
  65.7 10.6 %collective-permute-start.4 = (f32[7,32,128]{2,1,0:T(8,128)S(1)}, f32[7,32,128]{2,1,0:T(8,128)S(1)}, u32[]{:S(2)}, u32[]{:S(2)}) collective-permute-start(f32[7,32,128]{2,1,0:T(8,128)S(1)} %get-tuple-element.71), channel_id=1, source_target_pairs={{1,0},{0,1},{3,2},{2,3},{5,4},{4,5},{7,6},{6,7},{9,8},{8,9},{11,10... | collective-permute-start | bytes 344072 | tf_op jit(solution)/shard_map/ppermute | solution.py:346
  67.6 22.5 %collective-permute-start.9 = (f32[8,32,128]{2,1,0:T(8,128)S(1)}, f32[8,32,128]{2,1,0:T(8,128)S(1)}, u32[]{:S(2)}, u32[]{:S(2)}) collective-permute-start(f32[8,32,128]{2,1,0:T(8,128)S(1)} %get-tuple-element.77), channel_id=1, source_target_pairs={{1,2},{2,1},{3,4},{4,3},{5,6},{6,5},{7,8},{8,7},{9,10},{10,9},{11,... | collective-permute-start | bytes 393224 | tf_op jit(solution)/shard_map/ppermute | solution.py:353
  78.0 17.1 %collective-permute-start.7 = (f32[8,32,128]{2,1,0:T(8,128)S(1)}, f32[8,32,128]{2,1,0:T(8,128)S(1)}, u32[]{:S(2)}, u32[]{:S(2)}) collective-permute-start(f32[8,32,128]{2,1,0:T(8,128)S(1)} %get-tuple-element.73.now.refs_9_), channel_id=1, source_target_pairs={{1,2},{2,1},{3,4},{4,3},{5,6},{6,5},{7,8},{8,7},{9,10},{10,9},{11,... | collective-permute-start | bytes 393224 | tf_op jit(solution)/shard_map/ppermute | solution.py:353
  85.7 4.3 %collective-permute-start.8 = (f32[7,32,128]{2,1,0:T(8,128)S(1)}, f32[7,32,128]{2,1,0:T(8,128)S(1)}, u32[]{:S(2)}, u32[]{:S(2)}) collective-permute-start(f32[7,32,128]{2,1,0:T(8,128)S(1)} %get-tuple-element.76), channel_id=1, source_target_pairs={{1,0},{0,1},{3,2},{2,3},{5,4},{4,5},{7,6},{6,7},{9,8},{8,9},{11,10... | collective-permute-start | bytes 344072 | tf_op jit(solution)/shard_map/ppermute | solution.py:346
  87.7 4.1 %collective-permute-start.6 = (f32[7,32,128]{2,1,0:T(8,128)S(1)}, f32[7,32,128]{2,1,0:T(8,128)S(1)}, u32[]{:S(2)}, u32[]{:S(2)}) collective-permute-start(f32[7,32,128]{2,1,0:T(8,128)S(1)} %get-tuple-element.74), channel_id=1, source_target_pairs={{1,0},{0,1},{3,2},{2,3},{5,4},{4,5},{7,6},{6,7},{9,8},{8,9},{11,10... | collective-permute-start | bytes 344072 | tf_op jit(solution)/shard_map/ppermute | solution.py:346
  96.7 17.1 %collective-permute-start.11 = (f32[8,32,128]{2,1,0:T(8,128)S(1)}, f32[8,32,128]{2,1,0:T(8,128)S(1)}, u32[]{:S(2)}, u32[]{:S(2)}) collective-permute-start(f32[8,32,128]{2,1,0:T(8,128)S(1)} %get-tuple-element.80.refs_3_), channel_id=1, source_target_pairs={{1,2},{2,1},{3,4},{4,3},{5,6},{6,5},{7,8},{8,7},{9,10},{10,9},{11,... | collective-permute-start | bytes 393224 | tf_op jit(solution)/shard_map/ppermute | solution.py:353
  104.5 3.2 %collective-permute-start.10 = (f32[7,32,128]{2,1,0:T(8,128)S(1)}, f32[7,32,128]{2,1,0:T(8,128)S(1)}, u32[]{:S(2)}, u32[]{:S(2)}) collective-permute-start(f32[7,32,128]{2,1,0:T(8,128)S(1)} %get-tuple-element.81), channel_id=1, source_target_pairs={{1,0},{0,1},{3,2},{2,3},{5,4},{4,5},{7,6},{6,7},{9,8},{8,9},{11,10... | collective-permute-start | bytes 344072 | tf_op jit(solution)/shard_map/ppermute | solution.py:346
  115.5 17.1 %collective-permute-start.13 = (f32[8,32,128]{2,1,0:T(8,128)S(1)}, f32[8,32,128]{2,1,0:T(8,128)S(1)}, u32[]{:S(2)}, u32[]{:S(2)}) collective-permute-start(f32[8,32,128]{2,1,0:T(8,128)S(1)} %get-tuple-element.83.refs_3_), channel_id=1, source_target_pairs={{1,2},{2,1},{3,4},{4,3},{5,6},{6,5},{7,8},{8,7},{9,10},{10,9},{11,... | collective-permute-start | bytes 393224 | tf_op jit(solution)/shard_map/ppermute | solution.py:353
  123.3 3.2 %collective-permute-start.12 = (f32[7,32,128]{2,1,0:T(8,128)S(1)}, f32[7,32,128]{2,1,0:T(8,128)S(1)}, u32[]{:S(2)}, u32[]{:S(2)}) collective-permute-start(f32[7,32,128]{2,1,0:T(8,128)S(1)} %get-tuple-element.84), channel_id=1, source_target_pairs={{1,0},{0,1},{3,2},{2,3},{5,4},{4,5},{7,6},{6,7},{9,8},{8,9},{11,10... | collective-permute-start | bytes 344072 | tf_op jit(solution)/shard_map/ppermute | solution.py:346
  134.3 17.1 %collective-permute-start.15 = (f32[8,32,128]{2,1,0:T(8,128)S(1)}, f32[8,32,128]{2,1,0:T(8,128)S(1)}, u32[]{:S(2)}, u32[]{:S(2)}) collective-permute-start(f32[8,32,128]{2,1,0:T(8,128)S(1)} %get-tuple-element.86.scaled), channel_id=1, source_target_pairs={{1,2},{2,1},{3,4},{4,3},{5,6},{6,5},{7,8},{8,7},{9,10},{10,9},{11,... | collective-permute-start | bytes 393224 | tf_op jit(solution)/shard_map/ppermute | solution.py:353
  142.1 3.4 %collective-permute-start.14 = (f32[4,32,128]{2,1,0:T(8,128)S(1)}, f32[4,32,128]{2,1,0:T(8,128)S(1)}, u32[]{:S(2)}, u32[]{:S(2)}) collective-permute-start(f32[4,32,128]{2,1,0:T(8,128)S(1)} %get-tuple-element.87), channel_id=1, source_target_pairs={{1,0},{0,1},{3,2},{2,3},{5,4},{4,5},{7,6},{6,7},{9,8},{8,9},{11,10... | collective-permute-start | bytes 196616 | tf_op jit(solution)/shard_map/ppermute | solution.py:346
  (1 other events, 0.7 us)

commit v7 on v6

--- a/solution.py
+++ b/solution.py
@@ -149,10 +149,15 @@
         out[n + 1] = total.reshape(CX, CY, CZ)
 
 
-def model_kernel(info, stiff, buoy, last, send_a, send_b, scaled):
+def model_kernel(info, stiff, buoy, last, now, send_a, send_b, scaled):
     scaled[...] = stiff[...] * last[...]
-    send_b[4:5] = buoy[0:1]
-    for_partner(info, send_a, lambda: buoy[0:4], lambda: buoy[4:8])
+    send_b[4:12] = now[...]
+    for_partner(
+        info,
+        send_a,
+        lambda: jnp.concatenate([buoy[0:4], now[0:7]], axis=0),
+        lambda: jnp.concatenate([buoy[4:8], now[1:8]], axis=0),
+    )
     for_partner(info, send_b.at[0:4], lambda: buoy[4:8], lambda: buoy[0:4])
 
 
@@ -184,12 +189,12 @@
 
 
 def first_kernel(
-    info, now, now_a, now_b, base, source, stiff, buoy, edge_a, edge_b, scaled,
+    info, now, base, source, stiff, buoy, edge_a, edge_b, scaled,
     p_out, send_a, near, far, div_out, slope_out, buoy_out,
     field, gx, gy, acc,
 ):
     widen_buoy(info, buoy, edge_a, edge_b, buoy_out)
-    place(info, field, now[...], now_a[...], now_b[...], 7)
+    place(info, field, now[...], edge_a[4:11], edge_b[4:12], 7)
 
     def store(cell, value):
         p_out[cell] = value
@@ -384,8 +389,6 @@
 
     p0, p_prev = pressure_now[0], pressure_prev[0]
     q4, q5 = adjoint_last[0], adjoint_after[0]
-    p0_b = swap_second(p0)
-    p0_a = swap_first(jnp.where(odd == 1, p0[0:7], p0[1:8]))
     own, seven, four = plane_field(CX), plane_field(7), plane_field(4)
     spots, base_p, base_q, p0, q4, source_planes = call(
         prepare_kernel,
@@ -398,8 +401,8 @@
     picked = jnp.broadcast_to(
         (column[None, :, None] == ids).astype(F32), (TILES, column.shape[0], CZ)
     )
-    block, p0_a, p0_b, spots, base_p, base_q, p0, q4, source_planes, picked = lax.optimization_barrier(
-        (block, p0_a, p0_b, spots, base_p, base_q, p0, q4, source_planes, picked)
+    block, spots, base_p, base_q, p0, q4, source_planes, picked = lax.optimization_barrier(
+        (block, spots, base_p, base_q, p0, q4, source_planes, picked)
     )
 
     stiff = block[:, 0].transpose(1, 0, 2)
@@ -408,7 +411,7 @@
     images = jax.ShapeDtypeStruct((2, CX, CY, CZ), F32)
 
     send_a, send_b, f4 = call(
-        model_kernel, [info], [stiff, buoy, q4], [four, plane_field(5), own]
+        model_kernel, [info], [stiff, buoy, q4, p0], [plane_field(11), plane_field(12), own]
     )
     edge_b = swap_second(send_b)
     edge_a = swap_first(send_a)
@@ -416,7 +419,7 @@
     p1, send_a, near, far, div0, slope0, wide = call(
         first_kernel,
         [info],
-        [p0, p0_a, p0_b, base_p, source_planes, stiff, buoy, edge_a, edge_b, f4],
+        [p0, base_p, source_planes, stiff, buoy, edge_a, edge_b, f4],
         [own, seven, seven, own, own, slopes, plane_field(CX + 8)],
         work(),
     )

time: 185 us -> 182 us (0.984)
  blocking collectives: 30.8 us -> 28.5 us
  starting transfers between devices: 95.2 us -> 93.1 us
    all_to_all x1, waiting for transfers between devices: 0.01 us -> 15.7 us  [shards(): block = lax.all_to_all(chosen, 'shot', 0, 0, tiled=True)]
    ppermute x8 -> x7, waiting for transfers between devices: 34 us -> 19.9 us  [swap_second(): return lax.ppermute(planes, 'dom', pairs)]
    ppermute x8 -> x7, starting transfers between devices: 16.9 us -> 13.9 us  [swap_first(): return lax.ppermute(planes, 'dom', [(i ^ 1, i) for i in range(count)])]
    all_to_all x1, blocking collectives: 30.8 us -> 28.5 us  [shards(): lax.all_to_all(image.transpose(2, 0, 1, 3), 'shot', 0, 0, tiled=True)]
    ppermute x8 -> x7, starting transfers between devices: 62.9 us -> 63.8 us  [swap_second(): return lax.ppermute(planes, 'dom', pairs)]
    ppermute x8 -> x7, waiting for transfers between devices: 3.81 us -> 3.97 us  [swap_first(): return lax.ppermute(planes, 'dom', [(i ^ 1, i) for i in range(count)])]
  transfers between devices with their start and end apart: 17 -> 15, of which waited for: 9 -> 9; matrix products, arithmetic and copies ran while one was open for 0% -> 0% of each run, Pallas kernels for 3% -> 3%
where the time goes in v7:
time: 182 us
  starting transfers between devices  93.1 us (51%)
  waiting for transfers between devices  39.6 us (22%)
  blocking collectives  28.5 us (16%)
  Pallas kernels  15.1 us (8%)
  other arithmetic  2.31 us (1%)
    ppermute x7, starting transfers between devices, swap_second(): return lax.ppermute(planes, 'dom', pairs)  63.8 us
    all_to_all x1, blocking collectives, shards(): lax.all_to_all(image.transpose(2, 0, 1, 3), 'shot', 0, 0, tiled=True)  28.5 us
    ppermute x7, waiting for transfers between devices, swap_second(): return lax.ppermute(planes, 'dom', pairs)  19.9 us
    all_to_all x1, waiting for transfers between devices, shards(): block = lax.all_to_all(chosen, 'shot', 0, 0, tiled=True)  15.7 us
    all_to_all x1, starting transfers between devices, shards(): block = lax.all_to_all(chosen, 'shot', 0, 0, tiled=True)  15.4 us
    pallas_call x12, Pallas kernels, call(): pl.pallas_call(kernel, out_shape=outs, in_specs=[SMEM] * len(scalars) + [...  15.1 us
    ppermute x7, starting transfers between devices, swap_first(): return lax.ppermute(planes, 'dom', [(i ^ 1, i) for i in range(count)])  13.9 us
    ppermute x7, waiting for transfers between devices, swap_first(): return lax.ppermute(planes, 'dom', [(i ^ 1, i) for i in range(count)])  3.97 us
  transfers between devices with their start and end apart: 15, of which 9 were waited for; matrix products, arithmetic and copies ran while one was open for 0% of the time, Pallas kernels for 3%

profile of v7, /device:TPU:7, one launch (start us, length us, event | category | flops | bytes accessed | tf_op | source)
XLA Modules:
  0.0 181.5 jit_solution(3620653304857563603)
XLA Ops:
  3.0 15.4 %all-to-all-start = ((f32[32,2,8,128]{3,2,1,0:T(8,128)}), f32[32,2,8,128]{3,2,1,0:T(8,128)S(1)}, u32[]{:S(2)}, u32[]{:S(2)}) async-start(f32[32,2,8,128]{3,2,1,0:T(8,128)} %select_select_fusion), calls=%async_computation | async-start | bytes 524288 | tf_op jit(solution)/shard_map/all_to_all | solution.py:388
  21.4 15.7 %all-to-all-done = f32[32,2,8,128]{3,2,1,0:T(8,128)S(1)} async-done(((f32[32,2,8,128]{3,2,1,0:T(8,128)}), f32[32,2,8,128]{3,2,1,0:T(8,128)S(1)}, u32[]{:S(2)}, u32[]{:S(2)}) %all-to-all-start) | async-done | bytes 262176 | tf_op jit(solution)/shard_map/all_to_all | solution.py:388
  37.9 9.5 %collective-permute-start.1 = (f32[12,32,128]{2,1,0:T(8,128)S(1)}, f32[12,32,128]{2,1,0:T(8,128)S(1)}, u32[]{:S(2)}, u32[]{:S(2)}) collective-permute-start(f32[12,32,128]{2,1,0:T(8,128)S(1)} %get-tuple-element.64), channel_id=1, source_target_pairs={{1,2},{2,1},{3,4},{4,3},{5,6},{6,5},{7,8},{8,7},{9,10},{10,9},{11,... | collective-permute-start | bytes 589832 | tf_op jit(solution)/shard_map/ppermute | solution.py:358
  47.4 1.9 %collective-permute-start = (f32[11,32,128]{2,1,0:T(8,128)S(1)}, f32[11,32,128]{2,1,0:T(8,128)S(1)}, u32[]{:S(2)}, u32[]{:S(2)}) collective-permute-start(f32[11,32,128]{2,1,0:T(8,128)S(1)} %get-tuple-element.63), channel_id=1, source_target_pairs={{1,0},{0,1},{3,2},{2,3},{5,4},{4,5},{7,6},{6,7},{9,8},{8,9},{11,10... | collective-permute-start | bytes 540680 | tf_op jit(solution)/shard_map/ppermute | solution.py:351
  50.7 5.1 %collective-permute-done.1.edge_b = f32[12,32,128]{2,1,0:T(8,128)S(1)} collective-permute-done((f32[12,32,128]{2,1,0:T(8,128)S(1)}, f32[12,32,128]{2,1,0:T(8,128)S(1)}, u32[]{:S(2)}, u32[]{:S(2)}) %collective-permute-start.1) | collective-permute-done | bytes 196640 | tf_op jit(solution)/shard_map/ppermute | solution.py:358
  55.9 1.7 shard_map.140
  57.6 9.5 %collective-permute-start.3 = (f32[8,32,128]{2,1,0:T(8,128)S(1)}, f32[8,32,128]{2,1,0:T(8,128)S(1)}, u32[]{:S(2)}, u32[]{:S(2)}) collective-permute-start(f32[8,32,128]{2,1,0:T(8,128)S(1)} %get-tuple-element.66.now.before.refs_9_), channel_id=1, source_target_pairs={{1,2},{2,1},{3,4},{4,3},{5,6},{6,5},{7,8},{8,7},{9,10},{10,9},{11,... | collective-permute-start | bytes 393224 | tf_op jit(solution)/shard_map/ppermute | solution.py:358
  67.1 1.9 %collective-permute-start.2 = (f32[7,32,128]{2,1,0:T(8,128)S(1)}, f32[7,32,128]{2,1,0:T(8,128)S(1)}, u32[]{:S(2)}, u32[]{:S(2)}) collective-permute-start(f32[7,32,128]{2,1,0:T(8,128)S(1)} %get-tuple-element.67), channel_id=1, source_target_pairs={{1,0},{0,1},{3,2},{2,3},{5,4},{4,5},{7,6},{6,7},{9,8},{8,9},{11,10... | collective-permute-start | bytes 344072 | tf_op jit(solution)/shard_map/ppermute | solution.py:351
  69.0 6.9 %collective-permute-start.7 = (f32[8,32,128]{2,1,0:T(8,128)S(1)}, f32[8,32,128]{2,1,0:T(8,128)S(1)}, u32[]{:S(2)}, u32[]{:S(2)}) collective-permute-start(f32[8,32,128]{2,1,0:T(8,128)S(1)} %get-tuple-element.73), channel_id=1, source_target_pairs={{1,2},{2,1},{3,4},{4,3},{5,6},{6,5},{7,8},{8,7},{9,10},{10,9},{11,... | collective-permute-start | bytes 393224 | tf_op jit(solution)/shard_map/ppermute | solution.py:358
  77.6 9.5 %collective-permute-start.5 = (f32[8,32,128]{2,1,0:T(8,128)S(1)}, f32[8,32,128]{2,1,0:T(8,128)S(1)}, u32[]{:S(2)}, u32[]{:S(2)}) collective-permute-start(f32[8,32,128]{2,1,0:T(8,128)S(1)} %get-tuple-element.69.now.refs_9_), channel_id=1, source_target_pairs={{1,2},{2,1},{3,4},{4,3},{5,6},{6,5},{7,8},{8,7},{9,10},{10,9},{11,... | collective-permute-start | bytes 393224 | tf_op jit(solution)/shard_map/ppermute | solution.py:358
  87.1 1.9 %collective-permute-start.6 = (f32[7,32,128]{2,1,0:T(8,128)S(1)}, f32[7,32,128]{2,1,0:T(8,128)S(1)}, u32[]{:S(2)}, u32[]{:S(2)}) collective-permute-start(f32[7,32,128]{2,1,0:T(8,128)S(1)} %get-tuple-element.72), channel_id=1, source_target_pairs={{1,0},{0,1},{3,2},{2,3},{5,4},{4,5},{7,6},{6,7},{9,8},{8,9},{11,10... | collective-permute-start | bytes 344072 | tf_op jit(solution)/shard_map/ppermute | solution.py:351
  89.0 2.4 %collective-permute-start.4 = (f32[7,32,128]{2,1,0:T(8,128)S(1)}, f32[7,32,128]{2,1,0:T(8,128)S(1)}, u32[]{:S(2)}, u32[]{:S(2)}) collective-permute-start(f32[7,32,128]{2,1,0:T(8,128)S(1)} %get-tuple-element.70), channel_id=1, source_target_pairs={{1,0},{0,1},{3,2},{2,3},{5,4},{4,5},{7,6},{6,7},{9,8},{8,9},{11,10... | collective-permute-start | bytes 344072 | tf_op jit(solution)/shard_map/ppermute | solution.py:351
  93.1 1.7 collective-permute-done.5.now_b
  96.4 9.5 %collective-permute-start.9 = (f32[8,32,128]{2,1,0:T(8,128)S(1)}, f32[8,32,128]{2,1,0:T(8,128)S(1)}, u32[]{:S(2)}, u32[]{:S(2)}) collective-permute-start(f32[8,32,128]{2,1,0:T(8,128)S(1)} %get-tuple-element.76.refs_3_), channel_id=1, source_target_pairs={{1,2},{2,1},{3,4},{4,3},{5,6},{6,5},{7,8},{8,7},{9,10},{10,9},{11,... | collective-permute-start | bytes 393224 | tf_op jit(solution)/shard_map/ppermute | solution.py:358
  105.9 1.9 %collective-permute-start.8 = (f32[7,32,128]{2,1,0:T(8,128)S(1)}, f32[7,32,128]{2,1,0:T(8,128)S(1)}, u32[]{:S(2)}, u32[]{:S(2)}) collective-permute-start(f32[7,32,128]{2,1,0:T(8,128)S(1)} %get-tuple-element.77), channel_id=1, source_target_pairs={{1,0},{0,1},{3,2},{2,3},{5,4},{4,5},{7,6},{6,7},{9,8},{8,9},{11,10... | collective-permute-start | bytes 344072 | tf_op jit(solution)/shard_map/ppermute | solution.py:351
  109.1 4.4 %collective-permute-done.9.refs_5_ = f32[8,32,128]{2,1,0:T(8,128)S(1)} collective-permute-done((f32[8,32,128]{2,1,0:T(8,128)S(1)}, f32[8,32,128]{2,1,0:T(8,128)S(1)}, u32[]{:S(2)}, u32[]{:S(2)}) %collective-permute-start.9) | collective-permute-done | bytes 131104 | tf_op jit(solution)/shard_map/ppermute | solution.py:358
  113.6 1.7 shard_map.144
  115.2 9.5 %collective-permute-start.11 = (f32[8,32,128]{2,1,0:T(8,128)S(1)}, f32[8,32,128]{2,1,0:T(8,128)S(1)}, u32[]{:S(2)}, u32[]{:S(2)}) collective-permute-start(f32[8,32,128]{2,1,0:T(8,128)S(1)} %get-tuple-element.79.refs_3_), channel_id=1, source_target_pairs={{1,2},{2,1},{3,4},{4,3},{5,6},{6,5},{7,8},{8,7},{9,10},{10,9},{11,... | collective-permute-start | bytes 393224 | tf_op jit(solution)/shard_map/ppermute | solution.py:358
  124.7 1.9 %collective-permute-start.10 = (f32[7,32,128]{2,1,0:T(8,128)S(1)}, f32[7,32,128]{2,1,0:T(8,128)S(1)}, u32[]{:S(2)}, u32[]{:S(2)}) collective-permute-start(f32[7,32,128]{2,1,0:T(8,128)S(1)} %get-tuple-element.80), channel_id=1, source_target_pairs={{1,0},{0,1},{3,2},{2,3},{5,4},{4,5},{7,6},{6,7},{9,8},{8,9},{11,10... | collective-permute-start | bytes 344072 | tf_op jit(solution)/shard_map/ppermute | solution.py:351
  127.9 4.4 %collective-permute-done.11.refs_5_ = f32[8,32,128]{2,1,0:T(8,128)S(1)} collective-permute-done((f32[8,32,128]{2,1,0:T(8,128)S(1)}, f32[8,32,128]{2,1,0:T(8,128)S(1)}, u32[]{:S(2)}, u32[]{:S(2)}) %collective-permute-start.11) | collective-permute-done | bytes 131104 | tf_op jit(solution)/shard_map/ppermute | solution.py:358
  134.0 9.5 %collective-permute-start.13 = (f32[8,32,128]{2,1,0:T(8,128)S(1)}, f32[8,32,128]{2,1,0:T(8,128)S(1)}, u32[]{:S(2)}, u32[]{:S(2)}) collective-permute-start(f32[8,32,128]{2,1,0:T(8,128)S(1)} %get-tuple-element.82.scaled), channel_id=1, source_target_pairs={{1,2},{2,1},{3,4},{4,3},{5,6},{6,5},{7,8},{8,7},{9,10},{10,9},{11,... | collective-permute-start | bytes 393224 | tf_op jit(solution)/shard_map/ppermute | solution.py:358
  143.5 1.9 %collective-permute-start.12 = (f32[4,32,128]{2,1,0:T(8,128)S(1)}, f32[4,32,128]{2,1,0:T(8,128)S(1)}, u32[]{:S(2)}, u32[]{:S(2)}) collective-permute-start(f32[4,32,128]{2,1,0:T(8,128)S(1)} %get-tuple-element.83), channel_id=1, source_target_pairs={{1,0},{0,1},{3,2},{2,3},{5,4},{4,5},{7,6},{6,7},{9,8},{8,9},{11,10... | collective-permute-start | bytes 196616 | tf_op jit(solution)/shard_map/ppermute | solution.py:351
  146.9 4.3 %collective-permute-done.13.scaled_b = f32[8,32,128]{2,1,0:T(8,128)S(1)} collective-permute-done((f32[8,32,128]{2,1,0:T(8,128)S(1)}, f32[8,32,128]{2,1,0:T(8,128)S(1)}, u32[]{:S(2)}, u32[]{:S(2)}) %collective-permute-start.13) | collective-permute-done | bytes 131104 | tf_op jit(solution)/shard_map/ppermute | solution.py:358
  152.2 28.5 %all_to_all.10.arrived = f32[32,2,8,128]{3,2,1,0:T(8,128)S(1)} all-to-all(f32[32,2,8,128]{3,2,1,0:T(8,128)S(1)} %bitcast.50), channel_id=1, replica_groups=mesh['shot'=32,'dom'=16] {'shot'}, dimensions={0} | all-to-all | bytes 524288 | tf_op jit(solution)/shard_map/all_to_all | solution.py:483
  (46 shorter events, 19.2 us)
Async XLA Ops:
  0.6 0.7 copy-start.6
  3.0 16.2 %copy-start.7 = (f32[1,3,512]{2,0,1:T(1,128)S(1)}, f32[1,3,512]{2,0,1:T(1,128)}, u32[]{:S(2)}) copy-start(f32[1,3,512]{2,0,1:T(1,128)} %param.21) | copy-start | bytes 18436
  3.0 16.3 %copy-start.1 = (f32[1,8,32,128]{3,2,1,0:T(8,128)S(1)}, f32[1,8,32,128]{3,2,1,0:T(8,128)}, u32[]{:S(2)}) copy-start(f32[1,8,32,128]{3,2,1,0:T(8,128)} %param.12) | copy-start | bytes 393220
  3.0 16.3 %copy-start.2 = (f32[1,8,32,128]{3,2,1,0:T(8,128)S(1)}, f32[1,8,32,128]{3,2,1,0:T(8,128)}, u32[]{:S(2)}) copy-start(f32[1,8,32,128]{3,2,1,0:T(8,128)} %param.13) | copy-start | bytes 393220
  3.0 16.3 %copy-start.3 = (f32[1,8,32,128]{3,2,1,0:T(8,128)S(1)}, f32[1,8,32,128]{3,2,1,0:T(8,128)}, u32[]{:S(2)}) copy-start(f32[1,8,32,128]{3,2,1,0:T(8,128)} %param.14) | copy-start | bytes 393220
  3.0 34.2 %all-to-all-start = ((f32[32,2,8,128]{3,2,1,0:T(8,128)}), f32[32,2,8,128]{3,2,1,0:T(8,128)S(1)}, u32[]{:S(2)}, u32[]{:S(2)}) async-start(f32[32,2,8,128]{3,2,1,0:T(8,128)} %select_select_fusion), calls=%async_computation | async-start | bytes 524288 | tf_op jit(solution)/shard_map/all_to_all | solution.py:388
  18.4 0.9 copy-start
  19.3 0.7 copy-start.4
  19.3 0.7 copy-start.5
  37.9 17.9 %collective-permute-start.1 = (f32[12,32,128]{2,1,0:T(8,128)S(1)}, f32[12,32,128]{2,1,0:T(8,128)S(1)}, u32[]{:S(2)}, u32[]{:S(2)}) collective-permute-start(f32[12,32,128]{2,1,0:T(8,128)S(1)} %get-tuple-element.64), channel_id=1, source_target_pairs={{1,2},{2,1},{3,4},{4,3},{5,6},{6,5},{7,8},{8,7},{9,10},{10,9},{11,... | collective-permute-start | bytes 589832 | tf_op jit(solution)/shard_map/ppermute | solution.py:358
  47.4 3.3 %collective-permute-start = (f32[11,32,128]{2,1,0:T(8,128)S(1)}, f32[11,32,128]{2,1,0:T(8,128)S(1)}, u32[]{:S(2)}, u32[]{:S(2)}) collective-permute-start(f32[11,32,128]{2,1,0:T(8,128)S(1)} %get-tuple-element.63), channel_id=1, source_target_pairs={{1,0},{0,1},{3,2},{2,3},{5,4},{4,5},{7,6},{6,7},{9,8},{8,9},{11,10... | collective-permute-start | bytes 540680 | tf_op jit(solution)/shard_map/ppermute | solution.py:351
  57.6 18.3 %collective-permute-start.3 = (f32[8,32,128]{2,1,0:T(8,128)S(1)}, f32[8,32,128]{2,1,0:T(8,128)S(1)}, u32[]{:S(2)}, u32[]{:S(2)}) collective-permute-start(f32[8,32,128]{2,1,0:T(8,128)S(1)} %get-tuple-element.66.now.before.refs_9_), channel_id=1, source_target_pairs={{1,2},{2,1},{3,4},{4,3},{5,6},{6,5},{7,8},{8,7},{9,10},{10,9},{11,... | collective-permute-start | bytes 393224 | tf_op jit(solution)/shard_map/ppermute | solution.py:358
  67.1 8.8 %collective-permute-start.2 = (f32[7,32,128]{2,1,0:T(8,128)S(1)}, f32[7,32,128]{2,1,0:T(8,128)S(1)}, u32[]{:S(2)}, u32[]{:S(2)}) collective-permute-start(f32[7,32,128]{2,1,0:T(8,128)S(1)} %get-tuple-element.67), channel_id=1, source_target_pairs={{1,0},{0,1},{3,2},{2,3},{5,4},{4,5},{7,6},{6,7},{9,8},{8,9},{11,10... | collective-permute-start | bytes 344072 | tf_op jit(solution)/shard_map/ppermute | solution.py:351
  69.0 22.5 %collective-permute-start.7 = (f32[8,32,128]{2,1,0:T(8,128)S(1)}, f32[8,32,128]{2,1,0:T(8,128)S(1)}, u32[]{:S(2)}, u32[]{:S(2)}) collective-permute-start(f32[8,32,128]{2,1,0:T(8,128)S(1)} %get-tuple-element.73), channel_id=1, source_target_pairs={{1,2},{2,1},{3,4},{4,3},{5,6},{6,5},{7,8},{8,7},{9,10},{10,9},{11,... | collective-permute-start | bytes 393224 | tf_op jit(solution)/shard_map/ppermute | solution.py:358
  77.6 17.2 %collective-permute-start.5 = (f32[8,32,128]{2,1,0:T(8,128)S(1)}, f32[8,32,128]{2,1,0:T(8,128)S(1)}, u32[]{:S(2)}, u32[]{:S(2)}) collective-permute-start(f32[8,32,128]{2,1,0:T(8,128)S(1)} %get-tuple-element.69.now.refs_9_), channel_id=1, source_target_pairs={{1,2},{2,1},{3,4},{4,3},{5,6},{6,5},{7,8},{8,7},{9,10},{10,9},{11,... | collective-permute-start | bytes 393224 | tf_op jit(solution)/shard_map/ppermute | solution.py:358
  87.1 4.3 %collective-permute-start.6 = (f32[7,32,128]{2,1,0:T(8,128)S(1)}, f32[7,32,128]{2,1,0:T(8,128)S(1)}, u32[]{:S(2)}, u32[]{:S(2)}) collective-permute-start(f32[7,32,128]{2,1,0:T(8,128)S(1)} %get-tuple-element.72), channel_id=1, source_target_pairs={{1,0},{0,1},{3,2},{2,3},{5,4},{4,5},{7,6},{6,7},{9,8},{8,9},{11,10... | collective-permute-start | bytes 344072 | tf_op jit(solution)/shard_map/ppermute | solution.py:351
  89.0 4.1 %collective-permute-start.4 = (f32[7,32,128]{2,1,0:T(8,128)S(1)}, f32[7,32,128]{2,1,0:T(8,128)S(1)}, u32[]{:S(2)}, u32[]{:S(2)}) collective-permute-start(f32[7,32,128]{2,1,0:T(8,128)S(1)} %get-tuple-element.70), channel_id=1, source_target_pairs={{1,0},{0,1},{3,2},{2,3},{5,4},{4,5},{7,6},{6,7},{9,8},{8,9},{11,10... | collective-permute-start | bytes 344072 | tf_op jit(solution)/shard_map/ppermute | solution.py:351
  96.4 17.1 %collective-permute-start.9 = (f32[8,32,128]{2,1,0:T(8,128)S(1)}, f32[8,32,128]{2,1,0:T(8,128)S(1)}, u32[]{:S(2)}, u32[]{:S(2)}) collective-permute-start(f32[8,32,128]{2,1,0:T(8,128)S(1)} %get-tuple-element.76.refs_3_), channel_id=1, source_target_pairs={{1,2},{2,1},{3,4},{4,3},{5,6},{6,5},{7,8},{8,7},{9,10},{10,9},{11,... | collective-permute-start | bytes 393224 | tf_op jit(solution)/shard_map/ppermute | solution.py:358
  105.9 3.2 %collective-permute-start.8 = (f32[7,32,128]{2,1,0:T(8,128)S(1)}, f32[7,32,128]{2,1,0:T(8,128)S(1)}, u32[]{:S(2)}, u32[]{:S(2)}) collective-permute-start(f32[7,32,128]{2,1,0:T(8,128)S(1)} %get-tuple-element.77), channel_id=1, source_target_pairs={{1,0},{0,1},{3,2},{2,3},{5,4},{4,5},{7,6},{6,7},{9,8},{8,9},{11,10... | collective-permute-start | bytes 344072 | tf_op jit(solution)/shard_map/ppermute | solution.py:351
  115.2 17.1 %collective-permute-start.11 = (f32[8,32,128]{2,1,0:T(8,128)S(1)}, f32[8,32,128]{2,1,0:T(8,128)S(1)}, u32[]{:S(2)}, u32[]{:S(2)}) collective-permute-start(f32[8,32,128]{2,1,0:T(8,128)S(1)} %get-tuple-element.79.refs_3_), channel_id=1, source_target_pairs={{1,2},{2,1},{3,4},{4,3},{5,6},{6,5},{7,8},{8,7},{9,10},{10,9},{11,... | collective-permute-start | bytes 393224 | tf_op jit(solution)/shard_map/ppermute | solution.py:358
  124.7 3.2 %collective-permute-start.10 = (f32[7,32,128]{2,1,0:T(8,128)S(1)}, f32[7,32,128]{2,1,0:T(8,128)S(1)}, u32[]{:S(2)}, u32[]{:S(2)}) collective-permute-start(f32[7,32,128]{2,1,0:T(8,128)S(1)} %get-tuple-element.80), channel_id=1, source_target_pairs={{1,0},{0,1},{3,2},{2,3},{5,4},{4,5},{7,6},{6,7},{9,8},{8,9},{11,10... | collective-permute-start | bytes 344072 | tf_op jit(solution)/shard_map/ppermute | solution.py:351
  134.0 17.1 %collective-permute-start.13 = (f32[8,32,128]{2,1,0:T(8,128)S(1)}, f32[8,32,128]{2,1,0:T(8,128)S(1)}, u32[]{:S(2)}, u32[]{:S(2)}) collective-permute-start(f32[8,32,128]{2,1,0:T(8,128)S(1)} %get-tuple-element.82.scaled), channel_id=1, source_target_pairs={{1,2},{2,1},{3,4},{4,3},{5,6},{6,5},{7,8},{8,7},{9,10},{10,9},{11,... | collective-permute-start | bytes 393224 | tf_op jit(solution)/shard_map/ppermute | solution.py:358
  143.5 3.4 %collective-permute-start.12 = (f32[4,32,128]{2,1,0:T(8,128)S(1)}, f32[4,32,128]{2,1,0:T(8,128)S(1)}, u32[]{:S(2)}, u32[]{:S(2)}) collective-permute-start(f32[4,32,128]{2,1,0:T(8,128)S(1)} %get-tuple-element.83), channel_id=1, source_target_pairs={{1,0},{0,1},{3,2},{2,3},{5,4},{4,5},{7,6},{6,7},{9,8},{8,9},{11,10... | collective-permute-start | bytes 196616 | tf_op jit(solution)/shard_map/ppermute | solution.py:351

commit v8 on v7

--- a/solution.py
+++ b/solution.py
@@ -27,6 +27,18 @@
     return jax.ShapeDtypeStruct((count, CY, CZ), F32)
 
 
+def far_rows(count):
+    return jax.ShapeDtypeStruct((count * CY + 8, CZ), F32)
+
+
+def rows_of(planes):
+    return planes.reshape(planes.shape[0] * CY, CZ)
+
+
+def planes_at(rows, start, count):
+    return rows[start * CY : (start + count) * CY, :].reshape(count, CY, CZ)
+
+
 def lane_shift(plane, by, lane):
     if by == 0:
         return plane
@@ -52,11 +64,11 @@
     @pl.when(odd)
     def _():
         target[0:width, inner, :] = first
-        target[width + CX : 2 * width + CX, inner, :] = second[0:width]
+        target[width + CX : 2 * width + CX, inner, :] = second
 
     @pl.when(jnp.logical_not(odd))
     def _():
-        target[0:width, inner, :] = second[second.shape[0] - width :]
+        target[0:width, inner, :] = second
         target[width + CX : 2 * width + CX, inner, :] = first
 
 
@@ -72,9 +84,16 @@
         target[...] = tail()
 
 
-def hand_over(info, send_a, field):
+def hand_over(info, send_a, send_b, field):
     width = send_a.shape[0]
     for_partner(info, send_a, lambda: field[0:width], lambda: field[CX - width : CX])
+    for_partner(
+        info,
+        send_b.at[0 : width * CY],
+        lambda: rows_of(field[CX - width : CX]),
+        lambda: rows_of(field[0:width]),
+    )
+    send_b[width * CY :, :] = jnp.zeros((8, CZ), F32)
 
 
 def slope_x(field, at):
@@ -151,14 +170,18 @@
 
 def model_kernel(info, stiff, buoy, last, now, send_a, send_b, scaled):
     scaled[...] = stiff[...] * last[...]
-    send_b[4:12] = now[...]
+
+    def head():
+        return jnp.concatenate([buoy[0:4], now[0:7]], axis=0)
+
+    def tail():
+        return jnp.concatenate([buoy[4:8], now[1:8]], axis=0)
+
+    for_partner(info, send_a, head, tail)
     for_partner(
-        info,
-        send_a,
-        lambda: jnp.concatenate([buoy[0:4], now[0:7]], axis=0),
-        lambda: jnp.concatenate([buoy[4:8], now[1:8]], axis=0),
-    )
-    for_partner(info, send_b.at[0:4], lambda: buoy[4:8], lambda: buoy[0:4])
+        info, send_b.at[0 : 11 * CY], lambda: rows_of(tail()), lambda: rows_of(head())
+    )
+    send_b[11 * CY :, :] = jnp.zeros((8, CZ), F32)
 
 
 def forward(info, source, base, stiff, field, buoy, gx, gy, acc, div_out, slope_out, store):
@@ -180,21 +203,21 @@
     @pl.when(odd)
     def _():
         target[0:4] = first[0:4]
-        target[4 + CX : 8 + CX] = second[0:4]
+        target[4 + CX : 8 + CX] = planes_at(second, 0, 4)
 
     @pl.when(jnp.logical_not(odd))
     def _():
-        target[0:4] = second[0:4]
+        target[0:4] = planes_at(second, 0, 4)
         target[4 + CX : 8 + CX] = first[0:4]
 
 
 def first_kernel(
     info, now, base, source, stiff, buoy, edge_a, edge_b, scaled,
-    p_out, send_a, near, far, div_out, slope_out, buoy_out,
+    p_out, send_a, send_b, near, far, div_out, slope_out, buoy_out,
     field, gx, gy, acc,
 ):
     widen_buoy(info, buoy, edge_a, edge_b, buoy_out)
-    place(info, field, now[...], edge_a[4:11], edge_b[4:12], 7)
+    place(info, field, now[...], edge_a[4:11], planes_at(edge_b, 4, 7), 7)
 
     def store(cell, value):
         p_out[cell] = value
@@ -203,9 +226,8 @@
         info, source[0], lambda cell: base[cell],
         stiff, field, buoy_out, gx, gy, acc, div_out, slope_out, store,
     )
-    hand_over(info, send_a, p_out)
-    hand_over(info, near, scaled)
-    far[...] = scaled[...]
+    hand_over(info, send_a, send_b, p_out)
+    hand_over(info, near, far, scaled)
 
 
 def adjoint_part_kernel(
@@ -213,17 +235,17 @@
     q_out,
     field, gx, gy, acc,
 ):
-    place(info, field, scaled[...], near[...], far[...], 7)
+    place(info, field, scaled[...], near[...], planes_at(far, 0, 7), 7)
     for cell, div in operate(field, 7, buoy, gx, gy, acc, lambda *_: None):
         q_out[cell] = base[cell] + step_squared * div
 
 
 def second_kernel(
     info, now, now_a, now_b, before, source, stiff, buoy,
-    p_out, send_a, div_out, slope_out,
+    p_out, send_a, send_b, div_out, slope_out,
     field, gx, gy, acc,
 ):
-    place(info, field, now[...], now_a[...], now_b[...], 7)
+    place(info, field, now[...], now_a[...], planes_at(now_b, 0, 7), 7)
 
     def store(cell, value):
         p_out[cell] = value
@@ -232,15 +254,15 @@
         info, source[1], lambda cell: 2.0 * now[cell] - before[cell],
         stiff, field, buoy, gx, gy, acc, div_out, slope_out, store,
     )
-    hand_over(info, send_a, p_out)
+    hand_over(info, send_a, send_b, p_out)
 
 
 def third_kernel(
     info, now, now_a, now_b, before, source, stiff, buoy, q_part, spots,
-    q_out, scaled, send_a, div_out, slope_out,
+    q_out, scaled, send_a, send_b, div_out, slope_out,
     field, gx, gy, acc,
 ):
-    place(info, field, now[...], now_a[...], now_b[...], 7)
+    place(info, field, now[...], now_a[...], planes_at(now_b, 0, 7), 7)
 
     def store(cell, value):
         q = q_part[cell] + (spots[0, cell] * value - spots[3, cell])
@@ -251,15 +273,15 @@
         info, source[2], lambda cell: 2.0 * now[cell] - before[cell],
         stiff, field, buoy, gx, gy, acc, div_out, slope_out, store,
     )
-    hand_over(info, send_a, scaled)
+    hand_over(info, send_a, send_b, scaled)
 
 
 def adjoint_kernel(
     n, info, q_now, q_after, scaled, scaled_a, scaled_b, stiff, buoy, spots, p_then,
-    q_out, scaled_out, send_a, slope_out,
+    q_out, scaled_out, send_a, send_b, slope_out,
     field, gx, gy, acc,
 ):
-    place(info, field, scaled[...], scaled_a[...], scaled_b[...], 7)
+    place(info, field, scaled[...], scaled_a[...], planes_at(scaled_b, 0, 7), 7)
 
     def keep(cell, sx, sy, sz):
         slope_out[0, cell] = sx
@@ -271,7 +293,7 @@
         q = q + (spots[0, cell] * p_then[cell] - spots[n + 1, cell])
         q_out[cell] = q
         scaled_out[cell] = stiff[cell] * q
-    hand_over(info, send_a, scaled_out)
+    hand_over(info, send_a, send_b, scaled_out)
 
 
 def adjoint_first_kernel(*refs):
@@ -302,7 +324,7 @@
 
 def image_kernel(info, q_now, scaled, scaled_a, scaled_b, div, slope, images, out, field):
     lane = lax.broadcasted_iota(jnp.int32, (CY, CZ), 1)
-    place(info, field, scaled[...], scaled_a[...], scaled_b[...], 4)
+    place(info, field, scaled[...], scaled_a[...], planes_at(scaled_b, 0, 4), 4)
     for cell in range(CX):
         plane = field[cell + 4, PAD : PAD + CY, :]
         rho = images[1, cell] + slope[0, cell] * slope_x(field, cell + 4)
@@ -411,63 +433,63 @@
     images = jax.ShapeDtypeStruct((2, CX, CY, CZ), F32)
 
     send_a, send_b, f4 = call(
-        model_kernel, [info], [stiff, buoy, q4, p0], [plane_field(11), plane_field(12), own]
+        model_kernel, [info], [stiff, buoy, q4, p0], [plane_field(11), far_rows(11), own]
     )
     edge_b = swap_second(send_b)
     edge_a = swap_first(send_a)
 
-    p1, send_a, near, far, div0, slope0, wide = call(
+    p1, send_a, send_b, near, far, div0, slope0, wide = call(
         first_kernel,
         [info],
         [p0, base_p, source_planes, stiff, buoy, edge_a, edge_b, f4],
-        [own, seven, seven, own, own, slopes, plane_field(CX + 8)],
+        [own, seven, far_rows(7), seven, far_rows(7), own, slopes, plane_field(CX + 8)],
         work(),
     )
-    from_b = swap_second(p1)
+    from_b = swap_second(send_b)
     from_a = swap_first(send_a)
     far = swap_second(far)
     near = swap_first(near)
     (q_part,) = call(adjoint_part_kernel, [info], [base_q, f4, near, far, wide], [own], work())
 
-    p2, send_a, div1, slope1 = call(
+    p2, send_a, send_b, div1, slope1 = call(
         second_kernel,
         [info],
         [p1, from_a, from_b, p0, source_planes, stiff, wide],
-        [own, seven, own, slopes],
+        [own, seven, far_rows(7), own, slopes],
         work(),
     )
-    from_b = swap_second(p2)
+    from_b = swap_second(send_b)
     from_a = swap_first(send_a)
 
-    q3, f3, send_a, div2, slope2 = call(
+    q3, f3, send_a, send_b, div2, slope2 = call(
         third_kernel,
         [info],
         [p2, from_a, from_b, p1, source_planes, stiff, wide, q_part, spots],
-        [own, own, seven, own, slopes],
+        [own, own, seven, far_rows(7), own, slopes],
         work(),
     )
-    from_b = swap_second(f3)
+    from_b = swap_second(send_b)
     from_a = swap_first(send_a)
 
-    q2, f2, send_a, slope_q = call(
+    q2, f2, send_a, send_b, slope_q = call(
         adjoint_first_kernel,
         [info],
         [q3, q4, f3, from_a, from_b, stiff, wide, spots, p2],
-        [own, own, seven, slopes],
+        [own, own, seven, far_rows(7), slopes],
         work(),
     )
-    from_b = swap_second(f2)
+    from_b = swap_second(send_b)
     from_a = swap_first(send_a)
     image, q2_out = call(image_first_kernel, [], [q3, slope_q, div2, slope2, q2], [images, own])
 
-    q1, f1, send_a, slope_q = call(
+    q1, f1, send_a, send_b, slope_q = call(
         adjoint_second_kernel,
         [info],
         [q2, q3, f2, from_a, from_b, stiff, wide, spots, p1],
-        [own, own, four, slopes],
+        [own, own, four, far_rows(4), slopes],
         work(),
     )
-    from_b = swap_second(f1)
+    from_b = swap_second(send_b)
     from_a = swap_first(send_a)
     image, q1_out = call(
         image_second_kernel, [], [q2, slope_q, div1, slope1, image, q1], [images, own]

time: 182 us -> 182 us (level)
  no operation moved by 1% of the time
where the time goes in v8:
time: 182 us; the launch traced here: 181 us
  starting transfers between devices  93.4 us (51%)
  waiting for transfers between devices  38 us (21%)
  blocking collectives  29 us (16%)
  Pallas kernels  15.3 us (8%)
  other arithmetic  2.31 us (1%)
    ppermute x7, starting transfers between devices, swap_second(): return lax.ppermute(planes, 'dom', pairs)  64.1 us
    all_to_all x1, blocking collectives, shards(): lax.all_to_all(image.transpose(2, 0, 1, 3), 'shot', 0, 0, tiled=True)  29 us
    ppermute x7, waiting for transfers between devices, swap_second(): return lax.ppermute(planes, 'dom', pairs)  18.3 us
    all_to_all x1, waiting for transfers between devices, shards(): block = lax.all_to_all(chosen, 'shot', 0, 0, tiled=True)  15.7 us
    all_to_all x1, starting transfers between devices, shards(): block = lax.all_to_all(chosen, 'shot', 0, 0, tiled=True)  15.4 us
    pallas_call x12, Pallas kernels, call(): pl.pallas_call(kernel, out_shape=outs, in_specs=[SMEM] * len(scalars) + [...  15.3 us
    ppermute x7, starting transfers between devices, swap_first(): return lax.ppermute(planes, 'dom', [(i ^ 1, i) for i in range(count)])  13.9 us
    ppermute x7, waiting for transfers between devices, swap_first(): return lax.ppermute(planes, 'dom', [(i ^ 1, i) for i in range(count)])  3.97 us
  transfers between devices with their start and end apart: 15, of which 9 were waited for; matrix products, arithmetic and copies ran while one was open for 0% of the time, Pallas kernels for 3%

profile of v8, /device:TPU:7, one launch (start us, length us, event | category | flops | bytes accessed | tf_op | source)
XLA Modules:
  0.0 180.9 jit_solution(2329273569361743447)
XLA Ops:
  3.0 15.4 %all-to-all-start = ((f32[32,2,8,128]{3,2,1,0:T(8,128)}), f32[32,2,8,128]{3,2,1,0:T(8,128)S(1)}, u32[]{:S(2)}, u32[]{:S(2)}) async-start(f32[32,2,8,128]{3,2,1,0:T(8,128)} %select_select_fusion), calls=%async_computation | async-start | bytes 524288 | tf_op jit(solution)/shard_map/all_to_all | solution.py:410
  21.4 15.7 %all-to-all-done = f32[32,2,8,128]{3,2,1,0:T(8,128)S(1)} async-done(((f32[32,2,8,128]{3,2,1,0:T(8,128)}), f32[32,2,8,128]{3,2,1,0:T(8,128)S(1)}, u32[]{:S(2)}, u32[]{:S(2)}) %all-to-all-start) | async-done | bytes 262176 | tf_op jit(solution)/shard_map/all_to_all | solution.py:410
  37.9 9.5 %collective-permute-start.1 = (f32[360,128]{1,0:T(8,128)S(1)}, f32[360,128]{1,0:T(8,128)S(1)}, u32[]{:S(2)}, u32[]{:S(2)}) collective-permute-start(f32[360,128]{1,0:T(8,128)S(1)} %get-tuple-element.69), channel_id=1, source_target_pairs={{1,2},{2,1},{3,4},{4,3},{5,6},{6,5},{7,8},{8,7},{9,10},{10,9},{11,... | collective-permute-start | bytes 552968 | tf_op jit(solution)/shard_map/ppermute | solution.py:380
  47.4 1.9 %collective-permute-start = (f32[11,32,128]{2,1,0:T(8,128)S(1)}, f32[11,32,128]{2,1,0:T(8,128)S(1)}, u32[]{:S(2)}, u32[]{:S(2)}) collective-permute-start(f32[11,32,128]{2,1,0:T(8,128)S(1)} %get-tuple-element.68), channel_id=1, source_target_pairs={{1,0},{0,1},{3,2},{2,3},{5,4},{4,5},{7,6},{6,7},{9,8},{8,9},{11,10... | collective-permute-start | bytes 540680 | tf_op jit(solution)/shard_map/ppermute | solution.py:373
  50.7 4.9 %collective-permute-done.1.edge_b = f32[360,128]{1,0:T(8,128)S(1)} collective-permute-done((f32[360,128]{1,0:T(8,128)S(1)}, f32[360,128]{1,0:T(8,128)S(1)}, u32[]{:S(2)}, u32[]{:S(2)}) %collective-permute-start.1) | collective-permute-done | bytes 184352 | tf_op jit(solution)/shard_map/ppermute | solution.py:380
  55.6 1.7 shard_map.140
  57.4 9.6 %collective-permute-start.3 = (f32[232,128]{1,0:T(8,128)S(1)}, f32[232,128]{1,0:T(8,128)S(1)}, u32[]{:S(2)}, u32[]{:S(2)}) collective-permute-start(f32[232,128]{1,0:T(8,128)S(1)} %get-tuple-element.73), channel_id=1, source_target_pairs={{1,2},{2,1},{3,4},{4,3},{5,6},{6,5},{7,8},{8,7},{9,10},{10,9},{11,... | collective-permute-start | bytes 356360 | tf_op jit(solution)/shard_map/ppermute | solution.py:380
  67.0 1.9 %collective-permute-start.2 = (f32[7,32,128]{2,1,0:T(8,128)S(1)}, f32[7,32,128]{2,1,0:T(8,128)S(1)}, u32[]{:S(2)}, u32[]{:S(2)}) collective-permute-start(f32[7,32,128]{2,1,0:T(8,128)S(1)} %get-tuple-element.72), channel_id=1, source_target_pairs={{1,0},{0,1},{3,2},{2,3},{5,4},{4,5},{7,6},{6,7},{9,8},{8,9},{11,10... | collective-permute-start | bytes 344072 | tf_op jit(solution)/shard_map/ppermute | solution.py:373
  68.9 6.8 %collective-permute-start.7 = (f32[232,128]{1,0:T(8,128)S(1)}, f32[232,128]{1,0:T(8,128)S(1)}, u32[]{:S(2)}, u32[]{:S(2)}) collective-permute-start(f32[232,128]{1,0:T(8,128)S(1)} %get-tuple-element.80), channel_id=1, source_target_pairs={{1,2},{2,1},{3,4},{4,3},{5,6},{6,5},{7,8},{8,7},{9,10},{10,9},{11,... | collective-permute-start | bytes 356360 | tf_op jit(solution)/shard_map/ppermute | solution.py:380
  77.4 9.6 %collective-permute-start.5 = (f32[232,128]{1,0:T(8,128)S(1)}, f32[232,128]{1,0:T(8,128)S(1)}, u32[]{:S(2)}, u32[]{:S(2)}) collective-permute-start(f32[232,128]{1,0:T(8,128)S(1)} %get-tuple-element.77), channel_id=1, source_target_pairs={{1,2},{2,1},{3,4},{4,3},{5,6},{6,5},{7,8},{8,7},{9,10},{10,9},{11,... | collective-permute-start | bytes 356360 | tf_op jit(solution)/shard_map/ppermute | solution.py:380
  87.0 1.9 %collective-permute-start.6 = (f32[7,32,128]{2,1,0:T(8,128)S(1)}, f32[7,32,128]{2,1,0:T(8,128)S(1)}, u32[]{:S(2)}, u32[]{:S(2)}) collective-permute-start(f32[7,32,128]{2,1,0:T(8,128)S(1)} %get-tuple-element.79), channel_id=1, source_target_pairs={{1,0},{0,1},{3,2},{2,3},{5,4},{4,5},{7,6},{6,7},{9,8},{8,9},{11,10... | collective-permute-start | bytes 344072 | tf_op jit(solution)/shard_map/ppermute | solution.py:373
  88.9 2.4 %collective-permute-start.4 = (f32[7,32,128]{2,1,0:T(8,128)S(1)}, f32[7,32,128]{2,1,0:T(8,128)S(1)}, u32[]{:S(2)}, u32[]{:S(2)}) collective-permute-start(f32[7,32,128]{2,1,0:T(8,128)S(1)} %get-tuple-element.76), channel_id=1, source_target_pairs={{1,0},{0,1},{3,2},{2,3},{5,4},{4,5},{7,6},{6,7},{9,8},{8,9},{11,10... | collective-permute-start | bytes 344072 | tf_op jit(solution)/shard_map/ppermute | solution.py:373
  96.1 9.7 %collective-permute-start.9 = (f32[232,128]{1,0:T(8,128)S(1)}, f32[232,128]{1,0:T(8,128)S(1)}, u32[]{:S(2)}, u32[]{:S(2)}) collective-permute-start(f32[232,128]{1,0:T(8,128)S(1)} %get-tuple-element.85), channel_id=1, source_target_pairs={{1,2},{2,1},{3,4},{4,3},{5,6},{6,5},{7,8},{8,7},{9,10},{10,9},{11,... | collective-permute-start | bytes 356360 | tf_op jit(solution)/shard_map/ppermute | solution.py:380
  105.7 1.9 %collective-permute-start.8 = (f32[7,32,128]{2,1,0:T(8,128)S(1)}, f32[7,32,128]{2,1,0:T(8,128)S(1)}, u32[]{:S(2)}, u32[]{:S(2)}) collective-permute-start(f32[7,32,128]{2,1,0:T(8,128)S(1)} %get-tuple-element.84), channel_id=1, source_target_pairs={{1,0},{0,1},{3,2},{2,3},{5,4},{4,5},{7,6},{6,7},{9,8},{8,9},{11,10... | collective-permute-start | bytes 344072 | tf_op jit(solution)/shard_map/ppermute | solution.py:373
  108.9 4.2 %collective-permute-done.9.refs_5_ = f32[232,128]{1,0:T(8,128)S(1)} collective-permute-done((f32[232,128]{1,0:T(8,128)S(1)}, f32[232,128]{1,0:T(8,128)S(1)}, u32[]{:S(2)}, u32[]{:S(2)}) %collective-permute-start.9) | collective-permute-done | bytes 118816 | tf_op jit(solution)/shard_map/ppermute | solution.py:380
  113.2 1.7 shard_map.144
  114.9 9.5 %collective-permute-start.11 = (f32[232,128]{1,0:T(8,128)S(1)}, f32[232,128]{1,0:T(8,128)S(1)}, u32[]{:S(2)}, u32[]{:S(2)}) collective-permute-start(f32[232,128]{1,0:T(8,128)S(1)} %get-tuple-element.89), channel_id=1, source_target_pairs={{1,2},{2,1},{3,4},{4,3},{5,6},{6,5},{7,8},{8,7},{9,10},{10,9},{11,... | collective-permute-start | bytes 356360 | tf_op jit(solution)/shard_map/ppermute | solution.py:380
  124.4 1.9 %collective-permute-start.10 = (f32[7,32,128]{2,1,0:T(8,128)S(1)}, f32[7,32,128]{2,1,0:T(8,128)S(1)}, u32[]{:S(2)}, u32[]{:S(2)}) collective-permute-start(f32[7,32,128]{2,1,0:T(8,128)S(1)} %get-tuple-element.88), channel_id=1, source_target_pairs={{1,0},{0,1},{3,2},{2,3},{5,4},{4,5},{7,6},{6,7},{9,8},{8,9},{11,10... | collective-permute-start | bytes 344072 | tf_op jit(solution)/shard_map/ppermute | solution.py:373
  127.6 4.3 %collective-permute-done.11.refs_5_ = f32[232,128]{1,0:T(8,128)S(1)} collective-permute-done((f32[232,128]{1,0:T(8,128)S(1)}, f32[232,128]{1,0:T(8,128)S(1)}, u32[]{:S(2)}, u32[]{:S(2)}) %collective-permute-start.11) | collective-permute-done | bytes 118816 | tf_op jit(solution)/shard_map/ppermute | solution.py:380
  131.9 1.7 shard_map.145
  133.6 9.5 %collective-permute-start.13 = (f32[136,128]{1,0:T(8,128)S(1)}, f32[136,128]{1,0:T(8,128)S(1)}, u32[]{:S(2)}, u32[]{:S(2)}) collective-permute-start(f32[136,128]{1,0:T(8,128)S(1)} %get-tuple-element.93), channel_id=1, source_target_pairs={{1,2},{2,1},{3,4},{4,3},{5,6},{6,5},{7,8},{8,7},{9,10},{10,9},{11,... | collective-permute-start | bytes 208904 | tf_op jit(solution)/shard_map/ppermute | solution.py:380
  143.1 1.9 %collective-permute-start.12 = (f32[4,32,128]{2,1,0:T(8,128)S(1)}, f32[4,32,128]{2,1,0:T(8,128)S(1)}, u32[]{:S(2)}, u32[]{:S(2)}) collective-permute-start(f32[4,32,128]{2,1,0:T(8,128)S(1)} %get-tuple-element.92), channel_id=1, source_target_pairs={{1,0},{0,1},{3,2},{2,3},{5,4},{4,5},{7,6},{6,7},{9,8},{8,9},{11,10... | collective-permute-start | bytes 196616 | tf_op jit(solution)/shard_map/ppermute | solution.py:373
  146.5 3.5 %collective-permute-done.13.scaled_b = f32[136,128]{1,0:T(8,128)S(1)} collective-permute-done((f32[136,128]{1,0:T(8,128)S(1)}, f32[136,128]{1,0:T(8,128)S(1)}, u32[]{:S(2)}, u32[]{:S(2)}) %collective-permute-start.13) | collective-permute-done | bytes 69664 | tf_op jit(solution)/shard_map/ppermute | solution.py:380
  151.1 29.0 %all_to_all.10.arrived = f32[32,2,8,128]{3,2,1,0:T(8,128)S(1)} all-to-all(f32[32,2,8,128]{3,2,1,0:T(8,128)S(1)} %bitcast.50), channel_id=1, replica_groups=mesh['shot'=32,'dom'=16] {'shot'}, dimensions={0} | all-to-all | bytes 524288 | tf_op jit(solution)/shard_map/all_to_all | solution.py:505
  (46 shorter events, 19.0 us)
Async XLA Ops:
  0.6 0.7 copy-start.6
  3.0 16.2 %copy-start.7 = (f32[1,3,512]{2,0,1:T(1,128)S(1)}, f32[1,3,512]{2,0,1:T(1,128)}, u32[]{:S(2)}) copy-start(f32[1,3,512]{2,0,1:T(1,128)} %param.21) | copy-start | bytes 18436
  3.0 16.3 %copy-start.1 = (f32[1,8,32,128]{3,2,1,0:T(8,128)S(1)}, f32[1,8,32,128]{3,2,1,0:T(8,128)}, u32[]{:S(2)}) copy-start(f32[1,8,32,128]{3,2,1,0:T(8,128)} %param.12) | copy-start | bytes 393220
  3.0 16.3 %copy-start.2 = (f32[1,8,32,128]{3,2,1,0:T(8,128)S(1)}, f32[1,8,32,128]{3,2,1,0:T(8,128)}, u32[]{:S(2)}) copy-start(f32[1,8,32,128]{3,2,1,0:T(8,128)} %param.13) | copy-start | bytes 393220
  3.0 16.3 %copy-start.3 = (f32[1,8,32,128]{3,2,1,0:T(8,128)S(1)}, f32[1,8,32,128]{3,2,1,0:T(8,128)}, u32[]{:S(2)}) copy-start(f32[1,8,32,128]{3,2,1,0:T(8,128)} %param.14) | copy-start | bytes 393220
  3.0 34.2 %all-to-all-start = ((f32[32,2,8,128]{3,2,1,0:T(8,128)}), f32[32,2,8,128]{3,2,1,0:T(8,128)S(1)}, u32[]{:S(2)}, u32[]{:S(2)}) async-start(f32[32,2,8,128]{3,2,1,0:T(8,128)} %select_select_fusion), calls=%async_computation | async-start | bytes 524288 | tf_op jit(solution)/shard_map/all_to_all | solution.py:410
  18.4 0.9 copy-start
  19.3 0.7 copy-start.4
  19.3 0.7 copy-start.5
  37.9 17.7 %collective-permute-start.1 = (f32[360,128]{1,0:T(8,128)S(1)}, f32[360,128]{1,0:T(8,128)S(1)}, u32[]{:S(2)}, u32[]{:S(2)}) collective-permute-start(f32[360,128]{1,0:T(8,128)S(1)} %get-tuple-element.69), channel_id=1, source_target_pairs={{1,2},{2,1},{3,4},{4,3},{5,6},{6,5},{7,8},{8,7},{9,10},{10,9},{11,... | collective-permute-start | bytes 552968 | tf_op jit(solution)/shard_map/ppermute | solution.py:380
  47.4 3.3 %collective-permute-start = (f32[11,32,128]{2,1,0:T(8,128)S(1)}, f32[11,32,128]{2,1,0:T(8,128)S(1)}, u32[]{:S(2)}, u32[]{:S(2)}) collective-permute-start(f32[11,32,128]{2,1,0:T(8,128)S(1)} %get-tuple-element.68), channel_id=1, source_target_pairs={{1,0},{0,1},{3,2},{2,3},{5,4},{4,5},{7,6},{6,7},{9,8},{8,9},{11,10... | collective-permute-start | bytes 540680 | tf_op jit(solution)/shard_map/ppermute | solution.py:373
  57.4 18.3 %collective-permute-start.3 = (f32[232,128]{1,0:T(8,128)S(1)}, f32[232,128]{1,0:T(8,128)S(1)}, u32[]{:S(2)}, u32[]{:S(2)}) collective-permute-start(f32[232,128]{1,0:T(8,128)S(1)} %get-tuple-element.73), channel_id=1, source_target_pairs={{1,2},{2,1},{3,4},{4,3},{5,6},{6,5},{7,8},{8,7},{9,10},{10,9},{11,... | collective-permute-start | bytes 356360 | tf_op jit(solution)/shard_map/ppermute | solution.py:380
  67.0 8.7 %collective-permute-start.2 = (f32[7,32,128]{2,1,0:T(8,128)S(1)}, f32[7,32,128]{2,1,0:T(8,128)S(1)}, u32[]{:S(2)}, u32[]{:S(2)}) collective-permute-start(f32[7,32,128]{2,1,0:T(8,128)S(1)} %get-tuple-element.72), channel_id=1, source_target_pairs={{1,0},{0,1},{3,2},{2,3},{5,4},{4,5},{7,6},{6,7},{9,8},{8,9},{11,10... | collective-permute-start | bytes 344072 | tf_op jit(solution)/shard_map/ppermute | solution.py:373
  68.9 22.5 %collective-permute-start.7 = (f32[232,128]{1,0:T(8,128)S(1)}, f32[232,128]{1,0:T(8,128)S(1)}, u32[]{:S(2)}, u32[]{:S(2)}) collective-permute-start(f32[232,128]{1,0:T(8,128)S(1)} %get-tuple-element.80), channel_id=1, source_target_pairs={{1,2},{2,1},{3,4},{4,3},{5,6},{6,5},{7,8},{8,7},{9,10},{10,9},{11,... | collective-permute-start | bytes 356360 | tf_op jit(solution)/shard_map/ppermute | solution.py:380
  77.4 17.0 %collective-permute-start.5 = (f32[232,128]{1,0:T(8,128)S(1)}, f32[232,128]{1,0:T(8,128)S(1)}, u32[]{:S(2)}, u32[]{:S(2)}) collective-permute-start(f32[232,128]{1,0:T(8,128)S(1)} %get-tuple-element.77), channel_id=1, source_target_pairs={{1,2},{2,1},{3,4},{4,3},{5,6},{6,5},{7,8},{8,7},{9,10},{10,9},{11,... | collective-permute-start | bytes 356360 | tf_op jit(solution)/shard_map/ppermute | solution.py:380
  87.0 4.3 %collective-permute-start.6 = (f32[7,32,128]{2,1,0:T(8,128)S(1)}, f32[7,32,128]{2,1,0:T(8,128)S(1)}, u32[]{:S(2)}, u32[]{:S(2)}) collective-permute-start(f32[7,32,128]{2,1,0:T(8,128)S(1)} %get-tuple-element.79), channel_id=1, source_target_pairs={{1,0},{0,1},{3,2},{2,3},{5,4},{4,5},{7,6},{6,7},{9,8},{8,9},{11,10... | collective-permute-start | bytes 344072 | tf_op jit(solution)/shard_map/ppermute | solution.py:373
  88.9 4.1 %collective-permute-start.4 = (f32[7,32,128]{2,1,0:T(8,128)S(1)}, f32[7,32,128]{2,1,0:T(8,128)S(1)}, u32[]{:S(2)}, u32[]{:S(2)}) collective-permute-start(f32[7,32,128]{2,1,0:T(8,128)S(1)} %get-tuple-element.76), channel_id=1, source_target_pairs={{1,0},{0,1},{3,2},{2,3},{5,4},{4,5},{7,6},{6,7},{9,8},{8,9},{11,10... | collective-permute-start | bytes 344072 | tf_op jit(solution)/shard_map/ppermute | solution.py:373
  96.1 17.1 %collective-permute-start.9 = (f32[232,128]{1,0:T(8,128)S(1)}, f32[232,128]{1,0:T(8,128)S(1)}, u32[]{:S(2)}, u32[]{:S(2)}) collective-permute-start(f32[232,128]{1,0:T(8,128)S(1)} %get-tuple-element.85), channel_id=1, source_target_pairs={{1,2},{2,1},{3,4},{4,3},{5,6},{6,5},{7,8},{8,7},{9,10},{10,9},{11,... | collective-permute-start | bytes 356360 | tf_op jit(solution)/shard_map/ppermute | solution.py:380
  105.7 3.2 %collective-permute-start.8 = (f32[7,32,128]{2,1,0:T(8,128)S(1)}, f32[7,32,128]{2,1,0:T(8,128)S(1)}, u32[]{:S(2)}, u32[]{:S(2)}) collective-permute-start(f32[7,32,128]{2,1,0:T(8,128)S(1)} %get-tuple-element.84), channel_id=1, source_target_pairs={{1,0},{0,1},{3,2},{2,3},{5,4},{4,5},{7,6},{6,7},{9,8},{8,9},{11,10... | collective-permute-start | bytes 344072 | tf_op jit(solution)/shard_map/ppermute | solution.py:373
  114.9 17.0 %collective-permute-start.11 = (f32[232,128]{1,0:T(8,128)S(1)}, f32[232,128]{1,0:T(8,128)S(1)}, u32[]{:S(2)}, u32[]{:S(2)}) collective-permute-start(f32[232,128]{1,0:T(8,128)S(1)} %get-tuple-element.89), channel_id=1, source_target_pairs={{1,2},{2,1},{3,4},{4,3},{5,6},{6,5},{7,8},{8,7},{9,10},{10,9},{11,... | collective-permute-start | bytes 356360 | tf_op jit(solution)/shard_map/ppermute | solution.py:380
  124.4 3.2 %collective-permute-start.10 = (f32[7,32,128]{2,1,0:T(8,128)S(1)}, f32[7,32,128]{2,1,0:T(8,128)S(1)}, u32[]{:S(2)}, u32[]{:S(2)}) collective-permute-start(f32[7,32,128]{2,1,0:T(8,128)S(1)} %get-tuple-element.88), channel_id=1, source_target_pairs={{1,0},{0,1},{3,2},{2,3},{5,4},{4,5},{7,6},{6,7},{9,8},{8,9},{11,10... | collective-permute-start | bytes 344072 | tf_op jit(solution)/shard_map/ppermute | solution.py:373
  133.6 16.5 %collective-permute-start.13 = (f32[136,128]{1,0:T(8,128)S(1)}, f32[136,128]{1,0:T(8,128)S(1)}, u32[]{:S(2)}, u32[]{:S(2)}) collective-permute-start(f32[136,128]{1,0:T(8,128)S(1)} %get-tuple-element.93), channel_id=1, source_target_pairs={{1,2},{2,1},{3,4},{4,3},{5,6},{6,5},{7,8},{8,7},{9,10},{10,9},{11,... | collective-permute-start | bytes 208904 | tf_op jit(solution)/shard_map/ppermute | solution.py:380
  143.1 3.4 %collective-permute-start.12 = (f32[4,32,128]{2,1,0:T(8,128)S(1)}, f32[4,32,128]{2,1,0:T(8,128)S(1)}, u32[]{:S(2)}, u32[]{:S(2)}) collective-permute-start(f32[4,32,128]{2,1,0:T(8,128)S(1)} %get-tuple-element.92), channel_id=1, source_target_pairs={{1,0},{0,1},{3,2},{2,3},{5,4},{4,5},{7,6},{6,7},{9,8},{8,9},{11,10... | collective-permute-start | bytes 196616 | tf_op jit(solution)/shard_map/ppermute | solution.py:373

commit v9 on v8

--- a/solution.py
+++ b/solution.py
@@ -168,20 +168,20 @@
         out[n + 1] = total.reshape(CX, CY, CZ)
 
 
-def model_kernel(info, stiff, buoy, last, now, send_a, send_b, scaled):
+def model_kernel(info, stiff, buoy, last, send_a, send_b, scaled):
     scaled[...] = stiff[...] * last[...]
-
-    def head():
-        return jnp.concatenate([buoy[0:4], now[0:7]], axis=0)
-
-    def tail():
-        return jnp.concatenate([buoy[4:8], now[1:8]], axis=0)
-
-    for_partner(info, send_a, head, tail)
+    for_partner(info, send_a, lambda: buoy[0:4], lambda: buoy[4:8])
     for_partner(
-        info, send_b.at[0 : 11 * CY], lambda: rows_of(tail()), lambda: rows_of(head())
-    )
-    send_b[11 * CY :, :] = jnp.zeros((8, CZ), F32)
+        info,
+        send_b.at[0 : 4 * CY],
+        lambda: rows_of(buoy[4:8]),
+        lambda: rows_of(buoy[0:4]),
+    )
+    send_b[4 * CY :, :] = jnp.zeros((8, CZ), F32)
+
+
+def widen_kernel(info, now, now_a, now_b, out):
+    place(info, out, now[...], now_a[...], now_b[...], 7)
 
 
 def forward(info, source, base, stiff, field, buoy, gx, gy, acc, div_out, slope_out, store):
@@ -212,19 +212,18 @@
 
 
 def first_kernel(
-    info, now, base, source, stiff, buoy, edge_a, edge_b, scaled,
+    info, padded, base, source, stiff, buoy, edge_a, edge_b, scaled,
     p_out, send_a, send_b, near, far, div_out, slope_out, buoy_out,
-    field, gx, gy, acc,
+    gx, gy, acc,
 ):
     widen_buoy(info, buoy, edge_a, edge_b, buoy_out)
-    place(info, field, now[...], edge_a[4:11], planes_at(edge_b, 4, 7), 7)
 
     def store(cell, value):
         p_out[cell] = value
 
     forward(
         info, source[0], lambda cell: base[cell],
-        stiff, field, buoy_out, gx, gy, acc, div_out, slope_out, store,
+        stiff, padded, buoy_out, gx, gy, acc, div_out, slope_out, store,
     )
     hand_over(info, send_a, send_b, p_out)
     hand_over(info, near, far, scaled)
@@ -411,6 +410,8 @@
 
     p0, p_prev = pressure_now[0], pressure_prev[0]
     q4, q5 = adjoint_last[0], adjoint_after[0]
+    p0_b = swap_second(jnp.where(odd == 1, pressure_now[0][1:8], pressure_now[0][0:7]))
+    p0_a = swap_first(jnp.where(odd == 1, pressure_now[0][0:7], pressure_now[0][1:8]))
     own, seven, four = plane_field(CX), plane_field(7), plane_field(4)
     spots, base_p, base_q, p0, q4, source_planes = call(
         prepare_kernel,
@@ -433,17 +434,23 @@
     images = jax.ShapeDtypeStruct((2, CX, CY, CZ), F32)
 
     send_a, send_b, f4 = call(
-        model_kernel, [info], [stiff, buoy, q4, p0], [plane_field(11), far_rows(11), own]
+        model_kernel, [info], [stiff, buoy, q4], [four, far_rows(4), own]
     )
     edge_b = swap_second(send_b)
     edge_a = swap_first(send_a)
 
+    (padded,) = call(
+        widen_kernel,
+        [info],
+        [p0, p0_a, p0_b],
+        [jax.ShapeDtypeStruct((WIDE, ROWS, CZ), F32)],
+    )
     p1, send_a, send_b, near, far, div0, slope0, wide = call(
         first_kernel,
         [info],
-        [p0, base_p, source_planes, stiff, buoy, edge_a, edge_b, f4],
+        [padded, base_p, source_planes, stiff, buoy, edge_a, edge_b, f4],
         [own, seven, far_rows(7), seven, far_rows(7), own, slopes, plane_field(CX + 8)],
-        work(),
+        work()[1:],
     )
     from_b = swap_second(send_b)
     from_a = swap_first(send_a)

time: 182 us -> 177 us (0.973)
  waiting for transfers between devices: 38 us -> 25.6 us
  starting transfers between devices: 93.4 us -> 104 us
  blocking collectives: 29 us -> 26.1 us
    all_to_all x1, waiting for transfers between devices: 15.7 us -> 4.95 us  [shards(): block = lax.all_to_all(chosen, 'shot', 0, 0, tiled=True)]
    ppermute x7 -> x8, starting transfers between devices: 64.1 us -> 72.6 us  [swap_second(): return lax.ppermute(planes, 'dom', pairs)]
    all_to_all x1, blocking collectives: 29 us -> 26.1 us  [shards(): lax.all_to_all(image.transpose(2, 0, 1, 3), 'shot', 0, 0, tiled=True)]
    ppermute x7 -> x8, starting transfers between devices: 13.9 us -> 15.8 us  [swap_first(): return lax.ppermute(planes, 'dom', [(i ^ 1, i) for i in range(count)])]
    ppermute x7 -> x8, waiting for transfers between devices: 18.3 us -> 17.4 us  [swap_second(): return lax.ppermute(planes, 'dom', pairs)]
    ppermute x7 -> x8, waiting for transfers between devices: 3.97 us -> 3.2 us  [swap_first(): return lax.ppermute(planes, 'dom', [(i ^ 1, i) for i in range(count)])]
    pallas_call x12 -> x13, Pallas kernels: 15.3 us -> 15.8 us  [call(): pl.pallas_call(kernel, out_shape=outs, in_specs=[SMEM] * len(scalars) + [...]
  transfers between devices with their start and end apart: 15 -> 17, of which waited for: 9 -> 9; matrix products, arithmetic and copies ran while one was open for 0% -> 0% of each run, Pallas kernels for 3% -> 4%
where the time goes in v9:
time: 177 us
  starting transfers between devices  104 us (59%)
  blocking collectives  26.1 us (15%)
  waiting for transfers between devices  25.6 us (14%)
  Pallas kernels  15.8 us (9%)
  other arithmetic  2.35 us (1%)
    ppermute x8, starting transfers between devices, swap_second(): return lax.ppermute(planes, 'dom', pairs)  72.6 us
    all_to_all x1, blocking collectives, shards(): lax.all_to_all(image.transpose(2, 0, 1, 3), 'shot', 0, 0, tiled=True)  26.1 us
    ppermute x8, waiting for transfers between devices, swap_second(): return lax.ppermute(planes, 'dom', pairs)  17.4 us
    ppermute x8, starting transfers between devices, swap_first(): return lax.ppermute(planes, 'dom', [(i ^ 1, i) for i in range(count)])  15.8 us
    pallas_call x13, Pallas kernels, call(): pl.pallas_call(kernel, out_shape=outs, in_specs=[SMEM] * len(scalars) + [...  15.8 us
    all_to_all x1, starting transfers between devices, shards(): block = lax.all_to_all(chosen, 'shot', 0, 0, tiled=True)  15.4 us
    all_to_all x1, waiting for transfers between devices, shards(): block = lax.all_to_all(chosen, 'shot', 0, 0, tiled=True)  4.95 us
  transfers between devices with their start and end apart: 17, of which 9 were waited for; matrix products, arithmetic and copies ran while one was open for 0% of the time, Pallas kernels for 4%

profile of v9, /device:TPU:7, one launch (start us, length us, event | category | flops | bytes accessed | tf_op | source)
XLA Modules:
  0.0 176.6 jit_solution(13028079410896732844)
XLA Ops:
  3.0 15.4 %all-to-all-start = ((f32[32,2,8,128]{3,2,1,0:T(8,128)}), f32[32,2,8,128]{3,2,1,0:T(8,128)S(1)}, u32[]{:S(2)}, u32[]{:S(2)}) async-start(f32[32,2,8,128]{3,2,1,0:T(8,128)} %select_select_fusion), calls=%async_computation | async-start | bytes 524288 | tf_op jit(solution)/shard_map/all_to_all | solution.py:409
  18.5 8.8 %collective-permute-start.1 = (f32[7,32,128]{2,1,0:T(8,128)S(1)}, f32[7,32,128]{2,1,0:T(8,128)S(1)}, u32[]{:S(2)}, u32[]{:S(2)}) collective-permute-start(f32[7,32,128]{2,1,0:T(8,128)S(1)} %get-tuple-element.112), channel_id=1, source_target_pairs={{1,2},{2,1},{3,4},{4,3},{5,6},{6,5},{7,8},{8,7},{9,10},{10,9},{11,... | collective-permute-start | bytes 344072 | tf_op jit(solution)/shard_map/ppermute | solution.py:379
  27.3 1.9 %collective-permute-start = (f32[7,32,128]{2,1,0:T(8,128)S(1)}, f32[7,32,128]{2,1,0:T(8,128)S(1)}, u32[]{:S(2)}, u32[]{:S(2)}) collective-permute-start(f32[7,32,128]{2,1,0:T(8,128)S(1)} %get-tuple-element.113), channel_id=1, source_target_pairs={{1,0},{0,1},{3,2},{2,3},{5,4},{4,5},{7,6},{6,7},{9,8},{8,9},{11,10... | collective-permute-start | bytes 344072 | tf_op jit(solution)/shard_map/ppermute | solution.py:372
  32.2 5.0 %all-to-all-done = f32[32,2,8,128]{3,2,1,0:T(8,128)S(1)} async-done(((f32[32,2,8,128]{3,2,1,0:T(8,128)}), f32[32,2,8,128]{3,2,1,0:T(8,128)S(1)}, u32[]{:S(2)}, u32[]{:S(2)}) %all-to-all-start) | async-done | bytes 262176 | tf_op jit(solution)/shard_map/all_to_all | solution.py:409
  37.9 9.5 %collective-permute-start.3 = (f32[136,128]{1,0:T(8,128)S(1)}, f32[136,128]{1,0:T(8,128)S(1)}, u32[]{:S(2)}, u32[]{:S(2)}) collective-permute-start(f32[136,128]{1,0:T(8,128)S(1)} %get-tuple-element.69), channel_id=1, source_target_pairs={{1,2},{2,1},{3,4},{4,3},{5,6},{6,5},{7,8},{8,7},{9,10},{10,9},{11,... | collective-permute-start | bytes 208904 | tf_op jit(solution)/shard_map/ppermute | solution.py:379
  47.4 1.9 %collective-permute-start.2 = (f32[4,32,128]{2,1,0:T(8,128)S(1)}, f32[4,32,128]{2,1,0:T(8,128)S(1)}, u32[]{:S(2)}, u32[]{:S(2)}) collective-permute-start(f32[4,32,128]{2,1,0:T(8,128)S(1)} %get-tuple-element.68), channel_id=1, source_target_pairs={{1,0},{0,1},{3,2},{2,3},{5,4},{4,5},{7,6},{6,7},{9,8},{8,9},{11,10... | collective-permute-start | bytes 196616 | tf_op jit(solution)/shard_map/ppermute | solution.py:372
  50.6 3.8 %collective-permute-done.3.edge_b = f32[136,128]{1,0:T(8,128)S(1)} collective-permute-done((f32[136,128]{1,0:T(8,128)S(1)}, f32[136,128]{1,0:T(8,128)S(1)}, u32[]{:S(2)}, u32[]{:S(2)}) %collective-permute-start.3) | collective-permute-done | bytes 69664 | tf_op jit(solution)/shard_map/ppermute | solution.py:379
  54.4 1.7 shard_map.141
  56.1 9.5 %collective-permute-start.5 = (f32[232,128]{1,0:T(8,128)S(1)}, f32[232,128]{1,0:T(8,128)S(1)}, u32[]{:S(2)}, u32[]{:S(2)}) collective-permute-start(f32[232,128]{1,0:T(8,128)S(1)} %get-tuple-element.73), channel_id=1, source_target_pairs={{1,2},{2,1},{3,4},{4,3},{5,6},{6,5},{7,8},{8,7},{9,10},{10,9},{11,... | collective-permute-start | bytes 356360 | tf_op jit(solution)/shard_map/ppermute | solution.py:379
  65.6 1.9 %collective-permute-start.4 = (f32[7,32,128]{2,1,0:T(8,128)S(1)}, f32[7,32,128]{2,1,0:T(8,128)S(1)}, u32[]{:S(2)}, u32[]{:S(2)}) collective-permute-start(f32[7,32,128]{2,1,0:T(8,128)S(1)} %get-tuple-element.72), channel_id=1, source_target_pairs={{1,0},{0,1},{3,2},{2,3},{5,4},{4,5},{7,6},{6,7},{9,8},{8,9},{11,10... | collective-permute-start | bytes 344072 | tf_op jit(solution)/shard_map/ppermute | solution.py:372
  67.5 6.9 %collective-permute-start.9 = (f32[232,128]{1,0:T(8,128)S(1)}, f32[232,128]{1,0:T(8,128)S(1)}, u32[]{:S(2)}, u32[]{:S(2)}) collective-permute-start(f32[232,128]{1,0:T(8,128)S(1)} %get-tuple-element.80), channel_id=1, source_target_pairs={{1,2},{2,1},{3,4},{4,3},{5,6},{6,5},{7,8},{8,7},{9,10},{10,9},{11,... | collective-permute-start | bytes 356360 | tf_op jit(solution)/shard_map/ppermute | solution.py:379
  76.1 9.5 %collective-permute-start.7 = (f32[232,128]{1,0:T(8,128)S(1)}, f32[232,128]{1,0:T(8,128)S(1)}, u32[]{:S(2)}, u32[]{:S(2)}) collective-permute-start(f32[232,128]{1,0:T(8,128)S(1)} %get-tuple-element.77), channel_id=1, source_target_pairs={{1,2},{2,1},{3,4},{4,3},{5,6},{6,5},{7,8},{8,7},{9,10},{10,9},{11,... | collective-permute-start | bytes 356360 | tf_op jit(solution)/shard_map/ppermute | solution.py:379
  85.6 1.9 %collective-permute-start.8 = (f32[7,32,128]{2,1,0:T(8,128)S(1)}, f32[7,32,128]{2,1,0:T(8,128)S(1)}, u32[]{:S(2)}, u32[]{:S(2)}) collective-permute-start(f32[7,32,128]{2,1,0:T(8,128)S(1)} %get-tuple-element.79), channel_id=1, source_target_pairs={{1,0},{0,1},{3,2},{2,3},{5,4},{4,5},{7,6},{6,7},{9,8},{8,9},{11,10... | collective-permute-start | bytes 344072 | tf_op jit(solution)/shard_map/ppermute | solution.py:372
  87.5 2.4 %collective-permute-start.6 = (f32[7,32,128]{2,1,0:T(8,128)S(1)}, f32[7,32,128]{2,1,0:T(8,128)S(1)}, u32[]{:S(2)}, u32[]{:S(2)}) collective-permute-start(f32[7,32,128]{2,1,0:T(8,128)S(1)} %get-tuple-element.76), channel_id=1, source_target_pairs={{1,0},{0,1},{3,2},{2,3},{5,4},{4,5},{7,6},{6,7},{9,8},{8,9},{11,10... | collective-permute-start | bytes 344072 | tf_op jit(solution)/shard_map/ppermute | solution.py:372
  94.7 9.5 %collective-permute-start.11 = (f32[232,128]{1,0:T(8,128)S(1)}, f32[232,128]{1,0:T(8,128)S(1)}, u32[]{:S(2)}, u32[]{:S(2)}) collective-permute-start(f32[232,128]{1,0:T(8,128)S(1)} %get-tuple-element.85), channel_id=1, source_target_pairs={{1,2},{2,1},{3,4},{4,3},{5,6},{6,5},{7,8},{8,7},{9,10},{10,9},{11,... | collective-permute-start | bytes 356360 | tf_op jit(solution)/shard_map/ppermute | solution.py:379
  104.2 1.9 %collective-permute-start.10 = (f32[7,32,128]{2,1,0:T(8,128)S(1)}, f32[7,32,128]{2,1,0:T(8,128)S(1)}, u32[]{:S(2)}, u32[]{:S(2)}) collective-permute-start(f32[7,32,128]{2,1,0:T(8,128)S(1)} %get-tuple-element.84), channel_id=1, source_target_pairs={{1,0},{0,1},{3,2},{2,3},{5,4},{4,5},{7,6},{6,7},{9,8},{8,9},{11,10... | collective-permute-start | bytes 344072 | tf_op jit(solution)/shard_map/ppermute | solution.py:372
  107.5 4.3 %collective-permute-done.11.refs_5_ = f32[232,128]{1,0:T(8,128)S(1)} collective-permute-done((f32[232,128]{1,0:T(8,128)S(1)}, f32[232,128]{1,0:T(8,128)S(1)}, u32[]{:S(2)}, u32[]{:S(2)}) %collective-permute-start.11) | collective-permute-done | bytes 118816 | tf_op jit(solution)/shard_map/ppermute | solution.py:379
  113.4 9.5 %collective-permute-start.13 = (f32[232,128]{1,0:T(8,128)S(1)}, f32[232,128]{1,0:T(8,128)S(1)}, u32[]{:S(2)}, u32[]{:S(2)}) collective-permute-start(f32[232,128]{1,0:T(8,128)S(1)} %get-tuple-element.89), channel_id=1, source_target_pairs={{1,2},{2,1},{3,4},{4,3},{5,6},{6,5},{7,8},{8,7},{9,10},{10,9},{11,... | collective-permute-start | bytes 356360 | tf_op jit(solution)/shard_map/ppermute | solution.py:379
  122.9 1.9 %collective-permute-start.12 = (f32[7,32,128]{2,1,0:T(8,128)S(1)}, f32[7,32,128]{2,1,0:T(8,128)S(1)}, u32[]{:S(2)}, u32[]{:S(2)}) collective-permute-start(f32[7,32,128]{2,1,0:T(8,128)S(1)} %get-tuple-element.88), channel_id=1, source_target_pairs={{1,0},{0,1},{3,2},{2,3},{5,4},{4,5},{7,6},{6,7},{9,8},{8,9},{11,10... | collective-permute-start | bytes 344072 | tf_op jit(solution)/shard_map/ppermute | solution.py:372
  126.1 4.3 %collective-permute-done.13.refs_5_ = f32[232,128]{1,0:T(8,128)S(1)} collective-permute-done((f32[232,128]{1,0:T(8,128)S(1)}, f32[232,128]{1,0:T(8,128)S(1)}, u32[]{:S(2)}, u32[]{:S(2)}) %collective-permute-start.13) | collective-permute-done | bytes 118816 | tf_op jit(solution)/shard_map/ppermute | solution.py:379
  132.1 9.5 %collective-permute-start.15 = (f32[136,128]{1,0:T(8,128)S(1)}, f32[136,128]{1,0:T(8,128)S(1)}, u32[]{:S(2)}, u32[]{:S(2)}) collective-permute-start(f32[136,128]{1,0:T(8,128)S(1)} %get-tuple-element.93), channel_id=1, source_target_pairs={{1,2},{2,1},{3,4},{4,3},{5,6},{6,5},{7,8},{8,7},{9,10},{10,9},{11,... | collective-permute-start | bytes 208904 | tf_op jit(solution)/shard_map/ppermute | solution.py:379
  141.6 1.9 %collective-permute-start.14 = (f32[4,32,128]{2,1,0:T(8,128)S(1)}, f32[4,32,128]{2,1,0:T(8,128)S(1)}, u32[]{:S(2)}, u32[]{:S(2)}) collective-permute-start(f32[4,32,128]{2,1,0:T(8,128)S(1)} %get-tuple-element.92), channel_id=1, source_target_pairs={{1,0},{0,1},{3,2},{2,3},{5,4},{4,5},{7,6},{6,7},{9,8},{8,9},{11,10... | collective-permute-start | bytes 196616 | tf_op jit(solution)/shard_map/ppermute | solution.py:372
  145.0 3.6 %collective-permute-done.15.scaled_b = f32[136,128]{1,0:T(8,128)S(1)} collective-permute-done((f32[136,128]{1,0:T(8,128)S(1)}, f32[136,128]{1,0:T(8,128)S(1)}, u32[]{:S(2)}, u32[]{:S(2)}) %collective-permute-start.15) | collective-permute-done | bytes 69664 | tf_op jit(solution)/shard_map/ppermute | solution.py:379
  149.6 26.1 %all_to_all.10.arrived = f32[32,2,8,128]{3,2,1,0:T(8,128)S(1)} all-to-all(f32[32,2,8,128]{3,2,1,0:T(8,128)S(1)} %bitcast.54), channel_id=1, replica_groups=mesh['shot'=32,'dom'=16] {'shot'}, dimensions={0} | all-to-all | bytes 524288 | tf_op jit(solution)/shard_map/all_to_all | solution.py:512
  (52 shorter events, 22.2 us)
Async XLA Ops:
  0.6 0.7 copy-start.6
  3.0 15.4 %copy-start = (f32[1,8,32,128]{3,2,1,0:T(8,128)S(1)}, f32[1,8,32,128]{3,2,1,0:T(8,128)}, u32[]{:S(2)}) copy-start(f32[1,8,32,128]{3,2,1,0:T(8,128)} %param.11) | copy-start | bytes 393220
  3.0 34.1 %all-to-all-start = ((f32[32,2,8,128]{3,2,1,0:T(8,128)}), f32[32,2,8,128]{3,2,1,0:T(8,128)S(1)}, u32[]{:S(2)}, u32[]{:S(2)}) async-start(f32[32,2,8,128]{3,2,1,0:T(8,128)} %select_select_fusion), calls=%async_computation | async-start | bytes 524288 | tf_op jit(solution)/shard_map/all_to_all | solution.py:409
  18.4 11.5 %copy-start.7 = (f32[1,3,512]{2,0,1:T(1,128)S(1)}, f32[1,3,512]{2,0,1:T(1,128)}, u32[]{:S(2)}) copy-start(f32[1,3,512]{2,0,1:T(1,128)} %param.21) | copy-start | bytes 18436
  18.4 11.7 %copy-start.2 = (f32[1,8,32,128]{3,2,1,0:T(8,128)S(1)}, f32[1,8,32,128]{3,2,1,0:T(8,128)}, u32[]{:S(2)}) copy-start(f32[1,8,32,128]{3,2,1,0:T(8,128)} %param.13) | copy-start | bytes 393220
  18.4 11.7 %copy-start.3 = (f32[1,8,32,128]{3,2,1,0:T(8,128)S(1)}, f32[1,8,32,128]{3,2,1,0:T(8,128)}, u32[]{:S(2)}) copy-start(f32[1,8,32,128]{3,2,1,0:T(8,128)} %param.14) | copy-start | bytes 393220
  18.5 11.6 %copy-start.1 = (f32[1,8,32,128]{3,2,1,0:T(8,128)S(1)}, f32[1,8,32,128]{3,2,1,0:T(8,128)}, u32[]{:S(2)}) copy-start(f32[1,8,32,128]{3,2,1,0:T(8,128)} %param.12) | copy-start | bytes 393220
  18.5 30.9 %collective-permute-start.1 = (f32[7,32,128]{2,1,0:T(8,128)S(1)}, f32[7,32,128]{2,1,0:T(8,128)S(1)}, u32[]{:S(2)}, u32[]{:S(2)}) collective-permute-start(f32[7,32,128]{2,1,0:T(8,128)S(1)} %get-tuple-element.112), channel_id=1, source_target_pairs={{1,2},{2,1},{3,4},{4,3},{5,6},{6,5},{7,8},{8,7},{9,10},{10,9},{11,... | collective-permute-start | bytes 344072 | tf_op jit(solution)/shard_map/ppermute | solution.py:379
  27.3 22.0 %collective-permute-start = (f32[7,32,128]{2,1,0:T(8,128)S(1)}, f32[7,32,128]{2,1,0:T(8,128)S(1)}, u32[]{:S(2)}, u32[]{:S(2)}) collective-permute-start(f32[7,32,128]{2,1,0:T(8,128)S(1)} %get-tuple-element.113), channel_id=1, source_target_pairs={{1,0},{0,1},{3,2},{2,3},{5,4},{4,5},{7,6},{6,7},{9,8},{8,9},{11,10... | collective-permute-start | bytes 344072 | tf_op jit(solution)/shard_map/ppermute | solution.py:372
  30.1 0.7 copy-start.5
  37.9 16.5 %collective-permute-start.3 = (f32[136,128]{1,0:T(8,128)S(1)}, f32[136,128]{1,0:T(8,128)S(1)}, u32[]{:S(2)}, u32[]{:S(2)}) collective-permute-start(f32[136,128]{1,0:T(8,128)S(1)} %get-tuple-element.69), channel_id=1, source_target_pairs={{1,2},{2,1},{3,4},{4,3},{5,6},{6,5},{7,8},{8,7},{9,10},{10,9},{11,... | collective-permute-start | bytes 208904 | tf_op jit(solution)/shard_map/ppermute | solution.py:379
  47.4 3.1 %collective-permute-start.2 = (f32[4,32,128]{2,1,0:T(8,128)S(1)}, f32[4,32,128]{2,1,0:T(8,128)S(1)}, u32[]{:S(2)}, u32[]{:S(2)}) collective-permute-start(f32[4,32,128]{2,1,0:T(8,128)S(1)} %get-tuple-element.68), channel_id=1, source_target_pairs={{1,0},{0,1},{3,2},{2,3},{5,4},{4,5},{7,6},{6,7},{9,8},{8,9},{11,10... | collective-permute-start | bytes 196616 | tf_op jit(solution)/shard_map/ppermute | solution.py:372
  56.1 18.3 %collective-permute-start.5 = (f32[232,128]{1,0:T(8,128)S(1)}, f32[232,128]{1,0:T(8,128)S(1)}, u32[]{:S(2)}, u32[]{:S(2)}) collective-permute-start(f32[232,128]{1,0:T(8,128)S(1)} %get-tuple-element.73), channel_id=1, source_target_pairs={{1,2},{2,1},{3,4},{4,3},{5,6},{6,5},{7,8},{8,7},{9,10},{10,9},{11,... | collective-permute-start | bytes 356360 | tf_op jit(solution)/shard_map/ppermute | solution.py:379
  65.6 8.8 %collective-permute-start.4 = (f32[7,32,128]{2,1,0:T(8,128)S(1)}, f32[7,32,128]{2,1,0:T(8,128)S(1)}, u32[]{:S(2)}, u32[]{:S(2)}) collective-permute-start(f32[7,32,128]{2,1,0:T(8,128)S(1)} %get-tuple-element.72), channel_id=1, source_target_pairs={{1,0},{0,1},{3,2},{2,3},{5,4},{4,5},{7,6},{6,7},{9,8},{8,9},{11,10... | collective-permute-start | bytes 344072 | tf_op jit(solution)/shard_map/ppermute | solution.py:372
  67.5 22.5 %collective-permute-start.9 = (f32[232,128]{1,0:T(8,128)S(1)}, f32[232,128]{1,0:T(8,128)S(1)}, u32[]{:S(2)}, u32[]{:S(2)}) collective-permute-start(f32[232,128]{1,0:T(8,128)S(1)} %get-tuple-element.80), channel_id=1, source_target_pairs={{1,2},{2,1},{3,4},{4,3},{5,6},{6,5},{7,8},{8,7},{9,10},{10,9},{11,... | collective-permute-start | bytes 356360 | tf_op jit(solution)/shard_map/ppermute | solution.py:379
  76.1 17.0 %collective-permute-start.7 = (f32[232,128]{1,0:T(8,128)S(1)}, f32[232,128]{1,0:T(8,128)S(1)}, u32[]{:S(2)}, u32[]{:S(2)}) collective-permute-start(f32[232,128]{1,0:T(8,128)S(1)} %get-tuple-element.77), channel_id=1, source_target_pairs={{1,2},{2,1},{3,4},{4,3},{5,6},{6,5},{7,8},{8,7},{9,10},{10,9},{11,... | collective-permute-start | bytes 356360 | tf_op jit(solution)/shard_map/ppermute | solution.py:379
  85.6 4.3 %collective-permute-start.8 = (f32[7,32,128]{2,1,0:T(8,128)S(1)}, f32[7,32,128]{2,1,0:T(8,128)S(1)}, u32[]{:S(2)}, u32[]{:S(2)}) collective-permute-start(f32[7,32,128]{2,1,0:T(8,128)S(1)} %get-tuple-element.79), channel_id=1, source_target_pairs={{1,0},{0,1},{3,2},{2,3},{5,4},{4,5},{7,6},{6,7},{9,8},{8,9},{11,10... | collective-permute-start | bytes 344072 | tf_op jit(solution)/shard_map/ppermute | solution.py:372
  87.5 4.1 %collective-permute-start.6 = (f32[7,32,128]{2,1,0:T(8,128)S(1)}, f32[7,32,128]{2,1,0:T(8,128)S(1)}, u32[]{:S(2)}, u32[]{:S(2)}) collective-permute-start(f32[7,32,128]{2,1,0:T(8,128)S(1)} %get-tuple-element.76), channel_id=1, source_target_pairs={{1,0},{0,1},{3,2},{2,3},{5,4},{4,5},{7,6},{6,7},{9,8},{8,9},{11,10... | collective-permute-start | bytes 344072 | tf_op jit(solution)/shard_map/ppermute | solution.py:372
  94.7 17.0 %collective-permute-start.11 = (f32[232,128]{1,0:T(8,128)S(1)}, f32[232,128]{1,0:T(8,128)S(1)}, u32[]{:S(2)}, u32[]{:S(2)}) collective-permute-start(f32[232,128]{1,0:T(8,128)S(1)} %get-tuple-element.85), channel_id=1, source_target_pairs={{1,2},{2,1},{3,4},{4,3},{5,6},{6,5},{7,8},{8,7},{9,10},{10,9},{11,... | collective-permute-start | bytes 356360 | tf_op jit(solution)/shard_map/ppermute | solution.py:379
  104.2 3.2 %collective-permute-start.10 = (f32[7,32,128]{2,1,0:T(8,128)S(1)}, f32[7,32,128]{2,1,0:T(8,128)S(1)}, u32[]{:S(2)}, u32[]{:S(2)}) collective-permute-start(f32[7,32,128]{2,1,0:T(8,128)S(1)} %get-tuple-element.84), channel_id=1, source_target_pairs={{1,0},{0,1},{3,2},{2,3},{5,4},{4,5},{7,6},{6,7},{9,8},{8,9},{11,10... | collective-permute-start | bytes 344072 | tf_op jit(solution)/shard_map/ppermute | solution.py:372
  113.4 17.0 %collective-permute-start.13 = (f32[232,128]{1,0:T(8,128)S(1)}, f32[232,128]{1,0:T(8,128)S(1)}, u32[]{:S(2)}, u32[]{:S(2)}) collective-permute-start(f32[232,128]{1,0:T(8,128)S(1)} %get-tuple-element.89), channel_id=1, source_target_pairs={{1,2},{2,1},{3,4},{4,3},{5,6},{6,5},{7,8},{8,7},{9,10},{10,9},{11,... | collective-permute-start | bytes 356360 | tf_op jit(solution)/shard_map/ppermute | solution.py:379
  122.9 3.2 %collective-permute-start.12 = (f32[7,32,128]{2,1,0:T(8,128)S(1)}, f32[7,32,128]{2,1,0:T(8,128)S(1)}, u32[]{:S(2)}, u32[]{:S(2)}) collective-permute-start(f32[7,32,128]{2,1,0:T(8,128)S(1)} %get-tuple-element.88), channel_id=1, source_target_pairs={{1,0},{0,1},{3,2},{2,3},{5,4},{4,5},{7,6},{6,7},{9,8},{8,9},{11,10... | collective-permute-start | bytes 344072 | tf_op jit(solution)/shard_map/ppermute | solution.py:372
  132.1 16.5 %collective-permute-start.15 = (f32[136,128]{1,0:T(8,128)S(1)}, f32[136,128]{1,0:T(8,128)S(1)}, u32[]{:S(2)}, u32[]{:S(2)}) collective-permute-start(f32[136,128]{1,0:T(8,128)S(1)} %get-tuple-element.93), channel_id=1, source_target_pairs={{1,2},{2,1},{3,4},{4,3},{5,6},{6,5},{7,8},{8,7},{9,10},{10,9},{11,... | collective-permute-start | bytes 208904 | tf_op jit(solution)/shard_map/ppermute | solution.py:379
  141.6 3.4 %collective-permute-start.14 = (f32[4,32,128]{2,1,0:T(8,128)S(1)}, f32[4,32,128]{2,1,0:T(8,128)S(1)}, u32[]{:S(2)}, u32[]{:S(2)}) collective-permute-start(f32[4,32,128]{2,1,0:T(8,128)S(1)} %get-tuple-element.92), channel_id=1, source_target_pairs={{1,0},{0,1},{3,2},{2,3},{5,4},{4,5},{7,6},{6,7},{9,8},{8,9},{11,10... | collective-permute-start | bytes 196616 | tf_op jit(solution)/shard_map/ppermute | solution.py:372
  (1 other events, 0.7 us)

commit v10 on v9

--- a/solution.py
+++ b/solution.py
@@ -58,18 +58,19 @@
     target[:, 0:PAD, :] = jnp.zeros((target.shape[0], PAD, CZ), F32)
     target[:, PAD + CY : ROWS, :] = jnp.zeros((target.shape[0], PAD, CZ), F32)
     inner = slice(PAD, PAD + CY)
-    target[width : width + CX, inner, :] = own
+    for cell in range(CX):
+        target[width + cell, inner, :] = own[cell]
     odd = info[0] == 1
 
     @pl.when(odd)
     def _():
-        target[0:width, inner, :] = first
-        target[width + CX : 2 * width + CX, inner, :] = second
+        target[0:width, inner, :] = first()
+        target[width + CX : 2 * width + CX, inner, :] = second()
 
     @pl.when(jnp.logical_not(odd))
     def _():
-        target[0:width, inner, :] = second
-        target[width + CX : 2 * width + CX, inner, :] = first
+        target[0:width, inner, :] = second()
+        target[width + CX : 2 * width + CX, inner, :] = first()
 
 
 def for_partner(info, target, head, tail):
@@ -108,22 +109,30 @@
     return stencil(lambda s: lane_shift(plane, s, lane))
 
 
-def operate(field, width, buoy, gx, gy, acc, slopes):
-    lane = lax.broadcasted_iota(jnp.int32, (CY, CZ), 1)
+def along_z(planes, table):
+    rows = planes.reshape(CX * CY, CZ)
+    out = lax.dot_general(
+        rows,
+        table,
+        (((1,), (0,)), ((), ())),
+        precision=lax.Precision.HIGHEST,
+        preferred_element_type=F32,
+    )
+    return out.reshape(CX, CY, CZ)
+
+
+def operate(field, width, buoy, tables, gx, gy, acc, slopes):
     gy[:, 0:PAD, :] = jnp.zeros((CX, PAD, CZ), F32)
     gy[:, PAD + CY : ROWS, :] = jnp.zeros((CX, PAD, CZ), F32)
+    slope = along_z(field[width : width + CX, PAD : PAD + CY, :], tables[0])
+    acc[...] = along_z(buoy[4 : 4 + CX] * slope, tables[1])
     for cell in range(-3, CX + 4):
         sx = slope_x(field, cell + width)
         gx[cell + 3] = buoy[cell + 4] * sx
         if 0 <= cell < CX:
-            weight = buoy[cell + 4]
-            plane = field[cell + width, PAD : PAD + CY, :]
             sy = slope_y(field, cell + width)
-            sz = slope_z(plane, lane)
-            gy[cell, PAD : PAD + CY, :] = weight * sy
-            gz = weight * sz
-            acc[cell] = stencil(lambda s: lane_shift(gz, s + 1, lane))
-            slopes(cell, sx, sy, sz)
+            gy[cell, PAD : PAD + CY, :] = buoy[cell + 4] * sy
+            slopes(cell, sx, sy, slope[cell])
     for cell in range(CX):
         div = stencil(lambda s: gx[cell + 4 + s])
         div = div + stencil(lambda s: gy[cell, PAD + 1 + s : PAD + 1 + s + CY, :])
@@ -131,8 +140,16 @@
 
 
 def prepare_kernel(
-    info, wave, cells, seen, now, before, last, after, out, base_p, base_q, now_out, last_out, source_out
-):
+    info, wave, cells, seen, now, before, last, after, out, base_p, base_q, now_out, last_out, source_out,
+    tables,
+):
+    gap = lax.broadcasted_iota(jnp.int32, (CZ, CZ), 0) - lax.broadcasted_iota(jnp.int32, (CZ, CZ), 1)
+    for at in range(2):
+        table = jnp.zeros((CZ, CZ), F32)
+        for k in range(1, 5):
+            table = table + jnp.where(gap == k - 1 + at, COEFFS[k - 1], 0.0)
+            table = table - jnp.where(gap == at - k, COEFFS[k - 1], 0.0)
+        tables[at] = table
     base_p[...] = 2.0 * now[...] - before[...]
     base_q[...] = 2.0 * last[...] - after[...]
     now_out[...] = now[...]
@@ -181,16 +198,16 @@
 
 
 def widen_kernel(info, now, now_a, now_b, out):
-    place(info, out, now[...], now_a[...], now_b[...], 7)
-
-
-def forward(info, source, base, stiff, field, buoy, gx, gy, acc, div_out, slope_out, store):
+    place(info, out, now, lambda: now_a[...], lambda: now_b[...], 7)
+
+
+def forward(info, source, base, stiff, field, buoy, tables, gx, gy, acc, div_out, slope_out, store):
     def keep(cell, sx, sy, sz):
         slope_out[0, cell] = sx
         slope_out[1, cell] = sy
         slope_out[2, cell] = sz
 
-    for cell, div in operate(field, 7, buoy, gx, gy, acc, keep):
+    for cell, div in operate(field, 7, buoy, tables, gx, gy, acc, keep):
         div_out[cell] = div
         value = base(cell) + step_squared * stiff[cell] * div
         store(cell, value + jnp.where(info[1] == cell, source, 0.0))
@@ -212,7 +229,7 @@
 
 
 def first_kernel(
-    info, padded, base, source, stiff, buoy, edge_a, edge_b, scaled,
+    info, tables, padded, base, source, stiff, buoy, edge_a, edge_b, scaled,
     p_out, send_a, send_b, near, far, div_out, slope_out, buoy_out,
     gx, gy, acc,
 ):
@@ -223,45 +240,45 @@
 
     forward(
         info, source[0], lambda cell: base[cell],
-        stiff, padded, buoy_out, gx, gy, acc, div_out, slope_out, store,
+        stiff, padded, buoy_out, tables, gx, gy, acc, div_out, slope_out, store,
     )
     hand_over(info, send_a, send_b, p_out)
     hand_over(info, near, far, scaled)
 
 
 def adjoint_part_kernel(
-    info, base, scaled, near, far, buoy,
+    info, tables, base, scaled, near, far, buoy,
     q_out,
     field, gx, gy, acc,
 ):
-    place(info, field, scaled[...], near[...], planes_at(far, 0, 7), 7)
-    for cell, div in operate(field, 7, buoy, gx, gy, acc, lambda *_: None):
+    place(info, field, scaled, lambda: near[...], lambda: planes_at(far, 0, 7), 7)
+    for cell, div in operate(field, 7, buoy, tables, gx, gy, acc, lambda *_: None):
         q_out[cell] = base[cell] + step_squared * div
 
 
 def second_kernel(
-    info, now, now_a, now_b, before, source, stiff, buoy,
+    info, tables, now, now_a, now_b, before, source, stiff, buoy,
     p_out, send_a, send_b, div_out, slope_out,
     field, gx, gy, acc,
 ):
-    place(info, field, now[...], now_a[...], planes_at(now_b, 0, 7), 7)
+    place(info, field, now, lambda: now_a[...], lambda: planes_at(now_b, 0, 7), 7)
 
     def store(cell, value):
         p_out[cell] = value
 
     forward(
         info, source[1], lambda cell: 2.0 * now[cell] - before[cell],
-        stiff, field, buoy, gx, gy, acc, div_out, slope_out, store,
+        stiff, field, buoy, tables, gx, gy, acc, div_out, slope_out, store,
     )
     hand_over(info, send_a, send_b, p_out)
 
 
 def third_kernel(
-    info, now, now_a, now_b, before, source, stiff, buoy, q_part, spots,
+    info, tables, now, now_a, now_b, before, source, stiff, buoy, q_part, spots,
     q_out, scaled, send_a, send_b, div_out, slope_out,
     field, gx, gy, acc,
 ):
-    place(info, field, now[...], now_a[...], planes_at(now_b, 0, 7), 7)
+    place(info, field, now, lambda: now_a[...], lambda: planes_at(now_b, 0, 7), 7)
 
     def store(cell, value):
         q = q_part[cell] + (spots[0, cell] * value - spots[3, cell])
@@ -270,24 +287,24 @@
 
     forward(
         info, source[2], lambda cell: 2.0 * now[cell] - before[cell],
-        stiff, field, buoy, gx, gy, acc, div_out, slope_out, store,
+        stiff, field, buoy, tables, gx, gy, acc, div_out, slope_out, store,
     )
     hand_over(info, send_a, send_b, scaled)
 
 
 def adjoint_kernel(
-    n, info, q_now, q_after, scaled, scaled_a, scaled_b, stiff, buoy, spots, p_then,
+    n, info, tables, q_now, q_after, scaled, scaled_a, scaled_b, stiff, buoy, spots, p_then,
     q_out, scaled_out, send_a, send_b, slope_out,
     field, gx, gy, acc,
 ):
-    place(info, field, scaled[...], scaled_a[...], planes_at(scaled_b, 0, 7), 7)
+    place(info, field, scaled, lambda: scaled_a[...], lambda: planes_at(scaled_b, 0, 7), 7)
 
     def keep(cell, sx, sy, sz):
         slope_out[0, cell] = sx
         slope_out[1, cell] = sy
         slope_out[2, cell] = sz
 
-    for cell, total in operate(field, 7, buoy, gx, gy, acc, keep):
+    for cell, total in operate(field, 7, buoy, tables, gx, gy, acc, keep):
         q = 2.0 * q_now[cell] - q_after[cell] + step_squared * total
         q = q + (spots[0, cell] * p_then[cell] - spots[n + 1, cell])
         q_out[cell] = q
@@ -323,7 +340,7 @@
 
 def image_kernel(info, q_now, scaled, scaled_a, scaled_b, div, slope, images, out, field):
     lane = lax.broadcasted_iota(jnp.int32, (CY, CZ), 1)
-    place(info, field, scaled[...], scaled_a[...], planes_at(scaled_b, 0, 4), 4)
+    place(info, field, scaled, lambda: scaled_a[...], lambda: planes_at(scaled_b, 0, 4), 4)
     for cell in range(CX):
         plane = field[cell + 4, PAD : PAD + CY, :]
         rho = images[1, cell] + slope[0, cell] * slope_x(field, cell + 4)
@@ -413,19 +430,20 @@
     p0_b = swap_second(jnp.where(odd == 1, pressure_now[0][1:8], pressure_now[0][0:7]))
     p0_a = swap_first(jnp.where(odd == 1, pressure_now[0][0:7], pressure_now[0][1:8]))
     own, seven, four = plane_field(CX), plane_field(7), plane_field(4)
-    spots, base_p, base_q, p0, q4, source_planes = call(
+    spots, base_p, base_q, p0, q4, source_planes, tables = call(
         prepare_kernel,
         [info, source_wave[0]],
         [receiver_cell, observed[0], p0, p_prev, q4, q5],
-        [jax.ShapeDtypeStruct((STEPS + 1, CX, CY, CZ), F32), own, own, own, own, plane_field(STEPS)],
+        [jax.ShapeDtypeStruct((STEPS + 1, CX, CY, CZ), F32), own, own, own, own, plane_field(STEPS),
+         jax.ShapeDtypeStruct((2, CZ, CZ), F32)],
         flops=400_000_000,
     )
     ids = jnp.arange(TILES, dtype=jnp.int32)[:, None, None]
     picked = jnp.broadcast_to(
         (column[None, :, None] == ids).astype(F32), (TILES, column.shape[0], CZ)
     )
-    block, spots, base_p, base_q, p0, q4, source_planes, picked = lax.optimization_barrier(
-        (block, spots, base_p, base_q, p0, q4, source_planes, picked)
+    block, spots, base_p, base_q, p0, q4, source_planes, picked, tables = lax.optimization_barrier(
+        (block, spots, base_p, base_q, p0, q4, source_planes, picked, tables)
     )
 
     stiff = block[:, 0].transpose(1, 0, 2)
@@ -448,7 +466,7 @@
     p1, send_a, send_b, near, far, div0, slope0, wide = call(
         first_kernel,
         [info],
-        [padded, base_p, source_planes, stiff, buoy, edge_a, edge_b, f4],
+        [tables, padded, base_p, source_planes, stiff, buoy, edge_a, edge_b, f4],
         [own, seven, far_rows(7), seven, far_rows(7), own, slopes, plane_field(CX + 8)],
         work()[1:],
     )
@@ -456,12 +474,12 @@
     from_a = swap_first(send_a)
     far = swap_second(far)
     near = swap_first(near)
-    (q_part,) = call(adjoint_part_kernel, [info], [base_q, f4, near, far, wide], [own], work())
+    (q_part,) = call(adjoint_part_kernel, [info], [tables, base_q, f4, near, far, wide], [own], work())
 
     p2, send_a, send_b, div1, slope1 = call(
         second_kernel,
         [info],
-        [p1, from_a, from_b, p0, source_planes, stiff, wide],
+        [tables, p1, from_a, from_b, p0, source_planes, stiff, wide],
         [own, seven, far_rows(7), own, slopes],
         work(),
     )
@@ -471,7 +489,7 @@
     q3, f3, send_a, send_b, div2, slope2 = call(
         third_kernel,
         [info],
-        [p2, from_a, from_b, p1, source_planes, stiff, wide, q_part, spots],
+        [tables, p2, from_a, from_b, p1, source_planes, stiff, wide, q_part, spots],
         [own, own, seven, far_rows(7), own, slopes],
         work(),
     )
@@ -481,7 +499,7 @@
     q2, f2, send_a, send_b, slope_q = call(
         adjoint_first_kernel,
         [info],
-        [q3, q4, f3, from_a, from_b, stiff, wide, spots, p2],
+        [tables, q3, q4, f3, from_a, from_b, stiff, wide, spots, p2],
         [own, own, seven, far_rows(7), slopes],
         work(),
     )
@@ -492,7 +510,7 @@
     q1, f1, send_a, send_b, slope_q = call(
         adjoint_second_kernel,
         [info],
-        [q2, q3, f2, from_a, from_b, stiff, wide, spots, p1],
+        [tables, q2, q3, f2, from_a, from_b, stiff, wide, spots, p1],
         [own, own, four, far_rows(4), slopes],
         work(),
     )

time: 177 us -> 176 us (level)
  no operation moved by 1% of the time
where the time goes in v10:
time: 176 us; the launch traced here: 175 us
  starting transfers between devices  104 us (59%)
  blocking collectives  26.1 us (15%)
  waiting for transfers between devices  25.8 us (15%)
  Pallas kernels  14.6 us (8%)
  other arithmetic  2.35 us (1%)
  between operations  1.76 us (1%)
    ppermute x8, starting transfers between devices, swap_second(): return lax.ppermute(planes, 'dom', pairs)  72.5 us
    all_to_all x1, blocking collectives, shards(): lax.all_to_all(image.transpose(2, 0, 1, 3), 'shot', 0, 0, tiled=True)  26.1 us
    ppermute x8, waiting for transfers between devices, swap_second(): return lax.ppermute(planes, 'dom', pairs)  17.7 us
    ppermute x8, starting transfers between devices, swap_first(): return lax.ppermute(planes, 'dom', [(i ^ 1, i) for i in range(count)])  15.8 us
    all_to_all x1, starting transfers between devices, shards(): block = lax.all_to_all(chosen, 'shot', 0, 0, tiled=True)  15.4 us
    pallas_call x13, Pallas kernels, call(): pl.pallas_call(kernel, out_shape=outs, in_specs=[SMEM] * len(scalars) + [...  14.6 us
    all_to_all x1, waiting for transfers between devices, shards(): block = lax.all_to_all(chosen, 'shot', 0, 0, tiled=True)  4.88 us
  transfers between devices with their start and end apart: 17, of which 9 were waited for; matrix products, arithmetic and copies ran while one was open for 0% of the time, Pallas kernels for 4%

profile of v10, /device:TPU:7, one launch (start us, length us, event | category | flops | bytes accessed | tf_op | source)
XLA Modules:
  0.0 175.5 jit_solution(14550670178029562425)
XLA Ops:
  3.0 15.4 %all-to-all-start = ((f32[32,2,8,128]{3,2,1,0:T(8,128)}), f32[32,2,8,128]{3,2,1,0:T(8,128)S(1)}, u32[]{:S(2)}, u32[]{:S(2)}) async-start(f32[32,2,8,128]{3,2,1,0:T(8,128)} %select_select_fusion), calls=%async_computation | async-start | bytes 524288 | tf_op jit(solution)/shard_map/all_to_all | solution.py:426
  18.5 8.8 %collective-permute-start.1 = (f32[7,32,128]{2,1,0:T(8,128)S(1)}, f32[7,32,128]{2,1,0:T(8,128)S(1)}, u32[]{:S(2)}, u32[]{:S(2)}) collective-permute-start(f32[7,32,128]{2,1,0:T(8,128)S(1)} %get-tuple-element.116), channel_id=1, source_target_pairs={{1,2},{2,1},{3,4},{4,3},{5,6},{6,5},{7,8},{8,7},{9,10},{10,9},{11,... | collective-permute-start | bytes 344072 | tf_op jit(solution)/shard_map/ppermute | solution.py:396
  27.3 1.9 %collective-permute-start = (f32[7,32,128]{2,1,0:T(8,128)S(1)}, f32[7,32,128]{2,1,0:T(8,128)S(1)}, u32[]{:S(2)}, u32[]{:S(2)}) collective-permute-start(f32[7,32,128]{2,1,0:T(8,128)S(1)} %get-tuple-element.117), channel_id=1, source_target_pairs={{1,0},{0,1},{3,2},{2,3},{5,4},{4,5},{7,6},{6,7},{9,8},{8,9},{11,10... | collective-permute-start | bytes 344072 | tf_op jit(solution)/shard_map/ppermute | solution.py:389
  32.3 4.9 %all-to-all-done = f32[32,2,8,128]{3,2,1,0:T(8,128)S(1)} async-done(((f32[32,2,8,128]{3,2,1,0:T(8,128)}), f32[32,2,8,128]{3,2,1,0:T(8,128)S(1)}, u32[]{:S(2)}, u32[]{:S(2)}) %all-to-all-start) | async-done | bytes 262176 | tf_op jit(solution)/shard_map/all_to_all | solution.py:426
  37.9 9.5 %collective-permute-start.3 = (f32[136,128]{1,0:T(8,128)S(1)}, f32[136,128]{1,0:T(8,128)S(1)}, u32[]{:S(2)}, u32[]{:S(2)}) collective-permute-start(f32[136,128]{1,0:T(8,128)S(1)} %get-tuple-element.73), channel_id=1, source_target_pairs={{1,2},{2,1},{3,4},{4,3},{5,6},{6,5},{7,8},{8,7},{9,10},{10,9},{11,... | collective-permute-start | bytes 208904 | tf_op jit(solution)/shard_map/ppermute | solution.py:396
  47.4 1.9 %collective-permute-start.2 = (f32[4,32,128]{2,1,0:T(8,128)S(1)}, f32[4,32,128]{2,1,0:T(8,128)S(1)}, u32[]{:S(2)}, u32[]{:S(2)}) collective-permute-start(f32[4,32,128]{2,1,0:T(8,128)S(1)} %get-tuple-element.72), channel_id=1, source_target_pairs={{1,0},{0,1},{3,2},{2,3},{5,4},{4,5},{7,6},{6,7},{9,8},{8,9},{11,10... | collective-permute-start | bytes 196616 | tf_op jit(solution)/shard_map/ppermute | solution.py:389
  50.6 3.8 %collective-permute-done.3.edge_b = f32[136,128]{1,0:T(8,128)S(1)} collective-permute-done((f32[136,128]{1,0:T(8,128)S(1)}, f32[136,128]{1,0:T(8,128)S(1)}, u32[]{:S(2)}, u32[]{:S(2)}) %collective-permute-start.3) | collective-permute-done | bytes 69664 | tf_op jit(solution)/shard_map/ppermute | solution.py:396
  55.9 9.5 %collective-permute-start.5 = (f32[232,128]{1,0:T(8,128)S(1)}, f32[232,128]{1,0:T(8,128)S(1)}, u32[]{:S(2)}, u32[]{:S(2)}) collective-permute-start(f32[232,128]{1,0:T(8,128)S(1)} %get-tuple-element.77), channel_id=1, source_target_pairs={{1,2},{2,1},{3,4},{4,3},{5,6},{6,5},{7,8},{8,7},{9,10},{10,9},{11,... | collective-permute-start | bytes 356360 | tf_op jit(solution)/shard_map/ppermute | solution.py:396
  65.4 1.9 %collective-permute-start.4 = (f32[7,32,128]{2,1,0:T(8,128)S(1)}, f32[7,32,128]{2,1,0:T(8,128)S(1)}, u32[]{:S(2)}, u32[]{:S(2)}) collective-permute-start(f32[7,32,128]{2,1,0:T(8,128)S(1)} %get-tuple-element.76), channel_id=1, source_target_pairs={{1,0},{0,1},{3,2},{2,3},{5,4},{4,5},{7,6},{6,7},{9,8},{8,9},{11,10... | collective-permute-start | bytes 344072 | tf_op jit(solution)/shard_map/ppermute | solution.py:389
  67.3 6.9 %collective-permute-start.9 = (f32[232,128]{1,0:T(8,128)S(1)}, f32[232,128]{1,0:T(8,128)S(1)}, u32[]{:S(2)}, u32[]{:S(2)}) collective-permute-start(f32[232,128]{1,0:T(8,128)S(1)} %get-tuple-element.84), channel_id=1, source_target_pairs={{1,2},{2,1},{3,4},{4,3},{5,6},{6,5},{7,8},{8,7},{9,10},{10,9},{11,... | collective-permute-start | bytes 356360 | tf_op jit(solution)/shard_map/ppermute | solution.py:396
  75.7 9.5 %collective-permute-start.7 = (f32[232,128]{1,0:T(8,128)S(1)}, f32[232,128]{1,0:T(8,128)S(1)}, u32[]{:S(2)}, u32[]{:S(2)}) collective-permute-start(f32[232,128]{1,0:T(8,128)S(1)} %get-tuple-element.81), channel_id=1, source_target_pairs={{1,2},{2,1},{3,4},{4,3},{5,6},{6,5},{7,8},{8,7},{9,10},{10,9},{11,... | collective-permute-start | bytes 356360 | tf_op jit(solution)/shard_map/ppermute | solution.py:396
  85.2 1.9 %collective-permute-start.8 = (f32[7,32,128]{2,1,0:T(8,128)S(1)}, f32[7,32,128]{2,1,0:T(8,128)S(1)}, u32[]{:S(2)}, u32[]{:S(2)}) collective-permute-start(f32[7,32,128]{2,1,0:T(8,128)S(1)} %get-tuple-element.83), channel_id=1, source_target_pairs={{1,0},{0,1},{3,2},{2,3},{5,4},{4,5},{7,6},{6,7},{9,8},{8,9},{11,10... | collective-permute-start | bytes 344072 | tf_op jit(solution)/shard_map/ppermute | solution.py:389
  87.1 2.4 %collective-permute-start.6 = (f32[7,32,128]{2,1,0:T(8,128)S(1)}, f32[7,32,128]{2,1,0:T(8,128)S(1)}, u32[]{:S(2)}, u32[]{:S(2)}) collective-permute-start(f32[7,32,128]{2,1,0:T(8,128)S(1)} %get-tuple-element.80), channel_id=1, source_target_pairs={{1,0},{0,1},{3,2},{2,3},{5,4},{4,5},{7,6},{6,7},{9,8},{8,9},{11,10... | collective-permute-start | bytes 344072 | tf_op jit(solution)/shard_map/ppermute | solution.py:389
  91.0 1.7 collective-permute-done.7.now_b
  94.2 9.5 %collective-permute-start.11 = (f32[232,128]{1,0:T(8,128)S(1)}, f32[232,128]{1,0:T(8,128)S(1)}, u32[]{:S(2)}, u32[]{:S(2)}) collective-permute-start(f32[232,128]{1,0:T(8,128)S(1)} %get-tuple-element.89), channel_id=1, source_target_pairs={{1,2},{2,1},{3,4},{4,3},{5,6},{6,5},{7,8},{8,7},{9,10},{10,9},{11,... | collective-permute-start | bytes 356360 | tf_op jit(solution)/shard_map/ppermute | solution.py:396
  103.7 1.9 %collective-permute-start.10 = (f32[7,32,128]{2,1,0:T(8,128)S(1)}, f32[7,32,128]{2,1,0:T(8,128)S(1)}, u32[]{:S(2)}, u32[]{:S(2)}) collective-permute-start(f32[7,32,128]{2,1,0:T(8,128)S(1)} %get-tuple-element.88), channel_id=1, source_target_pairs={{1,0},{0,1},{3,2},{2,3},{5,4},{4,5},{7,6},{6,7},{9,8},{8,9},{11,10... | collective-permute-start | bytes 344072 | tf_op jit(solution)/shard_map/ppermute | solution.py:389
  106.9 4.3 %collective-permute-done.11.refs_6_ = f32[232,128]{1,0:T(8,128)S(1)} collective-permute-done((f32[232,128]{1,0:T(8,128)S(1)}, f32[232,128]{1,0:T(8,128)S(1)}, u32[]{:S(2)}, u32[]{:S(2)}) %collective-permute-start.11) | collective-permute-done | bytes 118816 | tf_op jit(solution)/shard_map/ppermute | solution.py:396
  112.6 9.5 %collective-permute-start.13 = (f32[232,128]{1,0:T(8,128)S(1)}, f32[232,128]{1,0:T(8,128)S(1)}, u32[]{:S(2)}, u32[]{:S(2)}) collective-permute-start(f32[232,128]{1,0:T(8,128)S(1)} %get-tuple-element.93), channel_id=1, source_target_pairs={{1,2},{2,1},{3,4},{4,3},{5,6},{6,5},{7,8},{8,7},{9,10},{10,9},{11,... | collective-permute-start | bytes 356360 | tf_op jit(solution)/shard_map/ppermute | solution.py:396
  122.1 1.9 %collective-permute-start.12 = (f32[7,32,128]{2,1,0:T(8,128)S(1)}, f32[7,32,128]{2,1,0:T(8,128)S(1)}, u32[]{:S(2)}, u32[]{:S(2)}) collective-permute-start(f32[7,32,128]{2,1,0:T(8,128)S(1)} %get-tuple-element.92), channel_id=1, source_target_pairs={{1,0},{0,1},{3,2},{2,3},{5,4},{4,5},{7,6},{6,7},{9,8},{8,9},{11,10... | collective-permute-start | bytes 344072 | tf_op jit(solution)/shard_map/ppermute | solution.py:389
  125.3 4.3 %collective-permute-done.13.refs_6_ = f32[232,128]{1,0:T(8,128)S(1)} collective-permute-done((f32[232,128]{1,0:T(8,128)S(1)}, f32[232,128]{1,0:T(8,128)S(1)}, u32[]{:S(2)}, u32[]{:S(2)}) %collective-permute-start.13) | collective-permute-done | bytes 118816 | tf_op jit(solution)/shard_map/ppermute | solution.py:396
  131.1 9.4 %collective-permute-start.15 = (f32[136,128]{1,0:T(8,128)S(1)}, f32[136,128]{1,0:T(8,128)S(1)}, u32[]{:S(2)}, u32[]{:S(2)}) collective-permute-start(f32[136,128]{1,0:T(8,128)S(1)} %get-tuple-element.97), channel_id=1, source_target_pairs={{1,2},{2,1},{3,4},{4,3},{5,6},{6,5},{7,8},{8,7},{9,10},{10,9},{11,... | collective-permute-start | bytes 208904 | tf_op jit(solution)/shard_map/ppermute | solution.py:396
  140.5 1.9 %collective-permute-start.14 = (f32[4,32,128]{2,1,0:T(8,128)S(1)}, f32[4,32,128]{2,1,0:T(8,128)S(1)}, u32[]{:S(2)}, u32[]{:S(2)}) collective-permute-start(f32[4,32,128]{2,1,0:T(8,128)S(1)} %get-tuple-element.96), channel_id=1, source_target_pairs={{1,0},{0,1},{3,2},{2,3},{5,4},{4,5},{7,6},{6,7},{9,8},{8,9},{11,10... | collective-permute-start | bytes 196616 | tf_op jit(solution)/shard_map/ppermute | solution.py:389
  143.9 3.6 %collective-permute-done.15.scaled_b = f32[136,128]{1,0:T(8,128)S(1)} collective-permute-done((f32[136,128]{1,0:T(8,128)S(1)}, f32[136,128]{1,0:T(8,128)S(1)}, u32[]{:S(2)}, u32[]{:S(2)}) %collective-permute-start.15) | collective-permute-done | bytes 69664 | tf_op jit(solution)/shard_map/ppermute | solution.py:396
  148.6 26.1 %all_to_all.10.arrived = f32[32,2,8,128]{3,2,1,0:T(8,128)S(1)} all-to-all(f32[32,2,8,128]{3,2,1,0:T(8,128)S(1)} %bitcast.54), channel_id=1, replica_groups=mesh['shot'=32,'dom'=16] {'shot'}, dimensions={0} | all-to-all | bytes 524288 | tf_op jit(solution)/shard_map/all_to_all | solution.py:530
  (52 shorter events, 21.3 us)
Async XLA Ops:
  0.6 0.7 copy-start.6
  3.0 15.4 %copy-start = (f32[1,8,32,128]{3,2,1,0:T(8,128)S(1)}, f32[1,8,32,128]{3,2,1,0:T(8,128)}, u32[]{:S(2)}) copy-start(f32[1,8,32,128]{3,2,1,0:T(8,128)} %param.11) | copy-start | bytes 393220
  3.0 34.1 %all-to-all-start = ((f32[32,2,8,128]{3,2,1,0:T(8,128)}), f32[32,2,8,128]{3,2,1,0:T(8,128)S(1)}, u32[]{:S(2)}, u32[]{:S(2)}) async-start(f32[32,2,8,128]{3,2,1,0:T(8,128)} %select_select_fusion), calls=%async_computation | async-start | bytes 524288 | tf_op jit(solution)/shard_map/all_to_all | solution.py:426
  18.4 11.5 %copy-start.7 = (f32[1,3,512]{2,0,1:T(1,128)S(1)}, f32[1,3,512]{2,0,1:T(1,128)}, u32[]{:S(2)}) copy-start(f32[1,3,512]{2,0,1:T(1,128)} %param.21) | copy-start | bytes 18436
  18.4 11.7 %copy-start.2 = (f32[1,8,32,128]{3,2,1,0:T(8,128)S(1)}, f32[1,8,32,128]{3,2,1,0:T(8,128)}, u32[]{:S(2)}) copy-start(f32[1,8,32,128]{3,2,1,0:T(8,128)} %param.13) | copy-start | bytes 393220
  18.4 11.7 %copy-start.3 = (f32[1,8,32,128]{3,2,1,0:T(8,128)S(1)}, f32[1,8,32,128]{3,2,1,0:T(8,128)}, u32[]{:S(2)}) copy-start(f32[1,8,32,128]{3,2,1,0:T(8,128)} %param.14) | copy-start | bytes 393220
  18.5 11.6 %copy-start.1 = (f32[1,8,32,128]{3,2,1,0:T(8,128)S(1)}, f32[1,8,32,128]{3,2,1,0:T(8,128)}, u32[]{:S(2)}) copy-start(f32[1,8,32,128]{3,2,1,0:T(8,128)} %param.12) | copy-start | bytes 393220
  18.5 30.9 %collective-permute-start.1 = (f32[7,32,128]{2,1,0:T(8,128)S(1)}, f32[7,32,128]{2,1,0:T(8,128)S(1)}, u32[]{:S(2)}, u32[]{:S(2)}) collective-permute-start(f32[7,32,128]{2,1,0:T(8,128)S(1)} %get-tuple-element.116), channel_id=1, source_target_pairs={{1,2},{2,1},{3,4},{4,3},{5,6},{6,5},{7,8},{8,7},{9,10},{10,9},{11,... | collective-permute-start | bytes 344072 | tf_op jit(solution)/shard_map/ppermute | solution.py:396
  27.3 22.0 %collective-permute-start = (f32[7,32,128]{2,1,0:T(8,128)S(1)}, f32[7,32,128]{2,1,0:T(8,128)S(1)}, u32[]{:S(2)}, u32[]{:S(2)}) collective-permute-start(f32[7,32,128]{2,1,0:T(8,128)S(1)} %get-tuple-element.117), channel_id=1, source_target_pairs={{1,0},{0,1},{3,2},{2,3},{5,4},{4,5},{7,6},{6,7},{9,8},{8,9},{11,10... | collective-permute-start | bytes 344072 | tf_op jit(solution)/shard_map/ppermute | solution.py:389
  30.1 0.7 copy-start.5
  37.9 16.5 %collective-permute-start.3 = (f32[136,128]{1,0:T(8,128)S(1)}, f32[136,128]{1,0:T(8,128)S(1)}, u32[]{:S(2)}, u32[]{:S(2)}) collective-permute-start(f32[136,128]{1,0:T(8,128)S(1)} %get-tuple-element.73), channel_id=1, source_target_pairs={{1,2},{2,1},{3,4},{4,3},{5,6},{6,5},{7,8},{8,7},{9,10},{10,9},{11,... | collective-permute-start | bytes 208904 | tf_op jit(solution)/shard_map/ppermute | solution.py:396
  47.4 3.1 %collective-permute-start.2 = (f32[4,32,128]{2,1,0:T(8,128)S(1)}, f32[4,32,128]{2,1,0:T(8,128)S(1)}, u32[]{:S(2)}, u32[]{:S(2)}) collective-permute-start(f32[4,32,128]{2,1,0:T(8,128)S(1)} %get-tuple-element.72), channel_id=1, source_target_pairs={{1,0},{0,1},{3,2},{2,3},{5,4},{4,5},{7,6},{6,7},{9,8},{8,9},{11,10... | collective-permute-start | bytes 196616 | tf_op jit(solution)/shard_map/ppermute | solution.py:389
  55.9 18.3 %collective-permute-start.5 = (f32[232,128]{1,0:T(8,128)S(1)}, f32[232,128]{1,0:T(8,128)S(1)}, u32[]{:S(2)}, u32[]{:S(2)}) collective-permute-start(f32[232,128]{1,0:T(8,128)S(1)} %get-tuple-element.77), channel_id=1, source_target_pairs={{1,2},{2,1},{3,4},{4,3},{5,6},{6,5},{7,8},{8,7},{9,10},{10,9},{11,... | collective-permute-start | bytes 356360 | tf_op jit(solution)/shard_map/ppermute | solution.py:396
  65.4 8.8 %collective-permute-start.4 = (f32[7,32,128]{2,1,0:T(8,128)S(1)}, f32[7,32,128]{2,1,0:T(8,128)S(1)}, u32[]{:S(2)}, u32[]{:S(2)}) collective-permute-start(f32[7,32,128]{2,1,0:T(8,128)S(1)} %get-tuple-element.76), channel_id=1, source_target_pairs={{1,0},{0,1},{3,2},{2,3},{5,4},{4,5},{7,6},{6,7},{9,8},{8,9},{11,10... | collective-permute-start | bytes 344072 | tf_op jit(solution)/shard_map/ppermute | solution.py:389
  67.3 22.2 %collective-permute-start.9 = (f32[232,128]{1,0:T(8,128)S(1)}, f32[232,128]{1,0:T(8,128)S(1)}, u32[]{:S(2)}, u32[]{:S(2)}) collective-permute-start(f32[232,128]{1,0:T(8,128)S(1)} %get-tuple-element.84), channel_id=1, source_target_pairs={{1,2},{2,1},{3,4},{4,3},{5,6},{6,5},{7,8},{8,7},{9,10},{10,9},{11,... | collective-permute-start | bytes 356360 | tf_op jit(solution)/shard_map/ppermute | solution.py:396
  75.7 17.0 %collective-permute-start.7 = (f32[232,128]{1,0:T(8,128)S(1)}, f32[232,128]{1,0:T(8,128)S(1)}, u32[]{:S(2)}, u32[]{:S(2)}) collective-permute-start(f32[232,128]{1,0:T(8,128)S(1)} %get-tuple-element.81), channel_id=1, source_target_pairs={{1,2},{2,1},{3,4},{4,3},{5,6},{6,5},{7,8},{8,7},{9,10},{10,9},{11,... | collective-permute-start | bytes 356360 | tf_op jit(solution)/shard_map/ppermute | solution.py:396
  85.2 4.3 %collective-permute-start.8 = (f32[7,32,128]{2,1,0:T(8,128)S(1)}, f32[7,32,128]{2,1,0:T(8,128)S(1)}, u32[]{:S(2)}, u32[]{:S(2)}) collective-permute-start(f32[7,32,128]{2,1,0:T(8,128)S(1)} %get-tuple-element.83), channel_id=1, source_target_pairs={{1,0},{0,1},{3,2},{2,3},{5,4},{4,5},{7,6},{6,7},{9,8},{8,9},{11,10... | collective-permute-start | bytes 344072 | tf_op jit(solution)/shard_map/ppermute | solution.py:389
  87.1 3.8 %collective-permute-start.6 = (f32[7,32,128]{2,1,0:T(8,128)S(1)}, f32[7,32,128]{2,1,0:T(8,128)S(1)}, u32[]{:S(2)}, u32[]{:S(2)}) collective-permute-start(f32[7,32,128]{2,1,0:T(8,128)S(1)} %get-tuple-element.80), channel_id=1, source_target_pairs={{1,0},{0,1},{3,2},{2,3},{5,4},{4,5},{7,6},{6,7},{9,8},{8,9},{11,10... | collective-permute-start | bytes 344072 | tf_op jit(solution)/shard_map/ppermute | solution.py:389
  94.2 17.0 %collective-permute-start.11 = (f32[232,128]{1,0:T(8,128)S(1)}, f32[232,128]{1,0:T(8,128)S(1)}, u32[]{:S(2)}, u32[]{:S(2)}) collective-permute-start(f32[232,128]{1,0:T(8,128)S(1)} %get-tuple-element.89), channel_id=1, source_target_pairs={{1,2},{2,1},{3,4},{4,3},{5,6},{6,5},{7,8},{8,7},{9,10},{10,9},{11,... | collective-permute-start | bytes 356360 | tf_op jit(solution)/shard_map/ppermute | solution.py:396
  103.7 3.2 %collective-permute-start.10 = (f32[7,32,128]{2,1,0:T(8,128)S(1)}, f32[7,32,128]{2,1,0:T(8,128)S(1)}, u32[]{:S(2)}, u32[]{:S(2)}) collective-permute-start(f32[7,32,128]{2,1,0:T(8,128)S(1)} %get-tuple-element.88), channel_id=1, source_target_pairs={{1,0},{0,1},{3,2},{2,3},{5,4},{4,5},{7,6},{6,7},{9,8},{8,9},{11,10... | collective-permute-start | bytes 344072 | tf_op jit(solution)/shard_map/ppermute | solution.py:389
  112.6 17.0 %collective-permute-start.13 = (f32[232,128]{1,0:T(8,128)S(1)}, f32[232,128]{1,0:T(8,128)S(1)}, u32[]{:S(2)}, u32[]{:S(2)}) collective-permute-start(f32[232,128]{1,0:T(8,128)S(1)} %get-tuple-element.93), channel_id=1, source_target_pairs={{1,2},{2,1},{3,4},{4,3},{5,6},{6,5},{7,8},{8,7},{9,10},{10,9},{11,... | collective-permute-start | bytes 356360 | tf_op jit(solution)/shard_map/ppermute | solution.py:396
  122.1 3.2 %collective-permute-start.12 = (f32[7,32,128]{2,1,0:T(8,128)S(1)}, f32[7,32,128]{2,1,0:T(8,128)S(1)}, u32[]{:S(2)}, u32[]{:S(2)}) collective-permute-start(f32[7,32,128]{2,1,0:T(8,128)S(1)} %get-tuple-element.92), channel_id=1, source_target_pairs={{1,0},{0,1},{3,2},{2,3},{5,4},{4,5},{7,6},{6,7},{9,8},{8,9},{11,10... | collective-permute-start | bytes 344072 | tf_op jit(solution)/shard_map/ppermute | solution.py:389
  131.1 16.5 %collective-permute-start.15 = (f32[136,128]{1,0:T(8,128)S(1)}, f32[136,128]{1,0:T(8,128)S(1)}, u32[]{:S(2)}, u32[]{:S(2)}) collective-permute-start(f32[136,128]{1,0:T(8,128)S(1)} %get-tuple-element.97), channel_id=1, source_target_pairs={{1,2},{2,1},{3,4},{4,3},{5,6},{6,5},{7,8},{8,7},{9,10},{10,9},{11,... | collective-permute-start | bytes 208904 | tf_op jit(solution)/shard_map/ppermute | solution.py:396
  140.5 3.4 %collective-permute-start.14 = (f32[4,32,128]{2,1,0:T(8,128)S(1)}, f32[4,32,128]{2,1,0:T(8,128)S(1)}, u32[]{:S(2)}, u32[]{:S(2)}) collective-permute-start(f32[4,32,128]{2,1,0:T(8,128)S(1)} %get-tuple-element.96), channel_id=1, source_target_pairs={{1,0},{0,1},{3,2},{2,3},{5,4},{4,5},{7,6},{6,7},{9,8},{8,9},{11,10... | collective-permute-start | bytes 196616 | tf_op jit(solution)/shard_map/ppermute | solution.py:389
  (1 other events, 0.7 us)

commit v11 on v10

--- a/solution.py
+++ b/solution.py
@@ -83,6 +83,19 @@
     @pl.when(jnp.logical_not(odd))
     def _():
         target[...] = tail()
+
+
+def choose_kernel(where, aperture, kappa, buoy, out):
+    lanes = lax.broadcasted_iota(jnp.int32, aperture.shape, 1)
+    mine = jnp.where(lanes == where[0], aperture[...], 0).astype(F32)
+    tiles = jnp.broadcast_to(jnp.sum(mine, axis=1, keepdims=True), (aperture.shape[0], CZ))
+    for s in range(out.shape[0]):
+        tile = jnp.broadcast_to(tiles[s : s + 1, :], (CX, CZ))
+        for half, model in enumerate((kappa, buoy)):
+            value = model[0]
+            for t in range(1, TILES):
+                value = jnp.where(tile == float(t), model[t], value)
+            out[s, half] = value
 
 
 def hand_over(info, send_a, send_b, field):
@@ -197,7 +210,8 @@
     send_b[4 * CY :, :] = jnp.zeros((8, CZ), F32)
 
 
-def widen_kernel(info, now, now_a, now_b, out):
+def widen_kernel(info, now, now_a, now_b, scaled, out, near, far):
+    hand_over(info, near, far, scaled)
     place(info, out, now, lambda: now_a[...], lambda: now_b[...], 7)
 
 
@@ -229,8 +243,8 @@
 
 
 def first_kernel(
-    info, tables, padded, base, source, stiff, buoy, edge_a, edge_b, scaled,
-    p_out, send_a, send_b, near, far, div_out, slope_out, buoy_out,
+    info, tables, padded, base, source, stiff, buoy, edge_a, edge_b,
+    p_out, send_a, send_b, div_out, slope_out, buoy_out,
     gx, gy, acc,
 ):
     widen_buoy(info, buoy, edge_a, edge_b, buoy_out)
@@ -243,7 +257,6 @@
         stiff, padded, buoy_out, tables, gx, gy, acc, div_out, slope_out, store,
     )
     hand_over(info, send_a, send_b, p_out)
-    hand_over(info, near, far, scaled)
 
 
 def adjoint_part_kernel(
@@ -338,14 +351,13 @@
         out[1, cell] = images[1, cell] + (rho + slope_p[2, cell] * slope_q[2, cell])
 
 
-def image_kernel(info, q_now, scaled, scaled_a, scaled_b, div, slope, images, out, field):
-    lane = lax.broadcasted_iota(jnp.int32, (CY, CZ), 1)
+def image_kernel(info, tables, q_now, scaled, scaled_a, scaled_b, div, slope, images, out, field):
     place(info, field, scaled, lambda: scaled_a[...], lambda: planes_at(scaled_b, 0, 4), 4)
+    along = along_z(field[4 : 4 + CX, PAD : PAD + CY, :], tables[0])
     for cell in range(CX):
-        plane = field[cell + 4, PAD : PAD + CY, :]
         rho = images[1, cell] + slope[0, cell] * slope_x(field, cell + 4)
         rho = rho + slope[1, cell] * slope_y(field, cell + 4)
-        rho = rho + slope[2, cell] * slope_z(plane, lane)
+        rho = rho + slope[2, cell] * along[cell]
         out[0, cell] = step_squared * (images[0, cell] + q_now[cell] * div[cell])
         out[1, cell] = -step_squared * rho
 
@@ -418,11 +430,12 @@
     ).astype(jnp.int32)
 
     column = lax.dynamic_index_in_dim(aperture, dom, 1, keepdims=False)
-    stacked = jnp.stack((kappa_model, buoy_model), axis=1)
-    picks = column[:, None, None, None]
-    chosen = stacked[0][None]
-    for t in range(1, TILES):
-        chosen = jnp.where(picks == t, stacked[t][None], chosen)
+    (chosen,) = call(
+        choose_kernel,
+        [dom.reshape(1).astype(jnp.int32)],
+        [aperture, kappa_model, buoy_model],
+        [jax.ShapeDtypeStruct((aperture.shape[0], 2, CX, CZ), F32)],
+    )
     block = lax.all_to_all(chosen, "shot", 0, 0, tiled=True)
 
     p0, p_prev = pressure_now[0], pressure_prev[0]
@@ -457,17 +470,17 @@
     edge_b = swap_second(send_b)
     edge_a = swap_first(send_a)
 
-    (padded,) = call(
+    padded, near, far = call(
         widen_kernel,
         [info],
-        [p0, p0_a, p0_b],
-        [jax.ShapeDtypeStruct((WIDE, ROWS, CZ), F32)],
-    )
-    p1, send_a, send_b, near, far, div0, slope0, wide = call(
+        [p0, p0_a, p0_b, f4],
+        [jax.ShapeDtypeStruct((WIDE, ROWS, CZ), F32), seven, far_rows(7)],
+    )
+    p1, send_a, send_b, div0, slope0, wide = call(
         first_kernel,
         [info],
-        [tables, padded, base_p, source_planes, stiff, buoy, edge_a, edge_b, f4],
-        [own, seven, far_rows(7), seven, far_rows(7), own, slopes, plane_field(CX + 8)],
+        [tables, padded, base_p, source_planes, stiff, buoy, edge_a, edge_b],
+        [own, seven, far_rows(7), own, slopes, plane_field(CX + 8)],
         work()[1:],
     )
     from_b = swap_second(send_b)
@@ -523,7 +536,7 @@
     (image,) = call(
         image_kernel,
         [info],
-        [q1, f1, from_a, from_b, div0, slope0, image],
+        [tables, q1, f1, from_a, from_b, div0, slope0, image],
         [images],
         [pltpu.VMEM((CX + 8, ROWS, CZ), F32)],
     )

time: 176 us -> 177 us (level)
  other arithmetic: 2.35 us -> 0.03 us
  local copies, waits for them, and re-layouts: 1.13 us -> 3.32 us
    pallas_call x13 -> x14, Pallas kernels: 14.6 us -> 15.4 us  [call(): pl.pallas_call(kernel, out_shape=outs, in_specs=[SMEM] * len(scalars) + [...]
  transfers between devices with their start and end apart: 17 -> 17, of which waited for: 9 -> 9; matrix products, arithmetic and copies ran while one was open for 0% -> 1% of each run, Pallas kernels for 4% -> 4%
where the time goes in v11:
time: 177 us; the launch traced here: 176 us
  starting transfers between devices  103 us (58%)
  blocking collectives  26 us (15%)
  waiting for transfers between devices  25.9 us (15%)
  Pallas kernels  15.4 us (9%)
  local copies, waits for them, and re-layouts  3.32 us (2%)
    ppermute x8, starting transfers between devices, swap_second(): return lax.ppermute(planes, 'dom', pairs)  72 us
    all_to_all x1, blocking collectives, shards(): lax.all_to_all(image.transpose(2, 0, 1, 3), 'shot', 0, 0, tiled=True)  26 us
    ppermute x8, waiting for transfers between devices, swap_second(): return lax.ppermute(planes, 'dom', pairs)  18.5 us
    ppermute x8, starting transfers between devices, swap_first(): return lax.ppermute(planes, 'dom', [(i ^ 1, i) for i in range(count)])  15.9 us
    pallas_call x14, Pallas kernels, call(): pl.pallas_call(kernel, out_shape=outs, in_specs=[SMEM] * len(scalars) + [...  15.4 us
    all_to_all x1, starting transfers between devices, shards(): block = lax.all_to_all(chosen, 'shot', 0, 0, tiled=True)  15.4 us
    all_to_all x1, waiting for transfers between devices, shards(): block = lax.all_to_all(chosen, 'shot', 0, 0, tiled=True)  4.18 us
  transfers between devices with their start and end apart: 17, of which 9 were waited for; matrix products, arithmetic and copies ran while one was open for 1% of the time, Pallas kernels for 4%

profile of v11, /device:TPU:7, one launch (start us, length us, event | category | flops | bytes accessed | tf_op | source)
XLA Modules:
  0.0 175.6 jit_solution(14684478902823447310)
XLA Ops:
  3.0 15.4 %all-to-all-start = ((f32[32,2,8,128]{3,2,1,0:T(8,128)}), f32[32,2,8,128]{3,2,1,0:T(8,128)S(1)}, u32[]{:S(2)}, u32[]{:S(2)}) async-start(f32[32,2,8,128]{3,2,1,0:T(8,128)} %shard_map.138), calls=%async_computation | async-start | bytes 524288 | tf_op jit(solution)/shard_map/all_to_all | solution.py:439
  18.5 8.8 %collective-permute-start.1 = (f32[7,32,128]{2,1,0:T(8,128)S(1)}, f32[7,32,128]{2,1,0:T(8,128)S(1)}, u32[]{:S(2)}, u32[]{:S(2)}) collective-permute-start(f32[7,32,128]{2,1,0:T(8,128)S(1)} %get-tuple-element.116), channel_id=1, source_target_pairs={{1,2},{2,1},{3,4},{4,3},{5,6},{6,5},{7,8},{8,7},{9,10},{10,9},{11,... | collective-permute-start | bytes 344072 | tf_op jit(solution)/shard_map/ppermute | solution.py:408
  27.3 1.9 %collective-permute-start = (f32[7,32,128]{2,1,0:T(8,128)S(1)}, f32[7,32,128]{2,1,0:T(8,128)S(1)}, u32[]{:S(2)}, u32[]{:S(2)}) collective-permute-start(f32[7,32,128]{2,1,0:T(8,128)S(1)} %get-tuple-element.117), channel_id=1, source_target_pairs={{1,0},{0,1},{3,2},{2,3},{5,4},{4,5},{7,6},{6,7},{9,8},{8,9},{11,10... | collective-permute-start | bytes 344072 | tf_op jit(solution)/shard_map/ppermute | solution.py:401
  32.9 4.2 %all-to-all-done = f32[32,2,8,128]{3,2,1,0:T(8,128)S(1)} async-done(((f32[32,2,8,128]{3,2,1,0:T(8,128)}), f32[32,2,8,128]{3,2,1,0:T(8,128)S(1)}, u32[]{:S(2)}, u32[]{:S(2)}) %all-to-all-start) | async-done | bytes 262176 | tf_op jit(solution)/shard_map/all_to_all | solution.py:439
  37.9 9.5 %collective-permute-start.3 = (f32[136,128]{1,0:T(8,128)S(1)}, f32[136,128]{1,0:T(8,128)S(1)}, u32[]{:S(2)}, u32[]{:S(2)}) collective-permute-start(f32[136,128]{1,0:T(8,128)S(1)} %get-tuple-element.76), channel_id=1, source_target_pairs={{1,2},{2,1},{3,4},{4,3},{5,6},{6,5},{7,8},{8,7},{9,10},{10,9},{11,... | collective-permute-start | bytes 208904 | tf_op jit(solution)/shard_map/ppermute | solution.py:408
  47.4 1.9 %collective-permute-start.2 = (f32[4,32,128]{2,1,0:T(8,128)S(1)}, f32[4,32,128]{2,1,0:T(8,128)S(1)}, u32[]{:S(2)}, u32[]{:S(2)}) collective-permute-start(f32[4,32,128]{2,1,0:T(8,128)S(1)} %get-tuple-element.75), channel_id=1, source_target_pairs={{1,0},{0,1},{3,2},{2,3},{5,4},{4,5},{7,6},{6,7},{9,8},{8,9},{11,10... | collective-permute-start | bytes 196616 | tf_op jit(solution)/shard_map/ppermute | solution.py:401
  50.5 3.8 %collective-permute-done.3.edge_b = f32[136,128]{1,0:T(8,128)S(1)} collective-permute-done((f32[136,128]{1,0:T(8,128)S(1)}, f32[136,128]{1,0:T(8,128)S(1)}, u32[]{:S(2)}, u32[]{:S(2)}) %collective-permute-start.3) | collective-permute-done | bytes 69664 | tf_op jit(solution)/shard_map/ppermute | solution.py:408
  55.8 9.5 %collective-permute-start.5 = (f32[232,128]{1,0:T(8,128)S(1)}, f32[232,128]{1,0:T(8,128)S(1)}, u32[]{:S(2)}, u32[]{:S(2)}) collective-permute-start(f32[232,128]{1,0:T(8,128)S(1)} %get-tuple-element.79), channel_id=1, source_target_pairs={{1,2},{2,1},{3,4},{4,3},{5,6},{6,5},{7,8},{8,7},{9,10},{10,9},{11,... | collective-permute-start | bytes 356360 | tf_op jit(solution)/shard_map/ppermute | solution.py:408
  65.3 1.9 %collective-permute-start.4 = (f32[7,32,128]{2,1,0:T(8,128)S(1)}, f32[7,32,128]{2,1,0:T(8,128)S(1)}, u32[]{:S(2)}, u32[]{:S(2)}) collective-permute-start(f32[7,32,128]{2,1,0:T(8,128)S(1)} %get-tuple-element.78), channel_id=1, source_target_pairs={{1,0},{0,1},{3,2},{2,3},{5,4},{4,5},{7,6},{6,7},{9,8},{8,9},{11,10... | collective-permute-start | bytes 344072 | tf_op jit(solution)/shard_map/ppermute | solution.py:401
  67.2 6.9 %collective-permute-start.9 = (f32[232,128]{1,0:T(8,128)S(1)}, f32[232,128]{1,0:T(8,128)S(1)}, u32[]{:S(2)}, u32[]{:S(2)}) collective-permute-start(f32[232,128]{1,0:T(8,128)S(1)} %get-tuple-element.86), channel_id=1, source_target_pairs={{1,2},{2,1},{3,4},{4,3},{5,6},{6,5},{7,8},{8,7},{9,10},{10,9},{11,... | collective-permute-start | bytes 356360 | tf_op jit(solution)/shard_map/ppermute | solution.py:408
  75.6 9.5 %collective-permute-start.7 = (f32[232,128]{1,0:T(8,128)S(1)}, f32[232,128]{1,0:T(8,128)S(1)}, u32[]{:S(2)}, u32[]{:S(2)}) collective-permute-start(f32[232,128]{1,0:T(8,128)S(1)} %get-tuple-element.83), channel_id=1, source_target_pairs={{1,2},{2,1},{3,4},{4,3},{5,6},{6,5},{7,8},{8,7},{9,10},{10,9},{11,... | collective-permute-start | bytes 356360 | tf_op jit(solution)/shard_map/ppermute | solution.py:408
  85.1 1.9 %collective-permute-start.8 = (f32[7,32,128]{2,1,0:T(8,128)S(1)}, f32[7,32,128]{2,1,0:T(8,128)S(1)}, u32[]{:S(2)}, u32[]{:S(2)}) collective-permute-start(f32[7,32,128]{2,1,0:T(8,128)S(1)} %get-tuple-element.85), channel_id=1, source_target_pairs={{1,0},{0,1},{3,2},{2,3},{5,4},{4,5},{7,6},{6,7},{9,8},{8,9},{11,10... | collective-permute-start | bytes 344072 | tf_op jit(solution)/shard_map/ppermute | solution.py:401
  87.1 2.4 %collective-permute-start.6 = (f32[7,32,128]{2,1,0:T(8,128)S(1)}, f32[7,32,128]{2,1,0:T(8,128)S(1)}, u32[]{:S(2)}, u32[]{:S(2)}) collective-permute-start(f32[7,32,128]{2,1,0:T(8,128)S(1)} %get-tuple-element.82), channel_id=1, source_target_pairs={{1,0},{0,1},{3,2},{2,3},{5,4},{4,5},{7,6},{6,7},{9,8},{8,9},{11,10... | collective-permute-start | bytes 344072 | tf_op jit(solution)/shard_map/ppermute | solution.py:401
  90.9 1.8 %collective-permute-done.7.now_b = f32[232,128]{1,0:T(8,128)S(1)} collective-permute-done((f32[232,128]{1,0:T(8,128)S(1)}, f32[232,128]{1,0:T(8,128)S(1)}, u32[]{:S(2)}, u32[]{:S(2)}) %collective-permute-start.7) | collective-permute-done | bytes 118816 | tf_op jit(solution)/shard_map/ppermute | solution.py:408
  94.2 9.4 %collective-permute-start.11 = (f32[232,128]{1,0:T(8,128)S(1)}, f32[232,128]{1,0:T(8,128)S(1)}, u32[]{:S(2)}, u32[]{:S(2)}) collective-permute-start(f32[232,128]{1,0:T(8,128)S(1)} %get-tuple-element.91), channel_id=1, source_target_pairs={{1,2},{2,1},{3,4},{4,3},{5,6},{6,5},{7,8},{8,7},{9,10},{10,9},{11,... | collective-permute-start | bytes 356360 | tf_op jit(solution)/shard_map/ppermute | solution.py:408
  103.6 1.9 %collective-permute-start.10 = (f32[7,32,128]{2,1,0:T(8,128)S(1)}, f32[7,32,128]{2,1,0:T(8,128)S(1)}, u32[]{:S(2)}, u32[]{:S(2)}) collective-permute-start(f32[7,32,128]{2,1,0:T(8,128)S(1)} %get-tuple-element.90), channel_id=1, source_target_pairs={{1,0},{0,1},{3,2},{2,3},{5,4},{4,5},{7,6},{6,7},{9,8},{8,9},{11,10... | collective-permute-start | bytes 344072 | tf_op jit(solution)/shard_map/ppermute | solution.py:401
  106.8 4.5 %collective-permute-done.11.refs_6_ = f32[232,128]{1,0:T(8,128)S(1)} collective-permute-done((f32[232,128]{1,0:T(8,128)S(1)}, f32[232,128]{1,0:T(8,128)S(1)}, u32[]{:S(2)}, u32[]{:S(2)}) %collective-permute-start.11) | collective-permute-done | bytes 118816 | tf_op jit(solution)/shard_map/ppermute | solution.py:408
  112.8 9.2 %collective-permute-start.13 = (f32[232,128]{1,0:T(8,128)S(1)}, f32[232,128]{1,0:T(8,128)S(1)}, u32[]{:S(2)}, u32[]{:S(2)}) collective-permute-start(f32[232,128]{1,0:T(8,128)S(1)} %get-tuple-element.95), channel_id=1, source_target_pairs={{1,2},{2,1},{3,4},{4,3},{5,6},{6,5},{7,8},{8,7},{9,10},{10,9},{11,... | collective-permute-start | bytes 356360 | tf_op jit(solution)/shard_map/ppermute | solution.py:408
  122.1 1.9 %collective-permute-start.12 = (f32[7,32,128]{2,1,0:T(8,128)S(1)}, f32[7,32,128]{2,1,0:T(8,128)S(1)}, u32[]{:S(2)}, u32[]{:S(2)}) collective-permute-start(f32[7,32,128]{2,1,0:T(8,128)S(1)} %get-tuple-element.94), channel_id=1, source_target_pairs={{1,0},{0,1},{3,2},{2,3},{5,4},{4,5},{7,6},{6,7},{9,8},{8,9},{11,10... | collective-permute-start | bytes 344072 | tf_op jit(solution)/shard_map/ppermute | solution.py:401
  125.3 4.6 %collective-permute-done.13.refs_6_ = f32[232,128]{1,0:T(8,128)S(1)} collective-permute-done((f32[232,128]{1,0:T(8,128)S(1)}, f32[232,128]{1,0:T(8,128)S(1)}, u32[]{:S(2)}, u32[]{:S(2)}) %collective-permute-start.13) | collective-permute-done | bytes 118816 | tf_op jit(solution)/shard_map/ppermute | solution.py:408
  131.3 9.2 %collective-permute-start.15 = (f32[136,128]{1,0:T(8,128)S(1)}, f32[136,128]{1,0:T(8,128)S(1)}, u32[]{:S(2)}, u32[]{:S(2)}) collective-permute-start(f32[136,128]{1,0:T(8,128)S(1)} %get-tuple-element.99), channel_id=1, source_target_pairs={{1,2},{2,1},{3,4},{4,3},{5,6},{6,5},{7,8},{8,7},{9,10},{10,9},{11,... | collective-permute-start | bytes 208904 | tf_op jit(solution)/shard_map/ppermute | solution.py:408
  140.5 1.9 %collective-permute-start.14 = (f32[4,32,128]{2,1,0:T(8,128)S(1)}, f32[4,32,128]{2,1,0:T(8,128)S(1)}, u32[]{:S(2)}, u32[]{:S(2)}) collective-permute-start(f32[4,32,128]{2,1,0:T(8,128)S(1)} %get-tuple-element.98), channel_id=1, source_target_pairs={{1,0},{0,1},{3,2},{2,3},{5,4},{4,5},{7,6},{6,7},{9,8},{8,9},{11,10... | collective-permute-start | bytes 196616 | tf_op jit(solution)/shard_map/ppermute | solution.py:401
  143.9 3.9 %collective-permute-done.15.scaled_b = f32[136,128]{1,0:T(8,128)S(1)} collective-permute-done((f32[136,128]{1,0:T(8,128)S(1)}, f32[136,128]{1,0:T(8,128)S(1)}, u32[]{:S(2)}, u32[]{:S(2)}) %collective-permute-start.15) | collective-permute-done | bytes 69664 | tf_op jit(solution)/shard_map/ppermute | solution.py:408
  148.8 26.0 %all_to_all.10.arrived = f32[32,2,8,128]{3,2,1,0:T(8,128)S(1)} all-to-all(f32[32,2,8,128]{3,2,1,0:T(8,128)S(1)} %bitcast.44), channel_id=1, replica_groups=mesh['shot'=32,'dom'=16] {'shot'}, dimensions={0} | all-to-all | bytes 524288 | tf_op jit(solution)/shard_map/all_to_all | solution.py:543
  (53 shorter events, 21.9 us)
Async XLA Ops:
  0.6 0.8 copy-start.1
  1.4 0.7 copy-start.2
  3.0 15.4 %copy-start = (f32[1,8,32,128]{3,2,1,0:T(8,128)S(1)}, f32[1,8,32,128]{3,2,1,0:T(8,128)}, u32[]{:S(2)}) copy-start(f32[1,8,32,128]{3,2,1,0:T(8,128)} %param.11) | copy-start | bytes 393220
  3.0 34.1 %all-to-all-start = ((f32[32,2,8,128]{3,2,1,0:T(8,128)}), f32[32,2,8,128]{3,2,1,0:T(8,128)S(1)}, u32[]{:S(2)}, u32[]{:S(2)}) async-start(f32[32,2,8,128]{3,2,1,0:T(8,128)} %shard_map.138), calls=%async_computation | async-start | bytes 524288 | tf_op jit(solution)/shard_map/all_to_all | solution.py:439
  18.4 11.5 %copy-start.8 = (f32[1,3,512]{2,0,1:T(1,128)S(1)}, f32[1,3,512]{2,0,1:T(1,128)}, u32[]{:S(2)}) copy-start(f32[1,3,512]{2,0,1:T(1,128)} %param.21) | copy-start | bytes 18436
  18.4 11.7 %copy-start.4 = (f32[1,8,32,128]{3,2,1,0:T(8,128)S(1)}, f32[1,8,32,128]{3,2,1,0:T(8,128)}, u32[]{:S(2)}) copy-start(f32[1,8,32,128]{3,2,1,0:T(8,128)} %param.13) | copy-start | bytes 393220
  18.4 11.7 %copy-start.5 = (f32[1,8,32,128]{3,2,1,0:T(8,128)S(1)}, f32[1,8,32,128]{3,2,1,0:T(8,128)}, u32[]{:S(2)}) copy-start(f32[1,8,32,128]{3,2,1,0:T(8,128)} %param.14) | copy-start | bytes 393220
  18.4 11.6 %copy-start.3 = (f32[1,8,32,128]{3,2,1,0:T(8,128)S(1)}, f32[1,8,32,128]{3,2,1,0:T(8,128)}, u32[]{:S(2)}) copy-start(f32[1,8,32,128]{3,2,1,0:T(8,128)} %param.12) | copy-start | bytes 393220
  18.5 30.9 %collective-permute-start.1 = (f32[7,32,128]{2,1,0:T(8,128)S(1)}, f32[7,32,128]{2,1,0:T(8,128)S(1)}, u32[]{:S(2)}, u32[]{:S(2)}) collective-permute-start(f32[7,32,128]{2,1,0:T(8,128)S(1)} %get-tuple-element.116), channel_id=1, source_target_pairs={{1,2},{2,1},{3,4},{4,3},{5,6},{6,5},{7,8},{8,7},{9,10},{10,9},{11,... | collective-permute-start | bytes 344072 | tf_op jit(solution)/shard_map/ppermute | solution.py:408
  27.3 22.0 %collective-permute-start = (f32[7,32,128]{2,1,0:T(8,128)S(1)}, f32[7,32,128]{2,1,0:T(8,128)S(1)}, u32[]{:S(2)}, u32[]{:S(2)}) collective-permute-start(f32[7,32,128]{2,1,0:T(8,128)S(1)} %get-tuple-element.117), channel_id=1, source_target_pairs={{1,0},{0,1},{3,2},{2,3},{5,4},{4,5},{7,6},{6,7},{9,8},{8,9},{11,10... | collective-permute-start | bytes 344072 | tf_op jit(solution)/shard_map/ppermute | solution.py:401
  37.9 16.5 %collective-permute-start.3 = (f32[136,128]{1,0:T(8,128)S(1)}, f32[136,128]{1,0:T(8,128)S(1)}, u32[]{:S(2)}, u32[]{:S(2)}) collective-permute-start(f32[136,128]{1,0:T(8,128)S(1)} %get-tuple-element.76), channel_id=1, source_target_pairs={{1,2},{2,1},{3,4},{4,3},{5,6},{6,5},{7,8},{8,7},{9,10},{10,9},{11,... | collective-permute-start | bytes 208904 | tf_op jit(solution)/shard_map/ppermute | solution.py:408
  47.4 3.1 %collective-permute-start.2 = (f32[4,32,128]{2,1,0:T(8,128)S(1)}, f32[4,32,128]{2,1,0:T(8,128)S(1)}, u32[]{:S(2)}, u32[]{:S(2)}) collective-permute-start(f32[4,32,128]{2,1,0:T(8,128)S(1)} %get-tuple-element.75), channel_id=1, source_target_pairs={{1,0},{0,1},{3,2},{2,3},{5,4},{4,5},{7,6},{6,7},{9,8},{8,9},{11,10... | collective-permute-start | bytes 196616 | tf_op jit(solution)/shard_map/ppermute | solution.py:401
  55.8 18.3 %collective-permute-start.5 = (f32[232,128]{1,0:T(8,128)S(1)}, f32[232,128]{1,0:T(8,128)S(1)}, u32[]{:S(2)}, u32[]{:S(2)}) collective-permute-start(f32[232,128]{1,0:T(8,128)S(1)} %get-tuple-element.79), channel_id=1, source_target_pairs={{1,2},{2,1},{3,4},{4,3},{5,6},{6,5},{7,8},{8,7},{9,10},{10,9},{11,... | collective-permute-start | bytes 356360 | tf_op jit(solution)/shard_map/ppermute | solution.py:408
  65.3 8.8 %collective-permute-start.4 = (f32[7,32,128]{2,1,0:T(8,128)S(1)}, f32[7,32,128]{2,1,0:T(8,128)S(1)}, u32[]{:S(2)}, u32[]{:S(2)}) collective-permute-start(f32[7,32,128]{2,1,0:T(8,128)S(1)} %get-tuple-element.78), channel_id=1, source_target_pairs={{1,0},{0,1},{3,2},{2,3},{5,4},{4,5},{7,6},{6,7},{9,8},{8,9},{11,10... | collective-permute-start | bytes 344072 | tf_op jit(solution)/shard_map/ppermute | solution.py:401
  67.2 22.2 %collective-permute-start.9 = (f32[232,128]{1,0:T(8,128)S(1)}, f32[232,128]{1,0:T(8,128)S(1)}, u32[]{:S(2)}, u32[]{:S(2)}) collective-permute-start(f32[232,128]{1,0:T(8,128)S(1)} %get-tuple-element.86), channel_id=1, source_target_pairs={{1,2},{2,1},{3,4},{4,3},{5,6},{6,5},{7,8},{8,7},{9,10},{10,9},{11,... | collective-permute-start | bytes 356360 | tf_op jit(solution)/shard_map/ppermute | solution.py:408
  75.6 17.0 %collective-permute-start.7 = (f32[232,128]{1,0:T(8,128)S(1)}, f32[232,128]{1,0:T(8,128)S(1)}, u32[]{:S(2)}, u32[]{:S(2)}) collective-permute-start(f32[232,128]{1,0:T(8,128)S(1)} %get-tuple-element.83), channel_id=1, source_target_pairs={{1,2},{2,1},{3,4},{4,3},{5,6},{6,5},{7,8},{8,7},{9,10},{10,9},{11,... | collective-permute-start | bytes 356360 | tf_op jit(solution)/shard_map/ppermute | solution.py:408
  85.1 4.3 %collective-permute-start.8 = (f32[7,32,128]{2,1,0:T(8,128)S(1)}, f32[7,32,128]{2,1,0:T(8,128)S(1)}, u32[]{:S(2)}, u32[]{:S(2)}) collective-permute-start(f32[7,32,128]{2,1,0:T(8,128)S(1)} %get-tuple-element.85), channel_id=1, source_target_pairs={{1,0},{0,1},{3,2},{2,3},{5,4},{4,5},{7,6},{6,7},{9,8},{8,9},{11,10... | collective-permute-start | bytes 344072 | tf_op jit(solution)/shard_map/ppermute | solution.py:401
  87.1 3.8 %collective-permute-start.6 = (f32[7,32,128]{2,1,0:T(8,128)S(1)}, f32[7,32,128]{2,1,0:T(8,128)S(1)}, u32[]{:S(2)}, u32[]{:S(2)}) collective-permute-start(f32[7,32,128]{2,1,0:T(8,128)S(1)} %get-tuple-element.82), channel_id=1, source_target_pairs={{1,0},{0,1},{3,2},{2,3},{5,4},{4,5},{7,6},{6,7},{9,8},{8,9},{11,10... | collective-permute-start | bytes 344072 | tf_op jit(solution)/shard_map/ppermute | solution.py:401
  94.2 17.2 %collective-permute-start.11 = (f32[232,128]{1,0:T(8,128)S(1)}, f32[232,128]{1,0:T(8,128)S(1)}, u32[]{:S(2)}, u32[]{:S(2)}) collective-permute-start(f32[232,128]{1,0:T(8,128)S(1)} %get-tuple-element.91), channel_id=1, source_target_pairs={{1,2},{2,1},{3,4},{4,3},{5,6},{6,5},{7,8},{8,7},{9,10},{10,9},{11,... | collective-permute-start | bytes 356360 | tf_op jit(solution)/shard_map/ppermute | solution.py:408
  103.6 3.2 %collective-permute-start.10 = (f32[7,32,128]{2,1,0:T(8,128)S(1)}, f32[7,32,128]{2,1,0:T(8,128)S(1)}, u32[]{:S(2)}, u32[]{:S(2)}) collective-permute-start(f32[7,32,128]{2,1,0:T(8,128)S(1)} %get-tuple-element.90), channel_id=1, source_target_pairs={{1,0},{0,1},{3,2},{2,3},{5,4},{4,5},{7,6},{6,7},{9,8},{8,9},{11,10... | collective-permute-start | bytes 344072 | tf_op jit(solution)/shard_map/ppermute | solution.py:401
  112.8 17.1 %collective-permute-start.13 = (f32[232,128]{1,0:T(8,128)S(1)}, f32[232,128]{1,0:T(8,128)S(1)}, u32[]{:S(2)}, u32[]{:S(2)}) collective-permute-start(f32[232,128]{1,0:T(8,128)S(1)} %get-tuple-element.95), channel_id=1, source_target_pairs={{1,2},{2,1},{3,4},{4,3},{5,6},{6,5},{7,8},{8,7},{9,10},{10,9},{11,... | collective-permute-start | bytes 356360 | tf_op jit(solution)/shard_map/ppermute | solution.py:408
  122.1 3.2 %collective-permute-start.12 = (f32[7,32,128]{2,1,0:T(8,128)S(1)}, f32[7,32,128]{2,1,0:T(8,128)S(1)}, u32[]{:S(2)}, u32[]{:S(2)}) collective-permute-start(f32[7,32,128]{2,1,0:T(8,128)S(1)} %get-tuple-element.94), channel_id=1, source_target_pairs={{1,0},{0,1},{3,2},{2,3},{5,4},{4,5},{7,6},{6,7},{9,8},{8,9},{11,10... | collective-permute-start | bytes 344072 | tf_op jit(solution)/shard_map/ppermute | solution.py:401
  131.3 16.5 %collective-permute-start.15 = (f32[136,128]{1,0:T(8,128)S(1)}, f32[136,128]{1,0:T(8,128)S(1)}, u32[]{:S(2)}, u32[]{:S(2)}) collective-permute-start(f32[136,128]{1,0:T(8,128)S(1)} %get-tuple-element.99), channel_id=1, source_target_pairs={{1,2},{2,1},{3,4},{4,3},{5,6},{6,5},{7,8},{8,7},{9,10},{10,9},{11,... | collective-permute-start | bytes 208904 | tf_op jit(solution)/shard_map/ppermute | solution.py:408
  140.5 3.4 %collective-permute-start.14 = (f32[4,32,128]{2,1,0:T(8,128)S(1)}, f32[4,32,128]{2,1,0:T(8,128)S(1)}, u32[]{:S(2)}, u32[]{:S(2)}) collective-permute-start(f32[4,32,128]{2,1,0:T(8,128)S(1)} %get-tuple-element.98), channel_id=1, source_target_pairs={{1,0},{0,1},{3,2},{2,3},{5,4},{4,5},{7,6},{6,7},{9,8},{8,9},{11,10... | collective-permute-start | bytes 196616 | tf_op jit(solution)/shard_map/ppermute | solution.py:401
  (2 other events, 1.4 us)
